TPU v7x, 256 devices: a whole 4x4x8 slice. The times are simulated.
256 devices in a mesh: context: 32 (over y, x, core), tensor: 8 (over z).
Axes of the slice: x: 4, y: 4, z: 8, core: 2. Of those that a mesh axis runs over, the one named last changes fastest.
Arguments:
- queries: bfloat16 [8192, 8192], P('context', 'tensor'), may hold values from -40 to 40
- keys: bfloat16 [8192, 1024], P('context', 'tensor'), may hold values from -6 to 6
- values: bfloat16 [8192, 1024], P('context', 'tensor'), may hold values from -6 to 6
- output_gradient: bfloat16 [8192, 8192], P('context', 'tensor'), may hold values from -6 to 6
- q_gain: float32 [128], replicated, may hold values from 0.5 to 5.5
- k_gain: float32 [128], replicated, may hold values from 0.5 to 5.5
- doc_ids: int32 [8192], P('context'), may hold values from 0 to 63, as said below
Outputs:
- attended: bfloat16 [8192, 8192], P('context', 'tensor')
- grad_queries: bfloat16 [8192, 8192], P('context', 'tensor')
- grad_keys: bfloat16 [8192, 1024], P('context', 'tensor')
- value_gradients: bfloat16 [8192, 1024], P('context', 'tensor')
- grad_q_gain: float32 [128], replicated
- grad_k_gain: float32 [128], replicated
Inputs may be any that keep to these rules, and one draw needn't show every extreme that they name: `doc_ids`: Non-decreasing along the pack; every one of the 64 documents holds 1 to 1024 consecutive tokens; document 0 holds at most 128 tokens, document 64 - 2 exactly 1024 and document 64 - 1 exactly 128.
All inputs are finite; a program needn't handle non-finite values.
Results may differ from a plain program's by a relative error of at most 0.024.
The roundings to bfloat16 on the way count: a program that leaves them out, or rounds other values in their place, can miss the bound.
Values may be sent and summed in bfloat16 or wider, within the bound.
No kernel may reach another device: no remote copies, remote signals or barrier semaphores. Data moves between devices by JAX's collectives and lax.ppermute only.
A program may use at most 64 MiB of HBM per device.

v0:
```python
import jax
import jax.numpy as jnp
from jax import lax
from jax.sharding import PartitionSpec as P

REACH = 4


THETA = 500000.0
EPSILON = 1e-06


def passed_along(block, axis, distance):
    devices = range(lax.axis_size(axis))
    route = [(i - distance, i) for i in devices if i - distance in devices]
    return lax.ppermute(block, axis, route)


def rotate(field, factor, position):
    head_size = field.shape[-1]
    halfway = head_size // 2
    normalized = (
        field * lax.rsqrt(jnp.mean(field * field, axis=-1, keepdims=True) + EPSILON) * factor
    )
    frequency = THETA ** (-(jnp.arange(halfway, dtype=jnp.float32) * 2.0 / head_size))
    angles = position.astype(jnp.float32)[:, None] * frequency[None, :]
    cosine = jnp.cos(angles)[:, None, :]
    sine_part = jnp.sin(angles)[:, None, :]
    leading = normalized[..., :halfway]
    second = normalized[..., halfway:]
    return jnp.concatenate(
        [leading * cosine - second * sine_part, second * cosine + leading * sine_part], axis=-1
    )


def offsets(window_ids):
    earlier = jnp.sum((window_ids[None, :] < window_ids[:, None]).astype(jnp.int32), axis=1)
    return jnp.arange(window_ids.shape[0], dtype=jnp.int32) - earlier


def body(queries, keys, values, output_gradient, q_gain, k_gain, doc_ids):
    row_count = queries.shape[0]
    head_size = q_gain.shape[0]
    heads_kv = keys.shape[1] // head_size
    query_group_count = queries.shape[1] // (heads_kv * head_size)
    window = (REACH + 1) * row_count
    marked = doc_ids + 1
    arrived = []
    for distance in range(1, REACH + 1):
        arrived.append(passed_along((keys, values, marked), "context", distance))
    arrived = arrived[::-1]
    window_ids = jnp.concatenate([received[2] for received in arrived] + [marked])
    position = offsets(window_ids)
    raw_keys = jnp.concatenate([received[0] for received in arrived] + [keys])
    raw_keys = raw_keys.reshape(window, heads_kv, head_size).astype(jnp.float32)
    key_hat = rotate(raw_keys, k_gain, position).astype(jnp.bfloat16)
    value_win = jnp.concatenate([received[1] for received in arrived] + [values])
    value_win = value_win.reshape(window, heads_kv, head_size)
    q_pos = position[-row_count:]
    q_raw = queries.reshape(row_count, heads_kv * query_group_count, head_size).astype(jnp.float32)
    normed_query = rotate(q_raw, q_gain, q_pos).astype(jnp.bfloat16)
    allowed = (window_ids[None, :] == marked[:, None]) & (
        jnp.arange(window)[None, :] <= REACH * row_count + jnp.arange(row_count)[:, None]
    )
    pair_count = heads_kv * query_group_count // 2
    half_group = query_group_count // 2
    q_pairs = normed_query.reshape(row_count, pair_count, 2, head_size).transpose(1, 0, 2, 3)
    d_pairs = output_gradient.reshape(row_count, pair_count, 2, head_size).transpose(1, 0, 2, 3)
    scaling = head_size ** (-0.5)

    def attend(carry, inputs):
        key_acc, value_running_sum = carry
        q_pair, d_pair, pair_index = inputs
        kv_index = pair_index // half_group
        key_one = lax.dynamic_index_in_dim(key_hat, kv_index, 1, keepdims=False)
        value_one = lax.dynamic_index_in_dim(value_win, kv_index, 1, keepdims=False)
        scores = (
            jnp.einsum("tgd,wd->gtw", q_pair, key_one, preferred_element_type=jnp.float32) * scaling
        )
        scores = jnp.where(allowed[None], scores, -1e30)
        highest = jnp.max(scores, axis=-1, keepdims=True)
        exponent = jnp.exp(scores - highest)
        weights = (exponent / jnp.sum(exponent, axis=-1, keepdims=True)).astype(jnp.bfloat16)
        attended = jnp.einsum("gtw,wd->tgd", weights, value_one, preferred_element_type=jnp.float32)
        d_weights = jnp.einsum("tgd,wd->gtw", d_pair, value_one, preferred_element_type=jnp.float32)
        weights_wide = weights.astype(jnp.float32)
        center = jnp.sum(weights_wide * d_weights, axis=-1, keepdims=True)
        d_scores = (weights_wide * (d_weights - center)).astype(jnp.bfloat16)
        d_query = (
            jnp.einsum("gtw,wd->tgd", d_scores, key_one, preferred_element_type=jnp.float32)
            * scaling
        )
        d_key = (
            jnp.einsum("gtw,tgd->wd", d_scores, q_pair, preferred_element_type=jnp.float32)
            * scaling
        )
        d_value = jnp.einsum("gtw,tgd->wd", weights, d_pair, preferred_element_type=jnp.float32)
        key_acc = key_acc.at[:, kv_index].add(d_key)
        value_running_sum = value_running_sum.at[:, kv_index].add(d_value)
        return ((key_acc, value_running_sum), (attended.astype(jnp.bfloat16), d_query))

    blank_block = jnp.zeros((window, heads_kv, head_size), jnp.float32)
    (key_grad, value_grad), (attended, d_query) = lax.scan(
        attend,
        (blank_block, blank_block),
        (q_pairs, d_pairs, jnp.arange(pair_count, dtype=jnp.int32)),
    )
    attended = attended.transpose(1, 0, 2, 3).reshape(
        row_count, heads_kv * query_group_count * head_size
    )
    d_query = d_query.transpose(1, 0, 2, 3).reshape(
        row_count, heads_kv * query_group_count, head_size
    )
    _, q_pullback = jax.vjp(lambda field, factor: rotate(field, factor, q_pos), q_raw, q_gain)
    query_gradient, q_gain_term = q_pullback(d_query)
    _, k_pullback = jax.vjp(lambda field, factor: rotate(field, factor, position), raw_keys, k_gain)
    key_terms, k_gain_term = k_pullback(key_grad)
    key_blocks = key_terms.reshape(REACH + 1, row_count, heads_kv * head_size)
    value_blocks = value_grad.reshape(REACH + 1, row_count, heads_kv * head_size)
    key_sum = key_blocks[REACH]
    value_sum = value_blocks[REACH]
    for distance in range(1, REACH + 1):
        returned = passed_along(
            (key_blocks[REACH - distance], value_blocks[REACH - distance]), "context", -distance
        )
        key_sum = key_sum + returned[0]
        value_sum = value_sum + returned[1]
    q_total, k_total = lax.psum((q_gain_term, k_gain_term), ("context", "tensor"))
    return (
        attended,
        query_gradient.reshape(row_count, -1).astype(jnp.bfloat16),
        key_sum.astype(jnp.bfloat16),
        value_sum.astype(jnp.bfloat16),
        q_total,
        k_total,
    )


def solution(mesh):
    placed = (
        P("context", "tensor"),
        P("context", "tensor"),
        P("context", "tensor"),
        P("context", "tensor"),
        P(),
        P(),
        P("context"),
    )
    return jax.shard_map(
        body,
        mesh=mesh,
        in_specs=placed,
        out_specs=(
            P("context", "tensor"),
            P("context", "tensor"),
            P("context", "tensor"),
            P("context", "tensor"),
            P(),
            P(),
        ),
        check_vma=False,
    )
```

profile of v0, /device:TPU:1, one launch (start us, length us, event | category | flops | bytes accessed | tf_op | source)
XLA Modules:
  0.0 267.0 jit_solution(9186621964168429853)
XLA Ops:
  1.3 5.5 %collective-permute-start = (s32[256]{0:T(256)S(1)}, s32[256]{0:T(256)S(1)}, u32[]{:S(2)}, u32[]{:S(2)}) collective-permute-start(s32[256]{0:T(256)S(1)} %broadcast_add_fusion), channel_id=1, source_target_pairs={{0,32},{8,40},{16,48},{24,56},{32,64},{40,72},{48,80},{56,88},{64,... | collective-permute-start | bytes 3080 | tf_op jit(solution)/shard_map/ppermute | solution.py:16
  6.8 4.0 %collective-permute-start.1 = (s32[256]{0:T(256)S(1)}, s32[256]{0:T(256)S(1)}, u32[]{:S(2)}, u32[]{:S(2)}) collective-permute-start(s32[256]{0:T(256)S(1)} %broadcast_add_fusion), channel_id=1, source_target_pairs={{0,24},{8,32},{16,40},{24,48},{32,56},{40,64},{48,72},{56,80},{64,... | collective-permute-start | bytes 3080 | tf_op jit(solution)/shard_map/ppermute | solution.py:16
  10.8 3.1 %collective-permute-start.2 = (s32[256]{0:T(256)S(1)}, s32[256]{0:T(256)S(1)}, u32[]{:S(2)}, u32[]{:S(2)}) collective-permute-start(s32[256]{0:T(256)S(1)} %broadcast_add_fusion), channel_id=1, source_target_pairs={{0,16},{8,24},{16,32},{24,40},{32,48},{40,56},{48,64},{56,72},{64,... | collective-permute-start | bytes 3080 | tf_op jit(solution)/shard_map/ppermute | solution.py:16
  15.9 5.2 %collective-permute-start.4 = (bf16[256,128]{1,0:T(8,128)(2,1)}, bf16[256,128]{1,0:T(8,128)(2,1)}, u32[]{:S(2)}, u32[]{:S(2)}) collective-permute-start(bf16[256,128]{1,0:T(8,128)(2,1)} %param.14), channel_id=1, source_target_pairs={{0,32},{8,40},{16,48},{24,56},{32,64},{40,72},{48,80},{56,88},{64,... | collective-permute-start | bytes 196616 | tf_op jit(solution)/shard_map/ppermute | solution.py:16
  25.3 3.2 %collective-permute-start.5 = (bf16[256,128]{1,0:T(8,128)(2,1)}, bf16[256,128]{1,0:T(8,128)(2,1)S(1)}, u32[]{:S(2)}, u32[]{:S(2)}) collective-permute-start(bf16[256,128]{1,0:T(8,128)(2,1)} %param.14), channel_id=1, source_target_pairs={{0,24},{8,32},{16,40},{24,48},{32,56},{40,64},{48,72},{56,80},{64,... | collective-permute-start | bytes 196616 | tf_op jit(solution)/shard_map/ppermute | solution.py:16
  28.6 3.1 %collective-permute-start.6 = (bf16[256,128]{1,0:T(8,128)(2,1)}, bf16[256,128]{1,0:T(8,128)(2,1)S(1)}, u32[]{:S(2)}, u32[]{:S(2)}) collective-permute-start(bf16[256,128]{1,0:T(8,128)(2,1)} %param.14), channel_id=1, source_target_pairs={{0,16},{8,24},{16,32},{24,40},{32,48},{40,56},{48,64},{56,72},{64,... | collective-permute-start | bytes 196616 | tf_op jit(solution)/shard_map/ppermute | solution.py:16
  31.7 2.7 %collective-permute-start.7 = (bf16[256,128]{1,0:T(8,128)(2,1)}, bf16[256,128]{1,0:T(8,128)(2,1)S(1)}, u32[]{:S(2)}, u32[]{:S(2)}) collective-permute-start(bf16[256,128]{1,0:T(8,128)(2,1)} %param.14), channel_id=1, source_target_pairs={{0,8},{8,16},{16,24},{24,32},{32,40},{40,48},{48,56},{56,64},{64,7... | collective-permute-start | bytes 196616 | tf_op jit(solution)/shard_map/ppermute | solution.py:16
  34.4 3.6 %collective-permute-start.8 = (bf16[256,128]{1,0:T(8,128)(2,1)}, bf16[256,128]{1,0:T(8,128)(2,1)S(1)}, u32[]{:S(2)}, u32[]{:S(2)}) collective-permute-start(bf16[256,128]{1,0:T(8,128)(2,1)} %param.15), channel_id=1, source_target_pairs={{0,32},{8,40},{16,48},{24,56},{32,64},{40,72},{48,80},{56,88},{64,... | collective-permute-start | bytes 196616 | tf_op jit(solution)/shard_map/ppermute | solution.py:16
  41.2 3.8 %collective-permute-start.9 = (bf16[256,128]{1,0:T(8,128)(2,1)}, bf16[256,128]{1,0:T(8,128)(2,1)S(1)}, u32[]{:S(2)}, u32[]{:S(2)}) collective-permute-start(bf16[256,128]{1,0:T(8,128)(2,1)} %param.15), channel_id=1, source_target_pairs={{0,24},{8,32},{16,40},{24,48},{32,56},{40,64},{48,72},{56,80},{64,... | collective-permute-start | bytes 196616 | tf_op jit(solution)/shard_map/ppermute | solution.py:16
  45.9 2.8 %collective-permute-start.10 = (bf16[256,128]{1,0:T(8,128)(2,1)}, bf16[256,128]{1,0:T(8,128)(2,1)S(1)}, u32[]{:S(2)}, u32[]{:S(2)}) collective-permute-start(bf16[256,128]{1,0:T(8,128)(2,1)} %param.15), channel_id=1, source_target_pairs={{0,16},{8,24},{16,32},{24,40},{32,48},{40,56},{48,64},{56,72},{64,... | collective-permute-start | bytes 196616 | tf_op jit(solution)/shard_map/ppermute | solution.py:16
  48.8 3.1 %collective-permute-start.11 = (bf16[256,128]{1,0:T(8,128)(2,1)}, bf16[256,128]{1,0:T(8,128)(2,1)S(1)}, u32[]{:S(2)}, u32[]{:S(2)}) collective-permute-start(bf16[256,128]{1,0:T(8,128)(2,1)} %param.15), channel_id=1, source_target_pairs={{0,8},{8,16},{16,24},{24,32},{32,40},{40,48},{48,56},{56,64},{64,7... | collective-permute-start | bytes 196616 | tf_op jit(solution)/shard_map/ppermute | solution.py:16
  54.7 3.0 %fusion.64 = (bf16[1280,1,64]{2,0,1:T(8,128)(2,1)S(1)}, bf16[1280,1,64]{2,0,1:T(8,128)(2,1)S(1)}) fusion(f32[1280,1,128]{2,0,1:T(8,128)S(1)} %fusion.61, f32[64]{0:T(128)S(1)} %copy-done.28, f32[1280]{0:T(1024)S(1)} %get-tuple-element.329), kind=kLoop, calls=%fused_computation.84 | loop fusion | flops 737280 | bytes 988416 | tf_op jit(solution)/shard_map/convert.1
  58.6 81.2 %while.21 = (s32[]{:T(128)}, f32[1280,1,128]{2,0,1:T(8,128)S(1)}, f32[1280,1,128]{2,0,1:T(8,128)}, bf16[4,256,2,128]{3,1,2,0:T(8,128)(2,1)}, f32[4,256,2,128]{3,...) while((s32[]{:T(128)}, f32[1280,1,128]{2,0,1:T(8,128)S(1)}, ...), condition=%wide.region_8.9_spmd.clone, body=%wide.region_3.8_spmd.clone.sunk | while | flops 1017414400 | bytes 32001016 | solution.py:103
  59.1 3.6 %fusion.122 = (f32[2,256]{1,0:T(2,128)S(1)}, f32[2,256,1280]{2,1,0:T(8,128)}) fusion(pred[256,1280]{1,0:T(8,128)(4,1)S(1)} %fusion.121, bf16[1280,1,128]{2,0,1:T(8,128)(2,1)} %get-tuple-element.467, bf16[4,256,2,128]{3,1,2,0:T(8,128)(2,1)} %get-tuple-element.466, s32[]{:T(128)} %get-tuple-element.441), kind=kOutput, calls=%fused_computation.143.clone.1 | convolution fusion | flops 170394880 | bytes 3410432 | tf_op jit(solution)/shard_map/while/body/eval_jaxpr/sub | solution.py:82
  62.8 2.5 fusion.123
  74.5 3.1 %fusion.126 = f32[1280,1,128]{2,0,1:T(8,128)} fusion(bf16[2,256,1280]{2,1,0:T(8,128)(2,1)S(1)} %get-tuple-element.419, f32[1280,1,128]{2,0,1:T(8,128)} %get-tuple-element.443, pred[]{:T(512)S(6)} %compare.41, pred[]{:T(512)} %and_reduce_fusion.2, bf16[4,256,2,128]{1,3,2,0:T(8,128)(2,1)} %copy-done.7, s32[]{:T(128)} %get-tuple-element.441), kind=kOutput, calls=%fused_computation.15.clone.1 | convolution fusion | flops 168263680 | bytes 2753537 | tf_op jit(solution)/shard_map/while/body/eval_jaxpr/gtw,tgd->wd/dot_general | solution.py:97
  79.2 3.6 %fusion.122 = (f32[2,256]{1,0:T(2,128)S(1)}, f32[2,256,1280]{2,1,0:T(8,128)}) fusion(pred[256,1280]{1,0:T(8,128)(4,1)S(1)} %fusion.121, bf16[1280,1,128]{2,0,1:T(8,128)(2,1)} %get-tuple-element.467, bf16[4,256,2,128]{3,1,2,0:T(8,128)(2,1)} %get-tuple-element.466, s32[]{:T(128)} %get-tuple-element.441), kind=kOutput, calls=%fused_computation.143.clone.1 | convolution fusion | flops 170394880 | bytes 3410432 | tf_op jit(solution)/shard_map/while/body/eval_jaxpr/sub | solution.py:82
  82.8 2.5 fusion.123
  92.2 2.4 fusion.125
  94.6 3.3 %fusion.126 = f32[1280,1,128]{2,0,1:T(8,128)} fusion(bf16[2,256,1280]{2,1,0:T(8,128)(2,1)S(1)} %get-tuple-element.419, f32[1280,1,128]{2,0,1:T(8,128)} %get-tuple-element.443, pred[]{:T(512)S(6)} %compare.41, pred[]{:T(512)} %and_reduce_fusion.2, bf16[4,256,2,128]{1,3,2,0:T(8,128)(2,1)} %copy-done.7, s32[]{:T(128)} %get-tuple-element.441), kind=kOutput, calls=%fused_computation.15.clone.1 | convolution fusion | flops 168263680 | bytes 2753537 | tf_op jit(solution)/shard_map/while/body/eval_jaxpr/gtw,tgd->wd/dot_general | solution.py:97
  99.6 3.6 %fusion.122 = (f32[2,256]{1,0:T(2,128)S(1)}, f32[2,256,1280]{2,1,0:T(8,128)}) fusion(pred[256,1280]{1,0:T(8,128)(4,1)S(1)} %fusion.121, bf16[1280,1,128]{2,0,1:T(8,128)(2,1)} %get-tuple-element.467, bf16[4,256,2,128]{3,1,2,0:T(8,128)(2,1)} %get-tuple-element.466, s32[]{:T(128)} %get-tuple-element.441), kind=kOutput, calls=%fused_computation.143.clone.1 | convolution fusion | flops 170394880 | bytes 3410432 | tf_op jit(solution)/shard_map/while/body/eval_jaxpr/sub | solution.py:82
  103.2 2.5 fusion.123
  112.6 2.4 fusion.125
  115.0 3.3 %fusion.126 = f32[1280,1,128]{2,0,1:T(8,128)} fusion(bf16[2,256,1280]{2,1,0:T(8,128)(2,1)S(1)} %get-tuple-element.419, f32[1280,1,128]{2,0,1:T(8,128)} %get-tuple-element.443, pred[]{:T(512)S(6)} %compare.41, pred[]{:T(512)} %and_reduce_fusion.2, bf16[4,256,2,128]{1,3,2,0:T(8,128)(2,1)} %copy-done.7, s32[]{:T(128)} %get-tuple-element.441), kind=kOutput, calls=%fused_computation.15.clone.1 | convolution fusion | flops 168263680 | bytes 2753537 | tf_op jit(solution)/shard_map/while/body/eval_jaxpr/gtw,tgd->wd/dot_general | solution.py:97
  120.0 3.6 %fusion.122 = (f32[2,256]{1,0:T(2,128)S(1)}, f32[2,256,1280]{2,1,0:T(8,128)}) fusion(pred[256,1280]{1,0:T(8,128)(4,1)S(1)} %fusion.121, bf16[1280,1,128]{2,0,1:T(8,128)(2,1)} %get-tuple-element.467, bf16[4,256,2,128]{3,1,2,0:T(8,128)(2,1)} %get-tuple-element.466, s32[]{:T(128)} %get-tuple-element.441), kind=kOutput, calls=%fused_computation.143.clone.1 | convolution fusion | flops 170394880 | bytes 3410432 | tf_op jit(solution)/shard_map/while/body/eval_jaxpr/sub | solution.py:82
  123.6 2.5 fusion.123
  133.0 2.4 fusion.125
  135.4 3.3 %fusion.126 = f32[1280,1,128]{2,0,1:T(8,128)} fusion(bf16[2,256,1280]{2,1,0:T(8,128)(2,1)S(1)} %get-tuple-element.419, f32[1280,1,128]{2,0,1:T(8,128)} %get-tuple-element.443, pred[]{:T(512)S(6)} %compare.41, pred[]{:T(512)} %and_reduce_fusion.2, bf16[4,256,2,128]{1,3,2,0:T(8,128)(2,1)} %copy-done.7, s32[]{:T(128)} %get-tuple-element.441), kind=kOutput, calls=%fused_computation.15.clone.1 | convolution fusion | flops 168263680 | bytes 2753537 | tf_op jit(solution)/shard_map/while/body/eval_jaxpr/gtw,tgd->wd/dot_general | solution.py:97
  139.9 3.0 %fusion.67 = (f32[1280,1,64]{2,0,1:T(8,128)S(1)}, f32[1280,1,64]{2,0,1:T(8,128)S(1)}) fusion(f32[1280,1,128]{2,0,1:T(8,128)S(1)} %get-tuple-element.173, f32[64]{0:T(128)S(1)} %copy-done.29, f32[1280]{0:T(1024)S(1)} %copy-done.17), kind=kLoop, calls=%fused_computation.87 | loop fusion | flops 655360 | bytes 1316096 | tf_op jit(solution)/shard_map/transpose(jvp())/add_any | solution.py:32
  166.4 86.1 %all-reduce.4 = (f32[128]{0:T(128)}, f32[128]{0:T(128)}) all-reduce(f32[128]{0:T(128)S(1)} %get-tuple-element.274, f32[128]{0:T(128)S(1)} %copy-done.31), channel_id=1, replica_groups=mesh['context'=32,'tensor'=8] {'context','tensor'}, use_global_device_ids=true, to_apply=%region_12.13 | all-reduce | flops 256 | bytes 2048 | tf_op jit(solution)/shard_map/psum | solution.py:128
  258.3 3.3 %collective-permute-done.14 = f32[256,128]{1,0:T(8,128)S(1)} collective-permute-done((f32[256,128]{1,0:T(8,128)S(1)}, f32[256,128]{1,0:T(8,128)S(1)}, u32[]{:S(2)}, u32[]{:S(2)}) %collective-permute-start.14) | collective-permute-done | bytes 131104 | tf_op jit(solution)/shard_map/ppermute | solution.py:16
  261.6 3.8 %collective-permute-done.15 = f32[256,128]{1,0:T(8,128)S(1)} collective-permute-done((f32[256,128]{1,0:T(8,128)S(1)}, f32[256,128]{1,0:T(8,128)S(1)}, u32[]{:S(2)}, u32[]{:S(2)}) %collective-permute-start.15) | collective-permute-done | bytes 131104 | tf_op jit(solution)/shard_map/ppermute | solution.py:16
  (201 shorter events, 70.0 us)
Async XLA Ops:
  0.6 23.0 %copy-start.25 = (f32[128]{0:T(128)S(1)}, f32[128]{0:T(128)}, u32[]{:S(2)}) copy-start(f32[128]{0:T(128)} %param.17) | copy-start | bytes 1540
  1.3 22.6 %copy-start.20 = (s32[256]{0:T(256)}, s32[256]{0:T(256)S(1)}, u32[]{:S(2)}) copy-start(s32[256]{0:T(256)S(1)} %broadcast_add_fusion) | copy-start | bytes 3076
  1.3 24.0 %collective-permute-start = (s32[256]{0:T(256)S(1)}, s32[256]{0:T(256)S(1)}, u32[]{:S(2)}, u32[]{:S(2)}) collective-permute-start(s32[256]{0:T(256)S(1)} %broadcast_add_fusion), channel_id=1, source_target_pairs={{0,32},{8,40},{16,48},{24,56},{32,64},{40,72},{48,80},{56,88},{64,... | collective-permute-start | bytes 3080 | tf_op jit(solution)/shard_map/ppermute | solution.py:16
  6.8 21.8 %collective-permute-start.1 = (s32[256]{0:T(256)S(1)}, s32[256]{0:T(256)S(1)}, u32[]{:S(2)}, u32[]{:S(2)}) collective-permute-start(s32[256]{0:T(256)S(1)} %broadcast_add_fusion), channel_id=1, source_target_pairs={{0,24},{8,32},{16,40},{24,48},{32,56},{40,64},{48,72},{56,80},{64,... | collective-permute-start | bytes 3080 | tf_op jit(solution)/shard_map/ppermute | solution.py:16
  10.8 20.9 %collective-permute-start.2 = (s32[256]{0:T(256)S(1)}, s32[256]{0:T(256)S(1)}, u32[]{:S(2)}, u32[]{:S(2)}) collective-permute-start(s32[256]{0:T(256)S(1)} %broadcast_add_fusion), channel_id=1, source_target_pairs={{0,16},{8,24},{16,32},{24,40},{32,48},{40,56},{48,64},{56,72},{64,... | collective-permute-start | bytes 3080 | tf_op jit(solution)/shard_map/ppermute | solution.py:16
  13.9 20.5 %collective-permute-start.3 = (s32[256]{0:T(256)S(1)}, s32[256]{0:T(256)S(1)}, u32[]{:S(2)}, u32[]{:S(2)}) collective-permute-start(s32[256]{0:T(256)S(1)} %broadcast_add_fusion), channel_id=1, source_target_pairs={{0,8},{8,16},{16,24},{24,32},{32,40},{40,48},{48,56},{56,64},{64,7... | collective-permute-start | bytes 3080 | tf_op jit(solution)/shard_map/ppermute | solution.py:16
  15.9 25.4 %collective-permute-start.4 = (bf16[256,128]{1,0:T(8,128)(2,1)}, bf16[256,128]{1,0:T(8,128)(2,1)}, u32[]{:S(2)}, u32[]{:S(2)}) collective-permute-start(bf16[256,128]{1,0:T(8,128)(2,1)} %param.14), channel_id=1, source_target_pairs={{0,32},{8,40},{16,48},{24,56},{32,64},{40,72},{48,80},{56,88},{64,... | collective-permute-start | bytes 196616 | tf_op jit(solution)/shard_map/ppermute | solution.py:16
  23.0 16.9 %copy-start = (f32[32,8,8,128]{3,2,1,0:T(8,128)}, f32[32,8,8,128]{3,2,1,0:T(8,128)S(1)}, u32[]{:S(2)}) copy-start(f32[32,8,8,128]{3,2,1,0:T(8,128)S(1)} %copy.67) | copy-start | bytes 3145732
  23.0 15.0 %copy-start.30 = (s32[256]{0:T(256)S(1)}, s32[256]{0:T(256)}, u32[]{:S(2)}) copy-start(s32[256]{0:T(256)} %param.19) | copy-start | bytes 3076
  24.0 16.1 %copy-start.27 = (f32[64]{0:T(128)}, f32[64]{0:T(128)S(1)}, u32[]{:S(2)}) copy-start(f32[64]{0:T(128)S(1)} %negate_power_fusion) | copy-start | bytes 772
  25.3 20.6 %collective-permute-start.5 = (bf16[256,128]{1,0:T(8,128)(2,1)}, bf16[256,128]{1,0:T(8,128)(2,1)S(1)}, u32[]{:S(2)}, u32[]{:S(2)}) collective-permute-start(bf16[256,128]{1,0:T(8,128)(2,1)} %param.14), channel_id=1, source_target_pairs={{0,24},{8,32},{16,40},{24,48},{32,56},{40,64},{48,72},{56,80},{64,... | collective-permute-start | bytes 196616 | tf_op jit(solution)/shard_map/ppermute | solution.py:16
  28.6 20.2 %collective-permute-start.6 = (bf16[256,128]{1,0:T(8,128)(2,1)}, bf16[256,128]{1,0:T(8,128)(2,1)S(1)}, u32[]{:S(2)}, u32[]{:S(2)}) collective-permute-start(bf16[256,128]{1,0:T(8,128)(2,1)} %param.14), channel_id=1, source_target_pairs={{0,16},{8,24},{16,32},{24,40},{32,48},{40,56},{48,64},{56,72},{64,... | collective-permute-start | bytes 196616 | tf_op jit(solution)/shard_map/ppermute | solution.py:16
  31.7 20.2 %collective-permute-start.7 = (bf16[256,128]{1,0:T(8,128)(2,1)}, bf16[256,128]{1,0:T(8,128)(2,1)S(1)}, u32[]{:S(2)}, u32[]{:S(2)}) collective-permute-start(bf16[256,128]{1,0:T(8,128)(2,1)} %param.14), channel_id=1, source_target_pairs={{0,8},{8,16},{16,24},{24,32},{32,40},{40,48},{48,56},{56,64},{64,7... | collective-permute-start | bytes 196616 | tf_op jit(solution)/shard_map/ppermute | solution.py:16
  34.4 18.7 %collective-permute-start.8 = (bf16[256,128]{1,0:T(8,128)(2,1)}, bf16[256,128]{1,0:T(8,128)(2,1)S(1)}, u32[]{:S(2)}, u32[]{:S(2)}) collective-permute-start(bf16[256,128]{1,0:T(8,128)(2,1)} %param.15), channel_id=1, source_target_pairs={{0,32},{8,40},{16,48},{24,56},{32,64},{40,72},{48,80},{56,88},{64,... | collective-permute-start | bytes 196616 | tf_op jit(solution)/shard_map/ppermute | solution.py:16
  38.8 15.8 %copy-start.16 = (f32[1280]{0:T(1024)}, f32[1280]{0:T(1024)S(1)}, u32[]{:S(2)}) copy-start(f32[1280]{0:T(1024)S(1)} %get-tuple-element.329) | copy-start | bytes 15364
  40.0 14.6 %copy-start.28 = (f32[64]{0:T(128)S(1)}, f32[64]{0:T(128)}, u32[]{:S(2)}) copy-start(f32[64]{0:T(128)} %copy-done.27) | copy-start | bytes 772
  41.2 11.9 %collective-permute-start.9 = (bf16[256,128]{1,0:T(8,128)(2,1)}, bf16[256,128]{1,0:T(8,128)(2,1)S(1)}, u32[]{:S(2)}, u32[]{:S(2)}) collective-permute-start(bf16[256,128]{1,0:T(8,128)(2,1)} %param.15), channel_id=1, source_target_pairs={{0,24},{8,32},{16,40},{24,48},{32,56},{40,64},{48,72},{56,80},{64,... | collective-permute-start | bytes 196616 | tf_op jit(solution)/shard_map/ppermute | solution.py:16
  45.9 7.2 %collective-permute-start.10 = (bf16[256,128]{1,0:T(8,128)(2,1)}, bf16[256,128]{1,0:T(8,128)(2,1)S(1)}, u32[]{:S(2)}, u32[]{:S(2)}) collective-permute-start(bf16[256,128]{1,0:T(8,128)(2,1)} %param.15), channel_id=1, source_target_pairs={{0,16},{8,24},{16,32},{24,40},{32,48},{40,56},{48,64},{56,72},{64,... | collective-permute-start | bytes 196616 | tf_op jit(solution)/shard_map/ppermute | solution.py:16
  48.8 4.8 %collective-permute-start.11 = (bf16[256,128]{1,0:T(8,128)(2,1)}, bf16[256,128]{1,0:T(8,128)(2,1)S(1)}, u32[]{:S(2)}, u32[]{:S(2)}) collective-permute-start(bf16[256,128]{1,0:T(8,128)(2,1)} %param.15), channel_id=1, source_target_pairs={{0,8},{8,16},{16,24},{24,32},{32,40},{40,48},{48,56},{56,64},{64,7... | collective-permute-start | bytes 196616 | tf_op jit(solution)/shard_map/ppermute | solution.py:16
  58.6 81.3 %copy-start.17 = (f32[1280]{0:T(1024)S(1)}, f32[1280]{0:T(1024)}, u32[]{:S(2)}) copy-start(f32[1280]{0:T(1024)} %copy-done.16) | copy-start | bytes 15364
  58.6 81.3 %copy-start.29 = (f32[64]{0:T(128)S(1)}, f32[64]{0:T(128)}, u32[]{:S(2)}) copy-start(f32[64]{0:T(128)} %copy-done.27) | copy-start | bytes 772
  146.7 105.7 %collective-permute-start.16 = (f32[256,128]{1,0:T(8,128)}, f32[256,128]{1,0:T(8,128)}, u32[]{:S(2)}, u32[]{:S(2)}) collective-permute-start(f32[256,128]{1,0:T(8,128)} %get-tuple-element.321), channel_id=1, source_target_pairs={{8,0},{16,8},{24,16},{32,24},{40,32},{48,40},{56,48},{64,56},{72,6... | collective-permute-start | bytes 393224 | tf_op jit(solution)/shard_map/ppermute | solution.py:16
  148.8 105.0 %collective-permute-start.17 = (f32[256,128]{1,0:T(8,128)}, f32[256,128]{1,0:T(8,128)}, u32[]{:S(2)}, u32[]{:S(2)}) collective-permute-start(f32[256,128]{1,0:T(8,128)} %get-tuple-element.322), channel_id=1, source_target_pairs={{16,0},{24,8},{32,16},{40,24},{48,32},{56,40},{64,48},{72,56},{80,... | collective-permute-start | bytes 393224 | tf_op jit(solution)/shard_map/ppermute | solution.py:16
  150.1 105.0 %collective-permute-start.18 = (f32[256,128]{1,0:T(8,128)}, f32[256,128]{1,0:T(8,128)}, u32[]{:S(2)}, u32[]{:S(2)}) collective-permute-start(f32[256,128]{1,0:T(8,128)} %get-tuple-element.324), channel_id=1, source_target_pairs={{24,0},{32,8},{40,16},{48,24},{56,32},{64,40},{72,48},{80,56},{88,... | collective-permute-start | bytes 393224 | tf_op jit(solution)/shard_map/ppermute | solution.py:16
  151.4 105.0 %collective-permute-start.19 = (f32[256,128]{1,0:T(8,128)}, f32[256,128]{1,0:T(8,128)}, u32[]{:S(2)}, u32[]{:S(2)}) collective-permute-start(f32[256,128]{1,0:T(8,128)} %get-tuple-element.323), channel_id=1, source_target_pairs={{32,0},{40,8},{48,16},{56,24},{64,32},{72,40},{80,48},{88,56},{96,... | collective-permute-start | bytes 393224 | tf_op jit(solution)/shard_map/ppermute | solution.py:16
  155.3 103.0 %collective-permute-start.12 = (f32[256,128]{1,0:T(8,128)}, f32[256,128]{1,0:T(8,128)}, u32[]{:S(2)}, u32[]{:S(2)}) collective-permute-start(f32[256,128]{1,0:T(8,128)} %get-tuple-element.325), channel_id=1, source_target_pairs={{8,0},{16,8},{24,16},{32,24},{40,32},{48,40},{56,48},{64,56},{72,6... | collective-permute-start | bytes 393224 | tf_op jit(solution)/shard_map/ppermute | solution.py:16
  162.7 89.8 %copy-start.15 = (f32[256,128]{1,0:T(8,128)S(1)}, f32[256,128]{1,0:T(8,128)}, u32[]{:S(2)}) copy-start(f32[256,128]{1,0:T(8,128)} %get-tuple-element.328) | copy-start | bytes 393220
  162.7 91.1 %copy-start.14 = (f32[256,128]{1,0:T(8,128)S(1)}, f32[256,128]{1,0:T(8,128)}, u32[]{:S(2)}) copy-start(f32[256,128]{1,0:T(8,128)} %get-tuple-element.327) | copy-start | bytes 393220
  162.7 92.4 %copy-start.13 = (f32[256,128]{1,0:T(8,128)S(1)}, f32[256,128]{1,0:T(8,128)}, u32[]{:S(2)}) copy-start(f32[256,128]{1,0:T(8,128)} %get-tuple-element.326) | copy-start | bytes 393220
  252.5 5.8 %collective-permute-start.13 = (f32[256,128]{1,0:T(8,128)S(1)}, f32[256,128]{1,0:T(8,128)S(1)}, u32[]{:S(2)}, u32[]{:S(2)}) collective-permute-start(f32[256,128]{1,0:T(8,128)S(1)} %copy-done.15), channel_id=1, source_target_pairs={{16,0},{24,8},{32,16},{40,24},{48,32},{56,40},{64,48},{72,56},{80,... | collective-permute-start | bytes 393224 | tf_op jit(solution)/shard_map/ppermute | solution.py:16
  253.8 7.8 %collective-permute-start.14 = (f32[256,128]{1,0:T(8,128)S(1)}, f32[256,128]{1,0:T(8,128)S(1)}, u32[]{:S(2)}, u32[]{:S(2)}) collective-permute-start(f32[256,128]{1,0:T(8,128)S(1)} %copy-done.14), channel_id=1, source_target_pairs={{24,0},{32,8},{40,16},{48,24},{56,32},{64,40},{72,48},{80,56},{88,... | collective-permute-start | bytes 393224 | tf_op jit(solution)/shard_map/ppermute | solution.py:16
  255.1 10.3 %collective-permute-start.15 = (f32[256,128]{1,0:T(8,128)S(1)}, f32[256,128]{1,0:T(8,128)S(1)}, u32[]{:S(2)}, u32[]{:S(2)}) collective-permute-start(f32[256,128]{1,0:T(8,128)S(1)} %copy-done.13), channel_id=1, source_target_pairs={{32,0},{40,8},{48,16},{56,24},{64,32},{72,40},{80,48},{88,56},{96,... | collective-permute-start | bytes 393224 | tf_op jit(solution)/shard_map/ppermute | solution.py:16
  (32 other events, 168.0 us)
where the time goes:
time: 270 us; the launch traced here: 267 us
  blocking collectives  86.1 us (32%)
  matrix products  60.5 us (22%)
  starting transfers between devices  54 us (20%)
  other arithmetic  29.2 us (11%)
  local copies, waits for them, and re-layouts  16.8 us (6%)
  loops' own time  11.4 us (4%)
  waiting for transfers between devices  7.51 us (3%)
    psum x1, blocking collectives, body(): lax.psum((q_gain_term, k_gain_term), ('context', 'tensor'))  86.1 us
    ppermute x20, starting transfers between devices, passed_along(): return lax.ppermute(block, axis, route)  54 us
    sub x4, matrix products, attend(): exponent = jnp.exp(scores - highest)  14.4 us
    dot_general x4, matrix products, attend(): jnp.einsum('gtw,tgd->wd', weights, d_pair, preferred_element_type=jnp.flo...  13.1 us
    another operation x1, loops' own time, body(): lax.scan(attend, (blank_block, blank_block), (q_pairs, d_pairs, jnp.arang...  11.4 us
    dot_general x4, matrix products, attend(): jnp.einsum('tgd,wd->gtw', d_pair, value_one, preferred_element_type=jnp.f...  10 us
    dot_general x4, matrix products, attend(): jnp.einsum('gtw,tgd->wd', d_scores, q_pair, preferred_element_type=jnp.fl...  9.65 us
    dot_general x4, matrix products, attend(): jnp.einsum('gtw,wd->tgd', d_scores, key_one, preferred_element_type=jnp.f...  8.76 us
  transfers between devices with their start and end apart: 20, of which 3 were waited for; matrix products, arithmetic and copies ran while one was open for 8% of the time, Pallas kernels for 0%

commit v1 on v0

v1 whole, which is shorter than its diff:
```python
import functools

import jax
import jax.numpy as jnp
import numpy as np
from jax import lax
from jax.experimental import pallas as pl
from jax.experimental.pallas import tpu as pltpu
from jax.sharding import PartitionSpec as P

REACH = 4
THETA = 500000.0
EPSILON = 1e-06
TOK = 256
HEAD = 128
HEADS = 8
WINDOW = (REACH + 1) * TOK
SUB = 128
SPAN = 1152
CHUNKS = SPAN // SUB
ID_ROWS = 16
MSG = 2 * TOK + ID_ROWS
SCALING = HEAD ** (-0.5)
EXP2 = float(SCALING * np.log2(np.e))
NT = (((1,), (1,)), ((), ()))

PIO2_A = 1.5703125
PIO2_B = float(np.float32(np.round((np.pi / 2 - PIO2_A) * 2.0**23) / 2.0**23))
PIO2_C = float(np.float32(np.pi / 2 - PIO2_A - PIO2_B))


def passed_along(block, axis, distance):
    devices = range(lax.axis_size(axis))
    route = [(i - distance, i) for i in devices if i - distance in devices]
    return lax.ppermute(block, axis, route)


def dot(a, b):
    return jnp.dot(a, b, preferred_element_type=jnp.float32)


def dot_nt(a, b):
    return lax.dot_general(a, b, NT, preferred_element_type=jnp.float32)


def half_turned(x):
    return pltpu.roll(x, HEAD // 2, 1)


def cos_sin(position, frequency):
    angle = position * frequency
    turns = jnp.floor(angle * np.float32(2.0 / np.pi) + 0.5)
    rest = ((angle - turns * PIO2_A) - turns * PIO2_B) - turns * PIO2_C
    square = rest * rest
    sine = rest + rest * square * (
        np.float32(-1.6666654611e-1)
        + square * (np.float32(8.3321608736e-3) + square * np.float32(-1.9515295891e-4))
    )
    cosine = (1.0 - 0.5 * square) + square * square * (
        np.float32(4.166664568298827e-2)
        + square * (np.float32(-1.388731625493765e-3) + square * np.float32(2.443315711809948e-5))
    )
    lane = lax.broadcasted_iota(jnp.int32, angle.shape, 1)
    quadrant = turns.astype(jnp.int32) + jnp.where(lane < HEAD // 2, 1, 0)
    value = jnp.where((quadrant & 1) == 1, cosine, sine)
    return jnp.where((quadrant & 2) == 2, -value, value)


def kernel(
    b4, b3, b2, b1, b0, q_ref, d_ref, qg_ref, kg_ref, f_ref,
    att_ref, gq_ref, r4, r3, r2, r1, own_ref, gain_ref,
    idc, cosine, sine, khat, vwin, khat_t, v_t, bias, qhat, dcat, dcat_t, s_ref, w_ref, ds_ref,
    dk, dv, qg_acc,
):
    blocks = (b4, b3, b2, b1, b0)
    lane = lax.broadcasted_iota(jnp.int32, (SUB, HEAD), 1)
    row = lax.broadcasted_iota(jnp.int32, (SUB, HEAD), 0)
    lane_f = lane.astype(jnp.float32)
    left = lane < HEAD // 2
    parts = WINDOW // SUB
    q_gain = qg_ref[...]
    k_gain = kg_ref[...]
    frequency = f_ref[...]

    id_rows = []
    for block in blocks:
        both = block[2 * TOK : MSG, :].astype(jnp.float32)
        id_rows += [both[0:1], both[1:2]]
    below = jnp.zeros((SUB, HEAD), jnp.float32)
    for j in range(parts):
        column = jnp.broadcast_to(id_rows[j], (SUB, HEAD)).T
        idc[j * SUB : (j + 1) * SUB, :] = column
        below = below + jnp.where(column < lane_f, 1.0, 0.0)
    first = jnp.sum(below, axis=0, keepdims=True)

    for j in range(parts):
        rows = slice(j * SUB, (j + 1) * SUB)
        here = slice((j % 2) * SUB, (j % 2 + 1) * SUB)
        block = blocks[j // 2]
        start = jnp.sum(jnp.where(idc[rows, :] == lane_f, first, 0.0), axis=1, keepdims=True)
        position = (row + j * SUB).astype(jnp.float32) - start
        both = cos_sin(position, frequency)
        turned = half_turned(both)
        c = jnp.where(left, both, turned)
        s = jnp.where(left, -turned, both)
        cosine[rows, :] = c
        sine[rows, :] = s
        x = block[here, :].astype(jnp.float32)
        normed = x * lax.rsqrt(jnp.mean(x * x, axis=1, keepdims=True) + EPSILON) * k_gain
        hat = normed * c + half_turned(normed) * s
        khat[rows, :] = hat.astype(jnp.bfloat16)
        khat_t[:, rows] = hat.T.astype(jnp.bfloat16)
        values = block[TOK + (j % 2) * SUB : TOK + (j % 2 + 1) * SUB, :]
        vwin[rows, :] = values
        v_t[:, rows] = values.astype(jnp.float32).T.astype(jnp.bfloat16)

    for h in range(HEADS):
        for sub in range(2):
            tokens = slice(sub * SUB, (sub + 1) * SUB)
            at = (h // 2) * 512 + sub * 256 + (h % 2) * SUB
            window_rows = slice(REACH * TOK + sub * SUB, REACH * TOK + (sub + 1) * SUB)
            x = q_ref[tokens, h * HEAD : (h + 1) * HEAD].astype(jnp.float32)
            normed = x * lax.rsqrt(jnp.mean(x * x, axis=1, keepdims=True) + EPSILON) * q_gain
            hat = normed * cosine[window_rows, :] + half_turned(normed) * sine[window_rows, :]
            qhat[at : at + SUB, :] = hat.astype(jnp.bfloat16)
            d = d_ref[tokens, h * HEAD : (h + 1) * HEAD]
            dcat[at : at + SUB, :] = d
            dcat_t[h // 2, :, (at % 512) : (at % 512) + SUB] = d.astype(jnp.float32).T

    for sub in range(2):
        ids_q = id_rows[2 * REACH + sub]
        for c in range(CHUNKS):
            j = sub + c
            kept = idc[j * SUB : (j + 1) * SUB, :] == ids_q
            if c == CHUNKS - 1:
                kept = kept & (row <= lane)
            bias[sub, c * SUB : (c + 1) * SUB, :] = jnp.where(kept, 0.0, -1e30)

    dk[...] = jnp.zeros_like(dk)
    dv[...] = jnp.zeros_like(dv)
    qg_acc[...] = jnp.zeros_like(qg_acc)
    zero = jnp.zeros((SUB, 256), jnp.bfloat16)
    for ref in (w_ref, ds_ref):
        ref[0:SUB, 256:512] = zero
        ref[SPAN:WINDOW, 0:256] = zero

    def pair_step(pair, carry):
        at = pl.multiple_of(pair * 512, 512)
        for sub in range(2):
            base = sub * SUB
            cols = slice(sub * 256, (sub + 1) * 256)
            q_pair = qhat[pl.ds(at + sub * 256, 256), :]
            d_pair = dcat[pl.ds(at + sub * 256, 256), :]
            top = jnp.full((8, 256), -1e30, jnp.float32)
            for c in range(CHUNKS):
                keys = slice(base + c * SUB, base + (c + 1) * SUB)
                block_bias = bias[sub, c * SUB : (c + 1) * SUB, :]
                s = dot_nt(khat[keys, :], q_pair) + jnp.concatenate([block_bias, block_bias], axis=1)
                s_ref[sub, c * SUB : (c + 1) * SUB, :] = s
                top = jnp.maximum(top, jnp.max(s.reshape(SUB // 8, 8, 256), axis=0))
            shift = jnp.max(top, axis=0, keepdims=True) * EXP2
            total = jnp.zeros((8, 256), jnp.float32)
            for c in range(CHUNKS):
                e = jnp.exp2(s_ref[sub, c * SUB : (c + 1) * SUB, :] * EXP2 - shift)
                s_ref[sub, c * SUB : (c + 1) * SUB, :] = e
                total = total + jnp.sum(e.reshape(SUB // 8, 8, 256), axis=0)
            inverse = 1.0 / jnp.sum(total, axis=0, keepdims=True)
            for c in range(CHUNKS):
                keys = slice(base + c * SUB, base + (c + 1) * SUB)
                w = s_ref[sub, c * SUB : (c + 1) * SUB, :] * inverse
                w_ref[keys, cols] = w.astype(jnp.bfloat16)
            span = slice(base, base + SPAN)
            att_t = dot(v_t[:, span], w_ref[span, cols])
            center = jnp.sum(att_t * dcat_t[pair, :, cols], axis=0, keepdims=True)
            for c in range(CHUNKS):
                keys = slice(base + c * SUB, base + (c + 1) * SUB)
                dw = dot_nt(vwin[keys, :], d_pair)
                ds = w_ref[keys, cols].astype(jnp.float32) * (dw - center)
                ds_ref[keys, cols] = ds.astype(jnp.bfloat16)
            dq_t = dot(khat_t[:, span], ds_ref[span, cols]) * SCALING
            tokens = slice(sub * SUB, (sub + 1) * SUB)
            window_rows = slice(REACH * TOK + sub * SUB, REACH * TOK + (sub + 1) * SUB)
            c_q = cosine[window_rows, :]
            s_q = sine[window_rows, :]
            for g in range(2):
                columns = pl.ds(pl.multiple_of(pair * 256 + g * HEAD, HEAD), HEAD)
                att = att_t[:, g * SUB : (g + 1) * SUB].T
                att_ref[tokens, columns] = att.astype(jnp.bfloat16)
                dq = dq_t[:, g * SUB : (g + 1) * SUB].T
                x = q_ref[tokens, columns].astype(jnp.float32)
                r = lax.rsqrt(jnp.mean(x * x, axis=1, keepdims=True) + EPSILON)
                xh = x * r
                dn = dq * c_q - half_turned(dq) * s_q
                qg_acc[...] += jnp.sum((dn * xh).reshape(SUB // 8, 8, HEAD), axis=0)
                dxh = dn * q_gain
                gq = r * (dxh - xh * jnp.mean(dxh * xh, axis=1, keepdims=True))
                gq_ref[tokens, columns] = gq.astype(jnp.bfloat16)
        q_four = qhat[pl.ds(at, 512), :]
        d_four = dcat[pl.ds(at, 512), :]
        for j in range(parts):
            rows = slice(j * SUB, (j + 1) * SUB)
            dk[rows, :] += dot(ds_ref[rows, :], q_four)
            dv[rows, :] += dot(w_ref[rows, :], d_four)
        return carry

    lax.fori_loop(0, HEADS // 2, pair_step, 0)

    kg = jnp.zeros((8, HEAD), jnp.float32)
    outs = (r4, r3, r2, r1, own_ref)
    for j in range(parts):
        rows = slice(j * SUB, (j + 1) * SUB)
        here = slice((j % 2) * SUB, (j % 2 + 1) * SUB)
        x = blocks[j // 2][here, :].astype(jnp.float32)
        r = lax.rsqrt(jnp.mean(x * x, axis=1, keepdims=True) + EPSILON)
        xh = x * r
        d = dk[rows, :] * SCALING
        dn = d * cosine[rows, :] - half_turned(d) * sine[rows, :]
        kg = kg + jnp.sum((dn * xh).reshape(SUB // 8, 8, HEAD), axis=0)
        dxh = dn * k_gain
        gk = r * (dxh - xh * jnp.mean(dxh * xh, axis=1, keepdims=True))
        out = outs[j // 2]
        out[here, :] = gk.astype(out.dtype)
        out[TOK + (j % 2) * SUB : TOK + (j % 2 + 1) * SUB, :] = dv[rows, :].astype(out.dtype)
    gain_ref[0:1, :] = jnp.sum(qg_acc[...], axis=0, keepdims=True)
    gain_ref[1:2, :] = jnp.sum(kg, axis=0, keepdims=True)


RETURN = jnp.float32


def attention(blocks, queries, output_gradient, q_gain, k_gain, frequency):
    vmem = pl.BlockSpec(memory_space=pltpu.VMEM)
    f32, bf16 = jnp.float32, jnp.bfloat16
    shape = jax.ShapeDtypeStruct
    return pl.pallas_call(
        kernel,
        out_shape=[
            shape((TOK, HEADS * HEAD), bf16),
            shape((TOK, HEADS * HEAD), bf16),
            *[shape((2 * TOK, HEAD), RETURN) for _ in range(REACH)],
            shape((2 * TOK, HEAD), f32),
            shape((2, HEAD), f32),
        ],
        in_specs=[vmem] * 10,
        out_specs=[vmem] * 8,
        scratch_shapes=[
            pltpu.VMEM((WINDOW, HEAD), f32),
            pltpu.VMEM((WINDOW, HEAD), f32),
            pltpu.VMEM((WINDOW, HEAD), f32),
            pltpu.VMEM((WINDOW, HEAD), bf16),
            pltpu.VMEM((WINDOW, HEAD), bf16),
            pltpu.VMEM((HEAD, WINDOW), bf16),
            pltpu.VMEM((HEAD, WINDOW), bf16),
            pltpu.VMEM((2, SPAN, SUB), f32),
            pltpu.VMEM((HEADS * TOK, HEAD), bf16),
            pltpu.VMEM((HEADS * TOK, HEAD), bf16),
            pltpu.VMEM((HEADS // 2, HEAD, 512), f32),
            pltpu.VMEM((2, SPAN, 256), f32),
            pltpu.VMEM((WINDOW, 512), bf16),
            pltpu.VMEM((WINDOW, 512), bf16),
            pltpu.VMEM((WINDOW, HEAD), f32),
            pltpu.VMEM((WINDOW, HEAD), f32),
            pltpu.VMEM((8, HEAD), f32),
        ],
        compiler_params=pltpu.CompilerParams(vmem_limit_bytes=40 * 1024 * 1024),
    )(*blocks, queries, output_gradient, q_gain, k_gain, frequency)


def body(queries, keys, values, output_gradient, q_gain, k_gain, doc_ids):
    ids = (doc_ids + 1).astype(jnp.bfloat16).reshape(2, HEAD)
    ids = jnp.concatenate([ids, jnp.zeros((ID_ROWS - 2, HEAD), jnp.bfloat16)])
    message = jnp.concatenate([keys, values, ids])
    blocks = [passed_along(message, "context", distance) for distance in range(REACH, 0, -1)]
    blocks.append(message)
    half = jnp.arange(HEAD // 2, dtype=jnp.float32)
    frequency = THETA ** (-(half * 2.0 / HEAD))
    frequency = jnp.concatenate([frequency, frequency]).reshape(1, HEAD)
    attended, query_gradient, *returns, own, gains = attention(
        blocks,
        queries,
        output_gradient,
        q_gain.reshape(1, HEAD),
        k_gain.reshape(1, HEAD),
        frequency,
    )
    everyone = lax.all_gather(gains, ("context", "tensor"))
    total = own
    for distance, block in zip(range(REACH, 0, -1), returns):
        total = total + passed_along(block, "context", -distance)
    total = total.astype(jnp.bfloat16)
    gain_total = jnp.sum(everyone, axis=0)
    return (
        attended,
        query_gradient,
        total[:TOK],
        total[TOK:],
        gain_total[0],
        gain_total[1],
    )


def solution(mesh):
    placed = (
        P("context", "tensor"),
        P("context", "tensor"),
        P("context", "tensor"),
        P("context", "tensor"),
        P(),
        P(),
        P("context"),
    )
    return jax.shard_map(
        body,
        mesh=mesh,
        in_specs=placed,
        out_specs=(
            P("context", "tensor"),
            P("context", "tensor"),
            P("context", "tensor"),
            P("context", "tensor"),
            P(),
            P(),
        ),
        check_vma=False,
    )
```

time: 270 us -> 131 us (0.49)
  matrix products: 60.5 us -> 0 us
  starting transfers between devices: 54 us -> 22.1 us
  other arithmetic: 29.2 us -> 2.12 us
  Pallas kernels: 0 us -> 21.5 us
  local copies, waits for them, and re-layouts: 16.8 us -> 4.02 us
  loops' own time: 11.4 us -> 0 us
  blocking collectives: 86.1 us -> 77.5 us
  waiting for transfers between devices: 7.51 us -> 1.87 us
    psum x1 -> x0, blocking collectives: 86.1 us -> none  [body(): lax.psum((q_gain_term, k_gain_term), ('context', 'tensor'))]
    all_gather x0 -> x1, blocking collectives: none -> 77.5 us  [body(): everyone = lax.all_gather(gains, ('context', 'tensor'))]
    dot_general x20 -> x0, matrix products: 46.1 us -> none  [the longest x4 13.1 us: attend(): jnp.einsum('gtw,tgd->wd', weights, d_pair, preferred_element_type=jnp.flo...]
    ppermute x20 -> x8, starting transfers between devices: 54 us -> 22.1 us  [passed_along(): return lax.ppermute(block, axis, route)]
    pallas_call x0 -> x1, Pallas kernels: none -> 21.5 us  [attention(): pl.pallas_call(kernel, out_shape=[shape((TOK, HEADS * HEAD), bf16), shape...]
    sub x4 -> x0, matrix products: 14.4 us -> none  [attend(): exponent = jnp.exp(scores - highest)]
    another operation x1 -> x0, loops' own time: 11.4 us -> none  [body(): lax.scan(attend, (blank_block, blank_block), (q_pairs, d_pairs, jnp.arang...]
    convert_element_type x9 -> x1, other arithmetic: 7.12 us -> 0.06 us  [body(): total = total.astype(jnp.bfloat16)]
  transfers between devices with their start and end apart: 20 -> 8, of which waited for: 3 -> 1; matrix products, arithmetic and copies ran while one was open for 8% -> 1% of each run, Pallas kernels for 0% -> 0%
where the time goes in v1:
time: 131 us; the launch traced here: 130 us
  blocking collectives  77.5 us (59%)
  starting transfers between devices  22.1 us (17%)
  Pallas kernels  21.5 us (16%)
  local copies, waits for them, and re-layouts  4.02 us (3%)
  other arithmetic  2.12 us (2%)
  waiting for transfers between devices  1.87 us (1%)
    all_gather x1, blocking collectives, body(): everyone = lax.all_gather(gains, ('context', 'tensor'))  77.5 us
    ppermute x8, starting transfers between devices, passed_along(): return lax.ppermute(block, axis, route)  22.1 us
    pallas_call x1, Pallas kernels, attention(): pl.pallas_call(kernel, out_shape=[shape((TOK, HEADS * HEAD), bf16), shape...  21.5 us
    unnamed x8, local copies, waits for them, and re-layouts  2.75 us
  transfers between devices with their start and end apart: 8, of which 1 were waited for; matrix products, arithmetic and copies ran while one was open for 1% of the time, Pallas kernels for 0%

profile of v1, /device:TPU:1, one launch (start us, length us, event | category | flops | bytes accessed | tf_op | source)
XLA Modules:
  0.0 129.8 jit_solution(17234676090561640274)
XLA Ops:
  0.6 0.7 fusion
  1.3 0.1 pad.5.clone
  1.4 1.0 maximum_maximum_fusion.b0
  2.4 4.5 %collective-permute-start.3 = (bf16[528,128]{1,0:T(8,128)(2,1)S(1)}, bf16[528,128]{1,0:T(8,128)(2,1)S(1)}, u32[]{:S(2)}, u32[]{:S(2)}) collective-permute-start(bf16[528,128]{1,0:T(8,128)(2,1)S(1)} %maximum_maximum_fusion.b0), channel_id=1, source_target_pairs={{0,8},{8,16},{16,24},{24,32},{32,40},{40,48},{48,56},{56,64},{64,7... | collective-permute-start | bytes 405512 | tf_op jit(solution)/shard_map/ppermute | solution.py:35
  6.9 3.1 %collective-permute-start.2 = (bf16[528,128]{1,0:T(8,128)(2,1)S(1)}, bf16[528,128]{1,0:T(8,128)(2,1)S(1)}, u32[]{:S(2)}, u32[]{:S(2)}) collective-permute-start(bf16[528,128]{1,0:T(8,128)(2,1)S(1)} %maximum_maximum_fusion.b0), channel_id=1, source_target_pairs={{0,16},{8,24},{16,32},{24,40},{32,48},{40,56},{48,64},{56,72},{64,... | collective-permute-start | bytes 405512 | tf_op jit(solution)/shard_map/ppermute | solution.py:35
  10.1 3.4 %collective-permute-start.1 = (bf16[528,128]{1,0:T(8,128)(2,1)S(1)}, bf16[528,128]{1,0:T(8,128)(2,1)S(1)}, u32[]{:S(2)}, u32[]{:S(2)}) collective-permute-start(bf16[528,128]{1,0:T(8,128)(2,1)S(1)} %maximum_maximum_fusion.b0), channel_id=1, source_target_pairs={{0,24},{8,32},{16,40},{24,48},{32,56},{40,64},{48,72},{56,80},{64,... | collective-permute-start | bytes 405512 | tf_op jit(solution)/shard_map/ppermute | solution.py:35
  13.5 3.4 %collective-permute-start = (bf16[528,128]{1,0:T(8,128)(2,1)S(1)}, bf16[528,128]{1,0:T(8,128)(2,1)S(1)}, u32[]{:S(2)}, u32[]{:S(2)}) collective-permute-start(bf16[528,128]{1,0:T(8,128)(2,1)S(1)} %maximum_maximum_fusion.b0), channel_id=1, source_target_pairs={{0,32},{8,40},{16,48},{24,56},{32,64},{40,72},{48,80},{56,88},{64,... | collective-permute-start | bytes 405512 | tf_op jit(solution)/shard_map/ppermute | solution.py:35
  17.0 0.1 maximum_bitcast_fusion.f_ref
  17.0 0.0 collective-permute-done.3.b1
  17.0 0.0 collective-permute-done.2.b2
  17.1 0.0 collective-permute-done.1.b3
  17.1 1.9 %collective-permute-done.b4 = bf16[528,128]{1,0:T(8,128)(2,1)S(1)} collective-permute-done((bf16[528,128]{1,0:T(8,128)(2,1)S(1)}, bf16[528,128]{1,0:T(8,128)(2,1)S(1)}, u32[]{:S(2)}, u32[]{:S(2)}) %collective-permute-start) | collective-permute-done | bytes 135200 | tf_op jit(solution)/shard_map/ppermute | solution.py:35
  18.9 0.0 copy-start.2
  18.9 0.0 copy-start.3
  18.9 0.7 copy-done.2
  19.6 0.0 copy-done.3
  19.6 1.0 copy-done
  20.6 1.0 copy-done.1
  21.7 21.5 %shard_map.118 = (bf16[256,1024]{1,0:T(8,128)(2,1)}, bf16[256,1024]{1,0:T(8,128)(2,1)}, f32[512,128]{1,0:T(8,128)S(1)}, f32[512,128]{1,0:T(8,128)S(1)}, f32[512,...) custom-call(bf16[528,128]{1,0:T(8,128)(2,1)S(1)} %collective-permute-done.b4, ...), custom_call_target="tpu_custom_call" | custom-call | tf_op jit(solution)/shard_map/pallas_call | solution.py:235
  43.1 1.3 collective-permute-start.4
  44.4 1.3 collective-permute-start.5
  45.7 1.3 collective-permute-start.6
  47.0 3.8 %collective-permute-start.7 = (f32[512,128]{1,0:T(8,128)S(1)}, f32[512,128]{1,0:T(8,128)S(1)}, u32[]{:S(2)}, u32[]{:S(2)}) collective-permute-start(f32[512,128]{1,0:T(8,128)S(1)} %get-tuple-element.20), channel_id=1, source_target_pairs={{8,0},{16,8},{24,16},{32,24},{40,32},{48,40},{56,48},{64,56},{72,6... | collective-permute-start | bytes 786440 | tf_op jit(solution)/shard_map/ppermute | solution.py:35
  50.8 77.5 %all-gather.1 = f32[256,2,128]{2,1,0:T(2,128)S(1)} all-gather(f32[1,2,128]{2,1,0:T(2,128)S(1)} %bitcast.11), channel_id=2, replica_groups=mesh['context'=32,'tensor'=8] {'context','tensor'}, dimensions={0}, use_global_device_ids=true | all-gather | bytes 263168 | tf_op jit(solution)/shard_map/all_gather | solution.py:286
  128.3 0.3 reduce_sum.9
  128.5 0.5 slice_bitcast_fusion
  129.1 0.0 collective-permute-done.4
  129.1 0.0 collective-permute-done.5
  129.1 0.0 collective-permute-done.6
  129.1 0.0 collective-permute-done.7
  129.1 0.1 add_convert_fusion
  129.2 0.7 fusion.1
  (4 shorter events, 0.0 us)
Async XLA Ops:
  2.4 14.6 %collective-permute-start.3 = (bf16[528,128]{1,0:T(8,128)(2,1)S(1)}, bf16[528,128]{1,0:T(8,128)(2,1)S(1)}, u32[]{:S(2)}, u32[]{:S(2)}) collective-permute-start(bf16[528,128]{1,0:T(8,128)(2,1)S(1)} %maximum_maximum_fusion.b0), channel_id=1, source_target_pairs={{0,8},{8,16},{16,24},{24,32},{32,40},{40,48},{48,56},{56,64},{64,7... | collective-permute-start | bytes 405512 | tf_op jit(solution)/shard_map/ppermute | solution.py:35
  6.9 10.1 %collective-permute-start.2 = (bf16[528,128]{1,0:T(8,128)(2,1)S(1)}, bf16[528,128]{1,0:T(8,128)(2,1)S(1)}, u32[]{:S(2)}, u32[]{:S(2)}) collective-permute-start(bf16[528,128]{1,0:T(8,128)(2,1)S(1)} %maximum_maximum_fusion.b0), channel_id=1, source_target_pairs={{0,16},{8,24},{16,32},{24,40},{32,48},{40,56},{48,64},{56,72},{64,... | collective-permute-start | bytes 405512 | tf_op jit(solution)/shard_map/ppermute | solution.py:35
  10.1 7.0 %collective-permute-start.1 = (bf16[528,128]{1,0:T(8,128)(2,1)S(1)}, bf16[528,128]{1,0:T(8,128)(2,1)S(1)}, u32[]{:S(2)}, u32[]{:S(2)}) collective-permute-start(bf16[528,128]{1,0:T(8,128)(2,1)S(1)} %maximum_maximum_fusion.b0), channel_id=1, source_target_pairs={{0,24},{8,32},{16,40},{24,48},{32,56},{40,64},{48,72},{56,80},{64,... | collective-permute-start | bytes 405512 | tf_op jit(solution)/shard_map/ppermute | solution.py:35
  13.5 5.4 %collective-permute-start = (bf16[528,128]{1,0:T(8,128)(2,1)S(1)}, bf16[528,128]{1,0:T(8,128)(2,1)S(1)}, u32[]{:S(2)}, u32[]{:S(2)}) collective-permute-start(bf16[528,128]{1,0:T(8,128)(2,1)S(1)} %maximum_maximum_fusion.b0), channel_id=1, source_target_pairs={{0,32},{8,40},{16,48},{24,56},{32,64},{40,72},{48,80},{56,88},{64,... | collective-permute-start | bytes 405512 | tf_op jit(solution)/shard_map/ppermute | solution.py:35
  18.9 0.7 copy-start.2
  18.9 0.7 copy-start.3
  19.6 1.0 copy-start
  20.6 1.0 copy-start.1
  43.1 86.0 %collective-permute-start.4 = (f32[512,128]{1,0:T(8,128)S(1)}, f32[512,128]{1,0:T(8,128)S(1)}, u32[]{:S(2)}, u32[]{:S(2)}) collective-permute-start(f32[512,128]{1,0:T(8,128)S(1)} %get-tuple-element.17), channel_id=1, source_target_pairs={{32,0},{40,8},{48,16},{56,24},{64,32},{72,40},{80,48},{88,56},{96,... | collective-permute-start | bytes 786440 | tf_op jit(solution)/shard_map/ppermute | solution.py:35
  44.4 84.7 %collective-permute-start.5 = (f32[512,128]{1,0:T(8,128)S(1)}, f32[512,128]{1,0:T(8,128)S(1)}, u32[]{:S(2)}, u32[]{:S(2)}) collective-permute-start(f32[512,128]{1,0:T(8,128)S(1)} %get-tuple-element.18), channel_id=1, source_target_pairs={{24,0},{32,8},{40,16},{48,24},{56,32},{64,40},{72,48},{80,56},{88,... | collective-permute-start | bytes 786440 | tf_op jit(solution)/shard_map/ppermute | solution.py:35
  45.7 83.4 %collective-permute-start.6 = (f32[512,128]{1,0:T(8,128)S(1)}, f32[512,128]{1,0:T(8,128)S(1)}, u32[]{:S(2)}, u32[]{:S(2)}) collective-permute-start(f32[512,128]{1,0:T(8,128)S(1)} %get-tuple-element.19), channel_id=1, source_target_pairs={{16,0},{24,8},{32,16},{40,24},{48,32},{56,40},{64,48},{72,56},{80,... | collective-permute-start | bytes 786440 | tf_op jit(solution)/shard_map/ppermute | solution.py:35
  47.0 82.1 %collective-permute-start.7 = (f32[512,128]{1,0:T(8,128)S(1)}, f32[512,128]{1,0:T(8,128)S(1)}, u32[]{:S(2)}, u32[]{:S(2)}) collective-permute-start(f32[512,128]{1,0:T(8,128)S(1)} %get-tuple-element.20), channel_id=1, source_target_pairs={{8,0},{16,8},{24,16},{32,24},{40,32},{48,40},{56,48},{64,56},{72,6... | collective-permute-start | bytes 786440 | tf_op jit(solution)/shard_map/ppermute | solution.py:35

commit v2 on v1

--- a/solution.py
+++ b/solution.py
@@ -1,5 +1,3 @@
-import functools
-
 import jax
 import jax.numpy as jnp
 import numpy as np
@@ -22,7 +20,6 @@
 MSG = 2 * TOK + ID_ROWS
 SCALING = HEAD ** (-0.5)
 EXP2 = float(SCALING * np.log2(np.e))
-NT = (((1,), (1,)), ((), ()))
 
 PIO2_A = 1.5703125
 PIO2_B = float(np.float32(np.round((np.pi / 2 - PIO2_A) * 2.0**23) / 2.0**23))
@@ -37,10 +34,6 @@
 
 def dot(a, b):
     return jnp.dot(a, b, preferred_element_type=jnp.float32)
-
-
-def dot_nt(a, b):
-    return lax.dot_general(a, b, NT, preferred_element_type=jnp.float32)
 
 
 def half_turned(x):
@@ -67,15 +60,20 @@
 
 
 def kernel(
-    b4, b3, b2, b1, b0, q_ref, d_ref, qg_ref, kg_ref, f_ref,
-    att_ref, gq_ref, r4, r3, r2, r1, own_ref, gain_ref,
-    idc, cosine, sine, khat, vwin, khat_t, v_t, bias, qhat, dcat, dcat_t, s_ref, w_ref, ds_ref,
-    dk, dv, qg_acc,
+    b4, b3, b2, b1, b0, q_hbm, d_hbm, qg_ref, kg_ref, f_ref,
+    att_hbm, gq_hbm, r4, r3, r2, r1, own_ref, gain_ref,
+    q_ref, d_ref, att_ref, gq_ref, cosine, sine, kext, vwin, khat_t, v_t, qhat, qext_t, dcat, dcat_t,
+    s_ref, w_ref, ds_ref, dk, dv, qg_acc, in_sem, att_sem, gq_sem,
 ):
+    q_copy = pltpu.make_async_copy(q_hbm, q_ref, in_sem.at[0])
+    d_copy = pltpu.make_async_copy(d_hbm, d_ref, in_sem.at[1])
+    q_copy.start()
+    d_copy.start()
     blocks = (b4, b3, b2, b1, b0)
     lane = lax.broadcasted_iota(jnp.int32, (SUB, HEAD), 1)
     row = lax.broadcasted_iota(jnp.int32, (SUB, HEAD), 0)
     lane_f = lane.astype(jnp.float32)
+    row_f = row.astype(jnp.float32)
     left = lane < HEAD // 2
     parts = WINDOW // SUB
     q_gain = qg_ref[...]
@@ -89,7 +87,7 @@
     below = jnp.zeros((SUB, HEAD), jnp.float32)
     for j in range(parts):
         column = jnp.broadcast_to(id_rows[j], (SUB, HEAD)).T
-        idc[j * SUB : (j + 1) * SUB, :] = column
+        kext[j * SUB : (j + 1) * SUB, HEAD:] = jnp.where(column == lane_f, 1.0, 0.0).astype(jnp.bfloat16)
         below = below + jnp.where(column < lane_f, 1.0, 0.0)
     first = jnp.sum(below, axis=0, keepdims=True)
 
@@ -97,7 +95,8 @@
         rows = slice(j * SUB, (j + 1) * SUB)
         here = slice((j % 2) * SUB, (j % 2 + 1) * SUB)
         block = blocks[j // 2]
-        start = jnp.sum(jnp.where(idc[rows, :] == lane_f, first, 0.0), axis=1, keepdims=True)
+        member = kext[rows, HEAD:].astype(jnp.float32)
+        start = jnp.sum(member * first, axis=1, keepdims=True)
         position = (row + j * SUB).astype(jnp.float32) - start
         both = cos_sin(position, frequency)
         turned = half_turned(both)
@@ -108,33 +107,32 @@
         x = block[here, :].astype(jnp.float32)
         normed = x * lax.rsqrt(jnp.mean(x * x, axis=1, keepdims=True) + EPSILON) * k_gain
         hat = normed * c + half_turned(normed) * s
-        khat[rows, :] = hat.astype(jnp.bfloat16)
+        kext[rows, 0:HEAD] = hat.astype(jnp.bfloat16)
         khat_t[:, rows] = hat.T.astype(jnp.bfloat16)
         values = block[TOK + (j % 2) * SUB : TOK + (j % 2 + 1) * SUB, :]
         vwin[rows, :] = values
         v_t[:, rows] = values.astype(jnp.float32).T.astype(jnp.bfloat16)
 
-    for h in range(HEADS):
-        for sub in range(2):
-            tokens = slice(sub * SUB, (sub + 1) * SUB)
+    q_copy.wait()
+    d_copy.wait()
+    for sub in range(2):
+        tokens = slice(sub * SUB, (sub + 1) * SUB)
+        window_rows = slice(REACH * TOK + sub * SUB, REACH * TOK + (sub + 1) * SUB)
+        c_q = cosine[window_rows, :]
+        s_q = sine[window_rows, :]
+        other = jnp.where(row_f == id_rows[2 * REACH + sub], 0.0, -1e30).astype(jnp.bfloat16)
+        for h in range(HEADS):
             at = (h // 2) * 512 + sub * 256 + (h % 2) * SUB
-            window_rows = slice(REACH * TOK + sub * SUB, REACH * TOK + (sub + 1) * SUB)
+            lanes = slice(at % 512, at % 512 + SUB)
             x = q_ref[tokens, h * HEAD : (h + 1) * HEAD].astype(jnp.float32)
             normed = x * lax.rsqrt(jnp.mean(x * x, axis=1, keepdims=True) + EPSILON) * q_gain
-            hat = normed * cosine[window_rows, :] + half_turned(normed) * sine[window_rows, :]
+            hat = normed * c_q + half_turned(normed) * s_q
             qhat[at : at + SUB, :] = hat.astype(jnp.bfloat16)
+            qext_t[h // 2, 0:HEAD, lanes] = hat.T.astype(jnp.bfloat16)
+            qext_t[h // 2, HEAD:, lanes] = other
             d = d_ref[tokens, h * HEAD : (h + 1) * HEAD]
             dcat[at : at + SUB, :] = d
-            dcat_t[h // 2, :, (at % 512) : (at % 512) + SUB] = d.astype(jnp.float32).T
-
-    for sub in range(2):
-        ids_q = id_rows[2 * REACH + sub]
-        for c in range(CHUNKS):
-            j = sub + c
-            kept = idc[j * SUB : (j + 1) * SUB, :] == ids_q
-            if c == CHUNKS - 1:
-                kept = kept & (row <= lane)
-            bias[sub, c * SUB : (c + 1) * SUB, :] = jnp.where(kept, 0.0, -1e30)
+            dcat_t[h // 2, :, lanes] = d.astype(jnp.float32).T.astype(jnp.bfloat16)
 
     dk[...] = jnp.zeros_like(dk)
     dv[...] = jnp.zeros_like(dv)
@@ -143,25 +141,40 @@
     for ref in (w_ref, ds_ref):
         ref[0:SUB, 256:512] = zero
         ref[SPAN:WINDOW, 0:256] = zero
+    later = jnp.where(row <= lane, 0.0, -1e30)
+    later = jnp.concatenate([later, later], axis=1)
+    last = SPAN - SUB
+
+    def copies(pair):
+        columns = pl.ds(pl.multiple_of(pair * 256, 256), 256)
+        return (
+            pltpu.make_async_copy(att_ref.at[:, columns], att_hbm.at[:, columns], att_sem.at[pair]),
+            pltpu.make_async_copy(gq_ref.at[:, columns], gq_hbm.at[:, columns], gq_sem.at[pair]),
+        )
 
     def pair_step(pair, carry):
         at = pl.multiple_of(pair * 512, 512)
+        spans = (slice(0, SPAN), slice(SUB, WINDOW))
+        columns_of = (slice(0, 256), slice(256, 512))
+        shifts = []
         for sub in range(2):
+            cols = columns_of[sub]
+            s = dot(kext[spans[sub], :], qext_t[pair, :, cols])
+            tail = s[last:] + later
+            s_ref[sub, 0:last, :] = s[:last]
+            s_ref[sub, last:, :] = tail
+            top = jnp.maximum(
+                jnp.max(s[:last].reshape(last // 8, 8, 256), axis=0),
+                jnp.max(tail.reshape(SUB // 8, 8, 256), axis=0),
+            )
+            shifts.append(jnp.max(top, axis=0, keepdims=True) * EXP2)
+        att_ts = []
+        for sub in range(2):
+            cols = columns_of[sub]
             base = sub * SUB
-            cols = slice(sub * 256, (sub + 1) * 256)
-            q_pair = qhat[pl.ds(at + sub * 256, 256), :]
-            d_pair = dcat[pl.ds(at + sub * 256, 256), :]
-            top = jnp.full((8, 256), -1e30, jnp.float32)
-            for c in range(CHUNKS):
-                keys = slice(base + c * SUB, base + (c + 1) * SUB)
-                block_bias = bias[sub, c * SUB : (c + 1) * SUB, :]
-                s = dot_nt(khat[keys, :], q_pair) + jnp.concatenate([block_bias, block_bias], axis=1)
-                s_ref[sub, c * SUB : (c + 1) * SUB, :] = s
-                top = jnp.maximum(top, jnp.max(s.reshape(SUB // 8, 8, 256), axis=0))
-            shift = jnp.max(top, axis=0, keepdims=True) * EXP2
             total = jnp.zeros((8, 256), jnp.float32)
             for c in range(CHUNKS):
-                e = jnp.exp2(s_ref[sub, c * SUB : (c + 1) * SUB, :] * EXP2 - shift)
+                e = jnp.exp2(s_ref[sub, c * SUB : (c + 1) * SUB, :] * EXP2 - shifts[sub])
                 s_ref[sub, c * SUB : (c + 1) * SUB, :] = e
                 total = total + jnp.sum(e.reshape(SUB // 8, 8, 256), axis=0)
             inverse = 1.0 / jnp.sum(total, axis=0, keepdims=True)
@@ -169,14 +182,16 @@
                 keys = slice(base + c * SUB, base + (c + 1) * SUB)
                 w = s_ref[sub, c * SUB : (c + 1) * SUB, :] * inverse
                 w_ref[keys, cols] = w.astype(jnp.bfloat16)
-            span = slice(base, base + SPAN)
-            att_t = dot(v_t[:, span], w_ref[span, cols])
-            center = jnp.sum(att_t * dcat_t[pair, :, cols], axis=0, keepdims=True)
-            for c in range(CHUNKS):
-                keys = slice(base + c * SUB, base + (c + 1) * SUB)
-                dw = dot_nt(vwin[keys, :], d_pair)
-                ds = w_ref[keys, cols].astype(jnp.float32) * (dw - center)
-                ds_ref[keys, cols] = ds.astype(jnp.bfloat16)
+            att_ts.append(dot(v_t[:, spans[sub]], w_ref[spans[sub], cols]))
+        for sub in range(2):
+            cols = columns_of[sub]
+            span = spans[sub]
+            att_t = att_ts[sub]
+            d_t = dcat_t[pair, :, cols]
+            center = jnp.sum(att_t * d_t.astype(jnp.float32), axis=0, keepdims=True)
+            dw = dot(vwin[span, :], d_t)
+            ds = w_ref[span, cols].astype(jnp.float32) * (dw - center)
+            ds_ref[span, cols] = ds.astype(jnp.bfloat16)
             dq_t = dot(khat_t[:, span], ds_ref[span, cols]) * SCALING
             tokens = slice(sub * SUB, (sub + 1) * SUB)
             window_rows = slice(REACH * TOK + sub * SUB, REACH * TOK + (sub + 1) * SUB)
@@ -195,12 +210,10 @@
                 dxh = dn * q_gain
                 gq = r * (dxh - xh * jnp.mean(dxh * xh, axis=1, keepdims=True))
                 gq_ref[tokens, columns] = gq.astype(jnp.bfloat16)
-        q_four = qhat[pl.ds(at, 512), :]
-        d_four = dcat[pl.ds(at, 512), :]
-        for j in range(parts):
-            rows = slice(j * SUB, (j + 1) * SUB)
-            dk[rows, :] += dot(ds_ref[rows, :], q_four)
-            dv[rows, :] += dot(w_ref[rows, :], d_four)
+        dk[...] += dot(ds_ref[...], qhat[pl.ds(at, 512), :])
+        dv[...] += dot(w_ref[...], dcat[pl.ds(at, 512), :])
+        for copy in copies(pair):
+            copy.start()
         return carry
 
     lax.fori_loop(0, HEADS // 2, pair_step, 0)
@@ -223,13 +236,17 @@
         out[TOK + (j % 2) * SUB : TOK + (j % 2 + 1) * SUB, :] = dv[rows, :].astype(out.dtype)
     gain_ref[0:1, :] = jnp.sum(qg_acc[...], axis=0, keepdims=True)
     gain_ref[1:2, :] = jnp.sum(kg, axis=0, keepdims=True)
-
-
-RETURN = jnp.float32
+    for pair in range(HEADS // 2):
+        for copy in copies(pair):
+            copy.wait()
+
+
+RETURN = jnp.bfloat16
 
 
 def attention(blocks, queries, output_gradient, q_gain, k_gain, frequency):
     vmem = pl.BlockSpec(memory_space=pltpu.VMEM)
+    hbm = pl.BlockSpec(memory_space=pl.ANY)
     f32, bf16 = jnp.float32, jnp.bfloat16
     shape = jax.ShapeDtypeStruct
     return pl.pallas_call(
@@ -241,35 +258,67 @@
             shape((2 * TOK, HEAD), f32),
             shape((2, HEAD), f32),
         ],
-        in_specs=[vmem] * 10,
-        out_specs=[vmem] * 8,
+        in_specs=[vmem] * 5 + [hbm] * 2 + [vmem] * 3,
+        out_specs=[hbm] * 2 + [vmem] * 6,
         scratch_shapes=[
+            pltpu.VMEM((TOK, HEADS * HEAD), bf16),
+            pltpu.VMEM((TOK, HEADS * HEAD), bf16),
+            pltpu.VMEM((TOK, HEADS * HEAD), bf16),
+            pltpu.VMEM((TOK, HEADS * HEAD), bf16),
             pltpu.VMEM((WINDOW, HEAD), f32),
             pltpu.VMEM((WINDOW, HEAD), f32),
-            pltpu.VMEM((WINDOW, HEAD), f32),
-            pltpu.VMEM((WINDOW, HEAD), bf16),
+            pltpu.VMEM((WINDOW, 2 * HEAD), bf16),
             pltpu.VMEM((WINDOW, HEAD), bf16),
             pltpu.VMEM((HEAD, WINDOW), bf16),
             pltpu.VMEM((HEAD, WINDOW), bf16),
-            pltpu.VMEM((2, SPAN, SUB), f32),
             pltpu.VMEM((HEADS * TOK, HEAD), bf16),
+            pltpu.VMEM((HEADS // 2, 2 * HEAD, 512), bf16),
             pltpu.VMEM((HEADS * TOK, HEAD), bf16),
-            pltpu.VMEM((HEADS // 2, HEAD, 512), f32),
+            pltpu.VMEM((HEADS // 2, HEAD, 512), bf16),
             pltpu.VMEM((2, SPAN, 256), f32),
             pltpu.VMEM((WINDOW, 512), bf16),
             pltpu.VMEM((WINDOW, 512), bf16),
             pltpu.VMEM((WINDOW, HEAD), f32),
             pltpu.VMEM((WINDOW, HEAD), f32),
             pltpu.VMEM((8, HEAD), f32),
+            pltpu.SemaphoreType.DMA((2,)),
+            pltpu.SemaphoreType.DMA((HEADS // 2,)),
+            pltpu.SemaphoreType.DMA((HEADS // 2,)),
         ],
         compiler_params=pltpu.CompilerParams(vmem_limit_bytes=40 * 1024 * 1024),
     )(*blocks, queries, output_gradient, q_gain, k_gain, frequency)
 
 
+def pack_kernel(keys, values, ids, out):
+    out[0:TOK, :] = keys[...]
+    out[TOK : 2 * TOK, :] = values[...]
+    marked = (ids[...] + 1).astype(jnp.float32)
+    out[2 * TOK :, :] = jnp.concatenate(
+        [marked, jnp.zeros((ID_ROWS - 2, HEAD), jnp.float32)]
+    ).astype(jnp.bfloat16)
+
+
+def pack(keys, values, ids):
+    vmem = pl.BlockSpec(memory_space=pltpu.VMEM)
+    return pl.pallas_call(
+        pack_kernel,
+        out_shape=jax.ShapeDtypeStruct((MSG, HEAD), jnp.bfloat16),
+        in_specs=[vmem] * 3,
+        out_specs=vmem,
+    )(keys, values, ids)
+
+
+def summed_over_all(terms):
+    total = jnp.sum(lax.all_gather(terms, "tensor"), axis=0)
+    rows = [list(range(8 * y, 8 * y + 8)) for y in range(4)]
+    columns = [[8 * y + k for y in range(4)] for k in range(8)]
+    for groups in (rows, columns):
+        total = jnp.sum(lax.all_gather(total, "context", axis_index_groups=groups), axis=0)
+    return total
+
+
 def body(queries, keys, values, output_gradient, q_gain, k_gain, doc_ids):
-    ids = (doc_ids + 1).astype(jnp.bfloat16).reshape(2, HEAD)
-    ids = jnp.concatenate([ids, jnp.zeros((ID_ROWS - 2, HEAD), jnp.bfloat16)])
-    message = jnp.concatenate([keys, values, ids])
+    message = pack(keys, values, doc_ids.reshape(2, HEAD))
     blocks = [passed_along(message, "context", distance) for distance in range(REACH, 0, -1)]
     blocks.append(message)
     half = jnp.arange(HEAD // 2, dtype=jnp.float32)
@@ -283,12 +332,11 @@
         k_gain.reshape(1, HEAD),
         frequency,
     )
-    everyone = lax.all_gather(gains, ("context", "tensor"))
     total = own
     for distance, block in zip(range(REACH, 0, -1), returns):
         total = total + passed_along(block, "context", -distance)
     total = total.astype(jnp.bfloat16)
-    gain_total = jnp.sum(everyone, axis=0)
+    gain_total = summed_over_all(gains)
     return (
         attended,
         query_gradient,

time: 131 us -> 101 us (0.77)
  the two profiles are of different devices: /device:TPU:1 before, /device:TPU:11 now
where the time goes in v2:
time: 101 us
  blocking collectives  35 us (35%)
  starting transfers between devices  29.5 us (29%)
  Pallas kernels  21.6 us (21%)
  waiting for transfers between devices  8.97 us (9%)
  local copies, waits for them, and re-layouts  4.84 us (5%)
    ppermute x8, starting transfers between devices, passed_along(): return lax.ppermute(block, axis, route)  29.5 us
    pallas_call x1, Pallas kernels, attention(): pl.pallas_call(kernel, out_shape=[shape((TOK, HEADS * HEAD), bf16), shape...  20 us
    all_gather x2, blocking collectives, summed_over_all(): lax.all_gather(total, 'context', axis_index_groups=groups)  19.6 us
    all_gather x1, blocking collectives, summed_over_all(): total = jnp.sum(lax.all_gather(terms, 'tensor'), axis=0)  15.4 us
    ppermute x8, waiting for transfers between devices, passed_along(): return lax.ppermute(block, axis, route)  8.97 us
    unnamed x10, local copies, waits for them, and re-layouts  3.66 us
  transfers between devices with their start and end apart: 8, of which 4 were waited for; matrix products, arithmetic and copies ran while one was open for 1% of the time, Pallas kernels for 0%

profile of v2, /device:TPU:11, one launch (start us, length us, event | category | flops | bytes accessed | tf_op | source)
XLA Modules:
  0.0 100.8 jit_solution(4770087332656470560)
XLA Ops:
  0.6 1.5 %shard_map.118.b0 = bf16[528,128]{1,0:T(8,128)(2,1)} custom-call(bf16[256,128]{1,0:T(8,128)(2,1)} %keys.1, bf16[256,128]{1,0:T(8,128)(2,1)} %values.1, s32[2,128]{1,0:T(2,128)} %bitcast.17), custom_call_target="tpu_custom_call" | custom-call | tf_op jit(solution)/shard_map/pallas_call | solution.py:303
  2.2 3.7 %collective-permute-start.3 = (bf16[528,128]{1,0:T(8,128)(2,1)}, bf16[528,128]{1,0:T(8,128)(2,1)S(1)}, u32[]{:S(2)}, u32[]{:S(2)}) collective-permute-start(bf16[528,128]{1,0:T(8,128)(2,1)} %shard_map.118.b0), channel_id=1, source_target_pairs={{0,8},{8,16},{16,24},{24,32},{32,40},{40,48},{48,56},{56,64},{64,7... | collective-permute-start | bytes 405512 | tf_op jit(solution)/shard_map/ppermute | solution.py:32
  5.9 2.8 %collective-permute-start.2 = (bf16[528,128]{1,0:T(8,128)(2,1)}, bf16[528,128]{1,0:T(8,128)(2,1)S(1)}, u32[]{:S(2)}, u32[]{:S(2)}) collective-permute-start(bf16[528,128]{1,0:T(8,128)(2,1)} %shard_map.118.b0), channel_id=1, source_target_pairs={{0,16},{8,24},{16,32},{24,40},{32,48},{40,56},{48,64},{56,72},{64,... | collective-permute-start | bytes 405512 | tf_op jit(solution)/shard_map/ppermute | solution.py:32
  8.7 3.1 %collective-permute-start.1 = (bf16[528,128]{1,0:T(8,128)(2,1)}, bf16[528,128]{1,0:T(8,128)(2,1)S(1)}, u32[]{:S(2)}, u32[]{:S(2)}) collective-permute-start(bf16[528,128]{1,0:T(8,128)(2,1)} %shard_map.118.b0), channel_id=1, source_target_pairs={{0,24},{8,32},{16,40},{24,48},{32,56},{40,64},{48,72},{56,80},{64,... | collective-permute-start | bytes 405512 | tf_op jit(solution)/shard_map/ppermute | solution.py:32
  11.8 4.0 %collective-permute-start = (bf16[528,128]{1,0:T(8,128)(2,1)}, bf16[528,128]{1,0:T(8,128)(2,1)S(1)}, u32[]{:S(2)}, u32[]{:S(2)}) collective-permute-start(bf16[528,128]{1,0:T(8,128)(2,1)} %shard_map.118.b0), channel_id=1, source_target_pairs={{0,32},{8,40},{16,48},{24,56},{32,64},{40,72},{48,80},{56,88},{64,... | collective-permute-start | bytes 405512 | tf_op jit(solution)/shard_map/ppermute | solution.py:32
  15.9 0.1 maximum_bitcast_fusion.f_ref
  16.0 0.0 collective-permute-done.3.b1
  16.0 0.0 collective-permute-done.2.b2
  16.0 0.8 collective-permute-done.1.b3
  16.7 4.4 %collective-permute-done.b4 = bf16[528,128]{1,0:T(8,128)(2,1)S(1)} collective-permute-done((bf16[528,128]{1,0:T(8,128)(2,1)}, bf16[528,128]{1,0:T(8,128)(2,1)S(1)}, u32[]{:S(2)}, u32[]{:S(2)}) %collective-permute-start) | collective-permute-done | bytes 135200 | tf_op jit(solution)/shard_map/ppermute | solution.py:32
  21.1 0.0 copy-start.3
  21.1 0.0 copy-start.4
  21.1 0.7 copy-done.3
  21.8 0.0 copy-done.4
  21.8 0.9 copy-done
  22.7 1.0 %copy-done.1 = bf16[256,1024]{1,0:T(8,128)(2,1)S(1)} copy-done((bf16[256,1024]{1,0:T(8,128)(2,1)S(1)}, bf16[256,1024]{1,0:T(8,128)(2,1)}, u32[]{:S(2)}) %copy-start.1) | copy-done | bytes 524312
  23.7 1.0 %copy-done.2 = bf16[256,1024]{1,0:T(8,128)(2,1)S(1)} copy-done((bf16[256,1024]{1,0:T(8,128)(2,1)S(1)}, bf16[256,1024]{1,0:T(8,128)(2,1)}, u32[]{:S(2)}) %copy-start.2) | copy-done | bytes 524312
  24.8 20.0 %shard_map.119 = (bf16[256,1024]{1,0:T(8,128)(2,1)}, bf16[256,1024]{1,0:T(8,128)(2,1)}, bf16[512,128]{1,0:T(8,128)(2,1)S(1)}, bf16[512,128]{1,0:T(8,128)(2,1)S(1...) custom-call(bf16[528,128]{1,0:T(8,128)(2,1)S(1)} %collective-permute, ...), custom_call_target="tpu_custom_call" | custom-call | tf_op jit(solution)/shard_map/pallas_call | solution.py:252
  44.8 15.4 %all-gather.3 = f32[8,2,128]{2,1,0:T(2,128)S(1)} all-gather(f32[1,2,128]{2,1,0:T(2,128)S(1)} %bitcast.12), channel_id=2, replica_groups=mesh['context'=32,'tensor'=8] {'tensor'}, dimensions={0}, use_global_device_ids=true | all-gather | bytes 9216 | tf_op jit(solution)/shard_map/all_gather | solution.py:312
  60.2 13.7 %all-gather.4 = f32[8,2,128]{2,1,0:T(2,128)S(1)} all-gather(f32[1,2,128]{2,1,0:T(2,128)S(1)} %bitcast.15), channel_id=3, replica_groups={{0,8,16,24,32,40,48,56},{64,72,80,88,96,104,112,120},{128,136,144,152,1..., dimensions={0}, use_global_device_ids=true | all-gather | bytes 9216 | tf_op jit(solution)/shard_map/all_gather | solution.py:316
  73.9 5.9 %all-gather.5 = f32[4,2,128]{2,1,0:T(2,128)S(1)} all-gather(f32[1,2,128]{2,1,0:T(2,128)S(1)} %bitcast.16), channel_id=4, replica_groups={{0,64,128,192},{8,72,136,200},{16,80,144,208},{24,88,152,216},{32,96,16..., dimensions={0}, use_global_device_ids=true | all-gather | bytes 5120 | tf_op jit(solution)/shard_map/all_gather | solution.py:316
  79.9 4.4 %collective-permute-start.4 = (bf16[512,128]{1,0:T(8,128)(2,1)S(1)}, bf16[512,128]{1,0:T(8,128)(2,1)S(1)}, u32[]{:S(2)}, u32[]{:S(2)}) collective-permute-start(bf16[512,128]{1,0:T(8,128)(2,1)S(1)} %get-tuple-element.17), channel_id=1, source_target_pairs={{32,0},{40,8},{48,16},{56,24},{64,32},{72,40},{80,48},{88,56},{96,... | collective-permute-start | bytes 393224 | tf_op jit(solution)/shard_map/ppermute | solution.py:32
  84.3 4.1 %collective-permute-start.5 = (bf16[512,128]{1,0:T(8,128)(2,1)S(1)}, bf16[512,128]{1,0:T(8,128)(2,1)S(1)}, u32[]{:S(2)}, u32[]{:S(2)}) collective-permute-start(bf16[512,128]{1,0:T(8,128)(2,1)S(1)} %get-tuple-element.18), channel_id=1, source_target_pairs={{24,0},{32,8},{40,16},{48,24},{56,32},{64,40},{72,48},{80,56},{88,... | collective-permute-start | bytes 393224 | tf_op jit(solution)/shard_map/ppermute | solution.py:32
  88.4 5.3 %collective-permute-start.6 = (bf16[512,128]{1,0:T(8,128)(2,1)S(1)}, bf16[512,128]{1,0:T(8,128)(2,1)S(1)}, u32[]{:S(2)}, u32[]{:S(2)}) collective-permute-start(bf16[512,128]{1,0:T(8,128)(2,1)S(1)} %get-tuple-element.19), channel_id=1, source_target_pairs={{16,0},{24,8},{32,16},{40,24},{48,32},{56,40},{64,48},{72,56},{80,... | collective-permute-start | bytes 393224 | tf_op jit(solution)/shard_map/ppermute | solution.py:32
  93.8 1.9 %collective-permute-start.7 = (bf16[512,128]{1,0:T(8,128)(2,1)S(1)}, bf16[512,128]{1,0:T(8,128)(2,1)S(1)}, u32[]{:S(2)}, u32[]{:S(2)}) collective-permute-start(bf16[512,128]{1,0:T(8,128)(2,1)S(1)} %get-tuple-element.20), channel_id=1, source_target_pairs={{8,0},{16,8},{24,16},{32,24},{40,32},{48,40},{56,48},{64,56},{72,6... | collective-permute-start | bytes 393224 | tf_op jit(solution)/shard_map/ppermute | solution.py:32
  95.7 0.5 slice_bitcast_fusion
  96.2 0.0 collective-permute-done.4
  96.2 0.0 collective-permute-done.5
  96.2 0.3 collective-permute-done.6
  96.5 3.5 %collective-permute-done.7 = bf16[512,128]{1,0:T(8,128)(2,1)S(1)} collective-permute-done((bf16[512,128]{1,0:T(8,128)(2,1)S(1)}, bf16[512,128]{1,0:T(8,128)(2,1)S(1)}, u32[]{:S(2)}, u32[]{:S(2)}) %collective-permute-start.7) | collective-permute-done | bytes 131104 | tf_op jit(solution)/shard_map/ppermute | solution.py:32
  100.1 0.1 add_convert_fusion
  100.2 0.7 fusion
  (7 shorter events, 0.1 us)
Async XLA Ops:
  2.2 13.8 %collective-permute-start.3 = (bf16[528,128]{1,0:T(8,128)(2,1)}, bf16[528,128]{1,0:T(8,128)(2,1)S(1)}, u32[]{:S(2)}, u32[]{:S(2)}) collective-permute-start(bf16[528,128]{1,0:T(8,128)(2,1)} %shard_map.118.b0), channel_id=1, source_target_pairs={{0,8},{8,16},{16,24},{24,32},{32,40},{40,48},{48,56},{56,64},{64,7... | collective-permute-start | bytes 405512 | tf_op jit(solution)/shard_map/ppermute | solution.py:32
  5.9 10.1 %collective-permute-start.2 = (bf16[528,128]{1,0:T(8,128)(2,1)}, bf16[528,128]{1,0:T(8,128)(2,1)S(1)}, u32[]{:S(2)}, u32[]{:S(2)}) collective-permute-start(bf16[528,128]{1,0:T(8,128)(2,1)} %shard_map.118.b0), channel_id=1, source_target_pairs={{0,16},{8,24},{16,32},{24,40},{32,48},{40,56},{48,64},{56,72},{64,... | collective-permute-start | bytes 405512 | tf_op jit(solution)/shard_map/ppermute | solution.py:32
  8.7 8.0 %collective-permute-start.1 = (bf16[528,128]{1,0:T(8,128)(2,1)}, bf16[528,128]{1,0:T(8,128)(2,1)S(1)}, u32[]{:S(2)}, u32[]{:S(2)}) collective-permute-start(bf16[528,128]{1,0:T(8,128)(2,1)} %shard_map.118.b0), channel_id=1, source_target_pairs={{0,24},{8,32},{16,40},{24,48},{32,56},{40,64},{48,72},{56,80},{64,... | collective-permute-start | bytes 405512 | tf_op jit(solution)/shard_map/ppermute | solution.py:32
  11.8 9.3 %collective-permute-start = (bf16[528,128]{1,0:T(8,128)(2,1)}, bf16[528,128]{1,0:T(8,128)(2,1)S(1)}, u32[]{:S(2)}, u32[]{:S(2)}) collective-permute-start(bf16[528,128]{1,0:T(8,128)(2,1)} %shard_map.118.b0), channel_id=1, source_target_pairs={{0,32},{8,40},{16,48},{24,56},{32,64},{40,72},{48,80},{56,88},{64,... | collective-permute-start | bytes 405512 | tf_op jit(solution)/shard_map/ppermute | solution.py:32
  21.1 0.7 copy-start.3
  21.1 0.7 copy-start.4
  21.8 0.9 copy-start
  22.7 1.0 %copy-start.1 = (bf16[256,1024]{1,0:T(8,128)(2,1)S(1)}, bf16[256,1024]{1,0:T(8,128)(2,1)}, u32[]{:S(2)}) copy-start(bf16[256,1024]{1,0:T(8,128)(2,1)} %q_hbm.1) | copy-start | bytes 1572868
  23.7 1.0 %copy-start.2 = (bf16[256,1024]{1,0:T(8,128)(2,1)S(1)}, bf16[256,1024]{1,0:T(8,128)(2,1)}, u32[]{:S(2)}) copy-start(bf16[256,1024]{1,0:T(8,128)(2,1)} %d_hbm.1) | copy-start | bytes 1572868
  79.9 16.3 %collective-permute-start.4 = (bf16[512,128]{1,0:T(8,128)(2,1)S(1)}, bf16[512,128]{1,0:T(8,128)(2,1)S(1)}, u32[]{:S(2)}, u32[]{:S(2)}) collective-permute-start(bf16[512,128]{1,0:T(8,128)(2,1)S(1)} %get-tuple-element.17), channel_id=1, source_target_pairs={{32,0},{40,8},{48,16},{56,24},{64,32},{72,40},{80,48},{88,56},{96,... | collective-permute-start | bytes 393224 | tf_op jit(solution)/shard_map/ppermute | solution.py:32
  84.3 11.9 %collective-permute-start.5 = (bf16[512,128]{1,0:T(8,128)(2,1)S(1)}, bf16[512,128]{1,0:T(8,128)(2,1)S(1)}, u32[]{:S(2)}, u32[]{:S(2)}) collective-permute-start(bf16[512,128]{1,0:T(8,128)(2,1)S(1)} %get-tuple-element.18), channel_id=1, source_target_pairs={{24,0},{32,8},{40,16},{48,24},{56,32},{64,40},{72,48},{80,56},{88,... | collective-permute-start | bytes 393224 | tf_op jit(solution)/shard_map/ppermute | solution.py:32
  88.4 8.1 %collective-permute-start.6 = (bf16[512,128]{1,0:T(8,128)(2,1)S(1)}, bf16[512,128]{1,0:T(8,128)(2,1)S(1)}, u32[]{:S(2)}, u32[]{:S(2)}) collective-permute-start(bf16[512,128]{1,0:T(8,128)(2,1)S(1)} %get-tuple-element.19), channel_id=1, source_target_pairs={{16,0},{24,8},{32,16},{40,24},{48,32},{56,40},{64,48},{72,56},{80,... | collective-permute-start | bytes 393224 | tf_op jit(solution)/shard_map/ppermute | solution.py:32
  93.8 6.3 %collective-permute-start.7 = (bf16[512,128]{1,0:T(8,128)(2,1)S(1)}, bf16[512,128]{1,0:T(8,128)(2,1)S(1)}, u32[]{:S(2)}, u32[]{:S(2)}) collective-permute-start(bf16[512,128]{1,0:T(8,128)(2,1)S(1)} %get-tuple-element.20), channel_id=1, source_target_pairs={{8,0},{16,8},{24,16},{32,24},{40,32},{48,40},{56,48},{64,56},{72,6... | collective-permute-start | bytes 393224 | tf_op jit(solution)/shard_map/ppermute | solution.py:32

commit v3 on v2

--- a/solution.py
+++ b/solution.py
@@ -60,15 +60,27 @@
 
 
 def kernel(
-    b4, b3, b2, b1, b0, q_hbm, d_hbm, qg_ref, kg_ref, f_ref,
+    b4, b2, b0, first_swap, middle_swap, last_swap, q_hbm, d_hbm, qg_ref, kg_ref, f_ref,
     att_hbm, gq_hbm, r4, r3, r2, r1, own_ref, gain_ref,
     q_ref, d_ref, att_ref, gq_ref, cosine, sine, kext, vwin, khat_t, v_t, qhat, qext_t, dcat, dcat_t,
-    s_ref, w_ref, ds_ref, dk, dv, qg_acc, in_sem, att_sem, gq_sem,
+    s_ref, w_ref, ds_ref, dk, dv, qg_acc, b3, b1, in_sem, att_sem, gq_sem,
 ):
     q_copy = pltpu.make_async_copy(q_hbm, q_ref, in_sem.at[0])
     d_copy = pltpu.make_async_copy(d_hbm, d_ref, in_sem.at[1])
     q_copy.start()
     d_copy.start()
+    even = lax.rem(lax.axis_index("context"), 2) == 0
+
+    @pl.when(even)
+    def _():
+        b3[...] = last_swap[...]
+        b1[...] = middle_swap[...]
+
+    @pl.when(jnp.logical_not(even))
+    def _():
+        b3[...] = middle_swap[...]
+        b1[...] = first_swap[...]
+
     blocks = (b4, b3, b2, b1, b0)
     lane = lax.broadcasted_iota(jnp.int32, (SUB, HEAD), 1)
     row = lax.broadcasted_iota(jnp.int32, (SUB, HEAD), 0)
@@ -258,7 +270,7 @@
             shape((2 * TOK, HEAD), f32),
             shape((2, HEAD), f32),
         ],
-        in_specs=[vmem] * 5 + [hbm] * 2 + [vmem] * 3,
+        in_specs=[vmem] * 6 + [hbm] * 2 + [vmem] * 3,
         out_specs=[hbm] * 2 + [vmem] * 6,
         scratch_shapes=[
             pltpu.VMEM((TOK, HEADS * HEAD), bf16),
@@ -281,6 +293,8 @@
             pltpu.VMEM((WINDOW, HEAD), f32),
             pltpu.VMEM((WINDOW, HEAD), f32),
             pltpu.VMEM((8, HEAD), f32),
+            pltpu.VMEM((MSG, HEAD), bf16),
+            pltpu.VMEM((MSG, HEAD), bf16),
             pltpu.SemaphoreType.DMA((2,)),
             pltpu.SemaphoreType.DMA((HEADS // 2,)),
             pltpu.SemaphoreType.DMA((HEADS // 2,)),
@@ -308,19 +322,24 @@
     )(keys, values, ids)
 
 
-def summed_over_all(terms):
-    total = jnp.sum(lax.all_gather(terms, "tensor"), axis=0)
-    rows = [list(range(8 * y, 8 * y + 8)) for y in range(4)]
-    columns = [[8 * y + k for y in range(4)] for k in range(8)]
-    for groups in (rows, columns):
-        total = jnp.sum(lax.all_gather(total, "context", axis_index_groups=groups), axis=0)
-    return total
+def swapped(block, ways=(0, 1)):
+    route = [(i, i ^ 1) for i in range(lax.axis_size("context")) if i % 2 in ways]
+    return lax.ppermute(block, "context", route)
+
+
+def summed_over(axis, terms):
+    copies = jnp.broadcast_to(terms, (lax.axis_size(axis),) + terms.shape)
+    return jnp.sum(lax.all_to_all(copies, axis, 0, 0), axis=0)
 
 
 def body(queries, keys, values, output_gradient, q_gain, k_gain, doc_ids):
     message = pack(keys, values, doc_ids.reshape(2, HEAD))
-    blocks = [passed_along(message, "context", distance) for distance in range(REACH, 0, -1)]
-    blocks.append(message)
+    two = passed_along(message, "context", 2)
+    first_swap = swapped(message, (0,))
+    four = passed_along(two, "context", 2)
+    middle_swap = swapped(two)
+    last_swap = swapped(four, (1,))
+    blocks = [four, two, message, first_swap, middle_swap, last_swap]
     half = jnp.arange(HEAD // 2, dtype=jnp.float32)
     frequency = THETA ** (-(half * 2.0 / HEAD))
     frequency = jnp.concatenate([frequency, frequency]).reshape(1, HEAD)
@@ -336,7 +355,7 @@
     for distance, block in zip(range(REACH, 0, -1), returns):
         total = total + passed_along(block, "context", -distance)
     total = total.astype(jnp.bfloat16)
-    gain_total = summed_over_all(gains)
+    gain_total = summed_over("context", summed_over("tensor", gains))
     return (
         attended,
         query_gradient,

time: 101 us -> 88.3 us (0.87)
  the two profiles are of different devices: /device:TPU:11 before, /device:TPU:15 now
where the time goes in v3:
time: 88.3 us; the launch traced here: 87.8 us
  starting transfers between devices  35.9 us (41%)
  Pallas kernels  21.6 us (24%)
  blocking collectives  14.6 us (17%)
  waiting for transfers between devices  9.25 us (10%)
  local copies, waits for them, and re-layouts  5.47 us (6%)
    ppermute x6, starting transfers between devices, passed_along(): return lax.ppermute(block, axis, route)  20.2 us
    pallas_call x1, Pallas kernels, attention(): pl.pallas_call(kernel, out_shape=[shape((TOK, HEADS * HEAD), bf16), shape...  20.1 us
    all_to_all x1, blocking collectives, summed_over(): return jnp.sum(lax.all_to_all(copies, axis, 0, 0), axis=0)  14.6 us
    all_to_all x1, starting transfers between devices, summed_over(): return jnp.sum(lax.all_to_all(copies, axis, 0, 0), axis=0)  9.48 us
    ppermute x6, waiting for transfers between devices, passed_along(): return lax.ppermute(block, axis, route)  8.38 us
    ppermute x3, starting transfers between devices, swapped(): return lax.ppermute(block, 'context', route)  6.25 us
    unnamed x10, local copies, waits for them, and re-layouts  3.66 us
  transfers between devices with their start and end apart: 10, of which 5 were waited for; matrix products, arithmetic and copies ran while one was open for 1% of the time, Pallas kernels for 0%

profile of v3, /device:TPU:15, one launch (start us, length us, event | category | flops | bytes accessed | tf_op | source)
XLA Modules:
  0.0 87.8 jit_solution(17786716106056858997)
XLA Ops:
  0.6 1.5 %shard_map.118.b0 = bf16[528,128]{1,0:T(8,128)(2,1)} custom-call(bf16[256,128]{1,0:T(8,128)(2,1)} %keys.1, bf16[256,128]{1,0:T(8,128)(2,1)} %values.1, s32[2,128]{1,0:T(2,128)} %bitcast.11), custom_call_target="tpu_custom_call" | custom-call | tf_op jit(solution)/shard_map/pallas_call | solution.py:317
  2.2 3.1 %collective-permute-start = (bf16[528,128]{1,0:T(8,128)(2,1)}, bf16[528,128]{1,0:T(8,128)(2,1)S(1)}, u32[]{:S(2)}, u32[]{:S(2)}) collective-permute-start(bf16[528,128]{1,0:T(8,128)(2,1)} %shard_map.118.b0), channel_id=1, source_target_pairs={{0,16},{8,24},{16,32},{24,40},{32,48},{40,56},{48,64},{56,72},{64,... | collective-permute-start | bytes 405512 | tf_op jit(solution)/shard_map/ppermute | solution.py:32
  5.3 3.4 %collective-permute-done.b2 = bf16[528,128]{1,0:T(8,128)(2,1)S(1)} collective-permute-done((bf16[528,128]{1,0:T(8,128)(2,1)}, bf16[528,128]{1,0:T(8,128)(2,1)S(1)}, u32[]{:S(2)}, u32[]{:S(2)}) %collective-permute-start) | collective-permute-done | bytes 135200 | tf_op jit(solution)/shard_map/ppermute | solution.py:32
  8.7 5.2 %collective-permute-start.1 = (bf16[528,128]{1,0:T(8,128)(2,1)S(1)}, bf16[528,128]{1,0:T(8,128)(2,1)S(1)}, u32[]{:S(2)}, u32[]{:S(2)}) collective-permute-start(bf16[528,128]{1,0:T(8,128)(2,1)S(1)} %collective-permute-done.b2), channel_id=1, source_target_pairs={{0,16},{8,24},{16,32},{24,40},{32,48},{40,56},{48,64},{56,72},{64,... | collective-permute-start | bytes 405512 | tf_op jit(solution)/shard_map/ppermute | solution.py:32
  13.9 1.3 %collective-permute-start.2 = (bf16[528,128]{1,0:T(8,128)(2,1)}, bf16[528,128]{1,0:T(8,128)(2,1)S(1)}, u32[]{:S(2)}, u32[]{:S(2)}) collective-permute-start(bf16[528,128]{1,0:T(8,128)(2,1)} %shard_map.118.b0), channel_id=1, source_target_pairs={{0,8},{16,24},{32,40},{48,56},{64,72},{80,88},{96,104},{112,120},{... | collective-permute-start | bytes 405512 | tf_op jit(solution)/shard_map/ppermute | solution.py:327
  15.2 1.9 %collective-permute-start.3 = (bf16[528,128]{1,0:T(8,128)(2,1)S(1)}, bf16[528,128]{1,0:T(8,128)(2,1)S(1)}, u32[]{:S(2)}, u32[]{:S(2)}) collective-permute-start(bf16[528,128]{1,0:T(8,128)(2,1)S(1)} %collective-permute-done.b2), channel_id=1, source_target_pairs={{0,8},{8,0},{16,24},{24,16},{32,40},{40,32},{48,56},{56,48},{64,72... | collective-permute-start | bytes 405512 | tf_op jit(solution)/shard_map/ppermute | solution.py:327
  17.2 0.0 collective-permute-done.1.b4
  17.2 3.0 %collective-permute-start.4 = (bf16[528,128]{1,0:T(8,128)(2,1)S(1)}, bf16[528,128]{1,0:T(8,128)(2,1)S(1)}, u32[]{:S(2)}, u32[]{:S(2)}) collective-permute-start(bf16[528,128]{1,0:T(8,128)(2,1)S(1)} %collective-permute-done.1.b4), channel_id=1, source_target_pairs={{8,0},{24,16},{40,32},{56,48},{72,64},{88,80},{104,96},{120,112},{... | collective-permute-start | bytes 405512 | tf_op jit(solution)/shard_map/ppermute | solution.py:327
  20.2 0.1 maximum_bitcast_fusion.f_ref
  20.3 0.0 collective-permute-done.2.first_swap
  20.3 0.0 collective-permute-done.3.middle_swap
  20.3 0.9 collective-permute-done.4.last_swap
  21.2 0.7 copy-done.3
  21.8 0.0 copy-done.4
  21.9 0.9 %copy-done = bf16[528,128]{1,0:T(8,128)(2,1)S(1)} copy-done((bf16[528,128]{1,0:T(8,128)(2,1)S(1)}, bf16[528,128]{1,0:T(8,128)(2,1)}, u32[]{:S(2)}) %copy-start) | copy-done | bytes 135192
  22.8 1.0 %copy-done.1 = bf16[256,1024]{1,0:T(8,128)(2,1)S(1)} copy-done((bf16[256,1024]{1,0:T(8,128)(2,1)S(1)}, bf16[256,1024]{1,0:T(8,128)(2,1)}, u32[]{:S(2)}) %copy-start.1) | copy-done | bytes 524312
  23.8 1.0 %copy-done.2 = bf16[256,1024]{1,0:T(8,128)(2,1)S(1)} copy-done((bf16[256,1024]{1,0:T(8,128)(2,1)S(1)}, bf16[256,1024]{1,0:T(8,128)(2,1)}, u32[]{:S(2)}) %copy-start.2) | copy-done | bytes 524312
  24.8 20.1 %shard_map.119 = (bf16[256,1024]{1,0:T(8,128)(2,1)}, bf16[256,1024]{1,0:T(8,128)(2,1)}, bf16[512,128]{1,0:T(8,128)(2,1)S(1)}, bf16[512,128]{1,0:T(8,128)(2,1)S(1...) custom-call(bf16[528,128]{1,0:T(8,128)(2,1)S(1)} %collective-permute, ...), custom_call_target="tpu_custom_call" | custom-call | tf_op jit(solution)/shard_map/pallas_call | solution.py:264
  44.9 14.6 %all_to_all.10 = f32[8,2,128]{2,1,0:T(2,128)S(1)} all-to-all(f32[8,2,128]{2,1,0:T(2,128)S(1)} %broadcast_in_dim.6), channel_id=1, replica_groups=mesh['context'=32,'tensor'=8] {'tensor'}, dimensions={0} | all-to-all | bytes 16384 | tf_op jit(solution)/shard_map/all_to_all | solution.py:332
  59.5 0.6 broadcast_in_dim.7
  60.1 9.5 %all-to-all-start.1 = ((f32[32,2,128]{2,1,0:T(2,128)}), f32[32,2,128]{2,1,0:T(2,128)S(1)}, u32[]{:S(2)}, u32[]{:S(2)}) async-start(f32[32,2,128]{2,1,0:T(2,128)} %broadcast_in_dim.7), calls=%async_computation.1 | async-start | bytes 65536 | tf_op jit(solution)/shard_map/all_to_all | solution.py:332
  69.6 3.1 %collective-permute-start.5 = (bf16[512,128]{1,0:T(8,128)(2,1)S(1)}, bf16[512,128]{1,0:T(8,128)(2,1)S(1)}, u32[]{:S(2)}, u32[]{:S(2)}) collective-permute-start(bf16[512,128]{1,0:T(8,128)(2,1)S(1)} %get-tuple-element.17), channel_id=1, source_target_pairs={{32,0},{40,8},{48,16},{56,24},{64,32},{72,40},{80,48},{88,56},{96,... | collective-permute-start | bytes 393224 | tf_op jit(solution)/shard_map/ppermute | solution.py:32
  72.7 2.1 %collective-permute-start.6 = (bf16[512,128]{1,0:T(8,128)(2,1)S(1)}, bf16[512,128]{1,0:T(8,128)(2,1)S(1)}, u32[]{:S(2)}, u32[]{:S(2)}) collective-permute-start(bf16[512,128]{1,0:T(8,128)(2,1)S(1)} %get-tuple-element.18), channel_id=1, source_target_pairs={{24,0},{32,8},{40,16},{48,24},{56,32},{64,40},{72,48},{80,56},{88,... | collective-permute-start | bytes 393224 | tf_op jit(solution)/shard_map/ppermute | solution.py:32
  74.9 3.7 %collective-permute-start.7 = (bf16[512,128]{1,0:T(8,128)(2,1)S(1)}, bf16[512,128]{1,0:T(8,128)(2,1)S(1)}, u32[]{:S(2)}, u32[]{:S(2)}) collective-permute-start(bf16[512,128]{1,0:T(8,128)(2,1)S(1)} %get-tuple-element.19), channel_id=1, source_target_pairs={{16,0},{24,8},{32,16},{40,24},{48,32},{56,40},{64,48},{72,56},{80,... | collective-permute-start | bytes 393224 | tf_op jit(solution)/shard_map/ppermute | solution.py:32
  78.6 3.0 %collective-permute-start.8 = (bf16[512,128]{1,0:T(8,128)(2,1)S(1)}, bf16[512,128]{1,0:T(8,128)(2,1)S(1)}, u32[]{:S(2)}, u32[]{:S(2)}) collective-permute-start(bf16[512,128]{1,0:T(8,128)(2,1)S(1)} %get-tuple-element.20), channel_id=1, source_target_pairs={{8,0},{16,8},{24,16},{32,24},{40,32},{48,40},{56,48},{64,56},{72,6... | collective-permute-start | bytes 393224 | tf_op jit(solution)/shard_map/ppermute | solution.py:32
  81.6 0.5 slice_bitcast_fusion
  82.1 0.0 collective-permute-done.5
  82.1 0.8 collective-permute-done.6
  82.9 1.4 %collective-permute-done.7 = bf16[512,128]{1,0:T(8,128)(2,1)S(1)} collective-permute-done((bf16[512,128]{1,0:T(8,128)(2,1)S(1)}, bf16[512,128]{1,0:T(8,128)(2,1)S(1)}, u32[]{:S(2)}, u32[]{:S(2)}) %collective-permute-start.7) | collective-permute-done | bytes 131104 | tf_op jit(solution)/shard_map/ppermute | solution.py:32
  84.3 2.7 %collective-permute-done.8 = bf16[512,128]{1,0:T(8,128)(2,1)S(1)} collective-permute-done((bf16[512,128]{1,0:T(8,128)(2,1)S(1)}, bf16[512,128]{1,0:T(8,128)(2,1)S(1)}, u32[]{:S(2)}, u32[]{:S(2)}) %collective-permute-start.8) | collective-permute-done | bytes 131104 | tf_op jit(solution)/shard_map/ppermute | solution.py:32
  87.0 0.1 add_convert_fusion
  87.1 0.7 fusion
  (10 shorter events, 0.1 us)
Async XLA Ops:
  2.2 6.5 %collective-permute-start = (bf16[528,128]{1,0:T(8,128)(2,1)}, bf16[528,128]{1,0:T(8,128)(2,1)S(1)}, u32[]{:S(2)}, u32[]{:S(2)}) collective-permute-start(bf16[528,128]{1,0:T(8,128)(2,1)} %shard_map.118.b0), channel_id=1, source_target_pairs={{0,16},{8,24},{16,32},{24,40},{32,48},{40,56},{48,64},{56,72},{64,... | collective-permute-start | bytes 405512 | tf_op jit(solution)/shard_map/ppermute | solution.py:32
  8.7 8.4 %collective-permute-start.1 = (bf16[528,128]{1,0:T(8,128)(2,1)S(1)}, bf16[528,128]{1,0:T(8,128)(2,1)S(1)}, u32[]{:S(2)}, u32[]{:S(2)}) collective-permute-start(bf16[528,128]{1,0:T(8,128)(2,1)S(1)} %collective-permute-done.b2), channel_id=1, source_target_pairs={{0,16},{8,24},{16,32},{24,40},{32,48},{40,56},{48,64},{56,72},{64,... | collective-permute-start | bytes 405512 | tf_op jit(solution)/shard_map/ppermute | solution.py:32
  13.9 6.4 %collective-permute-start.2 = (bf16[528,128]{1,0:T(8,128)(2,1)}, bf16[528,128]{1,0:T(8,128)(2,1)S(1)}, u32[]{:S(2)}, u32[]{:S(2)}) collective-permute-start(bf16[528,128]{1,0:T(8,128)(2,1)} %shard_map.118.b0), channel_id=1, source_target_pairs={{0,8},{16,24},{32,40},{48,56},{64,72},{80,88},{96,104},{112,120},{... | collective-permute-start | bytes 405512 | tf_op jit(solution)/shard_map/ppermute | solution.py:327
  15.2 5.1 %collective-permute-start.3 = (bf16[528,128]{1,0:T(8,128)(2,1)S(1)}, bf16[528,128]{1,0:T(8,128)(2,1)S(1)}, u32[]{:S(2)}, u32[]{:S(2)}) collective-permute-start(bf16[528,128]{1,0:T(8,128)(2,1)S(1)} %collective-permute-done.b2), channel_id=1, source_target_pairs={{0,8},{8,0},{16,24},{24,16},{32,40},{40,32},{48,56},{56,48},{64,72... | collective-permute-start | bytes 405512 | tf_op jit(solution)/shard_map/ppermute | solution.py:327
  17.2 4.0 %collective-permute-start.4 = (bf16[528,128]{1,0:T(8,128)(2,1)S(1)}, bf16[528,128]{1,0:T(8,128)(2,1)S(1)}, u32[]{:S(2)}, u32[]{:S(2)}) collective-permute-start(bf16[528,128]{1,0:T(8,128)(2,1)S(1)} %collective-permute-done.1.b4), channel_id=1, source_target_pairs={{8,0},{24,16},{40,32},{56,48},{72,64},{88,80},{104,96},{120,112},{... | collective-permute-start | bytes 405512 | tf_op jit(solution)/shard_map/ppermute | solution.py:327
  21.2 0.7 copy-start.3
  21.2 0.7 copy-start.4
  21.9 0.9 %copy-start = (bf16[528,128]{1,0:T(8,128)(2,1)S(1)}, bf16[528,128]{1,0:T(8,128)(2,1)}, u32[]{:S(2)}) copy-start(bf16[528,128]{1,0:T(8,128)(2,1)} %shard_map.118.b0) | copy-start | bytes 405508
  22.8 1.0 %copy-start.1 = (bf16[256,1024]{1,0:T(8,128)(2,1)S(1)}, bf16[256,1024]{1,0:T(8,128)(2,1)}, u32[]{:S(2)}) copy-start(bf16[256,1024]{1,0:T(8,128)(2,1)} %q_hbm.1) | copy-start | bytes 1572868
  23.8 1.0 %copy-start.2 = (bf16[256,1024]{1,0:T(8,128)(2,1)S(1)}, bf16[256,1024]{1,0:T(8,128)(2,1)}, u32[]{:S(2)}) copy-start(bf16[256,1024]{1,0:T(8,128)(2,1)} %d_hbm.1) | copy-start | bytes 1572868
  60.1 21.4 %all-to-all-start.1 = ((f32[32,2,128]{2,1,0:T(2,128)}), f32[32,2,128]{2,1,0:T(2,128)S(1)}, u32[]{:S(2)}, u32[]{:S(2)}) async-start(f32[32,2,128]{2,1,0:T(2,128)} %broadcast_in_dim.7), calls=%async_computation.1 | async-start | bytes 65536 | tf_op jit(solution)/shard_map/all_to_all | solution.py:332
  69.6 12.5 %collective-permute-start.5 = (bf16[512,128]{1,0:T(8,128)(2,1)S(1)}, bf16[512,128]{1,0:T(8,128)(2,1)S(1)}, u32[]{:S(2)}, u32[]{:S(2)}) collective-permute-start(bf16[512,128]{1,0:T(8,128)(2,1)S(1)} %get-tuple-element.17), channel_id=1, source_target_pairs={{32,0},{40,8},{48,16},{56,24},{64,32},{72,40},{80,48},{88,56},{96,... | collective-permute-start | bytes 393224 | tf_op jit(solution)/shard_map/ppermute | solution.py:32
  72.7 10.1 %collective-permute-start.6 = (bf16[512,128]{1,0:T(8,128)(2,1)S(1)}, bf16[512,128]{1,0:T(8,128)(2,1)S(1)}, u32[]{:S(2)}, u32[]{:S(2)}) collective-permute-start(bf16[512,128]{1,0:T(8,128)(2,1)S(1)} %get-tuple-element.18), channel_id=1, source_target_pairs={{24,0},{32,8},{40,16},{48,24},{56,32},{64,40},{72,48},{80,56},{88,... | collective-permute-start | bytes 393224 | tf_op jit(solution)/shard_map/ppermute | solution.py:32
  74.9 9.4 %collective-permute-start.7 = (bf16[512,128]{1,0:T(8,128)(2,1)S(1)}, bf16[512,128]{1,0:T(8,128)(2,1)S(1)}, u32[]{:S(2)}, u32[]{:S(2)}) collective-permute-start(bf16[512,128]{1,0:T(8,128)(2,1)S(1)} %get-tuple-element.19), channel_id=1, source_target_pairs={{16,0},{24,8},{32,16},{40,24},{48,32},{56,40},{64,48},{72,56},{80,... | collective-permute-start | bytes 393224 | tf_op jit(solution)/shard_map/ppermute | solution.py:32
  78.6 8.5 %collective-permute-start.8 = (bf16[512,128]{1,0:T(8,128)(2,1)S(1)}, bf16[512,128]{1,0:T(8,128)(2,1)S(1)}, u32[]{:S(2)}, u32[]{:S(2)}) collective-permute-start(bf16[512,128]{1,0:T(8,128)(2,1)S(1)} %get-tuple-element.20), channel_id=1, source_target_pairs={{8,0},{16,8},{24,16},{32,24},{40,32},{48,40},{56,48},{64,56},{72,6... | collective-permute-start | bytes 393224 | tf_op jit(solution)/shard_map/ppermute | solution.py:32

commit v4 on v3

--- a/solution.py
+++ b/solution.py
@@ -59,16 +59,45 @@
     return jnp.where((quadrant & 2) == 2, -value, value)
 
 
+def prepare_kernel(q_ref, d_ref, xh_ref, scale_ref, dcat, dcat_t):
+    for sub in range(2):
+        tokens = slice(sub * SUB, (sub + 1) * SUB)
+        for h in range(HEADS):
+            at = (h // 2) * 512 + sub * 256 + (h % 2) * SUB
+            rows = slice(at, at + SUB)
+            x = q_ref[tokens, h * HEAD : (h + 1) * HEAD].astype(jnp.float32)
+            r = lax.rsqrt(jnp.mean(x * x, axis=1, keepdims=True) + EPSILON)
+            xh_ref[rows, :] = x * r
+            scale_ref[rows, :] = jnp.broadcast_to(r, (SUB, HEAD))
+            d = d_ref[tokens, h * HEAD : (h + 1) * HEAD]
+            dcat[rows, :] = d
+            dcat_t[h // 2, :, at % 512 : at % 512 + SUB] = d.astype(jnp.float32).T.astype(jnp.bfloat16)
+
+
+def prepare(queries, output_gradient):
+    vmem = pl.BlockSpec(memory_space=pltpu.VMEM)
+    f32, bf16 = jnp.float32, jnp.bfloat16
+    shape = jax.ShapeDtypeStruct
+    return pl.pallas_call(
+        prepare_kernel,
+        out_shape=[
+            shape((HEADS * TOK, HEAD), f32),
+            shape((HEADS * TOK, HEAD), f32),
+            shape((HEADS * TOK, HEAD), bf16),
+            shape((HEADS // 2, HEAD, 512), bf16),
+        ],
+        in_specs=[vmem] * 2,
+        out_specs=[vmem] * 4,
+        cost_estimate=pl.CostEstimate(flops=10**9, bytes_accessed=4 * 2**20, transcendentals=0),
+    )(queries, output_gradient)
+
+
 def kernel(
-    b4, b2, b0, first_swap, middle_swap, last_swap, q_hbm, d_hbm, qg_ref, kg_ref, f_ref,
+    b4, b2, b0, first_swap, middle_swap, last_swap, xh_ref, scale_ref, dcat, dcat_t, qg_ref, kg_ref, f_ref,
     att_hbm, gq_hbm, r4, r3, r2, r1, own_ref, gain_ref,
-    q_ref, d_ref, att_ref, gq_ref, cosine, sine, kext, vwin, khat_t, v_t, qhat, qext_t, dcat, dcat_t,
-    s_ref, w_ref, ds_ref, dk, dv, qg_acc, b3, b1, in_sem, att_sem, gq_sem,
+    att_ref, gq_ref, cosine, sine, kext, vwin, khat_t, v_t, qhat, qext_t,
+    s_ref, w_ref, ds_ref, dk, dv, qg_acc, b3, b1, att_sem, gq_sem,
 ):
-    q_copy = pltpu.make_async_copy(q_hbm, q_ref, in_sem.at[0])
-    d_copy = pltpu.make_async_copy(d_hbm, d_ref, in_sem.at[1])
-    q_copy.start()
-    d_copy.start()
     even = lax.rem(lax.axis_index("context"), 2) == 0
 
     @pl.when(even)
@@ -125,10 +154,7 @@
         vwin[rows, :] = values
         v_t[:, rows] = values.astype(jnp.float32).T.astype(jnp.bfloat16)
 
-    q_copy.wait()
-    d_copy.wait()
     for sub in range(2):
-        tokens = slice(sub * SUB, (sub + 1) * SUB)
         window_rows = slice(REACH * TOK + sub * SUB, REACH * TOK + (sub + 1) * SUB)
         c_q = cosine[window_rows, :]
         s_q = sine[window_rows, :]
@@ -136,26 +162,25 @@
         for h in range(HEADS):
             at = (h // 2) * 512 + sub * 256 + (h % 2) * SUB
             lanes = slice(at % 512, at % 512 + SUB)
-            x = q_ref[tokens, h * HEAD : (h + 1) * HEAD].astype(jnp.float32)
-            normed = x * lax.rsqrt(jnp.mean(x * x, axis=1, keepdims=True) + EPSILON) * q_gain
+            normed = xh_ref[at : at + SUB, :] * q_gain
             hat = normed * c_q + half_turned(normed) * s_q
             qhat[at : at + SUB, :] = hat.astype(jnp.bfloat16)
             qext_t[h // 2, 0:HEAD, lanes] = hat.T.astype(jnp.bfloat16)
             qext_t[h // 2, HEAD:, lanes] = other
-            d = d_ref[tokens, h * HEAD : (h + 1) * HEAD]
-            dcat[at : at + SUB, :] = d
-            dcat_t[h // 2, :, lanes] = d.astype(jnp.float32).T.astype(jnp.bfloat16)
 
     dk[...] = jnp.zeros_like(dk)
     dv[...] = jnp.zeros_like(dv)
     qg_acc[...] = jnp.zeros_like(qg_acc)
     zero = jnp.zeros((SUB, 256), jnp.bfloat16)
     for ref in (w_ref, ds_ref):
-        ref[0:SUB, 256:512] = zero
-        ref[SPAN:WINDOW, 0:256] = zero
+        ref[0, 0:SUB, 256:512] = zero
+        ref[0, SPAN:WINDOW, 0:256] = zero
+        ref[1] = jnp.zeros((WINDOW, 512), jnp.bfloat16)
     later = jnp.where(row <= lane, 0.0, -1e30)
     later = jnp.concatenate([later, later], axis=1)
     last = SPAN - SUB
+    spans = (slice(0, SPAN), slice(SUB, WINDOW))
+    columns_of = (slice(0, 256), slice(256, 512))
 
     def copies(pair):
         columns = pl.ds(pl.multiple_of(pair * 256, 256), 256)
@@ -164,14 +189,17 @@
             pltpu.make_async_copy(gq_ref.at[:, columns], gq_hbm.at[:, columns], gq_sem.at[pair]),
         )
 
+    def key_terms(pair, slot):
+        at = pl.multiple_of(pair * 512, 512)
+        dk[...] += dot(ds_ref[slot], qhat[pl.ds(at, 512), :])
+        dv[...] += dot(w_ref[slot], dcat[pl.ds(at, 512), :])
+
     def pair_step(pair, carry):
         at = pl.multiple_of(pair * 512, 512)
-        spans = (slice(0, SPAN), slice(SUB, WINDOW))
-        columns_of = (slice(0, 256), slice(256, 512))
-        shifts = []
-        for sub in range(2):
-            cols = columns_of[sub]
-            s = dot(kext[spans[sub], :], qext_t[pair, :, cols])
+        slot = lax.rem(pair, 2)
+
+        def scores(sub):
+            s = dot(kext[spans[sub], :], qext_t[pair, :, columns_of[sub]])
             tail = s[last:] + later
             s_ref[sub, 0:last, :] = s[:last]
             s_ref[sub, last:, :] = tail
@@ -179,56 +207,80 @@
                 jnp.max(s[:last].reshape(last // 8, 8, 256), axis=0),
                 jnp.max(tail.reshape(SUB // 8, 8, 256), axis=0),
             )
-            shifts.append(jnp.max(top, axis=0, keepdims=True) * EXP2)
-        att_ts = []
-        for sub in range(2):
-            cols = columns_of[sub]
-            base = sub * SUB
+            return jnp.max(top, axis=0, keepdims=True) * EXP2
+
+        def exponents(sub, shift):
             total = jnp.zeros((8, 256), jnp.float32)
             for c in range(CHUNKS):
-                e = jnp.exp2(s_ref[sub, c * SUB : (c + 1) * SUB, :] * EXP2 - shifts[sub])
+                e = jnp.exp2(s_ref[sub, c * SUB : (c + 1) * SUB, :] * EXP2 - shift)
                 s_ref[sub, c * SUB : (c + 1) * SUB, :] = e
                 total = total + jnp.sum(e.reshape(SUB // 8, 8, 256), axis=0)
-            inverse = 1.0 / jnp.sum(total, axis=0, keepdims=True)
+            return 1.0 / jnp.sum(total, axis=0, keepdims=True)
+
+        def weigh(sub, inverse):
             for c in range(CHUNKS):
-                keys = slice(base + c * SUB, base + (c + 1) * SUB)
+                keys = slice((sub + c) * SUB, (sub + c + 1) * SUB)
                 w = s_ref[sub, c * SUB : (c + 1) * SUB, :] * inverse
-                w_ref[keys, cols] = w.astype(jnp.bfloat16)
-            att_ts.append(dot(v_t[:, spans[sub]], w_ref[spans[sub], cols]))
-        for sub in range(2):
-            cols = columns_of[sub]
-            span = spans[sub]
-            att_t = att_ts[sub]
-            d_t = dcat_t[pair, :, cols]
+                w_ref[slot, keys, columns_of[sub]] = w.astype(jnp.bfloat16)
+
+        def attend(sub):
+            att_t = dot(v_t[:, spans[sub]], w_ref[slot, spans[sub], columns_of[sub]])
+            d_t = dcat_t[pair, :, columns_of[sub]]
             center = jnp.sum(att_t * d_t.astype(jnp.float32), axis=0, keepdims=True)
-            dw = dot(vwin[span, :], d_t)
-            ds = w_ref[span, cols].astype(jnp.float32) * (dw - center)
-            ds_ref[span, cols] = ds.astype(jnp.bfloat16)
-            dq_t = dot(khat_t[:, span], ds_ref[span, cols]) * SCALING
+            tokens = slice(sub * SUB, (sub + 1) * SUB)
+            for g in range(2):
+                columns = pl.ds(pl.multiple_of(pair * 256 + g * HEAD, HEAD), HEAD)
+                att_ref[tokens, columns] = att_t[:, g * SUB : (g + 1) * SUB].T.astype(jnp.bfloat16)
+            return center
+
+        def score_terms(sub, center):
+            dw = dot(vwin[spans[sub], :], dcat_t[pair, :, columns_of[sub]])
+            w = w_ref[slot, spans[sub], columns_of[sub]].astype(jnp.float32)
+            ds_ref[slot, spans[sub], columns_of[sub]] = (w * (dw - center)).astype(jnp.bfloat16)
+
+        def query_terms(sub):
+            dq_t = dot(khat_t[:, spans[sub]], ds_ref[slot, spans[sub], columns_of[sub]]) * SCALING
             tokens = slice(sub * SUB, (sub + 1) * SUB)
             window_rows = slice(REACH * TOK + sub * SUB, REACH * TOK + (sub + 1) * SUB)
             c_q = cosine[window_rows, :]
             s_q = sine[window_rows, :]
             for g in range(2):
                 columns = pl.ds(pl.multiple_of(pair * 256 + g * HEAD, HEAD), HEAD)
-                att = att_t[:, g * SUB : (g + 1) * SUB].T
-                att_ref[tokens, columns] = att.astype(jnp.bfloat16)
+                rows = pl.ds(pl.multiple_of(at + sub * 256 + g * SUB, SUB), SUB)
                 dq = dq_t[:, g * SUB : (g + 1) * SUB].T
-                x = q_ref[tokens, columns].astype(jnp.float32)
-                r = lax.rsqrt(jnp.mean(x * x, axis=1, keepdims=True) + EPSILON)
-                xh = x * r
+                xh = xh_ref[rows, :]
                 dn = dq * c_q - half_turned(dq) * s_q
                 qg_acc[...] += jnp.sum((dn * xh).reshape(SUB // 8, 8, HEAD), axis=0)
                 dxh = dn * q_gain
-                gq = r * (dxh - xh * jnp.mean(dxh * xh, axis=1, keepdims=True))
+                gq = scale_ref[rows, :] * (dxh - xh * jnp.mean(dxh * xh, axis=1, keepdims=True))
                 gq_ref[tokens, columns] = gq.astype(jnp.bfloat16)
-        dk[...] += dot(ds_ref[...], qhat[pl.ds(at, 512), :])
-        dv[...] += dot(w_ref[...], dcat[pl.ds(at, 512), :])
+
+        shift_0 = scores(0)
+        shift_1 = scores(1)
+        inverse_0 = exponents(0, shift_0)
+        key_terms(jnp.maximum(pair - 1, 0), 1 - slot)
+        weigh(0, inverse_0)
+        inverse_1 = exponents(1, shift_1)
+        center_0 = attend(0)
+        score_terms(0, center_0)
+        weigh(1, inverse_1)
+        query_terms(0)
+        center_1 = attend(1)
+        score_terms(1, center_1)
+        query_terms(1)
         for copy in copies(pair):
             copy.start()
+
+        @pl.when(pair == 0)
+        def _():
+            for ref in (w_ref, ds_ref):
+                ref[1, 0:SUB, 256:512] = zero
+                ref[1, SPAN:WINDOW, 0:256] = zero
+
         return carry
 
     lax.fori_loop(0, HEADS // 2, pair_step, 0)
+    key_terms(HEADS // 2 - 1, 1)
 
     kg = jnp.zeros((8, HEAD), jnp.float32)
     outs = (r4, r3, r2, r1, own_ref)
@@ -246,17 +298,21 @@
         out = outs[j // 2]
         out[here, :] = gk.astype(out.dtype)
         out[TOK + (j % 2) * SUB : TOK + (j % 2 + 1) * SUB, :] = dv[rows, :].astype(out.dtype)
-    gain_ref[0:1, :] = jnp.sum(qg_acc[...], axis=0, keepdims=True)
-    gain_ref[1:2, :] = jnp.sum(kg, axis=0, keepdims=True)
+    gains = jnp.concatenate(
+        [jnp.sum(qg_acc[...], axis=0, keepdims=True), jnp.sum(kg, axis=0, keepdims=True)]
+    )
+    for i in range(gain_ref.shape[0]):
+        gain_ref[i] = gains
     for pair in range(HEADS // 2):
         for copy in copies(pair):
             copy.wait()
 
 
 RETURN = jnp.bfloat16
-
-
-def attention(blocks, queries, output_gradient, q_gain, k_gain, frequency):
+GROUP = 16
+
+
+def attention(blocks, prepared, q_gain, k_gain, frequency):
     vmem = pl.BlockSpec(memory_space=pltpu.VMEM)
     hbm = pl.BlockSpec(memory_space=pl.ANY)
     f32, bf16 = jnp.float32, jnp.bfloat16
@@ -268,13 +324,11 @@
             shape((TOK, HEADS * HEAD), bf16),
             *[shape((2 * TOK, HEAD), RETURN) for _ in range(REACH)],
             shape((2 * TOK, HEAD), f32),
-            shape((2, HEAD), f32),
+            shape((GROUP, 2, HEAD), f32),
         ],
-        in_specs=[vmem] * 6 + [hbm] * 2 + [vmem] * 3,
+        in_specs=[vmem] * 13,
         out_specs=[hbm] * 2 + [vmem] * 6,
         scratch_shapes=[
-            pltpu.VMEM((TOK, HEADS * HEAD), bf16),
-            pltpu.VMEM((TOK, HEADS * HEAD), bf16),
             pltpu.VMEM((TOK, HEADS * HEAD), bf16),
             pltpu.VMEM((TOK, HEADS * HEAD), bf16),
             pltpu.VMEM((WINDOW, HEAD), f32),
@@ -285,22 +339,19 @@
             pltpu.VMEM((HEAD, WINDOW), bf16),
             pltpu.VMEM((HEADS * TOK, HEAD), bf16),
             pltpu.VMEM((HEADS // 2, 2 * HEAD, 512), bf16),
-            pltpu.VMEM((HEADS * TOK, HEAD), bf16),
-            pltpu.VMEM((HEADS // 2, HEAD, 512), bf16),
             pltpu.VMEM((2, SPAN, 256), f32),
-            pltpu.VMEM((WINDOW, 512), bf16),
-            pltpu.VMEM((WINDOW, 512), bf16),
+            pltpu.VMEM((2, WINDOW, 512), bf16),
+            pltpu.VMEM((2, WINDOW, 512), bf16),
             pltpu.VMEM((WINDOW, HEAD), f32),
             pltpu.VMEM((WINDOW, HEAD), f32),
             pltpu.VMEM((8, HEAD), f32),
             pltpu.VMEM((MSG, HEAD), bf16),
             pltpu.VMEM((MSG, HEAD), bf16),
-            pltpu.SemaphoreType.DMA((2,)),
             pltpu.SemaphoreType.DMA((HEADS // 2,)),
             pltpu.SemaphoreType.DMA((HEADS // 2,)),
         ],
         compiler_params=pltpu.CompilerParams(vmem_limit_bytes=40 * 1024 * 1024),
-    )(*blocks, queries, output_gradient, q_gain, k_gain, frequency)
+    )(*blocks, *prepared, q_gain, k_gain, frequency)
 
 
 def pack_kernel(keys, values, ids, out):
@@ -327,16 +378,18 @@
     return lax.ppermute(block, "context", route)
 
 
-def summed_over(axis, terms):
-    copies = jnp.broadcast_to(terms, (lax.axis_size(axis),) + terms.shape)
-    return jnp.sum(lax.all_to_all(copies, axis, 0, 0), axis=0)
+def group_terms(copies, groups):
+    everyone = lax.all_to_all(copies, ("context", "tensor"), 0, 0, axis_index_groups=groups)
+    return jnp.sum(everyone, axis=0)
 
 
 def body(queries, keys, values, output_gradient, q_gain, k_gain, doc_ids):
     message = pack(keys, values, doc_ids.reshape(2, HEAD))
     two = passed_along(message, "context", 2)
     first_swap = swapped(message, (0,))
-    four = passed_along(two, "context", 2)
+    four = passed_along(message, "context", 4)
+    prepared = prepare(queries, output_gradient)
+    two, *prepared = lax.optimization_barrier((two, *prepared))
     middle_swap = swapped(two)
     last_swap = swapped(four, (1,))
     blocks = [four, two, message, first_swap, middle_swap, last_swap]
@@ -345,8 +398,7 @@
     frequency = jnp.concatenate([frequency, frequency]).reshape(1, HEAD)
     attended, query_gradient, *returns, own, gains = attention(
         blocks,
-        queries,
-        output_gradient,
+        prepared,
         q_gain.reshape(1, HEAD),
         k_gain.reshape(1, HEAD),
         frequency,
@@ -355,7 +407,10 @@
     for distance, block in zip(range(REACH, 0, -1), returns):
         total = total + passed_along(block, "context", -distance)
     total = total.astype(jnp.bfloat16)
-    gain_total = summed_over("context", summed_over("tensor", gains))
+    chips = [[GROUP * n + k for k in range(GROUP)] for n in range(GROUP)]
+    places = [[GROUP * n + k for n in range(GROUP)] for k in range(GROUP)]
+    chip_gains = group_terms(gains, chips)
+    gain_total = group_terms(jnp.broadcast_to(chip_gains, gains.shape), places)
     return (
         attended,
         query_gradient,

time: 88.3 us -> 84.9 us (0.961)
  starting transfers between devices: 35.9 us -> 29.8 us
  Pallas kernels: 21.6 us -> 24.2 us
  waiting for transfers between devices: 9.25 us -> 6.67 us
  local copies, waits for them, and re-layouts: 5.47 us -> 6.99 us
  blocking collectives: 14.6 us -> 15.6 us
    pallas_call x0 -> x1, Pallas kernels: none -> 3.36 us  [prepare(): pl.pallas_call(prepare_kernel, out_shape=[shape((HEADS * TOK, HEAD), f32)...]
    all_to_all x1, starting transfers between devices: 9.48 us -> 6.19 us  [group_terms(): lax.all_to_all(copies, ('context', 'tensor'), 0, 0, axis_index_groups=gro...]
    ppermute x6, waiting for transfers between devices: 8.38 us -> 5.79 us  [passed_along(): return lax.ppermute(block, axis, route)]
    ppermute x3, starting transfers between devices: 6.25 us -> 4.46 us  [swapped(): return lax.ppermute(block, 'context', route)]
    unnamed x10 -> x14, local copies, waits for them, and re-layouts: 3.66 us -> 5.2 us
    all_to_all x1, blocking collectives: 14.6 us -> 15.6 us  [group_terms(): lax.all_to_all(copies, ('context', 'tensor'), 0, 0, axis_index_groups=gro...]
    ppermute x6, starting transfers between devices: 20.2 us -> 19.1 us  [passed_along(): return lax.ppermute(block, axis, route)]
  transfers between devices with their start and end apart: 10 -> 10, of which waited for: 5 -> 3; matrix products, arithmetic and copies ran while one was open for 1% -> 1% of each run, Pallas kernels for 0% -> 4%
where the time goes in v4:
time: 84.9 us; the launch traced here: 84.3 us
  starting transfers between devices  29.8 us (35%)
  Pallas kernels  24.2 us (29%)
  blocking collectives  15.6 us (18%)
  local copies, waits for them, and re-layouts  6.99 us (8%)
  waiting for transfers between devices  6.67 us (8%)
    pallas_call x1, Pallas kernels, attention(): pl.pallas_call(kernel, out_shape=[shape((TOK, HEADS * HEAD), bf16), shape...  19.4 us
    ppermute x6, starting transfers between devices, passed_along(): return lax.ppermute(block, axis, route)  19.1 us
    all_to_all x1, blocking collectives, group_terms(): lax.all_to_all(copies, ('context', 'tensor'), 0, 0, axis_index_groups=gro...  15.6 us
    all_to_all x1, starting transfers between devices, group_terms(): lax.all_to_all(copies, ('context', 'tensor'), 0, 0, axis_index_groups=gro...  6.19 us
    ppermute x6, waiting for transfers between devices, passed_along(): return lax.ppermute(block, axis, route)  5.79 us
    unnamed x14, local copies, waits for them, and re-layouts  5.2 us
    ppermute x3, starting transfers between devices, swapped(): return lax.ppermute(block, 'context', route)  4.46 us
    pallas_call x1, Pallas kernels, prepare(): pl.pallas_call(prepare_kernel, out_shape=[shape((HEADS * TOK, HEAD), f32)...  3.36 us
  transfers between devices with their start and end apart: 10, of which 3 were waited for; matrix products, arithmetic and copies ran while one was open for 1% of the time, Pallas kernels for 4%

profile of v4, /device:TPU:15, one launch (start us, length us, event | category | flops | bytes accessed | tf_op | source)
XLA Modules:
  0.0 84.3 jit_solution(3845465985340667638)
XLA Ops:
  0.6 1.5 %shard_map.118.b0 = bf16[528,128]{1,0:T(8,128)(2,1)} custom-call(bf16[256,128]{1,0:T(8,128)(2,1)} %keys.1, bf16[256,128]{1,0:T(8,128)(2,1)} %values.1, s32[2,128]{1,0:T(2,128)} %bitcast.11), custom_call_target="tpu_custom_call" | custom-call | tf_op jit(solution)/shard_map/pallas_call | solution.py:368
  2.2 3.2 %collective-permute-start.1 = (bf16[528,128]{1,0:T(8,128)(2,1)}, bf16[528,128]{1,0:T(8,128)(2,1)S(1)}, u32[]{:S(2)}, u32[]{:S(2)}) collective-permute-start(bf16[528,128]{1,0:T(8,128)(2,1)} %shard_map.118.b0), channel_id=1, source_target_pairs={{0,16},{8,24},{16,32},{24,40},{32,48},{40,56},{48,64},{56,72},{64,... | collective-permute-start | bytes 405512 | tf_op jit(solution)/shard_map/ppermute | solution.py:32
  5.4 4.0 %collective-permute-start = (bf16[528,128]{1,0:T(8,128)(2,1)}, bf16[528,128]{1,0:T(8,128)(2,1)S(1)}, u32[]{:S(2)}, u32[]{:S(2)}) collective-permute-start(bf16[528,128]{1,0:T(8,128)(2,1)} %shard_map.118.b0), channel_id=1, source_target_pairs={{0,32},{8,40},{16,48},{24,56},{32,64},{40,72},{48,80},{56,88},{64,... | collective-permute-start | bytes 405512 | tf_op jit(solution)/shard_map/ppermute | solution.py:32
  9.5 1.3 %collective-permute-start.2 = (bf16[528,128]{1,0:T(8,128)(2,1)}, bf16[528,128]{1,0:T(8,128)(2,1)S(1)}, u32[]{:S(2)}, u32[]{:S(2)}) collective-permute-start(bf16[528,128]{1,0:T(8,128)(2,1)} %shard_map.118.b0), channel_id=1, source_target_pairs={{0,8},{16,24},{32,40},{48,56},{64,72},{80,88},{96,104},{112,120},{... | collective-permute-start | bytes 405512 | tf_op jit(solution)/shard_map/ppermute | solution.py:378
  10.8 3.4 %shard_map.119 = (f32[2048,128]{1,0:T(8,128)}, f32[2048,128]{1,0:T(8,128)}, bf16[2048,128]{1,0:T(8,128)(2,1)}, bf16[4,128,512]{2,1,0:T(8,128)(2,1)}) custom-call(bf16[256,1024]{1,0:T(8,128)(2,1)} %q_ref.1, bf16[256,1024]{1,0:T(8,128)(2,1)} %d_ref.1), custom_call_target="tpu_custom_call" | custom-call | flops 1000000000 | bytes 4194304 | tf_op jit(solution)/shard_map/pallas_call | solution.py:81
  14.1 1.2 %collective-permute-start.3 = (bf16[528,128]{1,0:T(8,128)(2,1)S(1)}, bf16[528,128]{1,0:T(8,128)(2,1)S(1)}, u32[]{:S(2)}, u32[]{:S(2)}) collective-permute-start(bf16[528,128]{1,0:T(8,128)(2,1)S(1)} %collective-permute-done.1.b2), channel_id=1, source_target_pairs={{0,8},{8,0},{16,24},{24,16},{32,40},{40,32},{48,56},{56,48},{64,72... | collective-permute-start | bytes 405512 | tf_op jit(solution)/shard_map/ppermute | solution.py:378
  15.4 0.0 collective-permute-done.b4
  15.4 1.9 %collective-permute-start.4 = (bf16[528,128]{1,0:T(8,128)(2,1)S(1)}, bf16[528,128]{1,0:T(8,128)(2,1)S(1)}, u32[]{:S(2)}, u32[]{:S(2)}) collective-permute-start(bf16[528,128]{1,0:T(8,128)(2,1)S(1)} %collective-permute-done.b4), channel_id=1, source_target_pairs={{8,0},{24,16},{40,32},{56,48},{72,64},{88,80},{104,96},{120,112},{... | collective-permute-start | bytes 405512 | tf_op jit(solution)/shard_map/ppermute | solution.py:378
  17.3 0.1 maximum_bitcast_fusion.f_ref
  17.4 0.9 %collective-permute-done.4.last_swap = bf16[528,128]{1,0:T(8,128)(2,1)S(1)} collective-permute-done((bf16[528,128]{1,0:T(8,128)(2,1)S(1)}, bf16[528,128]{1,0:T(8,128)(2,1)S(1)}, u32[]{:S(2)}, u32[]{:S(2)}) %collective-permute-start.4) | collective-permute-done | bytes 135200 | tf_op jit(solution)/shard_map/ppermute | solution.py:378
  18.3 0.0 collective-permute-done.3.middle_swap
  18.3 0.6 copy-done.5
  18.9 0.0 copy-done.6
  19.0 1.2 %copy-done = f32[2048,128]{1,0:T(8,128)S(1)} copy-done((f32[2048,128]{1,0:T(8,128)S(1)}, f32[2048,128]{1,0:T(8,128)}, u32[]{:S(2)}) %copy-start) | copy-done | bytes 1048600
  20.2 1.2 %copy-done.1 = f32[2048,128]{1,0:T(8,128)S(1)} copy-done((f32[2048,128]{1,0:T(8,128)S(1)}, f32[2048,128]{1,0:T(8,128)}, u32[]{:S(2)}) %copy-start.1) | copy-done | bytes 1048600
  21.4 1.0 %copy-done.3 = bf16[2048,128]{1,0:T(8,128)(2,1)S(1)} copy-done((bf16[2048,128]{1,0:T(8,128)(2,1)S(1)}, bf16[2048,128]{1,0:T(8,128)(2,1)}, u32[]{:S(2)}) %copy-start.3) | copy-done | bytes 524312
  22.5 1.0 %copy-done.4 = bf16[4,128,512]{2,1,0:T(8,128)(2,1)S(1)} copy-done((bf16[4,128,512]{2,1,0:T(8,128)(2,1)S(1)}, bf16[4,128,512]{2,1,0:T(8,128)(2,1)}, u32[]{:S(2)}) %copy-start.4) | copy-done | bytes 524312
  23.5 19.4 %shard_map.120 = (bf16[256,1024]{1,0:T(8,128)(2,1)}, bf16[256,1024]{1,0:T(8,128)(2,1)}, bf16[512,128]{1,0:T(8,128)(2,1)S(1)}, bf16[512,128]{1,0:T(8,128)(2,1)S(1...) custom-call(bf16[528,128]{1,0:T(8,128)(2,1)S(1)} %collective-permute, ...), custom_call_target="tpu_custom_call" | custom-call | tf_op jit(solution)/shard_map/pallas_call | solution.py:320
  42.8 15.6 %all_to_all.10 = f32[16,2,128]{2,1,0:T(2,128)S(1)} all-to-all(f32[16,2,128]{2,1,0:T(2,128)S(1)} %get-tuple-element.39), channel_id=1, replica_groups={{0,1,2,3,4,5,6,7,8,9,10,11,12,13,14,15},{16,17,18,19,20,21,22,23,24,25,..., dimensions={0} | all-to-all | bytes 32768 | tf_op jit(solution)/shard_map/all_to_all | solution.py:382
  58.5 0.6 broadcast_in_dim.3
  59.1 6.2 %all-to-all-start.1 = ((f32[16,2,128]{2,1,0:T(2,128)}), f32[16,2,128]{2,1,0:T(2,128)S(1)}, u32[]{:S(2)}, u32[]{:S(2)}) async-start(f32[16,2,128]{2,1,0:T(2,128)} %broadcast_in_dim.3), calls=%async_computation.1 | async-start | bytes 32768 | tf_op jit(solution)/shard_map/all_to_all | solution.py:382
  65.3 3.1 %collective-permute-start.5 = (bf16[512,128]{1,0:T(8,128)(2,1)S(1)}, bf16[512,128]{1,0:T(8,128)(2,1)S(1)}, u32[]{:S(2)}, u32[]{:S(2)}) collective-permute-start(bf16[512,128]{1,0:T(8,128)(2,1)S(1)} %get-tuple-element.35), channel_id=1, source_target_pairs={{32,0},{40,8},{48,16},{56,24},{64,32},{72,40},{80,48},{88,56},{96,... | collective-permute-start | bytes 393224 | tf_op jit(solution)/shard_map/ppermute | solution.py:32
  68.4 3.0 %collective-permute-start.6 = (bf16[512,128]{1,0:T(8,128)(2,1)S(1)}, bf16[512,128]{1,0:T(8,128)(2,1)S(1)}, u32[]{:S(2)}, u32[]{:S(2)}) collective-permute-start(bf16[512,128]{1,0:T(8,128)(2,1)S(1)} %get-tuple-element.36), channel_id=1, source_target_pairs={{24,0},{32,8},{40,16},{48,24},{56,32},{64,40},{72,48},{80,56},{88,... | collective-permute-start | bytes 393224 | tf_op jit(solution)/shard_map/ppermute | solution.py:32
  71.4 3.7 %collective-permute-start.7 = (bf16[512,128]{1,0:T(8,128)(2,1)S(1)}, bf16[512,128]{1,0:T(8,128)(2,1)S(1)}, u32[]{:S(2)}, u32[]{:S(2)}) collective-permute-start(bf16[512,128]{1,0:T(8,128)(2,1)S(1)} %get-tuple-element.37), channel_id=1, source_target_pairs={{16,0},{24,8},{32,16},{40,24},{48,32},{56,40},{64,48},{72,56},{80,... | collective-permute-start | bytes 393224 | tf_op jit(solution)/shard_map/ppermute | solution.py:32
  75.1 2.0 %collective-permute-start.8 = (bf16[512,128]{1,0:T(8,128)(2,1)S(1)}, bf16[512,128]{1,0:T(8,128)(2,1)S(1)}, u32[]{:S(2)}, u32[]{:S(2)}) collective-permute-start(bf16[512,128]{1,0:T(8,128)(2,1)S(1)} %get-tuple-element.38), channel_id=1, source_target_pairs={{8,0},{16,8},{24,16},{32,24},{40,32},{48,40},{56,48},{64,56},{72,6... | collective-permute-start | bytes 393224 | tf_op jit(solution)/shard_map/ppermute | solution.py:32
  77.2 0.0 all-to-all-done.1
  77.2 0.5 slice_bitcast_fusion
  77.7 0.0 collective-permute-done.5
  77.8 2.9 %collective-permute-done.7 = bf16[512,128]{1,0:T(8,128)(2,1)S(1)} collective-permute-done((bf16[512,128]{1,0:T(8,128)(2,1)S(1)}, bf16[512,128]{1,0:T(8,128)(2,1)S(1)}, u32[]{:S(2)}, u32[]{:S(2)}) %collective-permute-start.7) | collective-permute-done | bytes 131104 | tf_op jit(solution)/shard_map/ppermute | solution.py:32
  80.7 2.9 %collective-permute-done.8 = bf16[512,128]{1,0:T(8,128)(2,1)S(1)} collective-permute-done((bf16[512,128]{1,0:T(8,128)(2,1)S(1)}, bf16[512,128]{1,0:T(8,128)(2,1)S(1)}, u32[]{:S(2)}, u32[]{:S(2)}) %collective-permute-start.8) | collective-permute-done | bytes 131104 | tf_op jit(solution)/shard_map/ppermute | solution.py:32
  83.5 0.1 add_convert_fusion
  83.6 0.7 fusion
  (14 shorter events, 0.1 us)
Async XLA Ops:
  2.2 16.1 %copy-start.2 = (bf16[528,128]{1,0:T(8,128)(2,1)S(1)}, bf16[528,128]{1,0:T(8,128)(2,1)}, u32[]{:S(2)}) copy-start(bf16[528,128]{1,0:T(8,128)(2,1)} %shard_map.118.b0) | copy-start | bytes 405508
  2.2 12.0 %collective-permute-start.1 = (bf16[528,128]{1,0:T(8,128)(2,1)}, bf16[528,128]{1,0:T(8,128)(2,1)S(1)}, u32[]{:S(2)}, u32[]{:S(2)}) collective-permute-start(bf16[528,128]{1,0:T(8,128)(2,1)} %shard_map.118.b0), channel_id=1, source_target_pairs={{0,16},{8,24},{16,32},{24,40},{32,48},{40,56},{48,64},{56,72},{64,... | collective-permute-start | bytes 405512 | tf_op jit(solution)/shard_map/ppermute | solution.py:32
  5.4 10.0 %collective-permute-start = (bf16[528,128]{1,0:T(8,128)(2,1)}, bf16[528,128]{1,0:T(8,128)(2,1)S(1)}, u32[]{:S(2)}, u32[]{:S(2)}) collective-permute-start(bf16[528,128]{1,0:T(8,128)(2,1)} %shard_map.118.b0), channel_id=1, source_target_pairs={{0,32},{8,40},{16,48},{24,56},{32,64},{40,72},{48,80},{56,88},{64,... | collective-permute-start | bytes 405512 | tf_op jit(solution)/shard_map/ppermute | solution.py:32
  9.5 7.9 %collective-permute-start.2 = (bf16[528,128]{1,0:T(8,128)(2,1)}, bf16[528,128]{1,0:T(8,128)(2,1)S(1)}, u32[]{:S(2)}, u32[]{:S(2)}) collective-permute-start(bf16[528,128]{1,0:T(8,128)(2,1)} %shard_map.118.b0), channel_id=1, source_target_pairs={{0,8},{16,24},{32,40},{48,56},{64,72},{80,88},{96,104},{112,120},{... | collective-permute-start | bytes 405512 | tf_op jit(solution)/shard_map/ppermute | solution.py:378
  14.1 4.1 %collective-permute-start.3 = (bf16[528,128]{1,0:T(8,128)(2,1)S(1)}, bf16[528,128]{1,0:T(8,128)(2,1)S(1)}, u32[]{:S(2)}, u32[]{:S(2)}) collective-permute-start(bf16[528,128]{1,0:T(8,128)(2,1)S(1)} %collective-permute-done.1.b2), channel_id=1, source_target_pairs={{0,8},{8,0},{16,24},{24,16},{32,40},{40,32},{48,56},{56,48},{64,72... | collective-permute-start | bytes 405512 | tf_op jit(solution)/shard_map/ppermute | solution.py:378
  15.4 2.9 %collective-permute-start.4 = (bf16[528,128]{1,0:T(8,128)(2,1)S(1)}, bf16[528,128]{1,0:T(8,128)(2,1)S(1)}, u32[]{:S(2)}, u32[]{:S(2)}) collective-permute-start(bf16[528,128]{1,0:T(8,128)(2,1)S(1)} %collective-permute-done.b4), channel_id=1, source_target_pairs={{8,0},{24,16},{40,32},{56,48},{72,64},{88,80},{104,96},{120,112},{... | collective-permute-start | bytes 405512 | tf_op jit(solution)/shard_map/ppermute | solution.py:378
  18.3 0.7 copy-start.5
  18.3 0.7 copy-start.6
  19.0 1.2 %copy-start = (f32[2048,128]{1,0:T(8,128)S(1)}, f32[2048,128]{1,0:T(8,128)}, u32[]{:S(2)}) copy-start(f32[2048,128]{1,0:T(8,128)} %get-tuple-element.28.xh_ref) | copy-start | bytes 3145732
  20.2 1.2 %copy-start.1 = (f32[2048,128]{1,0:T(8,128)S(1)}, f32[2048,128]{1,0:T(8,128)}, u32[]{:S(2)}) copy-start(f32[2048,128]{1,0:T(8,128)} %get-tuple-element.29.scale_ref) | copy-start | bytes 3145732
  21.4 1.0 %copy-start.3 = (bf16[2048,128]{1,0:T(8,128)(2,1)S(1)}, bf16[2048,128]{1,0:T(8,128)(2,1)}, u32[]{:S(2)}) copy-start(bf16[2048,128]{1,0:T(8,128)(2,1)} %get-tuple-element.30.dcat) | copy-start | bytes 1572868
  22.4 1.0 %copy-start.4 = (bf16[4,128,512]{2,1,0:T(8,128)(2,1)S(1)}, bf16[4,128,512]{2,1,0:T(8,128)(2,1)}, u32[]{:S(2)}) copy-start(bf16[4,128,512]{2,1,0:T(8,128)(2,1)} %get-tuple-element.31.dcat_t) | copy-start | bytes 1572868
  59.1 18.1 %all-to-all-start.1 = ((f32[16,2,128]{2,1,0:T(2,128)}), f32[16,2,128]{2,1,0:T(2,128)S(1)}, u32[]{:S(2)}, u32[]{:S(2)}) async-start(f32[16,2,128]{2,1,0:T(2,128)} %broadcast_in_dim.3), calls=%async_computation.1 | async-start | bytes 32768 | tf_op jit(solution)/shard_map/all_to_all | solution.py:382
  65.3 12.4 %collective-permute-start.5 = (bf16[512,128]{1,0:T(8,128)(2,1)S(1)}, bf16[512,128]{1,0:T(8,128)(2,1)S(1)}, u32[]{:S(2)}, u32[]{:S(2)}) collective-permute-start(bf16[512,128]{1,0:T(8,128)(2,1)S(1)} %get-tuple-element.35), channel_id=1, source_target_pairs={{32,0},{40,8},{48,16},{56,24},{64,32},{72,40},{80,48},{88,56},{96,... | collective-permute-start | bytes 393224 | tf_op jit(solution)/shard_map/ppermute | solution.py:32
  68.4 9.4 %collective-permute-start.6 = (bf16[512,128]{1,0:T(8,128)(2,1)S(1)}, bf16[512,128]{1,0:T(8,128)(2,1)S(1)}, u32[]{:S(2)}, u32[]{:S(2)}) collective-permute-start(bf16[512,128]{1,0:T(8,128)(2,1)S(1)} %get-tuple-element.36), channel_id=1, source_target_pairs={{24,0},{32,8},{40,16},{48,24},{56,32},{64,40},{72,48},{80,56},{88,... | collective-permute-start | bytes 393224 | tf_op jit(solution)/shard_map/ppermute | solution.py:32
  71.4 9.2 %collective-permute-start.7 = (bf16[512,128]{1,0:T(8,128)(2,1)S(1)}, bf16[512,128]{1,0:T(8,128)(2,1)S(1)}, u32[]{:S(2)}, u32[]{:S(2)}) collective-permute-start(bf16[512,128]{1,0:T(8,128)(2,1)S(1)} %get-tuple-element.37), channel_id=1, source_target_pairs={{16,0},{24,8},{32,16},{40,24},{48,32},{56,40},{64,48},{72,56},{80,... | collective-permute-start | bytes 393224 | tf_op jit(solution)/shard_map/ppermute | solution.py:32
  75.1 8.4 %collective-permute-start.8 = (bf16[512,128]{1,0:T(8,128)(2,1)S(1)}, bf16[512,128]{1,0:T(8,128)(2,1)S(1)}, u32[]{:S(2)}, u32[]{:S(2)}) collective-permute-start(bf16[512,128]{1,0:T(8,128)(2,1)S(1)} %get-tuple-element.38), channel_id=1, source_target_pairs={{8,0},{16,8},{24,16},{32,24},{40,32},{48,40},{56,48},{64,56},{72,6... | collective-permute-start | bytes 393224 | tf_op jit(solution)/shard_map/ppermute | solution.py:32

commit v5 on v4

--- a/solution.py
+++ b/solution.py
@@ -59,7 +59,9 @@
     return jnp.where((quadrant & 2) == 2, -value, value)
 
 
-def prepare_kernel(q_ref, d_ref, xh_ref, scale_ref, dcat, dcat_t):
+def prepare_kernel(q_ref, d_ref, qg_ref, kg_ref, xh_ref, scale_ref, dcat, dcat_t, gains):
+    gains[0:1, :] = qg_ref[...]
+    gains[1:2, :] = kg_ref[...]
     for sub in range(2):
         tokens = slice(sub * SUB, (sub + 1) * SUB)
         for h in range(HEADS):
@@ -74,7 +76,7 @@
             dcat_t[h // 2, :, at % 512 : at % 512 + SUB] = d.astype(jnp.float32).T.astype(jnp.bfloat16)
 
 
-def prepare(queries, output_gradient):
+def prepare(queries, output_gradient, q_gain, k_gain):
     vmem = pl.BlockSpec(memory_space=pltpu.VMEM)
     f32, bf16 = jnp.float32, jnp.bfloat16
     shape = jax.ShapeDtypeStruct
@@ -85,15 +87,17 @@
             shape((HEADS * TOK, HEAD), f32),
             shape((HEADS * TOK, HEAD), bf16),
             shape((HEADS // 2, HEAD, 512), bf16),
+            shape((2, HEAD), f32),
         ],
-        in_specs=[vmem] * 2,
-        out_specs=[vmem] * 4,
+        in_specs=[vmem] * 4,
+        out_specs=[vmem] * 5,
+        compiler_params=pltpu.CompilerParams(vmem_limit_bytes=16 * 1024 * 1024),
         cost_estimate=pl.CostEstimate(flops=10**9, bytes_accessed=4 * 2**20, transcendentals=0),
-    )(queries, output_gradient)
+    )(queries, output_gradient, q_gain, k_gain)
 
 
 def kernel(
-    b4, b2, b0, first_swap, middle_swap, last_swap, xh_ref, scale_ref, dcat, dcat_t, qg_ref, kg_ref, f_ref,
+    b4, b2, b0, first_swap, middle_swap, last_swap, xh_ref, scale_ref, dcat, dcat_t, gains_ref, f_ref,
     att_hbm, gq_hbm, r4, r3, r2, r1, own_ref, gain_ref,
     att_ref, gq_ref, cosine, sine, kext, vwin, khat_t, v_t, qhat, qext_t,
     s_ref, w_ref, ds_ref, dk, dv, qg_acc, b3, b1, att_sem, gq_sem,
@@ -117,8 +121,8 @@
     row_f = row.astype(jnp.float32)
     left = lane < HEAD // 2
     parts = WINDOW // SUB
-    q_gain = qg_ref[...]
-    k_gain = kg_ref[...]
+    q_gain = gains_ref[0:1, :]
+    k_gain = gains_ref[1:2, :]
     frequency = f_ref[...]
 
     id_rows = []
@@ -173,9 +177,9 @@
     qg_acc[...] = jnp.zeros_like(qg_acc)
     zero = jnp.zeros((SUB, 256), jnp.bfloat16)
     for ref in (w_ref, ds_ref):
-        ref[0, 0:SUB, 256:512] = zero
-        ref[0, SPAN:WINDOW, 0:256] = zero
-        ref[1] = jnp.zeros((WINDOW, 512), jnp.bfloat16)
+        for slot in range(2):
+            ref[slot, 0:SUB, 256:512] = zero
+            ref[slot, SPAN:WINDOW, 0:256] = zero
     later = jnp.where(row <= lane, 0.0, -1e30)
     later = jnp.concatenate([later, later], axis=1)
     last = SPAN - SUB
@@ -183,20 +187,19 @@
     columns_of = (slice(0, 256), slice(256, 512))
 
     def copies(pair):
-        columns = pl.ds(pl.multiple_of(pair * 256, 256), 256)
+        columns = slice(pair * 256, (pair + 1) * 256)
         return (
             pltpu.make_async_copy(att_ref.at[:, columns], att_hbm.at[:, columns], att_sem.at[pair]),
             pltpu.make_async_copy(gq_ref.at[:, columns], gq_hbm.at[:, columns], gq_sem.at[pair]),
         )
 
     def key_terms(pair, slot):
-        at = pl.multiple_of(pair * 512, 512)
-        dk[...] += dot(ds_ref[slot], qhat[pl.ds(at, 512), :])
-        dv[...] += dot(w_ref[slot], dcat[pl.ds(at, 512), :])
-
-    def pair_step(pair, carry):
-        at = pl.multiple_of(pair * 512, 512)
-        slot = lax.rem(pair, 2)
+        rows = slice(pair * 512, (pair + 1) * 512)
+        dk[...] += dot(ds_ref[slot], qhat[rows, :])
+        dv[...] += dot(w_ref[slot], dcat[rows, :])
+
+    for pair in range(HEADS // 2):
+        slot = pair % 2
 
         def scores(sub):
             s = dot(kext[spans[sub], :], qext_t[pair, :, columns_of[sub]])
@@ -229,7 +232,7 @@
             center = jnp.sum(att_t * d_t.astype(jnp.float32), axis=0, keepdims=True)
             tokens = slice(sub * SUB, (sub + 1) * SUB)
             for g in range(2):
-                columns = pl.ds(pl.multiple_of(pair * 256 + g * HEAD, HEAD), HEAD)
+                columns = slice(pair * 256 + g * HEAD, pair * 256 + (g + 1) * HEAD)
                 att_ref[tokens, columns] = att_t[:, g * SUB : (g + 1) * SUB].T.astype(jnp.bfloat16)
             return center
 
@@ -245,8 +248,9 @@
             c_q = cosine[window_rows, :]
             s_q = sine[window_rows, :]
             for g in range(2):
-                columns = pl.ds(pl.multiple_of(pair * 256 + g * HEAD, HEAD), HEAD)
-                rows = pl.ds(pl.multiple_of(at + sub * 256 + g * SUB, SUB), SUB)
+                columns = slice(pair * 256 + g * HEAD, pair * 256 + (g + 1) * HEAD)
+                at = pair * 512 + sub * 256 + g * SUB
+                rows = slice(at, at + SUB)
                 dq = dq_t[:, g * SUB : (g + 1) * SUB].T
                 xh = xh_ref[rows, :]
                 dn = dq * c_q - half_turned(dq) * s_q
@@ -258,7 +262,8 @@
         shift_0 = scores(0)
         shift_1 = scores(1)
         inverse_0 = exponents(0, shift_0)
-        key_terms(jnp.maximum(pair - 1, 0), 1 - slot)
+        if pair > 0:
+            key_terms(pair - 1, 1 - slot)
         weigh(0, inverse_0)
         inverse_1 = exponents(1, shift_1)
         center_0 = attend(0)
@@ -271,15 +276,6 @@
         for copy in copies(pair):
             copy.start()
 
-        @pl.when(pair == 0)
-        def _():
-            for ref in (w_ref, ds_ref):
-                ref[1, 0:SUB, 256:512] = zero
-                ref[1, SPAN:WINDOW, 0:256] = zero
-
-        return carry
-
-    lax.fori_loop(0, HEADS // 2, pair_step, 0)
     key_terms(HEADS // 2 - 1, 1)
 
     kg = jnp.zeros((8, HEAD), jnp.float32)
@@ -301,18 +297,16 @@
     gains = jnp.concatenate(
         [jnp.sum(qg_acc[...], axis=0, keepdims=True), jnp.sum(kg, axis=0, keepdims=True)]
     )
-    for i in range(gain_ref.shape[0]):
-        gain_ref[i] = gains
+    gain_ref[...] = gains
     for pair in range(HEADS // 2):
         for copy in copies(pair):
             copy.wait()
 
 
 RETURN = jnp.bfloat16
-GROUP = 16
-
-
-def attention(blocks, prepared, q_gain, k_gain, frequency):
+
+
+def attention(blocks, prepared, frequency):
     vmem = pl.BlockSpec(memory_space=pltpu.VMEM)
     hbm = pl.BlockSpec(memory_space=pl.ANY)
     f32, bf16 = jnp.float32, jnp.bfloat16
@@ -324,9 +318,9 @@
             shape((TOK, HEADS * HEAD), bf16),
             *[shape((2 * TOK, HEAD), RETURN) for _ in range(REACH)],
             shape((2 * TOK, HEAD), f32),
-            shape((GROUP, 2, HEAD), f32),
+            shape((2, HEAD), f32),
         ],
-        in_specs=[vmem] * 13,
+        in_specs=[vmem] * 12,
         out_specs=[hbm] * 2 + [vmem] * 6,
         scratch_shapes=[
             pltpu.VMEM((TOK, HEADS * HEAD), bf16),
@@ -351,7 +345,7 @@
             pltpu.SemaphoreType.DMA((HEADS // 2,)),
         ],
         compiler_params=pltpu.CompilerParams(vmem_limit_bytes=40 * 1024 * 1024),
-    )(*blocks, *prepared, q_gain, k_gain, frequency)
+    )(*blocks, *prepared, frequency)
 
 
 def pack_kernel(keys, values, ids, out):
@@ -378,9 +372,10 @@
     return lax.ppermute(block, "context", route)
 
 
-def group_terms(copies, groups):
-    everyone = lax.all_to_all(copies, ("context", "tensor"), 0, 0, axis_index_groups=groups)
-    return jnp.sum(everyone, axis=0)
+def summed_over_all(terms):
+    axes = ("context", "tensor")
+    copies = jnp.broadcast_to(terms, (lax.axis_size(axes),) + terms.shape)
+    return jnp.sum(lax.all_to_all(copies, axes, 0, 0), axis=0)
 
 
 def body(queries, keys, values, output_gradient, q_gain, k_gain, doc_ids):
@@ -388,7 +383,7 @@
     two = passed_along(message, "context", 2)
     first_swap = swapped(message, (0,))
     four = passed_along(message, "context", 4)
-    prepared = prepare(queries, output_gradient)
+    prepared = prepare(queries, output_gradient, q_gain.reshape(1, HEAD), k_gain.reshape(1, HEAD))
     two, *prepared = lax.optimization_barrier((two, *prepared))
     middle_swap = swapped(two)
     last_swap = swapped(four, (1,))
@@ -399,18 +394,13 @@
     attended, query_gradient, *returns, own, gains = attention(
         blocks,
         prepared,
-        q_gain.reshape(1, HEAD),
-        k_gain.reshape(1, HEAD),
         frequency,
     )
     total = own
     for distance, block in zip(range(REACH, 0, -1), returns):
         total = total + passed_along(block, "context", -distance)
     total = total.astype(jnp.bfloat16)
-    chips = [[GROUP * n + k for k in range(GROUP)] for n in range(GROUP)]
-    places = [[GROUP * n + k for n in range(GROUP)] for k in range(GROUP)]
-    chip_gains = group_terms(gains, chips)
-    gain_total = group_terms(jnp.broadcast_to(chip_gains, gains.shape), places)
+    gain_total = summed_over_all(gains)
     return (
         attended,
         query_gradient,

time: 84.9 us -> 80.4 us (0.947)
  the two profiles are of different devices: /device:TPU:15 before, /device:TPU:1 now
where the time goes in v5:
time: 80.4 us; the launch traced here: 79.9 us
  starting transfers between devices  39.9 us (50%)
  Pallas kernels  18.2 us (23%)
  waiting for transfers between devices  15.9 us (20%)
  local copies, waits for them, and re-layouts  4.68 us (6%)
    all_to_all x1, starting transfers between devices, summed_over_all(): return jnp.sum(lax.all_to_all(copies, axes, 0, 0), axis=0)  20.9 us
    pallas_call x1, Pallas kernels, attention(): pl.pallas_call(kernel, out_shape=[shape((TOK, HEADS * HEAD), bf16), shape...  16.1 us
    all_to_all x1, waiting for transfers between devices, summed_over_all(): return jnp.sum(lax.all_to_all(copies, axes, 0, 0), axis=0)  15.1 us
    ppermute x6, starting transfers between devices, passed_along(): return lax.ppermute(block, axis, route)  14.4 us
    ppermute x3, starting transfers between devices, swapped(): return lax.ppermute(block, 'context', route)  4.55 us
    unnamed x10, local copies, waits for them, and re-layouts  2.74 us
  transfers between devices with their start and end apart: 10, of which 2 were waited for; matrix products, arithmetic and copies ran while one was open for 2% of the time, Pallas kernels for 1%

profile of v5, /device:TPU:1, one launch (start us, length us, event | category | flops | bytes accessed | tf_op | source)
XLA Modules:
  0.0 79.9 jit_solution(12330052271285902671)
XLA Ops:
  0.6 1.5 %shard_map.118.b0 = bf16[528,128]{1,0:T(8,128)(2,1)} custom-call(bf16[256,128]{1,0:T(8,128)(2,1)} %keys.1, bf16[256,128]{1,0:T(8,128)(2,1)} %values.1, s32[2,128]{1,0:T(2,128)} %bitcast.11), custom_call_target="tpu_custom_call" | custom-call | tf_op jit(solution)/shard_map/pallas_call | solution.py:362
  2.2 3.9 %collective-permute-start.1 = (bf16[528,128]{1,0:T(8,128)(2,1)}, bf16[528,128]{1,0:T(8,128)(2,1)S(1)}, u32[]{:S(2)}, u32[]{:S(2)}) collective-permute-start(bf16[528,128]{1,0:T(8,128)(2,1)} %shard_map.118.b0), channel_id=1, source_target_pairs={{0,16},{8,24},{16,32},{24,40},{32,48},{40,56},{48,64},{56,72},{64,... | collective-permute-start | bytes 405512 | tf_op jit(solution)/shard_map/ppermute | solution.py:32
  6.1 4.4 %collective-permute-start = (bf16[528,128]{1,0:T(8,128)(2,1)}, bf16[528,128]{1,0:T(8,128)(2,1)S(1)}, u32[]{:S(2)}, u32[]{:S(2)}) collective-permute-start(bf16[528,128]{1,0:T(8,128)(2,1)} %shard_map.118.b0), channel_id=1, source_target_pairs={{0,32},{8,40},{16,48},{24,56},{32,64},{40,72},{48,80},{56,88},{64,... | collective-permute-start | bytes 405512 | tf_op jit(solution)/shard_map/ppermute | solution.py:32
  10.5 1.3 %collective-permute-start.2 = (bf16[528,128]{1,0:T(8,128)(2,1)}, bf16[528,128]{1,0:T(8,128)(2,1)S(1)}, u32[]{:S(2)}, u32[]{:S(2)}) collective-permute-start(bf16[528,128]{1,0:T(8,128)(2,1)} %shard_map.118.b0), channel_id=1, source_target_pairs={{0,8},{16,24},{32,40},{48,56},{64,72},{80,88},{96,104},{112,120},{... | collective-permute-start | bytes 405512 | tf_op jit(solution)/shard_map/ppermute | solution.py:372
  11.8 0.0 copy-start.3
  11.8 0.0 copy-start.4
  11.8 0.6 copy-done.3
  12.4 0.0 copy-done.4
  12.5 1.0 %copy-done.1 = bf16[256,1024]{1,0:T(8,128)(2,1)S(1)} copy-done((bf16[256,1024]{1,0:T(8,128)(2,1)S(1)}, bf16[256,1024]{1,0:T(8,128)(2,1)}, u32[]{:S(2)}) %copy-start.1) | copy-done | bytes 524312
  13.5 1.0 %copy-done.2 = bf16[256,1024]{1,0:T(8,128)(2,1)S(1)} copy-done((bf16[256,1024]{1,0:T(8,128)(2,1)S(1)}, bf16[256,1024]{1,0:T(8,128)(2,1)}, u32[]{:S(2)}) %copy-start.2) | copy-done | bytes 524312
  14.6 0.5 shard_map.119
  15.1 0.0 collective-permute-done.1.b2
  15.1 1.3 %collective-permute-start.3 = (bf16[528,128]{1,0:T(8,128)(2,1)S(1)}, bf16[528,128]{1,0:T(8,128)(2,1)S(1)}, u32[]{:S(2)}, u32[]{:S(2)}) collective-permute-start(bf16[528,128]{1,0:T(8,128)(2,1)S(1)} %collective-permute-done.1.b2), channel_id=1, source_target_pairs={{0,8},{8,0},{16,24},{24,16},{32,40},{40,32},{48,56},{56,48},{64,72... | collective-permute-start | bytes 405512 | tf_op jit(solution)/shard_map/ppermute | solution.py:372
  16.4 0.0 collective-permute-done.b4
  16.4 1.9 %collective-permute-start.4 = (bf16[528,128]{1,0:T(8,128)(2,1)S(1)}, bf16[528,128]{1,0:T(8,128)(2,1)S(1)}, u32[]{:S(2)}, u32[]{:S(2)}) collective-permute-start(bf16[528,128]{1,0:T(8,128)(2,1)S(1)} %collective-permute-done.b4), channel_id=1, source_target_pairs={{8,0},{24,16},{40,32},{56,48},{72,64},{88,80},{104,96},{120,112},{... | collective-permute-start | bytes 405512 | tf_op jit(solution)/shard_map/ppermute | solution.py:372
  18.4 0.1 maximum_bitcast_fusion.f_ref
  18.4 0.9 %collective-permute-done.4.last_swap = bf16[528,128]{1,0:T(8,128)(2,1)S(1)} collective-permute-done((bf16[528,128]{1,0:T(8,128)(2,1)S(1)}, bf16[528,128]{1,0:T(8,128)(2,1)S(1)}, u32[]{:S(2)}, u32[]{:S(2)}) %collective-permute-start.4) | collective-permute-done | bytes 135200 | tf_op jit(solution)/shard_map/ppermute | solution.py:372
  19.3 0.0 collective-permute-done.3.middle_swap
  19.3 16.1 %shard_map.120 = (bf16[256,1024]{1,0:T(8,128)(2,1)}, bf16[256,1024]{1,0:T(8,128)(2,1)}, bf16[512,128]{1,0:T(8,128)(2,1)S(1)}, bf16[512,128]{1,0:T(8,128)(2,1)S(1...) custom-call(bf16[528,128]{1,0:T(8,128)(2,1)S(1)} %collective-permute, ...), custom_call_target="tpu_custom_call" | custom-call | tf_op jit(solution)/shard_map/pallas_call | solution.py:314
  35.5 1.3 %collective-permute-start.5 = (bf16[512,128]{1,0:T(8,128)(2,1)S(1)}, bf16[512,128]{1,0:T(8,128)(2,1)S(1)}, u32[]{:S(2)}, u32[]{:S(2)}) collective-permute-start(bf16[512,128]{1,0:T(8,128)(2,1)S(1)} %get-tuple-element.39), channel_id=1, source_target_pairs={{32,0},{40,8},{48,16},{56,24},{64,32},{72,40},{80,48},{88,56},{96,... | collective-permute-start | bytes 393224 | tf_op jit(solution)/shard_map/ppermute | solution.py:32
  36.8 1.3 %collective-permute-start.6 = (bf16[512,128]{1,0:T(8,128)(2,1)S(1)}, bf16[512,128]{1,0:T(8,128)(2,1)S(1)}, u32[]{:S(2)}, u32[]{:S(2)}) collective-permute-start(bf16[512,128]{1,0:T(8,128)(2,1)S(1)} %get-tuple-element.40), channel_id=1, source_target_pairs={{24,0},{32,8},{40,16},{48,24},{56,32},{64,40},{72,48},{80,56},{88,... | collective-permute-start | bytes 393224 | tf_op jit(solution)/shard_map/ppermute | solution.py:32
  38.1 1.3 %collective-permute-start.7 = (bf16[512,128]{1,0:T(8,128)(2,1)S(1)}, bf16[512,128]{1,0:T(8,128)(2,1)S(1)}, u32[]{:S(2)}, u32[]{:S(2)}) collective-permute-start(bf16[512,128]{1,0:T(8,128)(2,1)S(1)} %get-tuple-element.41), channel_id=1, source_target_pairs={{16,0},{24,8},{32,16},{40,24},{48,32},{56,40},{64,48},{72,56},{80,... | collective-permute-start | bytes 393224 | tf_op jit(solution)/shard_map/ppermute | solution.py:32
  39.4 2.3 %collective-permute-start.8 = (bf16[512,128]{1,0:T(8,128)(2,1)S(1)}, bf16[512,128]{1,0:T(8,128)(2,1)S(1)}, u32[]{:S(2)}, u32[]{:S(2)}) collective-permute-start(bf16[512,128]{1,0:T(8,128)(2,1)S(1)} %get-tuple-element.42), channel_id=1, source_target_pairs={{8,0},{16,8},{24,16},{32,24},{40,32},{48,40},{56,48},{64,56},{72,6... | collective-permute-start | bytes 393224 | tf_op jit(solution)/shard_map/ppermute | solution.py:32
  41.6 0.8 broadcast_in_dim.3
  42.4 20.9 %all-to-all-start = ((f32[256,2,128]{2,1,0:T(2,128)}), f32[256,2,128]{2,1,0:T(2,128)S(1)}, u32[]{:S(2)}, u32[]{:S(2)}) async-start(f32[256,2,128]{2,1,0:T(2,128)} %broadcast_in_dim.3), calls=%async_computation | async-start | bytes 524288 | tf_op jit(solution)/shard_map/all_to_all | solution.py:378
  63.3 0.0 collective-permute-done.6
  63.3 0.0 collective-permute-done.7
  63.3 0.1 add_convert_fusion
  63.4 0.7 fusion
  64.1 15.1 %all-to-all-done = f32[256,2,128]{2,1,0:T(2,128)S(1)} async-done(((f32[256,2,128]{2,1,0:T(2,128)}), f32[256,2,128]{2,1,0:T(2,128)S(1)}, u32[]{:S(2)}, u32[]{:S(2)}) %all-to-all-start) | async-done | bytes 262176 | tf_op jit(solution)/shard_map/all_to_all | solution.py:378
  79.1 0.3 reduce_sum.9
  79.4 0.5 slice_bitcast_fusion
  (8 shorter events, 0.0 us)
Async XLA Ops:
  2.2 12.9 %collective-permute-start.1 = (bf16[528,128]{1,0:T(8,128)(2,1)}, bf16[528,128]{1,0:T(8,128)(2,1)S(1)}, u32[]{:S(2)}, u32[]{:S(2)}) collective-permute-start(bf16[528,128]{1,0:T(8,128)(2,1)} %shard_map.118.b0), channel_id=1, source_target_pairs={{0,16},{8,24},{16,32},{24,40},{32,48},{40,56},{48,64},{56,72},{64,... | collective-permute-start | bytes 405512 | tf_op jit(solution)/shard_map/ppermute | solution.py:32
  6.1 10.3 %collective-permute-start = (bf16[528,128]{1,0:T(8,128)(2,1)}, bf16[528,128]{1,0:T(8,128)(2,1)S(1)}, u32[]{:S(2)}, u32[]{:S(2)}) collective-permute-start(bf16[528,128]{1,0:T(8,128)(2,1)} %shard_map.118.b0), channel_id=1, source_target_pairs={{0,32},{8,40},{16,48},{24,56},{32,64},{40,72},{48,80},{56,88},{64,... | collective-permute-start | bytes 405512 | tf_op jit(solution)/shard_map/ppermute | solution.py:32
  10.5 8.0 %collective-permute-start.2 = (bf16[528,128]{1,0:T(8,128)(2,1)}, bf16[528,128]{1,0:T(8,128)(2,1)S(1)}, u32[]{:S(2)}, u32[]{:S(2)}) collective-permute-start(bf16[528,128]{1,0:T(8,128)(2,1)} %shard_map.118.b0), channel_id=1, source_target_pairs={{0,8},{16,24},{32,40},{48,56},{64,72},{80,88},{96,104},{112,120},{... | collective-permute-start | bytes 405512 | tf_op jit(solution)/shard_map/ppermute | solution.py:372
  11.8 0.7 copy-start.3
  11.8 0.7 copy-start.4
  12.5 1.0 %copy-start.1 = (bf16[256,1024]{1,0:T(8,128)(2,1)S(1)}, bf16[256,1024]{1,0:T(8,128)(2,1)}, u32[]{:S(2)}) copy-start(bf16[256,1024]{1,0:T(8,128)(2,1)} %q_ref.1) | copy-start | bytes 1572868
  13.5 1.0 %copy-start.2 = (bf16[256,1024]{1,0:T(8,128)(2,1)S(1)}, bf16[256,1024]{1,0:T(8,128)(2,1)}, u32[]{:S(2)}) copy-start(bf16[256,1024]{1,0:T(8,128)(2,1)} %d_ref.1) | copy-start | bytes 1572868
  14.5 4.8 %copy-start = (bf16[528,128]{1,0:T(8,128)(2,1)S(1)}, bf16[528,128]{1,0:T(8,128)(2,1)}, u32[]{:S(2)}) copy-start(bf16[528,128]{1,0:T(8,128)(2,1)} %shard_map.118.b0) | copy-start | bytes 405508
  15.1 4.2 %collective-permute-start.3 = (bf16[528,128]{1,0:T(8,128)(2,1)S(1)}, bf16[528,128]{1,0:T(8,128)(2,1)S(1)}, u32[]{:S(2)}, u32[]{:S(2)}) collective-permute-start(bf16[528,128]{1,0:T(8,128)(2,1)S(1)} %collective-permute-done.1.b2), channel_id=1, source_target_pairs={{0,8},{8,0},{16,24},{24,16},{32,40},{40,32},{48,56},{56,48},{64,72... | collective-permute-start | bytes 405512 | tf_op jit(solution)/shard_map/ppermute | solution.py:372
  16.4 2.9 %collective-permute-start.4 = (bf16[528,128]{1,0:T(8,128)(2,1)S(1)}, bf16[528,128]{1,0:T(8,128)(2,1)S(1)}, u32[]{:S(2)}, u32[]{:S(2)}) collective-permute-start(bf16[528,128]{1,0:T(8,128)(2,1)S(1)} %collective-permute-done.b4), channel_id=1, source_target_pairs={{8,0},{24,16},{40,32},{56,48},{72,64},{88,80},{104,96},{120,112},{... | collective-permute-start | bytes 405512 | tf_op jit(solution)/shard_map/ppermute | solution.py:372
  35.5 27.8 %collective-permute-start.5 = (bf16[512,128]{1,0:T(8,128)(2,1)S(1)}, bf16[512,128]{1,0:T(8,128)(2,1)S(1)}, u32[]{:S(2)}, u32[]{:S(2)}) collective-permute-start(bf16[512,128]{1,0:T(8,128)(2,1)S(1)} %get-tuple-element.39), channel_id=1, source_target_pairs={{32,0},{40,8},{48,16},{56,24},{64,32},{72,40},{80,48},{88,56},{96,... | collective-permute-start | bytes 393224 | tf_op jit(solution)/shard_map/ppermute | solution.py:32
  36.8 26.5 %collective-permute-start.6 = (bf16[512,128]{1,0:T(8,128)(2,1)S(1)}, bf16[512,128]{1,0:T(8,128)(2,1)S(1)}, u32[]{:S(2)}, u32[]{:S(2)}) collective-permute-start(bf16[512,128]{1,0:T(8,128)(2,1)S(1)} %get-tuple-element.40), channel_id=1, source_target_pairs={{24,0},{32,8},{40,16},{48,24},{56,32},{64,40},{72,48},{80,56},{88,... | collective-permute-start | bytes 393224 | tf_op jit(solution)/shard_map/ppermute | solution.py:32
  38.1 25.2 %collective-permute-start.7 = (bf16[512,128]{1,0:T(8,128)(2,1)S(1)}, bf16[512,128]{1,0:T(8,128)(2,1)S(1)}, u32[]{:S(2)}, u32[]{:S(2)}) collective-permute-start(bf16[512,128]{1,0:T(8,128)(2,1)S(1)} %get-tuple-element.41), channel_id=1, source_target_pairs={{16,0},{24,8},{32,16},{40,24},{48,32},{56,40},{64,48},{72,56},{80,... | collective-permute-start | bytes 393224 | tf_op jit(solution)/shard_map/ppermute | solution.py:32
  39.4 23.9 %collective-permute-start.8 = (bf16[512,128]{1,0:T(8,128)(2,1)S(1)}, bf16[512,128]{1,0:T(8,128)(2,1)S(1)}, u32[]{:S(2)}, u32[]{:S(2)}) collective-permute-start(bf16[512,128]{1,0:T(8,128)(2,1)S(1)} %get-tuple-element.42), channel_id=1, source_target_pairs={{8,0},{16,8},{24,16},{32,24},{40,32},{48,40},{56,48},{64,56},{72,6... | collective-permute-start | bytes 393224 | tf_op jit(solution)/shard_map/ppermute | solution.py:32
  42.4 36.7 %all-to-all-start = ((f32[256,2,128]{2,1,0:T(2,128)}), f32[256,2,128]{2,1,0:T(2,128)S(1)}, u32[]{:S(2)}, u32[]{:S(2)}) async-start(f32[256,2,128]{2,1,0:T(2,128)} %broadcast_in_dim.3), calls=%async_computation | async-start | bytes 524288 | tf_op jit(solution)/shard_map/all_to_all | solution.py:378

commit v6 on v5

--- a/solution.py
+++ b/solution.py
@@ -16,6 +16,7 @@
 SUB = 128
 SPAN = 1152
 CHUNKS = SPAN // SUB
+WIDE = 384
 ID_ROWS = 16
 MSG = 2 * TOK + ID_ROWS
 SCALING = HEAD ** (-0.5)
@@ -98,7 +99,7 @@
 
 def kernel(
     b4, b2, b0, first_swap, middle_swap, last_swap, xh_ref, scale_ref, dcat, dcat_t, gains_ref, f_ref,
-    att_hbm, gq_hbm, r4, r3, r2, r1, own_ref, gain_ref,
+    att_hbm, gq_hbm, four_ref, two_ref, own_ref, swap_ref, gain_ref,
     att_ref, gq_ref, cosine, sine, kext, vwin, khat_t, v_t, qhat, qext_t,
     s_ref, w_ref, ds_ref, dk, dv, qg_acc, b3, b1, att_sem, gq_sem,
 ):
@@ -182,7 +183,6 @@
             ref[slot, SPAN:WINDOW, 0:256] = zero
     later = jnp.where(row <= lane, 0.0, -1e30)
     later = jnp.concatenate([later, later], axis=1)
-    last = SPAN - SUB
     spans = (slice(0, SPAN), slice(SUB, WINDOW))
     columns_of = (slice(0, 256), slice(256, 512))
 
@@ -202,28 +202,28 @@
         slot = pair % 2
 
         def scores(sub):
-            s = dot(kext[spans[sub], :], qext_t[pair, :, columns_of[sub]])
-            tail = s[last:] + later
-            s_ref[sub, 0:last, :] = s[:last]
-            s_ref[sub, last:, :] = tail
-            top = jnp.maximum(
-                jnp.max(s[:last].reshape(last // 8, 8, 256), axis=0),
-                jnp.max(tail.reshape(SUB // 8, 8, 256), axis=0),
-            )
+            q = qext_t[pair, :, columns_of[sub]]
+            top = jnp.full((8, 256), -1e30, jnp.float32)
+            for start in range(0, SPAN, WIDE):
+                s = dot(kext[sub * SUB + start : sub * SUB + start + WIDE, :], q)
+                if start + WIDE == SPAN:
+                    s = jnp.concatenate([s[: WIDE - SUB], s[WIDE - SUB :] + later])
+                s_ref[slot, sub, start : start + WIDE, :] = s
+                top = jnp.maximum(top, jnp.max(s.reshape(WIDE // 8, 8, 256), axis=0))
             return jnp.max(top, axis=0, keepdims=True) * EXP2
 
         def exponents(sub, shift):
             total = jnp.zeros((8, 256), jnp.float32)
             for c in range(CHUNKS):
-                e = jnp.exp2(s_ref[sub, c * SUB : (c + 1) * SUB, :] * EXP2 - shift)
-                s_ref[sub, c * SUB : (c + 1) * SUB, :] = e
+                e = jnp.exp2(s_ref[slot, sub, c * SUB : (c + 1) * SUB, :] * EXP2 - shift)
+                s_ref[slot, sub, c * SUB : (c + 1) * SUB, :] = e
                 total = total + jnp.sum(e.reshape(SUB // 8, 8, 256), axis=0)
             return 1.0 / jnp.sum(total, axis=0, keepdims=True)
 
         def weigh(sub, inverse):
             for c in range(CHUNKS):
                 keys = slice((sub + c) * SUB, (sub + c + 1) * SUB)
-                w = s_ref[sub, c * SUB : (c + 1) * SUB, :] * inverse
+                w = s_ref[slot, sub, c * SUB : (c + 1) * SUB, :] * inverse
                 w_ref[slot, keys, columns_of[sub]] = w.astype(jnp.bfloat16)
 
         def attend(sub):
@@ -237,9 +237,12 @@
             return center
 
         def score_terms(sub, center):
-            dw = dot(vwin[spans[sub], :], dcat_t[pair, :, columns_of[sub]])
-            w = w_ref[slot, spans[sub], columns_of[sub]].astype(jnp.float32)
-            ds_ref[slot, spans[sub], columns_of[sub]] = (w * (dw - center)).astype(jnp.bfloat16)
+            d_t = dcat_t[pair, :, columns_of[sub]]
+            for start in range(0, SPAN, WIDE):
+                keys = slice(sub * SUB + start, sub * SUB + start + WIDE)
+                dw = dot(vwin[keys, :], d_t)
+                w = w_ref[slot, keys, columns_of[sub]].astype(jnp.float32)
+                ds_ref[slot, keys, columns_of[sub]] = (w * (dw - center)).astype(jnp.bfloat16)
 
         def query_terms(sub):
             dq_t = dot(khat_t[:, spans[sub]], ds_ref[slot, spans[sub], columns_of[sub]]) * SCALING
@@ -279,7 +282,7 @@
     key_terms(HEADS // 2 - 1, 1)
 
     kg = jnp.zeros((8, HEAD), jnp.float32)
-    outs = (r4, r3, r2, r1, own_ref)
+    outs = ((four_ref, 0), (swap_ref, 2 * TOK), (two_ref, 0), (swap_ref, 0), (own_ref, 0))
     for j in range(parts):
         rows = slice(j * SUB, (j + 1) * SUB)
         here = slice((j % 2) * SUB, (j % 2 + 1) * SUB)
@@ -291,19 +294,23 @@
         kg = kg + jnp.sum((dn * xh).reshape(SUB // 8, 8, HEAD), axis=0)
         dxh = dn * k_gain
         gk = r * (dxh - xh * jnp.mean(dxh * xh, axis=1, keepdims=True))
-        out = outs[j // 2]
-        out[here, :] = gk.astype(out.dtype)
-        out[TOK + (j % 2) * SUB : TOK + (j % 2 + 1) * SUB, :] = dv[rows, :].astype(out.dtype)
+        out, at = outs[j // 2]
+        at = at + (j % 2) * SUB
+        out[at : at + SUB, :] = gk.astype(out.dtype)
+        out[at + TOK : at + TOK + SUB, :] = dv[rows, :].astype(out.dtype)
     gains = jnp.concatenate(
         [jnp.sum(qg_acc[...], axis=0, keepdims=True), jnp.sum(kg, axis=0, keepdims=True)]
     )
     gain_ref[...] = gains
+    high = gains.astype(jnp.bfloat16).astype(jnp.float32)
+    middle = (gains - high).astype(jnp.bfloat16).astype(jnp.float32)
+    low = gains - high - middle
+    swap_ref[4 * TOK :, :] = jnp.concatenate(
+        [high, middle, low, jnp.zeros((ID_ROWS - 6, HEAD), jnp.float32)]
+    ).astype(jnp.bfloat16)
     for pair in range(HEADS // 2):
         for copy in copies(pair):
             copy.wait()
-
-
-RETURN = jnp.bfloat16
 
 
 def attention(blocks, prepared, frequency):
@@ -316,12 +323,14 @@
         out_shape=[
             shape((TOK, HEADS * HEAD), bf16),
             shape((TOK, HEADS * HEAD), bf16),
-            *[shape((2 * TOK, HEAD), RETURN) for _ in range(REACH)],
             shape((2 * TOK, HEAD), f32),
+            shape((2 * TOK, HEAD), f32),
+            shape((2 * TOK, HEAD), f32),
+            shape((4 * TOK + ID_ROWS, HEAD), bf16),
             shape((2, HEAD), f32),
         ],
         in_specs=[vmem] * 12,
-        out_specs=[hbm] * 2 + [vmem] * 6,
+        out_specs=[hbm] * 2 + [vmem] * 5,
         scratch_shapes=[
             pltpu.VMEM((TOK, HEADS * HEAD), bf16),
             pltpu.VMEM((TOK, HEADS * HEAD), bf16),
@@ -333,7 +342,7 @@
             pltpu.VMEM((HEAD, WINDOW), bf16),
             pltpu.VMEM((HEADS * TOK, HEAD), bf16),
             pltpu.VMEM((HEADS // 2, 2 * HEAD, 512), bf16),
-            pltpu.VMEM((2, SPAN, 256), f32),
+            pltpu.VMEM((2, 2, SPAN, 256), f32),
             pltpu.VMEM((2, WINDOW, 512), bf16),
             pltpu.VMEM((2, WINDOW, 512), bf16),
             pltpu.VMEM((WINDOW, HEAD), f32),
@@ -372,10 +381,46 @@
     return lax.ppermute(block, "context", route)
 
 
-def summed_over_all(terms):
-    axes = ("context", "tensor")
-    copies = jnp.broadcast_to(terms, (lax.axis_size(axes),) + terms.shape)
-    return jnp.sum(lax.all_to_all(copies, axes, 0, 0), axis=0)
+def chip_kernel(swap, four, two, own, gains, four_out, two_out, own_out, gains_out):
+    even = lax.rem(lax.axis_index("context"), 2) == 0
+    one, three = slice(0, 2 * TOK), slice(2 * TOK, 4 * TOK)
+
+    @pl.when(even)
+    def _():
+        four_out[...] = four[...].astype(jnp.bfloat16)
+        two_out[...] = (two[...] + swap[three, :].astype(jnp.float32)).astype(jnp.bfloat16)
+        own_out[...] = own[...] + swap[one, :].astype(jnp.float32)
+
+    @pl.when(jnp.logical_not(even))
+    def _():
+        four_out[...] = (four[...] + swap[three, :].astype(jnp.float32)).astype(jnp.bfloat16)
+        two_out[...] = (two[...] + swap[one, :].astype(jnp.float32)).astype(jnp.bfloat16)
+        own_out[...] = own[...]
+
+    split = swap[4 * TOK :, :].astype(jnp.float32)
+    gains_out[...] = gains[...] + ((split[0:2] + split[2:4]) + split[4:6])
+
+
+def chip_terms(swap, four, two, own, gains):
+    vmem = pl.BlockSpec(memory_space=pltpu.VMEM)
+    shape = jax.ShapeDtypeStruct
+    return pl.pallas_call(
+        chip_kernel,
+        out_shape=[
+            shape((2 * TOK, HEAD), jnp.bfloat16),
+            shape((2 * TOK, HEAD), jnp.bfloat16),
+            shape((2 * TOK, HEAD), jnp.float32),
+            shape((2, HEAD), jnp.float32),
+        ],
+        in_specs=[vmem] * 5,
+        out_specs=[vmem] * 4,
+        compiler_params=pltpu.CompilerParams(vmem_limit_bytes=16 * 1024 * 1024),
+    )(swap, four, two, own, gains)
+
+
+def added(terms, axis, bit):
+    route = [(i, i ^ bit) for i in range(lax.axis_size(axis))]
+    return terms + lax.ppermute(terms, axis, route)
 
 
 def body(queries, keys, values, output_gradient, q_gain, k_gain, doc_ids):
@@ -391,23 +436,25 @@
     half = jnp.arange(HEAD // 2, dtype=jnp.float32)
     frequency = THETA ** (-(half * 2.0 / HEAD))
     frequency = jnp.concatenate([frequency, frequency]).reshape(1, HEAD)
-    attended, query_gradient, *returns, own, gains = attention(
-        blocks,
-        prepared,
-        frequency,
-    )
-    total = own
-    for distance, block in zip(range(REACH, 0, -1), returns):
-        total = total + passed_along(block, "context", -distance)
-    total = total.astype(jnp.bfloat16)
-    gain_total = summed_over_all(gains)
+    attended, query_gradient, four, two, own, swap, gains = attention(blocks, prepared, frequency)
+    four, two, own, gains = chip_terms(swapped(swap), four, two, own, gains)
+    four = passed_along(four, "context", -4)
+    for bit in (1, 2, 4):
+        gains = added(gains, "tensor", bit)
+    four, two, gains = lax.optimization_barrier((four, two, gains))
+    two = passed_along(two, "context", -2)
+    for bit in (8, 16, 2):
+        gains = added(gains, "context", bit)
+    two, gains = lax.optimization_barrier((two, gains))
+    gains = added(gains, "context", 4)
+    keys, values = slice(0, TOK), slice(TOK, 2 * TOK)
     return (
         attended,
         query_gradient,
-        total[:TOK],
-        total[TOK:],
-        gain_total[0],
-        gain_total[1],
+        ((own[keys] + two[keys]) + four[keys]).astype(jnp.bfloat16),
+        ((own[values] + two[values]) + four[values]).astype(jnp.bfloat16),
+        gains[0],
+        gains[1],
     )
 
 

time: 80.4 us -> 78.8 us (0.980)
  the two profiles are of different devices: /device:TPU:1 before, /device:TPU:24 now
where the time goes in v6:
time: 78.8 us; the launch traced here: 78.4 us
  starting transfers between devices  32.6 us (41%)
  waiting for transfers between devices  23.5 us (30%)
  Pallas kernels  17.5 us (22%)
  local copies, waits for them, and re-layouts  3.26 us (4%)
  other arithmetic  0.81 us (1%)
    ppermute x7, waiting for transfers between devices, added(): return terms + lax.ppermute(terms, axis, route)  20 us
    ppermute x4, starting transfers between devices, passed_along(): return lax.ppermute(block, axis, route)  16.2 us
    pallas_call x1, Pallas kernels, attention(): pl.pallas_call(kernel, out_shape=[shape((TOK, HEADS * HEAD), bf16), shape...  15.4 us
    ppermute x7, starting transfers between devices, added(): return terms + lax.ppermute(terms, axis, route)  13.5 us
    ppermute x4, waiting for transfers between devices, swapped(): return lax.ppermute(block, 'context', route)  3.25 us
    ppermute x4, starting transfers between devices, swapped(): return lax.ppermute(block, 'context', route)  2.91 us
    unnamed x10, local copies, waits for them, and re-layouts  2.74 us
  transfers between devices with their start and end apart: 15, of which 10 were waited for; matrix products, arithmetic and copies ran while one was open for 1% of the time, Pallas kernels for 1%

profile of v6, /device:TPU:24, one launch (start us, length us, event | category | flops | bytes accessed | tf_op | source)
XLA Modules:
  0.0 78.4 jit_solution(6521319118713368829)
XLA Ops:
  0.6 1.5 %shard_map.118.b0 = bf16[528,128]{1,0:T(8,128)(2,1)} custom-call(bf16[256,128]{1,0:T(8,128)(2,1)} %keys.1, bf16[256,128]{1,0:T(8,128)(2,1)} %values.1, s32[2,128]{1,0:T(2,128)} %bitcast.11), custom_call_target="tpu_custom_call" | custom-call | tf_op jit(solution)/shard_map/pallas_call | solution.py:371
  2.2 3.4 %collective-permute-start.1 = (bf16[528,128]{1,0:T(8,128)(2,1)}, bf16[528,128]{1,0:T(8,128)(2,1)S(1)}, u32[]{:S(2)}, u32[]{:S(2)}) collective-permute-start(bf16[528,128]{1,0:T(8,128)(2,1)} %shard_map.118.b0), channel_id=1, source_target_pairs={{0,16},{8,24},{16,32},{24,40},{32,48},{40,56},{48,64},{56,72},{64,... | collective-permute-start | bytes 405512 | tf_op jit(solution)/shard_map/ppermute | solution.py:33
  5.6 4.6 %collective-permute-start = (bf16[528,128]{1,0:T(8,128)(2,1)}, bf16[528,128]{1,0:T(8,128)(2,1)S(1)}, u32[]{:S(2)}, u32[]{:S(2)}) collective-permute-start(bf16[528,128]{1,0:T(8,128)(2,1)} %shard_map.118.b0), channel_id=1, source_target_pairs={{0,32},{8,40},{16,48},{24,56},{32,64},{40,72},{48,80},{56,88},{64,... | collective-permute-start | bytes 405512 | tf_op jit(solution)/shard_map/ppermute | solution.py:33
  10.2 1.3 %collective-permute-start.2 = (bf16[528,128]{1,0:T(8,128)(2,1)}, bf16[528,128]{1,0:T(8,128)(2,1)S(1)}, u32[]{:S(2)}, u32[]{:S(2)}) collective-permute-start(bf16[528,128]{1,0:T(8,128)(2,1)} %shard_map.118.b0), channel_id=1, source_target_pairs={{0,8},{16,24},{32,40},{48,56},{64,72},{80,88},{96,104},{112,120},{... | collective-permute-start | bytes 405512 | tf_op jit(solution)/shard_map/ppermute | solution.py:381
  11.5 0.6 copy-done.3
  12.2 1.0 %copy-done.1 = bf16[256,1024]{1,0:T(8,128)(2,1)S(1)} copy-done((bf16[256,1024]{1,0:T(8,128)(2,1)S(1)}, bf16[256,1024]{1,0:T(8,128)(2,1)}, u32[]{:S(2)}) %copy-start.1) | copy-done | bytes 524312
  13.2 1.0 %copy-done.2 = bf16[256,1024]{1,0:T(8,128)(2,1)S(1)} copy-done((bf16[256,1024]{1,0:T(8,128)(2,1)S(1)}, bf16[256,1024]{1,0:T(8,128)(2,1)}, u32[]{:S(2)}) %copy-start.2) | copy-done | bytes 524312
  14.3 0.5 shard_map.119
  14.8 0.1 collective-permute-start.3
  14.9 0.2 collective-permute-done.b4
  15.1 1.3 %collective-permute-start.4 = (bf16[528,128]{1,0:T(8,128)(2,1)S(1)}, bf16[528,128]{1,0:T(8,128)(2,1)S(1)}, u32[]{:S(2)}, u32[]{:S(2)}) collective-permute-start(bf16[528,128]{1,0:T(8,128)(2,1)S(1)} %collective-permute-done.b4), channel_id=1, source_target_pairs={{8,0},{24,16},{40,32},{56,48},{72,64},{88,80},{104,96},{120,112},{... | collective-permute-start | bytes 405512 | tf_op jit(solution)/shard_map/ppermute | solution.py:381
  16.5 1.9 %collective-permute-done.4.last_swap = bf16[528,128]{1,0:T(8,128)(2,1)S(1)} collective-permute-done((bf16[528,128]{1,0:T(8,128)(2,1)S(1)}, bf16[528,128]{1,0:T(8,128)(2,1)S(1)}, u32[]{:S(2)}, u32[]{:S(2)}) %collective-permute-start.4) | collective-permute-done | bytes 135200 | tf_op jit(solution)/shard_map/ppermute | solution.py:381
  18.4 15.4 %shard_map.120 = (bf16[256,1024]{1,0:T(8,128)(2,1)}, bf16[256,1024]{1,0:T(8,128)(2,1)}, f32[512,128]{1,0:T(8,128)S(1)}, f32[512,128]{1,0:T(8,128)S(1)}, f32[512,...) custom-call(bf16[528,128]{1,0:T(8,128)(2,1)S(1)} %collective-permute-done.b4, ...), custom_call_target="tpu_custom_call" | custom-call | tf_op jit(solution)/shard_map/pallas_call | solution.py:321
  33.7 0.2 collective-permute-start.5
  34.0 1.4 %collective-permute-done.5.swap = bf16[1040,128]{1,0:T(8,128)(2,1)S(1)} collective-permute-done((bf16[1040,128]{1,0:T(8,128)(2,1)S(1)}, bf16[1040,128]{1,0:T(8,128)(2,1)S(1)}, u32[]{:S(2)}, u32[]{:S(2)}) %collective-permute-start.5) | collective-permute-done | bytes 266272 | tf_op jit(solution)/shard_map/ppermute | solution.py:381
  35.4 3.9 %collective-permute-start.6 = (bf16[512,128]{1,0:T(8,128)(2,1)S(1)}, bf16[512,128]{1,0:T(8,128)(2,1)S(1)}, u32[]{:S(2)}, u32[]{:S(2)}) collective-permute-start(bf16[512,128]{1,0:T(8,128)(2,1)S(1)} %get-tuple-element.52), channel_id=1, source_target_pairs={{32,0},{40,8},{48,16},{56,24},{64,32},{72,40},{80,48},{88,56},{96,... | collective-permute-start | bytes 393224 | tf_op jit(solution)/shard_map/ppermute | solution.py:33
  39.4 2.0 %collective-permute-start.7 = (f32[2,128]{1,0:T(2,128)S(1)}, f32[2,128]{1,0:T(2,128)S(1)}, u32[]{:S(2)}, u32[]{:S(2)}) collective-permute-start(f32[2,128]{1,0:T(2,128)S(1)} %get-tuple-element.54), channel_id=1, source_target_pairs={{0,1},{1,0},{2,3},{3,2},{4,5},{5,4},{6,7},{7,6},{8,9},{9,8},{10,11... | collective-permute-start | bytes 3080 | tf_op jit(solution)/shard_map/ppermute | solution.py:423
  41.4 1.7 %collective-permute-done.7 = f32[2,128]{1,0:T(2,128)S(1)} collective-permute-done((f32[2,128]{1,0:T(2,128)S(1)}, f32[2,128]{1,0:T(2,128)S(1)}, u32[]{:S(2)}, u32[]{:S(2)}) %collective-permute-start.7) | collective-permute-done | bytes 1056 | tf_op jit(solution)/shard_map/ppermute | solution.py:423
  43.0 3.3 %collective-permute-start.8 = (f32[2,128]{1,0:T(2,128)S(1)}, f32[2,128]{1,0:T(2,128)S(1)}, u32[]{:S(2)}, u32[]{:S(2)}) collective-permute-start(f32[2,128]{1,0:T(2,128)S(1)} %add.33), channel_id=1, source_target_pairs={{0,2},{1,3},{2,0},{3,1},{4,6},{5,7},{6,4},{7,5},{8,10},{9,11},{10,... | collective-permute-start | bytes 3080 | tf_op jit(solution)/shard_map/ppermute | solution.py:423
  46.3 1.5 %collective-permute-done.8 = f32[2,128]{1,0:T(2,128)S(1)} collective-permute-done((f32[2,128]{1,0:T(2,128)S(1)}, f32[2,128]{1,0:T(2,128)S(1)}, u32[]{:S(2)}, u32[]{:S(2)}) %collective-permute-start.8) | collective-permute-done | bytes 1056 | tf_op jit(solution)/shard_map/ppermute | solution.py:423
  47.8 6.8 %collective-permute-start.9 = (f32[2,128]{1,0:T(2,128)S(1)}, f32[2,128]{1,0:T(2,128)S(1)}, u32[]{:S(2)}, u32[]{:S(2)}) collective-permute-start(f32[2,128]{1,0:T(2,128)S(1)} %add.34), channel_id=1, source_target_pairs={{0,4},{1,5},{2,6},{3,7},{4,0},{5,1},{6,2},{7,3},{8,12},{9,13},{10,... | collective-permute-start | bytes 3080 | tf_op jit(solution)/shard_map/ppermute | solution.py:423
  54.7 1.5 %collective-permute-done.9 = f32[2,128]{1,0:T(2,128)S(1)} collective-permute-done((f32[2,128]{1,0:T(2,128)S(1)}, f32[2,128]{1,0:T(2,128)S(1)}, u32[]{:S(2)}, u32[]{:S(2)}) %collective-permute-start.9) | collective-permute-done | bytes 1056 | tf_op jit(solution)/shard_map/ppermute | solution.py:423
  56.2 4.2 %collective-permute-start.10 = (bf16[512,128]{1,0:T(8,128)(2,1)S(1)}, bf16[512,128]{1,0:T(8,128)(2,1)S(1)}, u32[]{:S(2)}, u32[]{:S(2)}) collective-permute-start(bf16[512,128]{1,0:T(8,128)(2,1)S(1)} %get-tuple-element.55), channel_id=1, source_target_pairs={{16,0},{24,8},{32,16},{40,24},{48,32},{56,40},{64,48},{72,56},{80,... | collective-permute-start | bytes 393224 | tf_op jit(solution)/shard_map/ppermute | solution.py:33
  60.5 0.5 collective-permute-start.11
  61.0 3.1 %collective-permute-done.11 = f32[2,128]{1,0:T(2,128)S(1)} collective-permute-done((f32[2,128]{1,0:T(2,128)S(1)}, f32[2,128]{1,0:T(2,128)S(1)}, u32[]{:S(2)}, u32[]{:S(2)}) %collective-permute-start.11) | collective-permute-done | bytes 1056 | tf_op jit(solution)/shard_map/ppermute | solution.py:423
  64.1 0.1 collective-permute-start.12
  64.3 4.9 %collective-permute-done.12 = f32[2,128]{1,0:T(2,128)S(1)} collective-permute-done((f32[2,128]{1,0:T(2,128)S(1)}, f32[2,128]{1,0:T(2,128)S(1)}, u32[]{:S(2)}, u32[]{:S(2)}) %collective-permute-start.12) | collective-permute-done | bytes 1056 | tf_op jit(solution)/shard_map/ppermute | solution.py:423
  69.2 3.6 %collective-permute-done.13 = f32[2,128]{1,0:T(2,128)S(1)} collective-permute-done((f32[2,128]{1,0:T(2,128)S(1)}, f32[2,128]{1,0:T(2,128)S(1)}, u32[]{:S(2)}, u32[]{:S(2)}) %collective-permute-start.13) | collective-permute-done | bytes 1056 | tf_op jit(solution)/shard_map/ppermute | solution.py:423
  72.8 0.7 collective-permute-start.14
  73.5 0.7 add_convert_fusion
  74.2 3.6 %collective-permute-done.14 = f32[2,128]{1,0:T(2,128)S(1)} collective-permute-done((f32[2,128]{1,0:T(2,128)S(1)}, f32[2,128]{1,0:T(2,128)S(1)}, u32[]{:S(2)}, u32[]{:S(2)}) %collective-permute-start.14) | collective-permute-done | bytes 1056 | tf_op jit(solution)/shard_map/ppermute | solution.py:423
  77.9 0.5 slice_bitcast_fusion
  (23 shorter events, 0.2 us)
Async XLA Ops:
  2.2 12.6 %collective-permute-start.1 = (bf16[528,128]{1,0:T(8,128)(2,1)}, bf16[528,128]{1,0:T(8,128)(2,1)S(1)}, u32[]{:S(2)}, u32[]{:S(2)}) collective-permute-start(bf16[528,128]{1,0:T(8,128)(2,1)} %shard_map.118.b0), channel_id=1, source_target_pairs={{0,16},{8,24},{16,32},{24,40},{32,48},{40,56},{48,64},{56,72},{64,... | collective-permute-start | bytes 405512 | tf_op jit(solution)/shard_map/ppermute | solution.py:33
  5.6 9.6 %collective-permute-start = (bf16[528,128]{1,0:T(8,128)(2,1)}, bf16[528,128]{1,0:T(8,128)(2,1)S(1)}, u32[]{:S(2)}, u32[]{:S(2)}) collective-permute-start(bf16[528,128]{1,0:T(8,128)(2,1)} %shard_map.118.b0), channel_id=1, source_target_pairs={{0,32},{8,40},{16,48},{24,56},{32,64},{40,72},{48,80},{56,88},{64,... | collective-permute-start | bytes 405512 | tf_op jit(solution)/shard_map/ppermute | solution.py:33
  10.2 6.3 %collective-permute-start.2 = (bf16[528,128]{1,0:T(8,128)(2,1)}, bf16[528,128]{1,0:T(8,128)(2,1)S(1)}, u32[]{:S(2)}, u32[]{:S(2)}) collective-permute-start(bf16[528,128]{1,0:T(8,128)(2,1)} %shard_map.118.b0), channel_id=1, source_target_pairs={{0,8},{16,24},{32,40},{48,56},{64,72},{80,88},{96,104},{112,120},{... | collective-permute-start | bytes 405512 | tf_op jit(solution)/shard_map/ppermute | solution.py:381
  11.5 0.7 copy-start.3
  11.5 0.7 copy-start.4
  12.2 1.0 %copy-start.1 = (bf16[256,1024]{1,0:T(8,128)(2,1)S(1)}, bf16[256,1024]{1,0:T(8,128)(2,1)}, u32[]{:S(2)}) copy-start(bf16[256,1024]{1,0:T(8,128)(2,1)} %q_ref.1) | copy-start | bytes 1572868
  13.2 1.0 %copy-start.2 = (bf16[256,1024]{1,0:T(8,128)(2,1)S(1)}, bf16[256,1024]{1,0:T(8,128)(2,1)}, u32[]{:S(2)}) copy-start(bf16[256,1024]{1,0:T(8,128)(2,1)} %d_ref.1) | copy-start | bytes 1572868
  14.3 4.1 %copy-start = (bf16[528,128]{1,0:T(8,128)(2,1)S(1)}, bf16[528,128]{1,0:T(8,128)(2,1)}, u32[]{:S(2)}) copy-start(bf16[528,128]{1,0:T(8,128)(2,1)} %shard_map.118.b0) | copy-start | bytes 405508
  14.8 3.6 %collective-permute-start.3 = (bf16[528,128]{1,0:T(8,128)(2,1)S(1)}, bf16[528,128]{1,0:T(8,128)(2,1)S(1)}, u32[]{:S(2)}, u32[]{:S(2)}) collective-permute-start(bf16[528,128]{1,0:T(8,128)(2,1)S(1)} %collective-permute-done.1.b2), channel_id=1, source_target_pairs={{0,8},{8,0},{16,24},{24,16},{32,40},{40,32},{48,56},{56,48},{64,72... | collective-permute-start | bytes 405512 | tf_op jit(solution)/shard_map/ppermute | solution.py:381
  15.1 3.2 %collective-permute-start.4 = (bf16[528,128]{1,0:T(8,128)(2,1)S(1)}, bf16[528,128]{1,0:T(8,128)(2,1)S(1)}, u32[]{:S(2)}, u32[]{:S(2)}) collective-permute-start(bf16[528,128]{1,0:T(8,128)(2,1)S(1)} %collective-permute-done.b4), channel_id=1, source_target_pairs={{8,0},{24,16},{40,32},{56,48},{72,64},{88,80},{104,96},{120,112},{... | collective-permute-start | bytes 405512 | tf_op jit(solution)/shard_map/ppermute | solution.py:381
  33.7 1.6 %collective-permute-start.5 = (bf16[1040,128]{1,0:T(8,128)(2,1)S(1)}, bf16[1040,128]{1,0:T(8,128)(2,1)S(1)}, u32[]{:S(2)}, u32[]{:S(2)}) collective-permute-start(bf16[1040,128]{1,0:T(8,128)(2,1)S(1)} %get-tuple-element.46), channel_id=1, source_target_pairs={{0,8},{8,0},{16,24},{24,16},{32,40},{40,32},{48,56},{56,48},{64,72... | collective-permute-start | bytes 798728 | tf_op jit(solution)/shard_map/ppermute | solution.py:381
  35.4 20.8 %collective-permute-start.6 = (bf16[512,128]{1,0:T(8,128)(2,1)S(1)}, bf16[512,128]{1,0:T(8,128)(2,1)S(1)}, u32[]{:S(2)}, u32[]{:S(2)}) collective-permute-start(bf16[512,128]{1,0:T(8,128)(2,1)S(1)} %get-tuple-element.52), channel_id=1, source_target_pairs={{32,0},{40,8},{48,16},{56,24},{64,32},{72,40},{80,48},{88,56},{96,... | collective-permute-start | bytes 393224 | tf_op jit(solution)/shard_map/ppermute | solution.py:33
  39.4 3.7 %collective-permute-start.7 = (f32[2,128]{1,0:T(2,128)S(1)}, f32[2,128]{1,0:T(2,128)S(1)}, u32[]{:S(2)}, u32[]{:S(2)}) collective-permute-start(f32[2,128]{1,0:T(2,128)S(1)} %get-tuple-element.54), channel_id=1, source_target_pairs={{0,1},{1,0},{2,3},{3,2},{4,5},{5,4},{6,7},{7,6},{8,9},{9,8},{10,11... | collective-permute-start | bytes 3080 | tf_op jit(solution)/shard_map/ppermute | solution.py:423
  43.0 4.8 %collective-permute-start.8 = (f32[2,128]{1,0:T(2,128)S(1)}, f32[2,128]{1,0:T(2,128)S(1)}, u32[]{:S(2)}, u32[]{:S(2)}) collective-permute-start(f32[2,128]{1,0:T(2,128)S(1)} %add.33), channel_id=1, source_target_pairs={{0,2},{1,3},{2,0},{3,1},{4,6},{5,7},{6,4},{7,5},{8,10},{9,11},{10,... | collective-permute-start | bytes 3080 | tf_op jit(solution)/shard_map/ppermute | solution.py:423
  47.8 8.4 %collective-permute-start.9 = (f32[2,128]{1,0:T(2,128)S(1)}, f32[2,128]{1,0:T(2,128)S(1)}, u32[]{:S(2)}, u32[]{:S(2)}) collective-permute-start(f32[2,128]{1,0:T(2,128)S(1)} %add.34), channel_id=1, source_target_pairs={{0,4},{1,5},{2,6},{3,7},{4,0},{5,1},{6,2},{7,3},{8,12},{9,13},{10,... | collective-permute-start | bytes 3080 | tf_op jit(solution)/shard_map/ppermute | solution.py:423
  56.2 16.6 %collective-permute-start.10 = (bf16[512,128]{1,0:T(8,128)(2,1)S(1)}, bf16[512,128]{1,0:T(8,128)(2,1)S(1)}, u32[]{:S(2)}, u32[]{:S(2)}) collective-permute-start(bf16[512,128]{1,0:T(8,128)(2,1)S(1)} %get-tuple-element.55), channel_id=1, source_target_pairs={{16,0},{24,8},{32,16},{40,24},{48,32},{56,40},{64,48},{72,56},{80,... | collective-permute-start | bytes 393224 | tf_op jit(solution)/shard_map/ppermute | solution.py:33
  60.5 3.7 %collective-permute-start.11 = (f32[2,128]{1,0:T(2,128)S(1)}, f32[2,128]{1,0:T(2,128)S(1)}, u32[]{:S(2)}, u32[]{:S(2)}) collective-permute-start(f32[2,128]{1,0:T(2,128)S(1)} %add.35), channel_id=1, source_target_pairs={{0,64},{8,72},{16,80},{24,88},{32,96},{40,104},{48,112},{56,120},{... | collective-permute-start | bytes 3080 | tf_op jit(solution)/shard_map/ppermute | solution.py:423
  64.1 5.1 %collective-permute-start.12 = (f32[2,128]{1,0:T(2,128)S(1)}, f32[2,128]{1,0:T(2,128)S(1)}, u32[]{:S(2)}, u32[]{:S(2)}) collective-permute-start(f32[2,128]{1,0:T(2,128)S(1)} %add.36), channel_id=1, source_target_pairs={{0,128},{8,136},{16,144},{24,152},{32,160},{40,168},{48,176},{56,1... | collective-permute-start | bytes 3080 | tf_op jit(solution)/shard_map/ppermute | solution.py:423
  69.2 3.6 %collective-permute-start.13 = (f32[2,128]{1,0:T(2,128)S(1)}, f32[2,128]{1,0:T(2,128)S(1)}, u32[]{:S(2)}, u32[]{:S(2)}) collective-permute-start(f32[2,128]{1,0:T(2,128)S(1)} %add.37), channel_id=1, source_target_pairs={{0,16},{8,24},{16,0},{24,8},{32,48},{40,56},{48,32},{56,40},{64,80... | collective-permute-start | bytes 3080 | tf_op jit(solution)/shard_map/ppermute | solution.py:423
  72.8 5.1 %collective-permute-start.14 = (f32[2,128]{1,0:T(2,128)S(1)}, f32[2,128]{1,0:T(2,128)S(1)}, u32[]{:S(2)}, u32[]{:S(2)}) collective-permute-start(f32[2,128]{1,0:T(2,128)S(1)} %add.38), channel_id=1, source_target_pairs={{0,32},{8,40},{16,48},{24,56},{32,0},{40,8},{48,16},{56,24},{64,96... | collective-permute-start | bytes 3080 | tf_op jit(solution)/shard_map/ppermute | solution.py:423

commit v7 on v6

--- a/solution.py
+++ b/solution.py
@@ -398,32 +398,40 @@
         own_out[...] = own[...]
 
     split = swap[4 * TOK :, :].astype(jnp.float32)
-    gains_out[...] = gains[...] + ((split[0:2] + split[2:4]) + split[4:6])
-
-
-def chip_terms(swap, four, two, own, gains):
+    total = gains[...] + ((split[0:2] + split[2:4]) + split[4:6])
+    for i in range(gains_out.shape[0]):
+        gains_out[i] = total
+
+
+def spread_kernel(terms, copies):
+    total = sum(terms[i] for i in range(terms.shape[0]))
+    for i in range(copies.shape[0]):
+        copies[i] = total
+
+
+def last_kernel(own, four, two, terms, keys, values, q_gain, k_gain):
+    total = own[...] + two[...].astype(jnp.float32) + four[...].astype(jnp.float32)
+    total = total.astype(jnp.bfloat16)
+    keys[...] = total[:TOK]
+    values[...] = total[TOK:]
+    gains = sum(terms[i] for i in range(terms.shape[0]))
+    q_gain[...] = gains[0:1]
+    k_gain[...] = gains[1:2]
+
+
+def small_call(kernel, out_shape, *operands):
     vmem = pl.BlockSpec(memory_space=pltpu.VMEM)
-    shape = jax.ShapeDtypeStruct
     return pl.pallas_call(
-        chip_kernel,
-        out_shape=[
-            shape((2 * TOK, HEAD), jnp.bfloat16),
-            shape((2 * TOK, HEAD), jnp.bfloat16),
-            shape((2 * TOK, HEAD), jnp.float32),
-            shape((2, HEAD), jnp.float32),
-        ],
-        in_specs=[vmem] * 5,
-        out_specs=[vmem] * 4,
+        kernel,
+        out_shape=[jax.ShapeDtypeStruct(shape, dtype) for shape, dtype in out_shape],
+        in_specs=[vmem] * len(operands),
+        out_specs=[vmem] * len(out_shape),
         compiler_params=pltpu.CompilerParams(vmem_limit_bytes=16 * 1024 * 1024),
-    )(swap, four, two, own, gains)
-
-
-def added(terms, axis, bit):
-    route = [(i, i ^ bit) for i in range(lax.axis_size(axis))]
-    return terms + lax.ppermute(terms, axis, route)
+    )(*operands)
 
 
 def body(queries, keys, values, output_gradient, q_gain, k_gain, doc_ids):
+    f32, bf16 = jnp.float32, jnp.bfloat16
     message = pack(keys, values, doc_ids.reshape(2, HEAD))
     two = passed_along(message, "context", 2)
     first_swap = swapped(message, (0,))
@@ -437,24 +445,34 @@
     frequency = THETA ** (-(half * 2.0 / HEAD))
     frequency = jnp.concatenate([frequency, frequency]).reshape(1, HEAD)
     attended, query_gradient, four, two, own, swap, gains = attention(blocks, prepared, frequency)
-    four, two, own, gains = chip_terms(swapped(swap), four, two, own, gains)
+
+    tensor, context = lax.axis_size("tensor"), lax.axis_size("context")
+    block = (2 * TOK, HEAD)
+    four, two, own, gains = small_call(
+        chip_kernel,
+        [(block, bf16), (block, bf16), (block, f32), ((tensor, 2, HEAD), f32)],
+        *(swapped(swap), four, two, own, gains),
+    )
     four = passed_along(four, "context", -4)
-    for bit in (1, 2, 4):
-        gains = added(gains, "tensor", bit)
+    two = passed_along(two, "context", -2)
+    gains = lax.all_to_all(gains, "tensor", 0, 0)
+    (gains,) = small_call(spread_kernel, [((context // 2, 2, HEAD), f32)], gains)
     four, two, gains = lax.optimization_barrier((four, two, gains))
-    two = passed_along(two, "context", -2)
-    for bit in (8, 16, 2):
-        gains = added(gains, "context", bit)
-    two, gains = lax.optimization_barrier((two, gains))
-    gains = added(gains, "context", 4)
-    keys, values = slice(0, TOK), slice(TOK, 2 * TOK)
+    plane = [[2 * n + core for n in range(context // 2)] for core in range(2)]
+    gains = lax.all_to_all(gains, "context", 0, 0, axis_index_groups=plane)
+    half_block = (TOK, HEAD)
+    key_gradient, value_gradient, q_total, k_total = small_call(
+        last_kernel,
+        [(half_block, bf16), (half_block, bf16), ((1, HEAD), f32), ((1, HEAD), f32)],
+        *(own, four, two, gains),
+    )
     return (
         attended,
         query_gradient,
-        ((own[keys] + two[keys]) + four[keys]).astype(jnp.bfloat16),
-        ((own[values] + two[values]) + four[values]).astype(jnp.bfloat16),
-        gains[0],
-        gains[1],
+        key_gradient,
+        value_gradient,
+        q_total.reshape(HEAD),
+        k_total.reshape(HEAD),
     )
 
 

time: 78.8 us -> 71.8 us (0.911)
  the two profiles are of different devices: /device:TPU:24 before, /device:TPU:2 now
where the time goes in v7:
time: 71.8 us; the launch traced here: 71.4 us
  blocking collectives  31.8 us (44%)
  Pallas kernels  18 us (25%)
  starting transfers between devices  14.7 us (20%)
  waiting for transfers between devices  3.26 us (5%)
  local copies, waits for them, and re-layouts  2.74 us (4%)
  between operations  0.76 us (1%)
    all_to_all x1, blocking collectives, body(): gains = lax.all_to_all(gains, 'tensor', 0, 0)  16 us
    all_to_all x1, blocking collectives, body(): gains = lax.all_to_all(gains, 'context', 0, 0, axis_index_groups=plane)  15.8 us
    pallas_call x1, Pallas kernels, attention(): pl.pallas_call(kernel, out_shape=[shape((TOK, HEADS * HEAD), bf16), shape...  15.2 us
    ppermute x4, starting transfers between devices, passed_along(): return lax.ppermute(block, axis, route)  11.8 us
    ppermute x4, waiting for transfers between devices, swapped(): return lax.ppermute(block, 'context', route)  3.25 us
    ppermute x4, starting transfers between devices, swapped(): return lax.ppermute(block, 'context', route)  2.92 us
    unnamed x10, local copies, waits for them, and re-layouts  2.74 us
    pallas_call x1, Pallas kernels, pack(): pl.pallas_call(pack_kernel, out_shape=jax.ShapeDtypeStruct((MSG, HEAD), j...  1.54 us
  transfers between devices with their start and end apart: 8, of which 2 were waited for; matrix products, arithmetic and copies ran while one was open for 0% of the time, Pallas kernels for 1%

profile of v7, /device:TPU:2, one launch (start us, length us, event | category | flops | bytes accessed | tf_op | source)
XLA Modules:
  0.0 71.4 jit_solution(9406737856550147263)
XLA Ops:
  0.6 1.5 %shard_map.118.b0 = bf16[528,128]{1,0:T(8,128)(2,1)} custom-call(bf16[256,128]{1,0:T(8,128)(2,1)} %keys.1, bf16[256,128]{1,0:T(8,128)(2,1)} %values.1, s32[2,128]{1,0:T(2,128)} %bitcast.9), custom_call_target="tpu_custom_call" | custom-call | tf_op jit(solution)/shard_map/pallas_call | solution.py:371
  2.2 3.4 %collective-permute-start.1 = (bf16[528,128]{1,0:T(8,128)(2,1)}, bf16[528,128]{1,0:T(8,128)(2,1)S(1)}, u32[]{:S(2)}, u32[]{:S(2)}) collective-permute-start(bf16[528,128]{1,0:T(8,128)(2,1)} %shard_map.118.b0), channel_id=1, source_target_pairs={{0,16},{8,24},{16,32},{24,40},{32,48},{40,56},{48,64},{56,72},{64,... | collective-permute-start | bytes 405512 | tf_op jit(solution)/shard_map/ppermute | solution.py:33
  5.6 4.0 %collective-permute-start = (bf16[528,128]{1,0:T(8,128)(2,1)}, bf16[528,128]{1,0:T(8,128)(2,1)S(1)}, u32[]{:S(2)}, u32[]{:S(2)}) collective-permute-start(bf16[528,128]{1,0:T(8,128)(2,1)} %shard_map.118.b0), channel_id=1, source_target_pairs={{0,32},{8,40},{16,48},{24,56},{32,64},{40,72},{48,80},{56,88},{64,... | collective-permute-start | bytes 405512 | tf_op jit(solution)/shard_map/ppermute | solution.py:33
  9.6 1.3 %collective-permute-start.2 = (bf16[528,128]{1,0:T(8,128)(2,1)}, bf16[528,128]{1,0:T(8,128)(2,1)S(1)}, u32[]{:S(2)}, u32[]{:S(2)}) collective-permute-start(bf16[528,128]{1,0:T(8,128)(2,1)} %shard_map.118.b0), channel_id=1, source_target_pairs={{0,8},{16,24},{32,40},{48,56},{64,72},{80,88},{96,104},{112,120},{... | collective-permute-start | bytes 405512 | tf_op jit(solution)/shard_map/ppermute | solution.py:381
  10.9 0.0 copy-start.3
  10.9 0.0 copy-start.4
  10.9 0.6 copy-done.3
  11.6 0.0 copy-done.4
  11.6 0.0 copy-start.1
  11.6 1.0 %copy-done.1 = bf16[256,1024]{1,0:T(8,128)(2,1)S(1)} copy-done((bf16[256,1024]{1,0:T(8,128)(2,1)S(1)}, bf16[256,1024]{1,0:T(8,128)(2,1)}, u32[]{:S(2)}) %copy-start.1) | copy-done | bytes 524312
  12.6 1.0 %copy-done.2 = bf16[256,1024]{1,0:T(8,128)(2,1)S(1)} copy-done((bf16[256,1024]{1,0:T(8,128)(2,1)S(1)}, bf16[256,1024]{1,0:T(8,128)(2,1)}, u32[]{:S(2)}) %copy-start.2) | copy-done | bytes 524312
  13.7 0.5 shard_map.119
  14.2 0.0 collective-permute-done.1.b2
  14.2 0.1 collective-permute-start.3
  14.3 0.0 collective-permute-done.b4
  14.3 1.3 %collective-permute-start.4 = (bf16[528,128]{1,0:T(8,128)(2,1)S(1)}, bf16[528,128]{1,0:T(8,128)(2,1)S(1)}, u32[]{:S(2)}, u32[]{:S(2)}) collective-permute-start(bf16[528,128]{1,0:T(8,128)(2,1)S(1)} %collective-permute-done.b4), channel_id=1, source_target_pairs={{8,0},{24,16},{40,32},{56,48},{72,64},{88,80},{104,96},{120,112},{... | collective-permute-start | bytes 405512 | tf_op jit(solution)/shard_map/ppermute | solution.py:381
  15.6 0.1 maximum_bitcast_fusion.f_ref
  15.7 0.0 collective-permute-done.2.first_swap
  15.7 1.9 %collective-permute-done.4.last_swap = bf16[528,128]{1,0:T(8,128)(2,1)S(1)} collective-permute-done((bf16[528,128]{1,0:T(8,128)(2,1)S(1)}, bf16[528,128]{1,0:T(8,128)(2,1)S(1)}, u32[]{:S(2)}, u32[]{:S(2)}) %collective-permute-start.4) | collective-permute-done | bytes 135200 | tf_op jit(solution)/shard_map/ppermute | solution.py:381
  17.6 0.0 collective-permute-done.3.middle_swap
  17.6 0.0 copy-done
  17.6 15.2 %shard_map.120 = (bf16[256,1024]{1,0:T(8,128)(2,1)}, bf16[256,1024]{1,0:T(8,128)(2,1)}, f32[512,128]{1,0:T(8,128)S(1)}, f32[512,128]{1,0:T(8,128)S(1)}, f32[512,...) custom-call(bf16[528,128]{1,0:T(8,128)(2,1)S(1)} %collective-permute-done.b4, ...), custom_call_target="tpu_custom_call" | custom-call | tf_op jit(solution)/shard_map/pallas_call | solution.py:321
  32.8 0.2 collective-permute-start.5
  33.0 1.4 %collective-permute-done.5.swap = bf16[1040,128]{1,0:T(8,128)(2,1)S(1)} collective-permute-done((bf16[1040,128]{1,0:T(8,128)(2,1)S(1)}, bf16[1040,128]{1,0:T(8,128)(2,1)S(1)}, u32[]{:S(2)}, u32[]{:S(2)}) %collective-permute-start.5) | collective-permute-done | bytes 266272 | tf_op jit(solution)/shard_map/ppermute | solution.py:381
  34.4 0.1 shard_map.121
  34.5 1.3 %collective-permute-start.6 = (bf16[512,128]{1,0:T(8,128)(2,1)S(1)}, bf16[512,128]{1,0:T(8,128)(2,1)S(1)}, u32[]{:S(2)}, u32[]{:S(2)}) collective-permute-start(bf16[512,128]{1,0:T(8,128)(2,1)S(1)} %get-tuple-element.54), channel_id=1, source_target_pairs={{32,0},{40,8},{48,16},{56,24},{64,32},{72,40},{80,48},{88,56},{96,... | collective-permute-start | bytes 393224 | tf_op jit(solution)/shard_map/ppermute | solution.py:33
  35.8 3.1 %collective-permute-start.7 = (bf16[512,128]{1,0:T(8,128)(2,1)S(1)}, bf16[512,128]{1,0:T(8,128)(2,1)S(1)}, u32[]{:S(2)}, u32[]{:S(2)}) collective-permute-start(bf16[512,128]{1,0:T(8,128)(2,1)S(1)} %get-tuple-element.55), channel_id=1, source_target_pairs={{16,0},{24,8},{32,16},{40,24},{48,32},{56,40},{64,48},{72,56},{80,... | collective-permute-start | bytes 393224 | tf_op jit(solution)/shard_map/ppermute | solution.py:33
  38.8 16.0 %all_to_all.10.terms = f32[8,2,128]{2,1,0:T(2,128)S(1)} all-to-all(f32[8,2,128]{2,1,0:T(2,128)S(1)} %get-tuple-element.56), channel_id=1, replica_groups=mesh['context'=32,'tensor'=8] {'tensor'}, dimensions={0} | all-to-all | bytes 16384 | tf_op jit(solution)/shard_map/all_to_all | solution.py:458
  54.8 0.0 collective-permute-done.6.four
  54.9 0.0 collective-permute-done.7.two
  54.9 15.8 %all_to_all.11.terms = f32[16,2,128]{2,1,0:T(2,128)S(1)} all-to-all(f32[16,2,128]{2,1,0:T(2,128)S(1)} %shard_map.122), channel_id=1, replica_groups={{0,16,32,48,64,80,96,112,128,144,160,176,192,208,224,240},{8,24,40,56,7..., dimensions={0} | all-to-all | bytes 32768 | tf_op jit(solution)/shard_map/all_to_all | solution.py:462
  70.7 0.7 shard_map.123
  (4 shorter events, 0.0 us)
Async XLA Ops:
  2.2 12.0 %collective-permute-start.1 = (bf16[528,128]{1,0:T(8,128)(2,1)}, bf16[528,128]{1,0:T(8,128)(2,1)S(1)}, u32[]{:S(2)}, u32[]{:S(2)}) collective-permute-start(bf16[528,128]{1,0:T(8,128)(2,1)} %shard_map.118.b0), channel_id=1, source_target_pairs={{0,16},{8,24},{16,32},{24,40},{32,48},{40,56},{48,64},{56,72},{64,... | collective-permute-start | bytes 405512 | tf_op jit(solution)/shard_map/ppermute | solution.py:33
  5.6 8.7 %collective-permute-start = (bf16[528,128]{1,0:T(8,128)(2,1)}, bf16[528,128]{1,0:T(8,128)(2,1)S(1)}, u32[]{:S(2)}, u32[]{:S(2)}) collective-permute-start(bf16[528,128]{1,0:T(8,128)(2,1)} %shard_map.118.b0), channel_id=1, source_target_pairs={{0,32},{8,40},{16,48},{24,56},{32,64},{40,72},{48,80},{56,88},{64,... | collective-permute-start | bytes 405512 | tf_op jit(solution)/shard_map/ppermute | solution.py:33
  9.6 6.1 %collective-permute-start.2 = (bf16[528,128]{1,0:T(8,128)(2,1)}, bf16[528,128]{1,0:T(8,128)(2,1)S(1)}, u32[]{:S(2)}, u32[]{:S(2)}) collective-permute-start(bf16[528,128]{1,0:T(8,128)(2,1)} %shard_map.118.b0), channel_id=1, source_target_pairs={{0,8},{16,24},{32,40},{48,56},{64,72},{80,88},{96,104},{112,120},{... | collective-permute-start | bytes 405512 | tf_op jit(solution)/shard_map/ppermute | solution.py:381
  10.9 0.7 copy-start.3
  10.9 0.7 copy-start.4
  11.6 1.0 %copy-start.1 = (bf16[256,1024]{1,0:T(8,128)(2,1)S(1)}, bf16[256,1024]{1,0:T(8,128)(2,1)}, u32[]{:S(2)}) copy-start(bf16[256,1024]{1,0:T(8,128)(2,1)} %q_ref.1) | copy-start | bytes 1572868
  12.6 1.0 %copy-start.2 = (bf16[256,1024]{1,0:T(8,128)(2,1)S(1)}, bf16[256,1024]{1,0:T(8,128)(2,1)}, u32[]{:S(2)}) copy-start(bf16[256,1024]{1,0:T(8,128)(2,1)} %d_ref.1) | copy-start | bytes 1572868
  13.7 3.9 %copy-start = (bf16[528,128]{1,0:T(8,128)(2,1)S(1)}, bf16[528,128]{1,0:T(8,128)(2,1)}, u32[]{:S(2)}) copy-start(bf16[528,128]{1,0:T(8,128)(2,1)} %shard_map.118.b0) | copy-start | bytes 405508
  14.2 3.4 %collective-permute-start.3 = (bf16[528,128]{1,0:T(8,128)(2,1)S(1)}, bf16[528,128]{1,0:T(8,128)(2,1)S(1)}, u32[]{:S(2)}, u32[]{:S(2)}) collective-permute-start(bf16[528,128]{1,0:T(8,128)(2,1)S(1)} %collective-permute-done.1.b2), channel_id=1, source_target_pairs={{0,8},{8,0},{16,24},{24,16},{32,40},{40,32},{48,56},{56,48},{64,72... | collective-permute-start | bytes 405512 | tf_op jit(solution)/shard_map/ppermute | solution.py:381
  14.3 3.2 %collective-permute-start.4 = (bf16[528,128]{1,0:T(8,128)(2,1)S(1)}, bf16[528,128]{1,0:T(8,128)(2,1)S(1)}, u32[]{:S(2)}, u32[]{:S(2)}) collective-permute-start(bf16[528,128]{1,0:T(8,128)(2,1)S(1)} %collective-permute-done.b4), channel_id=1, source_target_pairs={{8,0},{24,16},{40,32},{56,48},{72,64},{88,80},{104,96},{120,112},{... | collective-permute-start | bytes 405512 | tf_op jit(solution)/shard_map/ppermute | solution.py:381
  32.8 1.6 %collective-permute-start.5 = (bf16[1040,128]{1,0:T(8,128)(2,1)S(1)}, bf16[1040,128]{1,0:T(8,128)(2,1)S(1)}, u32[]{:S(2)}, u32[]{:S(2)}) collective-permute-start(bf16[1040,128]{1,0:T(8,128)(2,1)S(1)} %get-tuple-element.48), channel_id=1, source_target_pairs={{0,8},{8,0},{16,24},{24,16},{32,40},{40,32},{48,56},{56,48},{64,72... | collective-permute-start | bytes 798728 | tf_op jit(solution)/shard_map/ppermute | solution.py:381
  34.5 20.4 %collective-permute-start.6 = (bf16[512,128]{1,0:T(8,128)(2,1)S(1)}, bf16[512,128]{1,0:T(8,128)(2,1)S(1)}, u32[]{:S(2)}, u32[]{:S(2)}) collective-permute-start(bf16[512,128]{1,0:T(8,128)(2,1)S(1)} %get-tuple-element.54), channel_id=1, source_target_pairs={{32,0},{40,8},{48,16},{56,24},{64,32},{72,40},{80,48},{88,56},{96,... | collective-permute-start | bytes 393224 | tf_op jit(solution)/shard_map/ppermute | solution.py:33
  35.8 19.1 %collective-permute-start.7 = (bf16[512,128]{1,0:T(8,128)(2,1)S(1)}, bf16[512,128]{1,0:T(8,128)(2,1)S(1)}, u32[]{:S(2)}, u32[]{:S(2)}) collective-permute-start(bf16[512,128]{1,0:T(8,128)(2,1)S(1)} %get-tuple-element.55), channel_id=1, source_target_pairs={{16,0},{24,8},{32,16},{40,24},{48,32},{56,40},{64,48},{72,56},{80,... | collective-permute-start | bytes 393224 | tf_op jit(solution)/shard_map/ppermute | solution.py:33

commit v8 on v7

--- a/solution.py
+++ b/solution.py
@@ -16,7 +16,7 @@
 SUB = 128
 SPAN = 1152
 CHUNKS = SPAN // SUB
-WIDE = 384
+WIDE = 128
 ID_ROWS = 16
 MSG = 2 * TOK + ID_ROWS
 SCALING = HEAD ** (-0.5)
@@ -207,7 +207,7 @@
             for start in range(0, SPAN, WIDE):
                 s = dot(kext[sub * SUB + start : sub * SUB + start + WIDE, :], q)
                 if start + WIDE == SPAN:
-                    s = jnp.concatenate([s[: WIDE - SUB], s[WIDE - SUB :] + later])
+                    s = s + later
                 s_ref[slot, sub, start : start + WIDE, :] = s
                 top = jnp.maximum(top, jnp.max(s.reshape(WIDE // 8, 8, 256), axis=0))
             return jnp.max(top, axis=0, keepdims=True) * EXP2
@@ -388,13 +388,13 @@
     @pl.when(even)
     def _():
         four_out[...] = four[...].astype(jnp.bfloat16)
-        two_out[...] = (two[...] + swap[three, :].astype(jnp.float32)).astype(jnp.bfloat16)
+        two_out[...] = two[...] + swap[three, :].astype(jnp.float32)
         own_out[...] = own[...] + swap[one, :].astype(jnp.float32)
 
     @pl.when(jnp.logical_not(even))
     def _():
         four_out[...] = (four[...] + swap[three, :].astype(jnp.float32)).astype(jnp.bfloat16)
-        two_out[...] = (two[...] + swap[one, :].astype(jnp.float32)).astype(jnp.bfloat16)
+        two_out[...] = two[...] + swap[one, :].astype(jnp.float32)
         own_out[...] = own[...]
 
     split = swap[4 * TOK :, :].astype(jnp.float32)
@@ -403,15 +403,15 @@
         gains_out[i] = total
 
 
-def spread_kernel(terms, copies):
+def plane_kernel(two, hop, terms, two_out, copies):
+    two_out[...] = (two[...] + hop[...].astype(jnp.float32)).astype(jnp.bfloat16)
     total = sum(terms[i] for i in range(terms.shape[0]))
     for i in range(copies.shape[0]):
         copies[i] = total
 
 
-def last_kernel(own, four, two, terms, keys, values, q_gain, k_gain):
-    total = own[...] + two[...].astype(jnp.float32) + four[...].astype(jnp.float32)
-    total = total.astype(jnp.bfloat16)
+def last_kernel(own, hop, terms, keys, values, q_gain, k_gain):
+    total = (own[...] + hop[...].astype(jnp.float32)).astype(jnp.bfloat16)
     keys[...] = total[:TOK]
     values[...] = total[TOK:]
     gains = sum(terms[i] for i in range(terms.shape[0]))
@@ -450,21 +450,22 @@
     block = (2 * TOK, HEAD)
     four, two, own, gains = small_call(
         chip_kernel,
-        [(block, bf16), (block, bf16), (block, f32), ((tensor, 2, HEAD), f32)],
+        [(block, bf16), (block, f32), (block, f32), ((tensor, 2, HEAD), f32)],
         *(swapped(swap), four, two, own, gains),
     )
-    four = passed_along(four, "context", -4)
-    two = passed_along(two, "context", -2)
+    hop = passed_along(four, "context", -2)
     gains = lax.all_to_all(gains, "tensor", 0, 0)
-    (gains,) = small_call(spread_kernel, [((context // 2, 2, HEAD), f32)], gains)
-    four, two, gains = lax.optimization_barrier((four, two, gains))
+    two, gains = small_call(
+        plane_kernel, [(block, bf16), ((context // 2, 2, HEAD), f32)], two, hop, gains
+    )
+    hop = passed_along(two, "context", -2)
     plane = [[2 * n + core for n in range(context // 2)] for core in range(2)]
     gains = lax.all_to_all(gains, "context", 0, 0, axis_index_groups=plane)
     half_block = (TOK, HEAD)
     key_gradient, value_gradient, q_total, k_total = small_call(
         last_kernel,
         [(half_block, bf16), (half_block, bf16), ((1, HEAD), f32), ((1, HEAD), f32)],
-        *(own, four, two, gains),
+        *(own, hop, gains),
     )
     return (
         attended,

time: 71.8 us -> 69.6 us (0.969)
  blocking collectives: 31.8 us -> 30.3 us
  Pallas kernels: 18 us -> 16.7 us
    all_to_all x1, blocking collectives: 15.8 us -> 14.3 us  [body(): gains = lax.all_to_all(gains, 'context', 0, 0, axis_index_groups=plane)]
    pallas_call x1, Pallas kernels: 15.2 us -> 13.8 us  [attention(): pl.pallas_call(kernel, out_shape=[shape((TOK, HEADS * HEAD), bf16), shape...]
where the time goes in v8:
time: 69.6 us; the launch traced here: 69.1 us
  blocking collectives  30.3 us (44%)
  Pallas kernels  16.7 us (24%)
  starting transfers between devices  15.3 us (22%)
  waiting for transfers between devices  3.26 us (5%)
  local copies, waits for them, and re-layouts  2.74 us (4%)
  between operations  0.75 us (1%)
    all_to_all x1, blocking collectives, body(): gains = lax.all_to_all(gains, 'tensor', 0, 0)  16 us
    all_to_all x1, blocking collectives, body(): gains = lax.all_to_all(gains, 'context', 0, 0, axis_index_groups=plane)  14.3 us
    pallas_call x1, Pallas kernels, attention(): pl.pallas_call(kernel, out_shape=[shape((TOK, HEADS * HEAD), bf16), shape...  13.8 us
    ppermute x4, starting transfers between devices, passed_along(): return lax.ppermute(block, axis, route)  12.4 us
    ppermute x4, waiting for transfers between devices, swapped(): return lax.ppermute(block, 'context', route)  3.25 us
    ppermute x4, starting transfers between devices, swapped(): return lax.ppermute(block, 'context', route)  2.92 us
    unnamed x10, local copies, waits for them, and re-layouts  2.74 us
    pallas_call x1, Pallas kernels, pack(): pl.pallas_call(pack_kernel, out_shape=jax.ShapeDtypeStruct((MSG, HEAD), j...  1.54 us
  transfers between devices with their start and end apart: 8, of which 2 were waited for; matrix products, arithmetic and copies ran while one was open for 0% of the time, Pallas kernels for 1%

profile of v8, /device:TPU:2, one launch (start us, length us, event | category | flops | bytes accessed | tf_op | source)
XLA Modules:
  0.0 69.1 jit_solution(14326959526255207548)
XLA Ops:
  0.6 1.5 %shard_map.118.b0 = bf16[528,128]{1,0:T(8,128)(2,1)} custom-call(bf16[256,128]{1,0:T(8,128)(2,1)} %keys.1, bf16[256,128]{1,0:T(8,128)(2,1)} %values.1, s32[2,128]{1,0:T(2,128)} %bitcast.9), custom_call_target="tpu_custom_call" | custom-call | tf_op jit(solution)/shard_map/pallas_call | solution.py:371
  2.2 3.4 %collective-permute-start.1 = (bf16[528,128]{1,0:T(8,128)(2,1)}, bf16[528,128]{1,0:T(8,128)(2,1)S(1)}, u32[]{:S(2)}, u32[]{:S(2)}) collective-permute-start(bf16[528,128]{1,0:T(8,128)(2,1)} %shard_map.118.b0), channel_id=1, source_target_pairs={{0,16},{8,24},{16,32},{24,40},{32,48},{40,56},{48,64},{56,72},{64,... | collective-permute-start | bytes 405512 | tf_op jit(solution)/shard_map/ppermute | solution.py:33
  5.6 4.0 %collective-permute-start = (bf16[528,128]{1,0:T(8,128)(2,1)}, bf16[528,128]{1,0:T(8,128)(2,1)S(1)}, u32[]{:S(2)}, u32[]{:S(2)}) collective-permute-start(bf16[528,128]{1,0:T(8,128)(2,1)} %shard_map.118.b0), channel_id=1, source_target_pairs={{0,32},{8,40},{16,48},{24,56},{32,64},{40,72},{48,80},{56,88},{64,... | collective-permute-start | bytes 405512 | tf_op jit(solution)/shard_map/ppermute | solution.py:33
  9.6 1.3 %collective-permute-start.2 = (bf16[528,128]{1,0:T(8,128)(2,1)}, bf16[528,128]{1,0:T(8,128)(2,1)S(1)}, u32[]{:S(2)}, u32[]{:S(2)}) collective-permute-start(bf16[528,128]{1,0:T(8,128)(2,1)} %shard_map.118.b0), channel_id=1, source_target_pairs={{0,8},{16,24},{32,40},{48,56},{64,72},{80,88},{96,104},{112,120},{... | collective-permute-start | bytes 405512 | tf_op jit(solution)/shard_map/ppermute | solution.py:381
  10.9 0.0 copy-start.3
  10.9 0.0 copy-start.4
  10.9 0.6 copy-done.3
  11.6 0.0 copy-done.4
  11.6 0.0 copy-start.1
  11.6 1.0 %copy-done.1 = bf16[256,1024]{1,0:T(8,128)(2,1)S(1)} copy-done((bf16[256,1024]{1,0:T(8,128)(2,1)S(1)}, bf16[256,1024]{1,0:T(8,128)(2,1)}, u32[]{:S(2)}) %copy-start.1) | copy-done | bytes 524312
  12.6 1.0 %copy-done.2 = bf16[256,1024]{1,0:T(8,128)(2,1)S(1)} copy-done((bf16[256,1024]{1,0:T(8,128)(2,1)S(1)}, bf16[256,1024]{1,0:T(8,128)(2,1)}, u32[]{:S(2)}) %copy-start.2) | copy-done | bytes 524312
  13.7 0.5 shard_map.119
  14.2 0.0 collective-permute-done.1.b2
  14.2 0.1 collective-permute-start.3
  14.3 0.0 collective-permute-done.b4
  14.3 1.3 %collective-permute-start.4 = (bf16[528,128]{1,0:T(8,128)(2,1)S(1)}, bf16[528,128]{1,0:T(8,128)(2,1)S(1)}, u32[]{:S(2)}, u32[]{:S(2)}) collective-permute-start(bf16[528,128]{1,0:T(8,128)(2,1)S(1)} %collective-permute-done.b4), channel_id=1, source_target_pairs={{8,0},{24,16},{40,32},{56,48},{72,64},{88,80},{104,96},{120,112},{... | collective-permute-start | bytes 405512 | tf_op jit(solution)/shard_map/ppermute | solution.py:381
  15.6 0.1 maximum_bitcast_fusion.f_ref
  15.7 0.0 collective-permute-done.2.first_swap
  15.7 1.9 %collective-permute-done.4.last_swap = bf16[528,128]{1,0:T(8,128)(2,1)S(1)} collective-permute-done((bf16[528,128]{1,0:T(8,128)(2,1)S(1)}, bf16[528,128]{1,0:T(8,128)(2,1)S(1)}, u32[]{:S(2)}, u32[]{:S(2)}) %collective-permute-start.4) | collective-permute-done | bytes 135200 | tf_op jit(solution)/shard_map/ppermute | solution.py:381
  17.6 0.0 collective-permute-done.3.middle_swap
  17.6 0.0 copy-done
  17.6 13.8 %shard_map.120 = (bf16[256,1024]{1,0:T(8,128)(2,1)}, bf16[256,1024]{1,0:T(8,128)(2,1)}, f32[512,128]{1,0:T(8,128)S(1)}, f32[512,128]{1,0:T(8,128)S(1)}, f32[512,...) custom-call(bf16[528,128]{1,0:T(8,128)(2,1)S(1)} %collective-permute-done.b4, ...), custom_call_target="tpu_custom_call" | custom-call | tf_op jit(solution)/shard_map/pallas_call | solution.py:321
  31.4 0.2 collective-permute-start.5
  31.7 1.4 %collective-permute-done.5.swap = bf16[1040,128]{1,0:T(8,128)(2,1)S(1)} collective-permute-done((bf16[1040,128]{1,0:T(8,128)(2,1)S(1)}, bf16[1040,128]{1,0:T(8,128)(2,1)S(1)}, u32[]{:S(2)}, u32[]{:S(2)}) %collective-permute-start.5) | collective-permute-done | bytes 266272 | tf_op jit(solution)/shard_map/ppermute | solution.py:381
  33.0 0.1 shard_map.121
  33.1 3.0 %collective-permute-start.6 = (bf16[512,128]{1,0:T(8,128)(2,1)S(1)}, bf16[512,128]{1,0:T(8,128)(2,1)S(1)}, u32[]{:S(2)}, u32[]{:S(2)}) collective-permute-start(bf16[512,128]{1,0:T(8,128)(2,1)S(1)} %get-tuple-element.54), channel_id=1, source_target_pairs={{16,0},{24,8},{32,16},{40,24},{48,32},{56,40},{64,48},{72,56},{80,... | collective-permute-start | bytes 393224 | tf_op jit(solution)/shard_map/ppermute | solution.py:33
  36.2 16.0 %all_to_all.10.terms = f32[8,2,128]{2,1,0:T(2,128)S(1)} all-to-all(f32[8,2,128]{2,1,0:T(2,128)S(1)} %get-tuple-element.55), channel_id=1, replica_groups=mesh['context'=32,'tensor'=8] {'tensor'}, dimensions={0} | all-to-all | bytes 16384 | tf_op jit(solution)/shard_map/all_to_all | solution.py:457
  52.2 0.0 collective-permute-done.6.hop
  52.2 1.9 %collective-permute-start.7 = (bf16[512,128]{1,0:T(8,128)(2,1)S(1)}, bf16[512,128]{1,0:T(8,128)(2,1)S(1)}, u32[]{:S(2)}, u32[]{:S(2)}) collective-permute-start(bf16[512,128]{1,0:T(8,128)(2,1)S(1)} %get-tuple-element.56), channel_id=1, source_target_pairs={{16,0},{24,8},{32,16},{40,24},{48,32},{56,40},{64,48},{72,56},{80,... | collective-permute-start | bytes 393224 | tf_op jit(solution)/shard_map/ppermute | solution.py:33
  54.1 14.3 %all_to_all.11.terms = f32[16,2,128]{2,1,0:T(2,128)S(1)} all-to-all(f32[16,2,128]{2,1,0:T(2,128)S(1)} %get-tuple-element.57), channel_id=1, replica_groups={{0,16,32,48,64,80,96,112,128,144,160,176,192,208,224,240},{8,24,40,56,7..., dimensions={0} | all-to-all | bytes 32768 | tf_op jit(solution)/shard_map/all_to_all | solution.py:463
  68.4 0.0 collective-permute-done.7.hop
  68.4 0.7 shard_map.123
  (4 shorter events, 0.1 us)
Async XLA Ops:
  2.2 12.0 %collective-permute-start.1 = (bf16[528,128]{1,0:T(8,128)(2,1)}, bf16[528,128]{1,0:T(8,128)(2,1)S(1)}, u32[]{:S(2)}, u32[]{:S(2)}) collective-permute-start(bf16[528,128]{1,0:T(8,128)(2,1)} %shard_map.118.b0), channel_id=1, source_target_pairs={{0,16},{8,24},{16,32},{24,40},{32,48},{40,56},{48,64},{56,72},{64,... | collective-permute-start | bytes 405512 | tf_op jit(solution)/shard_map/ppermute | solution.py:33
  5.6 8.7 %collective-permute-start = (bf16[528,128]{1,0:T(8,128)(2,1)}, bf16[528,128]{1,0:T(8,128)(2,1)S(1)}, u32[]{:S(2)}, u32[]{:S(2)}) collective-permute-start(bf16[528,128]{1,0:T(8,128)(2,1)} %shard_map.118.b0), channel_id=1, source_target_pairs={{0,32},{8,40},{16,48},{24,56},{32,64},{40,72},{48,80},{56,88},{64,... | collective-permute-start | bytes 405512 | tf_op jit(solution)/shard_map/ppermute | solution.py:33
  9.6 6.1 %collective-permute-start.2 = (bf16[528,128]{1,0:T(8,128)(2,1)}, bf16[528,128]{1,0:T(8,128)(2,1)S(1)}, u32[]{:S(2)}, u32[]{:S(2)}) collective-permute-start(bf16[528,128]{1,0:T(8,128)(2,1)} %shard_map.118.b0), channel_id=1, source_target_pairs={{0,8},{16,24},{32,40},{48,56},{64,72},{80,88},{96,104},{112,120},{... | collective-permute-start | bytes 405512 | tf_op jit(solution)/shard_map/ppermute | solution.py:381
  10.9 0.7 copy-start.3
  10.9 0.7 copy-start.4
  11.6 1.0 %copy-start.1 = (bf16[256,1024]{1,0:T(8,128)(2,1)S(1)}, bf16[256,1024]{1,0:T(8,128)(2,1)}, u32[]{:S(2)}) copy-start(bf16[256,1024]{1,0:T(8,128)(2,1)} %q_ref.1) | copy-start | bytes 1572868
  12.6 1.0 %copy-start.2 = (bf16[256,1024]{1,0:T(8,128)(2,1)S(1)}, bf16[256,1024]{1,0:T(8,128)(2,1)}, u32[]{:S(2)}) copy-start(bf16[256,1024]{1,0:T(8,128)(2,1)} %d_ref.1) | copy-start | bytes 1572868
  13.7 3.9 %copy-start = (bf16[528,128]{1,0:T(8,128)(2,1)S(1)}, bf16[528,128]{1,0:T(8,128)(2,1)}, u32[]{:S(2)}) copy-start(bf16[528,128]{1,0:T(8,128)(2,1)} %shard_map.118.b0) | copy-start | bytes 405508
  14.2 3.4 %collective-permute-start.3 = (bf16[528,128]{1,0:T(8,128)(2,1)S(1)}, bf16[528,128]{1,0:T(8,128)(2,1)S(1)}, u32[]{:S(2)}, u32[]{:S(2)}) collective-permute-start(bf16[528,128]{1,0:T(8,128)(2,1)S(1)} %collective-permute-done.1.b2), channel_id=1, source_target_pairs={{0,8},{8,0},{16,24},{24,16},{32,40},{40,32},{48,56},{56,48},{64,72... | collective-permute-start | bytes 405512 | tf_op jit(solution)/shard_map/ppermute | solution.py:381
  14.3 3.2 %collective-permute-start.4 = (bf16[528,128]{1,0:T(8,128)(2,1)S(1)}, bf16[528,128]{1,0:T(8,128)(2,1)S(1)}, u32[]{:S(2)}, u32[]{:S(2)}) collective-permute-start(bf16[528,128]{1,0:T(8,128)(2,1)S(1)} %collective-permute-done.b4), channel_id=1, source_target_pairs={{8,0},{24,16},{40,32},{56,48},{72,64},{88,80},{104,96},{120,112},{... | collective-permute-start | bytes 405512 | tf_op jit(solution)/shard_map/ppermute | solution.py:381
  31.4 1.6 %collective-permute-start.5 = (bf16[1040,128]{1,0:T(8,128)(2,1)S(1)}, bf16[1040,128]{1,0:T(8,128)(2,1)S(1)}, u32[]{:S(2)}, u32[]{:S(2)}) collective-permute-start(bf16[1040,128]{1,0:T(8,128)(2,1)S(1)} %get-tuple-element.47), channel_id=1, source_target_pairs={{0,8},{8,0},{16,24},{24,16},{32,40},{40,32},{48,56},{56,48},{64,72... | collective-permute-start | bytes 798728 | tf_op jit(solution)/shard_map/ppermute | solution.py:381
  33.1 19.0 %collective-permute-start.6 = (bf16[512,128]{1,0:T(8,128)(2,1)S(1)}, bf16[512,128]{1,0:T(8,128)(2,1)S(1)}, u32[]{:S(2)}, u32[]{:S(2)}) collective-permute-start(bf16[512,128]{1,0:T(8,128)(2,1)S(1)} %get-tuple-element.54), channel_id=1, source_target_pairs={{16,0},{24,8},{32,16},{40,24},{48,32},{56,40},{64,48},{72,56},{80,... | collective-permute-start | bytes 393224 | tf_op jit(solution)/shard_map/ppermute | solution.py:33
  52.2 16.2 %collective-permute-start.7 = (bf16[512,128]{1,0:T(8,128)(2,1)S(1)}, bf16[512,128]{1,0:T(8,128)(2,1)S(1)}, u32[]{:S(2)}, u32[]{:S(2)}) collective-permute-start(bf16[512,128]{1,0:T(8,128)(2,1)S(1)} %get-tuple-element.56), channel_id=1, source_target_pairs={{16,0},{24,8},{32,16},{40,24},{48,32},{56,40},{64,48},{72,56},{80,... | collective-permute-start | bytes 393224 | tf_op jit(solution)/shard_map/ppermute | solution.py:33

commit v9 on v8

--- a/solution.py
+++ b/solution.py
@@ -17,14 +17,19 @@
 SPAN = 1152
 CHUNKS = SPAN // SUB
 WIDE = 128
+KEY_BLOCKS = (
+    [(0, SUB, 0, 256)]
+    + [(start, start + 256, 0, 512) for start in range(SUB, SPAN, 256)]
+    + [(SPAN, WINDOW, 256, 512)]
+)
 ID_ROWS = 16
 MSG = 2 * TOK + ID_ROWS
 SCALING = HEAD ** (-0.5)
 EXP2 = float(SCALING * np.log2(np.e))
 
-PIO2_A = 1.5703125
-PIO2_B = float(np.float32(np.round((np.pi / 2 - PIO2_A) * 2.0**23) / 2.0**23))
-PIO2_C = float(np.float32(np.pi / 2 - PIO2_A - PIO2_B))
+PI_A = 3.140625
+PI_B = float(np.round((np.pi - PI_A) * 2.0**23) / 2.0**23)
+PI_C = float(np.pi - PI_A - PI_B)
 
 
 def passed_along(block, axis, distance):
@@ -43,21 +48,17 @@
 
 def cos_sin(position, frequency):
     angle = position * frequency
-    turns = jnp.floor(angle * np.float32(2.0 / np.pi) + 0.5)
-    rest = ((angle - turns * PIO2_A) - turns * PIO2_B) - turns * PIO2_C
+    lane = lax.broadcasted_iota(jnp.int32, (1, HEAD), 1)
+    quarter = jnp.where(lane < HEAD // 2, 0.5, 0.0)
+    turns = jnp.floor(angle * np.float32(1.0 / np.pi) + (quarter + 0.5))
+    count = turns - quarter
+    rest = ((angle - count * PI_A) - count * PI_B) - count * PI_C
     square = rest * rest
-    sine = rest + rest * square * (
-        np.float32(-1.6666654611e-1)
-        + square * (np.float32(8.3321608736e-3) + square * np.float32(-1.9515295891e-4))
-    )
-    cosine = (1.0 - 0.5 * square) + square * square * (
-        np.float32(4.166664568298827e-2)
-        + square * (np.float32(-1.388731625493765e-3) + square * np.float32(2.443315711809948e-5))
-    )
-    lane = lax.broadcasted_iota(jnp.int32, angle.shape, 1)
-    quadrant = turns.astype(jnp.int32) + jnp.where(lane < HEAD // 2, 1, 0)
-    value = jnp.where((quadrant & 1) == 1, cosine, sine)
-    return jnp.where((quadrant & 2) == 2, -value, value)
+    series = np.float32(-1.9806614727713168e-4) + square * np.float32(2.6000534489867277e-6)
+    series = np.float32(8.333017118275166e-3) + square * series
+    series = np.float32(-1.6666656732559204e-1) + square * series
+    value = rest + rest * (square * series)
+    return jnp.where((turns.astype(jnp.int32) & 1) == 1, -value, value)
 
 
 def prepare_kernel(q_ref, d_ref, qg_ref, kg_ref, xh_ref, scale_ref, dcat, dcat_t, gains):
@@ -176,11 +177,6 @@
     dk[...] = jnp.zeros_like(dk)
     dv[...] = jnp.zeros_like(dv)
     qg_acc[...] = jnp.zeros_like(qg_acc)
-    zero = jnp.zeros((SUB, 256), jnp.bfloat16)
-    for ref in (w_ref, ds_ref):
-        for slot in range(2):
-            ref[slot, 0:SUB, 256:512] = zero
-            ref[slot, SPAN:WINDOW, 0:256] = zero
     later = jnp.where(row <= lane, 0.0, -1e30)
     later = jnp.concatenate([later, later], axis=1)
     spans = (slice(0, SPAN), slice(SUB, WINDOW))
@@ -194,9 +190,11 @@
         )
 
     def key_terms(pair, slot):
-        rows = slice(pair * 512, (pair + 1) * 512)
-        dk[...] += dot(ds_ref[slot], qhat[rows, :])
-        dv[...] += dot(w_ref[slot], dcat[rows, :])
+        for start, stop, low, high in KEY_BLOCKS:
+            keys, lanes = slice(start, stop), slice(low, high)
+            rows = slice(pair * 512 + low, pair * 512 + high)
+            dk[keys, :] += dot(ds_ref[slot, keys, lanes], qhat[rows, :])
+            dv[keys, :] += dot(w_ref[slot, keys, lanes], dcat[rows, :])
 
     for pair in range(HEADS // 2):
         slot = pair % 2
@@ -403,18 +401,15 @@
         gains_out[i] = total
 
 
-def plane_kernel(two, hop, terms, two_out, copies):
+def hop_kernel(two, hop, two_out):
     two_out[...] = (two[...] + hop[...].astype(jnp.float32)).astype(jnp.bfloat16)
-    total = sum(terms[i] for i in range(terms.shape[0]))
-    for i in range(copies.shape[0]):
-        copies[i] = total
 
 
 def last_kernel(own, hop, terms, keys, values, q_gain, k_gain):
     total = (own[...] + hop[...].astype(jnp.float32)).astype(jnp.bfloat16)
     keys[...] = total[:TOK]
     values[...] = total[TOK:]
-    gains = sum(terms[i] for i in range(terms.shape[0]))
+    gains = jnp.sum(terms[...], axis=0)
     q_gain[...] = gains[0:1]
     k_gain[...] = gains[1:2]
 
@@ -446,21 +441,23 @@
     frequency = jnp.concatenate([frequency, frequency]).reshape(1, HEAD)
     attended, query_gradient, four, two, own, swap, gains = attention(blocks, prepared, frequency)
 
-    tensor, context = lax.axis_size("tensor"), lax.axis_size("context")
+    axes = ("context", "tensor")
+    chips = lax.axis_size(axes) // 2
     block = (2 * TOK, HEAD)
     four, two, own, gains = small_call(
         chip_kernel,
-        [(block, bf16), (block, f32), (block, f32), ((tensor, 2, HEAD), f32)],
+        [(block, bf16), (block, f32), (block, f32), ((chips, 2, HEAD), f32)],
         *(swapped(swap), four, two, own, gains),
     )
     hop = passed_along(four, "context", -2)
-    gains = lax.all_to_all(gains, "tensor", 0, 0)
-    two, gains = small_call(
-        plane_kernel, [(block, bf16), ((context // 2, 2, HEAD), f32)], two, hop, gains
-    )
+    width = lax.axis_size("tensor")
+    cores = [
+        [(2 * n + core) * width + z for n in range(chips // width) for z in range(width)]
+        for core in range(2)
+    ]
+    gains = lax.all_to_all(gains, axes, 0, 0, axis_index_groups=cores)
+    (two,) = small_call(hop_kernel, [(block, bf16)], two, hop)
     hop = passed_along(two, "context", -2)
-    plane = [[2 * n + core for n in range(context // 2)] for core in range(2)]
-    gains = lax.all_to_all(gains, "context", 0, 0, axis_index_groups=plane)
     half_block = (TOK, HEAD)
     key_gradient, value_gradient, q_total, k_total = small_call(
         last_kernel,

time: 69.6 us -> 65.4 us (0.940)
  the two profiles are of different devices: /device:TPU:2 before, /device:TPU:1 now
where the time goes in v9:
time: 65.4 us; the launch traced here: 65 us
  starting transfers between devices  32.6 us (50%)
  Pallas kernels  16.6 us (25%)
  waiting for transfers between devices  12.1 us (19%)
  local copies, waits for them, and re-layouts  2.74 us (4%)
  between operations  0.75 us (1%)
    all_to_all x1, starting transfers between devices, body(): gains = lax.all_to_all(gains, axes, 0, 0, axis_index_groups=cores)  16.6 us
    pallas_call x1, Pallas kernels, attention(): pl.pallas_call(kernel, out_shape=[shape((TOK, HEADS * HEAD), bf16), shape...  13.1 us
    ppermute x4, starting transfers between devices, passed_along(): return lax.ppermute(block, axis, route)  10.9 us
    all_to_all x1, waiting for transfers between devices, body(): gains = lax.all_to_all(gains, axes, 0, 0, axis_index_groups=cores)  10.1 us
    ppermute x4, starting transfers between devices, swapped(): return lax.ppermute(block, 'context', route)  5.19 us
    unnamed x10, local copies, waits for them, and re-layouts  2.74 us
    ppermute x4, waiting for transfers between devices, swapped(): return lax.ppermute(block, 'context', route)  2.05 us
    pallas_call x1, Pallas kernels, pack(): pl.pallas_call(pack_kernel, out_shape=jax.ShapeDtypeStruct((MSG, HEAD), j...  1.54 us
  transfers between devices with their start and end apart: 9, of which 3 were waited for; matrix products, arithmetic and copies ran while one was open for 0% of the time, Pallas kernels for 1%

profile of v9, /device:TPU:1, one launch (start us, length us, event | category | flops | bytes accessed | tf_op | source)
XLA Modules:
  0.0 65.0 jit_solution(15863410675375221379)
XLA Ops:
  0.6 1.5 %shard_map.118.b0 = bf16[528,128]{1,0:T(8,128)(2,1)} custom-call(bf16[256,128]{1,0:T(8,128)(2,1)} %keys.1, bf16[256,128]{1,0:T(8,128)(2,1)} %values.1, s32[2,128]{1,0:T(2,128)} %bitcast.9), custom_call_target="tpu_custom_call" | custom-call | tf_op jit(solution)/shard_map/pallas_call | solution.py:369
  2.2 3.9 %collective-permute-start.1 = (bf16[528,128]{1,0:T(8,128)(2,1)}, bf16[528,128]{1,0:T(8,128)(2,1)S(1)}, u32[]{:S(2)}, u32[]{:S(2)}) collective-permute-start(bf16[528,128]{1,0:T(8,128)(2,1)} %shard_map.118.b0), channel_id=1, source_target_pairs={{0,16},{8,24},{16,32},{24,40},{32,48},{40,56},{48,64},{56,72},{64,... | collective-permute-start | bytes 405512 | tf_op jit(solution)/shard_map/ppermute | solution.py:38
  6.1 4.4 %collective-permute-start = (bf16[528,128]{1,0:T(8,128)(2,1)}, bf16[528,128]{1,0:T(8,128)(2,1)S(1)}, u32[]{:S(2)}, u32[]{:S(2)}) collective-permute-start(bf16[528,128]{1,0:T(8,128)(2,1)} %shard_map.118.b0), channel_id=1, source_target_pairs={{0,32},{8,40},{16,48},{24,56},{32,64},{40,72},{48,80},{56,88},{64,... | collective-permute-start | bytes 405512 | tf_op jit(solution)/shard_map/ppermute | solution.py:38
  10.5 1.3 %collective-permute-start.2 = (bf16[528,128]{1,0:T(8,128)(2,1)}, bf16[528,128]{1,0:T(8,128)(2,1)S(1)}, u32[]{:S(2)}, u32[]{:S(2)}) collective-permute-start(bf16[528,128]{1,0:T(8,128)(2,1)} %shard_map.118.b0), channel_id=1, source_target_pairs={{0,8},{16,24},{32,40},{48,56},{64,72},{80,88},{96,104},{112,120},{... | collective-permute-start | bytes 405512 | tf_op jit(solution)/shard_map/ppermute | solution.py:379
  11.8 0.0 copy-start.3
  11.8 0.0 copy-start.4
  11.8 0.6 copy-done.3
  12.4 0.0 copy-done.4
  12.5 0.0 copy-start.1
  12.5 1.0 %copy-done.1 = bf16[256,1024]{1,0:T(8,128)(2,1)S(1)} copy-done((bf16[256,1024]{1,0:T(8,128)(2,1)S(1)}, bf16[256,1024]{1,0:T(8,128)(2,1)}, u32[]{:S(2)}) %copy-start.1) | copy-done | bytes 524312
  13.5 1.0 %copy-done.2 = bf16[256,1024]{1,0:T(8,128)(2,1)S(1)} copy-done((bf16[256,1024]{1,0:T(8,128)(2,1)S(1)}, bf16[256,1024]{1,0:T(8,128)(2,1)}, u32[]{:S(2)}) %copy-start.2) | copy-done | bytes 524312
  14.6 0.5 shard_map.119
  15.1 0.0 collective-permute-done.1.b2
  15.1 1.3 %collective-permute-start.3 = (bf16[528,128]{1,0:T(8,128)(2,1)S(1)}, bf16[528,128]{1,0:T(8,128)(2,1)S(1)}, u32[]{:S(2)}, u32[]{:S(2)}) collective-permute-start(bf16[528,128]{1,0:T(8,128)(2,1)S(1)} %collective-permute-done.1.b2), channel_id=1, source_target_pairs={{0,8},{8,0},{16,24},{24,16},{32,40},{40,32},{48,56},{56,48},{64,72... | collective-permute-start | bytes 405512 | tf_op jit(solution)/shard_map/ppermute | solution.py:379
  16.4 0.0 collective-permute-done.b4
  16.4 1.9 %collective-permute-start.4 = (bf16[528,128]{1,0:T(8,128)(2,1)S(1)}, bf16[528,128]{1,0:T(8,128)(2,1)S(1)}, u32[]{:S(2)}, u32[]{:S(2)}) collective-permute-start(bf16[528,128]{1,0:T(8,128)(2,1)S(1)} %collective-permute-done.b4), channel_id=1, source_target_pairs={{8,0},{24,16},{40,32},{56,48},{72,64},{88,80},{104,96},{120,112},{... | collective-permute-start | bytes 405512 | tf_op jit(solution)/shard_map/ppermute | solution.py:379
  18.4 0.1 maximum_bitcast_fusion.f_ref
  18.4 0.0 collective-permute-done.2.first_swap
  18.4 0.9 %collective-permute-done.4.last_swap = bf16[528,128]{1,0:T(8,128)(2,1)S(1)} collective-permute-done((bf16[528,128]{1,0:T(8,128)(2,1)S(1)}, bf16[528,128]{1,0:T(8,128)(2,1)S(1)}, u32[]{:S(2)}, u32[]{:S(2)}) %collective-permute-start.4) | collective-permute-done | bytes 135200 | tf_op jit(solution)/shard_map/ppermute | solution.py:379
  19.3 0.0 collective-permute-done.3.middle_swap
  19.3 0.0 copy-done
  19.3 13.1 %shard_map.120 = (bf16[256,1024]{1,0:T(8,128)(2,1)}, bf16[256,1024]{1,0:T(8,128)(2,1)}, f32[512,128]{1,0:T(8,128)S(1)}, f32[512,128]{1,0:T(8,128)S(1)}, f32[512,...) custom-call(bf16[528,128]{1,0:T(8,128)(2,1)S(1)} %collective-permute-done.b4, ...), custom_call_target="tpu_custom_call" | custom-call | tf_op jit(solution)/shard_map/pallas_call | solution.py:319
  32.4 0.6 collective-permute-start.5
  33.1 1.2 %collective-permute-done.5.swap = bf16[1040,128]{1,0:T(8,128)(2,1)S(1)} collective-permute-done((bf16[1040,128]{1,0:T(8,128)(2,1)S(1)}, bf16[1040,128]{1,0:T(8,128)(2,1)S(1)}, u32[]{:S(2)}, u32[]{:S(2)}) %collective-permute-start.5) | collective-permute-done | bytes 266272 | tf_op jit(solution)/shard_map/ppermute | solution.py:379
  34.2 0.8 %shard_map.121 = (bf16[512,128]{1,0:T(8,128)(2,1)S(1)}, f32[512,128]{1,0:T(8,128)S(1)}, f32[512,128]{1,0:T(8,128)S(1)}, f32[128,2,128]{2,1,0:T(2,128)}) custom-call(bf16[1040,128]{1,0:T(8,128)(2,1)S(1)} %collective-permute-done.5.swap, f32[512,128]{1,0:T(8,128)S(1)} %get-tuple-element.46.four, f32[512,128]{1,0:T(8,128)S(1)} %get-tuple-element.47.two, ...), custom_call_target="tpu_custom_call" | custom-call | tf_op jit(solution)/shard_map/pallas_call | solution.py:419
  35.0 1.3 %collective-permute-start.6 = (bf16[512,128]{1,0:T(8,128)(2,1)S(1)}, bf16[512,128]{1,0:T(8,128)(2,1)S(1)}, u32[]{:S(2)}, u32[]{:S(2)}) collective-permute-start(bf16[512,128]{1,0:T(8,128)(2,1)S(1)} %get-tuple-element.52), channel_id=1, source_target_pairs={{16,0},{24,8},{32,16},{40,24},{48,32},{56,40},{64,48},{72,56},{80,... | collective-permute-start | bytes 393224 | tf_op jit(solution)/shard_map/ppermute | solution.py:38
  36.3 16.6 %all-to-all-start = ((f32[128,2,128]{2,1,0:T(2,128)}), f32[128,2,128]{2,1,0:T(2,128)S(1)}, u32[]{:S(2)}, u32[]{:S(2)}) async-start(f32[128,2,128]{2,1,0:T(2,128)} %get-tuple-element.53), calls=%async_computation | async-start | bytes 262144 | tf_op jit(solution)/shard_map/all_to_all | solution.py:458
  52.9 0.0 collective-permute-done.6.hop
  52.9 1.3 %collective-permute-start.7 = (bf16[512,128]{1,0:T(8,128)(2,1)S(1)}, bf16[512,128]{1,0:T(8,128)(2,1)S(1)}, u32[]{:S(2)}, u32[]{:S(2)}) collective-permute-start(bf16[512,128]{1,0:T(8,128)(2,1)S(1)} %shard_map.122), channel_id=1, source_target_pairs={{16,0},{24,8},{32,16},{40,24},{48,32},{56,40},{64,48},{72,56},{80,... | collective-permute-start | bytes 393224 | tf_op jit(solution)/shard_map/ppermute | solution.py:38
  54.2 10.1 %all-to-all-done.terms = f32[128,2,128]{2,1,0:T(2,128)S(1)} async-done(((f32[128,2,128]{2,1,0:T(2,128)}), f32[128,2,128]{2,1,0:T(2,128)S(1)}, u32[]{:S(2)}, u32[]{:S(2)}) %all-to-all-start) | async-done | bytes 131104 | tf_op jit(solution)/shard_map/all_to_all | solution.py:458
  64.3 0.0 collective-permute-done.7.hop
  64.3 0.7 %shard_map.123 = (bf16[256,128]{1,0:T(8,128)(2,1)}, bf16[256,128]{1,0:T(8,128)(2,1)}, f32[1,128]{1,0:T(1,128)}, f32[1,128]{1,0:T(1,128)}) custom-call(f32[512,128]{1,0:T(8,128)S(1)} %get-tuple-element.50.own, bf16[512,128]{1,0:T(8,128)(2,1)S(1)} %collective-permute-done.7.hop, f32[128,2,128]{2,1,0:T(2,128)S(1)} %all-to-all-done.terms), custom_call_target="tpu_custom_call" | custom-call | tf_op jit(solution)/shard_map/pallas_call | solution.py:419
  (4 shorter events, 0.0 us)
Async XLA Ops:
  2.2 12.9 %collective-permute-start.1 = (bf16[528,128]{1,0:T(8,128)(2,1)}, bf16[528,128]{1,0:T(8,128)(2,1)S(1)}, u32[]{:S(2)}, u32[]{:S(2)}) collective-permute-start(bf16[528,128]{1,0:T(8,128)(2,1)} %shard_map.118.b0), channel_id=1, source_target_pairs={{0,16},{8,24},{16,32},{24,40},{32,48},{40,56},{48,64},{56,72},{64,... | collective-permute-start | bytes 405512 | tf_op jit(solution)/shard_map/ppermute | solution.py:38
  6.1 10.3 %collective-permute-start = (bf16[528,128]{1,0:T(8,128)(2,1)}, bf16[528,128]{1,0:T(8,128)(2,1)S(1)}, u32[]{:S(2)}, u32[]{:S(2)}) collective-permute-start(bf16[528,128]{1,0:T(8,128)(2,1)} %shard_map.118.b0), channel_id=1, source_target_pairs={{0,32},{8,40},{16,48},{24,56},{32,64},{40,72},{48,80},{56,88},{64,... | collective-permute-start | bytes 405512 | tf_op jit(solution)/shard_map/ppermute | solution.py:38
  10.5 8.0 %collective-permute-start.2 = (bf16[528,128]{1,0:T(8,128)(2,1)}, bf16[528,128]{1,0:T(8,128)(2,1)S(1)}, u32[]{:S(2)}, u32[]{:S(2)}) collective-permute-start(bf16[528,128]{1,0:T(8,128)(2,1)} %shard_map.118.b0), channel_id=1, source_target_pairs={{0,8},{16,24},{32,40},{48,56},{64,72},{80,88},{96,104},{112,120},{... | collective-permute-start | bytes 405512 | tf_op jit(solution)/shard_map/ppermute | solution.py:379
  11.8 0.7 %copy-start.3 = (f32[128]{0:T(128)S(1)}, f32[128]{0:T(128)}, u32[]{:S(2)}) copy-start(f32[128]{0:T(128)} %param.11) | copy-start | bytes 1540
  11.8 0.7 %copy-start.4 = (f32[128]{0:T(128)S(1)}, f32[128]{0:T(128)}, u32[]{:S(2)}) copy-start(f32[128]{0:T(128)} %param.12) | copy-start | bytes 1540
  12.5 1.0 %copy-start.1 = (bf16[256,1024]{1,0:T(8,128)(2,1)S(1)}, bf16[256,1024]{1,0:T(8,128)(2,1)}, u32[]{:S(2)}) copy-start(bf16[256,1024]{1,0:T(8,128)(2,1)} %q_ref.1) | copy-start | bytes 1572868
  13.5 1.0 %copy-start.2 = (bf16[256,1024]{1,0:T(8,128)(2,1)S(1)}, bf16[256,1024]{1,0:T(8,128)(2,1)}, u32[]{:S(2)}) copy-start(bf16[256,1024]{1,0:T(8,128)(2,1)} %d_ref.1) | copy-start | bytes 1572868
  14.5 4.8 %copy-start = (bf16[528,128]{1,0:T(8,128)(2,1)S(1)}, bf16[528,128]{1,0:T(8,128)(2,1)}, u32[]{:S(2)}) copy-start(bf16[528,128]{1,0:T(8,128)(2,1)} %shard_map.118.b0) | copy-start | bytes 405508
  15.1 4.2 %collective-permute-start.3 = (bf16[528,128]{1,0:T(8,128)(2,1)S(1)}, bf16[528,128]{1,0:T(8,128)(2,1)S(1)}, u32[]{:S(2)}, u32[]{:S(2)}) collective-permute-start(bf16[528,128]{1,0:T(8,128)(2,1)S(1)} %collective-permute-done.1.b2), channel_id=1, source_target_pairs={{0,8},{8,0},{16,24},{24,16},{32,40},{40,32},{48,56},{56,48},{64,72... | collective-permute-start | bytes 405512 | tf_op jit(solution)/shard_map/ppermute | solution.py:379
  16.4 2.9 %collective-permute-start.4 = (bf16[528,128]{1,0:T(8,128)(2,1)S(1)}, bf16[528,128]{1,0:T(8,128)(2,1)S(1)}, u32[]{:S(2)}, u32[]{:S(2)}) collective-permute-start(bf16[528,128]{1,0:T(8,128)(2,1)S(1)} %collective-permute-done.b4), channel_id=1, source_target_pairs={{8,0},{24,16},{40,32},{56,48},{72,64},{88,80},{104,96},{120,112},{... | collective-permute-start | bytes 405512 | tf_op jit(solution)/shard_map/ppermute | solution.py:379
  32.4 1.8 %collective-permute-start.5 = (bf16[1040,128]{1,0:T(8,128)(2,1)S(1)}, bf16[1040,128]{1,0:T(8,128)(2,1)S(1)}, u32[]{:S(2)}, u32[]{:S(2)}) collective-permute-start(bf16[1040,128]{1,0:T(8,128)(2,1)S(1)} %get-tuple-element.45), channel_id=1, source_target_pairs={{0,8},{8,0},{16,24},{24,16},{32,40},{40,32},{48,56},{56,48},{64,72... | collective-permute-start | bytes 798728 | tf_op jit(solution)/shard_map/ppermute | solution.py:379
  35.0 17.9 %collective-permute-start.6 = (bf16[512,128]{1,0:T(8,128)(2,1)S(1)}, bf16[512,128]{1,0:T(8,128)(2,1)S(1)}, u32[]{:S(2)}, u32[]{:S(2)}) collective-permute-start(bf16[512,128]{1,0:T(8,128)(2,1)S(1)} %get-tuple-element.52), channel_id=1, source_target_pairs={{16,0},{24,8},{32,16},{40,24},{48,32},{56,40},{64,48},{72,56},{80,... | collective-permute-start | bytes 393224 | tf_op jit(solution)/shard_map/ppermute | solution.py:38
  36.3 28.0 %all-to-all-start = ((f32[128,2,128]{2,1,0:T(2,128)}), f32[128,2,128]{2,1,0:T(2,128)S(1)}, u32[]{:S(2)}, u32[]{:S(2)}) async-start(f32[128,2,128]{2,1,0:T(2,128)} %get-tuple-element.53), calls=%async_computation | async-start | bytes 262144 | tf_op jit(solution)/shard_map/all_to_all | solution.py:458
  52.9 11.4 %collective-permute-start.7 = (bf16[512,128]{1,0:T(8,128)(2,1)S(1)}, bf16[512,128]{1,0:T(8,128)(2,1)S(1)}, u32[]{:S(2)}, u32[]{:S(2)}) collective-permute-start(bf16[512,128]{1,0:T(8,128)(2,1)S(1)} %shard_map.122), channel_id=1, source_target_pairs={{16,0},{24,8},{32,16},{40,24},{48,32},{56,40},{64,48},{72,56},{80,... | collective-permute-start | bytes 393224 | tf_op jit(solution)/shard_map/ppermute | solution.py:38

commit v10 on v9

--- a/solution.py
+++ b/solution.py
@@ -16,7 +16,6 @@
 SUB = 128
 SPAN = 1152
 CHUNKS = SPAN // SUB
-WIDE = 128
 KEY_BLOCKS = (
     [(0, SUB, 0, 256)]
     + [(start, start + 256, 0, 512) for start in range(SUB, SPAN, 256)]
@@ -189,95 +188,119 @@
             pltpu.make_async_copy(gq_ref.at[:, columns], gq_hbm.at[:, columns], gq_sem.at[pair]),
         )
 
-    def key_terms(pair, slot):
+    shifts, inverses, centers = {}, {}, {}
+
+    def scores(pair, sub):
+        q = qext_t[pair, :, columns_of[sub]]
+        top = jnp.full((8, 256), -1e30, jnp.float32)
+        for start in range(0, SPAN, SUB):
+            s = dot(kext[sub * SUB + start : sub * SUB + start + SUB, :], q)
+            if start + SUB == SPAN:
+                s = s + later
+            s_ref[pair % 2, sub, start : start + SUB, :] = s
+            top = jnp.maximum(top, jnp.max(s.reshape(SUB // 8, 8, 256), axis=0))
+            yield
+        shifts[pair, sub] = jnp.max(top, axis=0, keepdims=True) * EXP2
+
+    def weights(pair, sub):
+        slot = pair % 2
+        shift = shifts[pair, sub]
+        total = jnp.zeros((8, 256), jnp.float32)
+        for c in range(CHUNKS):
+            e = jnp.exp2(s_ref[slot, sub, c * SUB : (c + 1) * SUB, :] * EXP2 - shift)
+            s_ref[slot, sub, c * SUB : (c + 1) * SUB, :] = e
+            total = total + jnp.sum(e.reshape(SUB // 8, 8, 256), axis=0)
+            yield
+        inverse = 1.0 / jnp.sum(total, axis=0, keepdims=True)
+        for c in range(CHUNKS):
+            keys = slice((sub + c) * SUB, (sub + c + 1) * SUB)
+            w = s_ref[slot, sub, c * SUB : (c + 1) * SUB, :] * inverse
+            w_ref[slot, keys, columns_of[sub]] = w.astype(jnp.bfloat16)
+            yield
+
+    def attend(pair, sub):
+        att_t = dot(v_t[:, spans[sub]], w_ref[pair % 2, spans[sub], columns_of[sub]])
+        d_t = dcat_t[pair, :, columns_of[sub]]
+        centers[pair, sub] = jnp.sum(att_t * d_t.astype(jnp.float32), axis=0, keepdims=True)
+        yield
+        tokens = slice(sub * SUB, (sub + 1) * SUB)
+        for g in range(2):
+            columns = slice(pair * 256 + g * HEAD, pair * 256 + (g + 1) * HEAD)
+            att_ref[tokens, columns] = att_t[:, g * SUB : (g + 1) * SUB].T.astype(jnp.bfloat16)
+            yield
+
+    def score_terms(pair, sub):
+        slot = pair % 2
+        d_t = dcat_t[pair, :, columns_of[sub]]
+        center = centers[pair, sub]
+        for c in range(CHUNKS):
+            keys = slice((sub + c) * SUB, (sub + c + 1) * SUB)
+            dw = dot(vwin[keys, :], d_t)
+            w = w_ref[slot, keys, columns_of[sub]].astype(jnp.float32)
+            ds_ref[slot, keys, columns_of[sub]] = (w * (dw - center)).astype(jnp.bfloat16)
+            yield
+
+    def query_terms(pair, sub):
+        dq_t = dot(khat_t[:, spans[sub]], ds_ref[pair % 2, spans[sub], columns_of[sub]]) * SCALING
+        yield
+        tokens = slice(sub * SUB, (sub + 1) * SUB)
+        window_rows = slice(REACH * TOK + sub * SUB, REACH * TOK + (sub + 1) * SUB)
+        c_q = cosine[window_rows, :]
+        s_q = sine[window_rows, :]
+        for g in range(2):
+            columns = slice(pair * 256 + g * HEAD, pair * 256 + (g + 1) * HEAD)
+            at = pair * 512 + sub * 256 + g * SUB
+            rows = slice(at, at + SUB)
+            dq = dq_t[:, g * SUB : (g + 1) * SUB].T
+            xh = xh_ref[rows, :]
+            dn = dq * c_q - half_turned(dq) * s_q
+            qg_acc[...] += jnp.sum((dn * xh).reshape(SUB // 8, 8, HEAD), axis=0)
+            dxh = dn * q_gain
+            gq = scale_ref[rows, :] * (dxh - xh * jnp.mean(dxh * xh, axis=1, keepdims=True))
+            gq_ref[tokens, columns] = gq.astype(jnp.bfloat16)
+            yield
+
+    def key_terms(pair):
         for start, stop, low, high in KEY_BLOCKS:
             keys, lanes = slice(start, stop), slice(low, high)
             rows = slice(pair * 512 + low, pair * 512 + high)
-            dk[keys, :] += dot(ds_ref[slot, keys, lanes], qhat[rows, :])
-            dv[keys, :] += dot(w_ref[slot, keys, lanes], dcat[rows, :])
-
-    for pair in range(HEADS // 2):
-        slot = pair % 2
-
-        def scores(sub):
-            q = qext_t[pair, :, columns_of[sub]]
-            top = jnp.full((8, 256), -1e30, jnp.float32)
-            for start in range(0, SPAN, WIDE):
-                s = dot(kext[sub * SUB + start : sub * SUB + start + WIDE, :], q)
-                if start + WIDE == SPAN:
-                    s = s + later
-                s_ref[slot, sub, start : start + WIDE, :] = s
-                top = jnp.maximum(top, jnp.max(s.reshape(WIDE // 8, 8, 256), axis=0))
-            return jnp.max(top, axis=0, keepdims=True) * EXP2
-
-        def exponents(sub, shift):
-            total = jnp.zeros((8, 256), jnp.float32)
-            for c in range(CHUNKS):
-                e = jnp.exp2(s_ref[slot, sub, c * SUB : (c + 1) * SUB, :] * EXP2 - shift)
-                s_ref[slot, sub, c * SUB : (c + 1) * SUB, :] = e
-                total = total + jnp.sum(e.reshape(SUB // 8, 8, 256), axis=0)
-            return 1.0 / jnp.sum(total, axis=0, keepdims=True)
-
-        def weigh(sub, inverse):
-            for c in range(CHUNKS):
-                keys = slice((sub + c) * SUB, (sub + c + 1) * SUB)
-                w = s_ref[slot, sub, c * SUB : (c + 1) * SUB, :] * inverse
-                w_ref[slot, keys, columns_of[sub]] = w.astype(jnp.bfloat16)
-
-        def attend(sub):
-            att_t = dot(v_t[:, spans[sub]], w_ref[slot, spans[sub], columns_of[sub]])
-            d_t = dcat_t[pair, :, columns_of[sub]]
-            center = jnp.sum(att_t * d_t.astype(jnp.float32), axis=0, keepdims=True)
-            tokens = slice(sub * SUB, (sub + 1) * SUB)
-            for g in range(2):
-                columns = slice(pair * 256 + g * HEAD, pair * 256 + (g + 1) * HEAD)
-                att_ref[tokens, columns] = att_t[:, g * SUB : (g + 1) * SUB].T.astype(jnp.bfloat16)
-            return center
-
-        def score_terms(sub, center):
-            d_t = dcat_t[pair, :, columns_of[sub]]
-            for start in range(0, SPAN, WIDE):
-                keys = slice(sub * SUB + start, sub * SUB + start + WIDE)
-                dw = dot(vwin[keys, :], d_t)
-                w = w_ref[slot, keys, columns_of[sub]].astype(jnp.float32)
-                ds_ref[slot, keys, columns_of[sub]] = (w * (dw - center)).astype(jnp.bfloat16)
-
-        def query_terms(sub):
-            dq_t = dot(khat_t[:, spans[sub]], ds_ref[slot, spans[sub], columns_of[sub]]) * SCALING
-            tokens = slice(sub * SUB, (sub + 1) * SUB)
-            window_rows = slice(REACH * TOK + sub * SUB, REACH * TOK + (sub + 1) * SUB)
-            c_q = cosine[window_rows, :]
-            s_q = sine[window_rows, :]
-            for g in range(2):
-                columns = slice(pair * 256 + g * HEAD, pair * 256 + (g + 1) * HEAD)
-                at = pair * 512 + sub * 256 + g * SUB
-                rows = slice(at, at + SUB)
-                dq = dq_t[:, g * SUB : (g + 1) * SUB].T
-                xh = xh_ref[rows, :]
-                dn = dq * c_q - half_turned(dq) * s_q
-                qg_acc[...] += jnp.sum((dn * xh).reshape(SUB // 8, 8, HEAD), axis=0)
-                dxh = dn * q_gain
-                gq = scale_ref[rows, :] * (dxh - xh * jnp.mean(dxh * xh, axis=1, keepdims=True))
-                gq_ref[tokens, columns] = gq.astype(jnp.bfloat16)
-
-        shift_0 = scores(0)
-        shift_1 = scores(1)
-        inverse_0 = exponents(0, shift_0)
-        if pair > 0:
-            key_terms(pair - 1, 1 - slot)
-        weigh(0, inverse_0)
-        inverse_1 = exponents(1, shift_1)
-        center_0 = attend(0)
-        score_terms(0, center_0)
-        weigh(1, inverse_1)
-        query_terms(0)
-        center_1 = attend(1)
-        score_terms(1, center_1)
-        query_terms(1)
-        for copy in copies(pair):
-            copy.start()
-
-    key_terms(HEADS // 2 - 1, 1)
+            dk[keys, :] += dot(ds_ref[pair % 2, keys, lanes], qhat[rows, :])
+            yield
+            dv[keys, :] += dot(w_ref[pair % 2, keys, lanes], dcat[rows, :])
+            yield
+
+    def in_turn(*streams):
+        for stream in streams:
+            yield from stream
+
+    def weave(first, second):
+        first, second = iter(first), iter(second)
+        done = object()
+        while True:
+            ends = [next(first, done) is done, next(second, done) is done]
+            if all(ends):
+                return
+
+    chains = [(pair, sub) for pair in range(HEADS // 2) for sub in range(2)]
+    weave(scores(*chains[0]), ())
+    for i, (pair, sub) in enumerate(chains):
+        ahead, behind = [], []
+        if i + 1 < len(chains):
+            ahead.append(scores(*chains[i + 1]))
+        if i > 0:
+            behind.append(query_terms(*chains[i - 1]))
+        if sub == 0 and pair > 0:
+            behind.append(key_terms(pair - 1))
+        weave(weights(pair, sub), in_turn(*ahead, *behind[:1]))
+        weave(attend(pair, sub), ())
+        weave(score_terms(pair, sub), in_turn(*behind[1:]))
+        if sub == 0 and pair > 0:
+            for copy in copies(pair - 1):
+                copy.start()
+    last = HEADS // 2 - 1
+    weave(query_terms(last, 1), key_terms(last))
+    for copy in copies(last):
+        copy.start()
 
     kg = jnp.zeros((8, HEAD), jnp.float32)
     outs = ((four_ref, 0), (swap_ref, 2 * TOK), (two_ref, 0), (swap_ref, 0), (own_ref, 0))
@@ -397,8 +420,7 @@
 
     split = swap[4 * TOK :, :].astype(jnp.float32)
     total = gains[...] + ((split[0:2] + split[2:4]) + split[4:6])
-    for i in range(gains_out.shape[0]):
-        gains_out[i] = total
+    gains_out[...] = jnp.concatenate([total] * (gains_out.shape[0] // 2))
 
 
 def hop_kernel(two, hop, two_out):
@@ -409,9 +431,9 @@
     total = (own[...] + hop[...].astype(jnp.float32)).astype(jnp.bfloat16)
     keys[...] = total[:TOK]
     values[...] = total[TOK:]
-    gains = jnp.sum(terms[...], axis=0)
-    q_gain[...] = gains[0:1]
-    k_gain[...] = gains[1:2]
+    gains = jnp.sum(terms[...].reshape(-1, 8, HEAD), axis=0)
+    q_gain[...] = (gains[0:1] + gains[2:3]) + (gains[4:5] + gains[6:7])
+    k_gain[...] = (gains[1:2] + gains[3:4]) + (gains[5:6] + gains[7:8])
 
 
 def small_call(kernel, out_shape, *operands):
@@ -446,7 +468,7 @@
     block = (2 * TOK, HEAD)
     four, two, own, gains = small_call(
         chip_kernel,
-        [(block, bf16), (block, f32), (block, f32), ((chips, 2, HEAD), f32)],
+        [(block, bf16), (block, f32), (block, f32), ((2 * chips, HEAD), f32)],
         *(swapped(swap), four, two, own, gains),
     )
     hop = passed_along(four, "context", -2)
@@ -455,7 +477,8 @@
         [(2 * n + core) * width + z for n in range(chips // width) for z in range(width)]
         for core in range(2)
     ]
-    gains = lax.all_to_all(gains, axes, 0, 0, axis_index_groups=cores)
+    gains = lax.all_to_all(gains.reshape(chips, 2, HEAD), axes, 0, 0, axis_index_groups=cores)
+    gains = gains.reshape(2 * chips, HEAD)
     (two,) = small_call(hop_kernel, [(block, bf16)], two, hop)
     hop = passed_along(two, "context", -2)
     half_block = (TOK, HEAD)

time: 65.4 us -> 64.5 us (0.986)
  Pallas kernels: 16.6 us -> 15.9 us
    pallas_call x1, Pallas kernels: 13.1 us -> 12.4 us  [attention(): pl.pallas_call(kernel, out_shape=[shape((TOK, HEADS * HEAD), bf16), shape...]
where the time goes in v10:
time: 64.5 us; the launch traced here: 64 us
  starting transfers between devices  32.5 us (50%)
  Pallas kernels  15.9 us (25%)
  waiting for transfers between devices  12.1 us (19%)
  local copies, waits for them, and re-layouts  2.74 us (4%)
  between operations  0.75 us (1%)
    all_to_all x1, starting transfers between devices, body(): lax.all_to_all(gains.reshape(chips, 2, HEAD), axes, 0, 0, axis_index_grou...  16.6 us
    pallas_call x1, Pallas kernels, attention(): pl.pallas_call(kernel, out_shape=[shape((TOK, HEADS * HEAD), bf16), shape...  12.4 us
    ppermute x4, starting transfers between devices, passed_along(): return lax.ppermute(block, axis, route)  10.9 us
    all_to_all x1, waiting for transfers between devices, body(): lax.all_to_all(gains.reshape(chips, 2, HEAD), axes, 0, 0, axis_index_grou...  10.1 us
    ppermute x4, starting transfers between devices, swapped(): return lax.ppermute(block, 'context', route)  5 us
    unnamed x10, local copies, waits for them, and re-layouts  2.74 us
    ppermute x4, waiting for transfers between devices, swapped(): return lax.ppermute(block, 'context', route)  2.06 us
    pallas_call x1, Pallas kernels, pack(): pl.pallas_call(pack_kernel, out_shape=jax.ShapeDtypeStruct((MSG, HEAD), j...  1.54 us
  transfers between devices with their start and end apart: 9, of which 3 were waited for; matrix products, arithmetic and copies ran while one was open for 0% of the time, Pallas kernels for 1%

profile of v10, /device:TPU:1, one launch (start us, length us, event | category | flops | bytes accessed | tf_op | source)
XLA Modules:
  0.0 64.0 jit_solution(18159934283889272172)
XLA Ops:
  0.6 1.5 %shard_map.118.b0 = bf16[528,128]{1,0:T(8,128)(2,1)} custom-call(bf16[256,128]{1,0:T(8,128)(2,1)} %keys.1, bf16[256,128]{1,0:T(8,128)(2,1)} %values.1, s32[2,128]{1,0:T(2,128)} %bitcast.12), custom_call_target="tpu_custom_call" | custom-call | tf_op jit(solution)/shard_map/pallas_call | solution.py:392
  2.2 3.9 %collective-permute-start.1 = (bf16[528,128]{1,0:T(8,128)(2,1)}, bf16[528,128]{1,0:T(8,128)(2,1)S(1)}, u32[]{:S(2)}, u32[]{:S(2)}) collective-permute-start(bf16[528,128]{1,0:T(8,128)(2,1)} %shard_map.118.b0), channel_id=1, source_target_pairs={{0,16},{8,24},{16,32},{24,40},{32,48},{40,56},{48,64},{56,72},{64,... | collective-permute-start | bytes 405512 | tf_op jit(solution)/shard_map/ppermute | solution.py:37
  6.1 4.4 %collective-permute-start = (bf16[528,128]{1,0:T(8,128)(2,1)}, bf16[528,128]{1,0:T(8,128)(2,1)S(1)}, u32[]{:S(2)}, u32[]{:S(2)}) collective-permute-start(bf16[528,128]{1,0:T(8,128)(2,1)} %shard_map.118.b0), channel_id=1, source_target_pairs={{0,32},{8,40},{16,48},{24,56},{32,64},{40,72},{48,80},{56,88},{64,... | collective-permute-start | bytes 405512 | tf_op jit(solution)/shard_map/ppermute | solution.py:37
  10.5 1.3 %collective-permute-start.2 = (bf16[528,128]{1,0:T(8,128)(2,1)}, bf16[528,128]{1,0:T(8,128)(2,1)S(1)}, u32[]{:S(2)}, u32[]{:S(2)}) collective-permute-start(bf16[528,128]{1,0:T(8,128)(2,1)} %shard_map.118.b0), channel_id=1, source_target_pairs={{0,8},{16,24},{32,40},{48,56},{64,72},{80,88},{96,104},{112,120},{... | collective-permute-start | bytes 405512 | tf_op jit(solution)/shard_map/ppermute | solution.py:402
  11.8 0.0 copy-start.3
  11.8 0.0 copy-start.4
  11.8 0.6 copy-done.3
  12.4 0.0 copy-done.4
  12.5 0.0 copy-start.1
  12.5 1.0 %copy-done.1 = bf16[256,1024]{1,0:T(8,128)(2,1)S(1)} copy-done((bf16[256,1024]{1,0:T(8,128)(2,1)S(1)}, bf16[256,1024]{1,0:T(8,128)(2,1)}, u32[]{:S(2)}) %copy-start.1) | copy-done | bytes 524312
  13.5 1.0 %copy-done.2 = bf16[256,1024]{1,0:T(8,128)(2,1)S(1)} copy-done((bf16[256,1024]{1,0:T(8,128)(2,1)S(1)}, bf16[256,1024]{1,0:T(8,128)(2,1)}, u32[]{:S(2)}) %copy-start.2) | copy-done | bytes 524312
  14.6 0.5 shard_map.119
  15.1 0.0 collective-permute-done.1.b2
  15.1 1.3 %collective-permute-start.3 = (bf16[528,128]{1,0:T(8,128)(2,1)S(1)}, bf16[528,128]{1,0:T(8,128)(2,1)S(1)}, u32[]{:S(2)}, u32[]{:S(2)}) collective-permute-start(bf16[528,128]{1,0:T(8,128)(2,1)S(1)} %collective-permute-done.1.b2), channel_id=1, source_target_pairs={{0,8},{8,0},{16,24},{24,16},{32,40},{40,32},{48,56},{56,48},{64,72... | collective-permute-start | bytes 405512 | tf_op jit(solution)/shard_map/ppermute | solution.py:402
  16.4 0.0 collective-permute-done.b4
  16.4 1.9 %collective-permute-start.4 = (bf16[528,128]{1,0:T(8,128)(2,1)S(1)}, bf16[528,128]{1,0:T(8,128)(2,1)S(1)}, u32[]{:S(2)}, u32[]{:S(2)}) collective-permute-start(bf16[528,128]{1,0:T(8,128)(2,1)S(1)} %collective-permute-done.b4), channel_id=1, source_target_pairs={{8,0},{24,16},{40,32},{56,48},{72,64},{88,80},{104,96},{120,112},{... | collective-permute-start | bytes 405512 | tf_op jit(solution)/shard_map/ppermute | solution.py:402
  18.4 0.1 maximum_bitcast_fusion.f_ref
  18.4 0.0 collective-permute-done.2.first_swap
  18.4 0.9 %collective-permute-done.4.last_swap = bf16[528,128]{1,0:T(8,128)(2,1)S(1)} collective-permute-done((bf16[528,128]{1,0:T(8,128)(2,1)S(1)}, bf16[528,128]{1,0:T(8,128)(2,1)S(1)}, u32[]{:S(2)}, u32[]{:S(2)}) %collective-permute-start.4) | collective-permute-done | bytes 135200 | tf_op jit(solution)/shard_map/ppermute | solution.py:402
  19.3 0.0 collective-permute-done.3.middle_swap
  19.3 0.0 copy-done
  19.3 12.4 %shard_map.120 = (bf16[256,1024]{1,0:T(8,128)(2,1)}, bf16[256,1024]{1,0:T(8,128)(2,1)}, f32[512,128]{1,0:T(8,128)S(1)}, f32[512,128]{1,0:T(8,128)S(1)}, f32[512,...) custom-call(bf16[528,128]{1,0:T(8,128)(2,1)S(1)} %collective-permute-done.b4, ...), custom_call_target="tpu_custom_call" | custom-call | tf_op jit(solution)/shard_map/pallas_call | solution.py:342
  31.7 0.4 collective-permute-start.5
  32.1 1.2 %collective-permute-done.5.swap = bf16[1040,128]{1,0:T(8,128)(2,1)S(1)} collective-permute-done((bf16[1040,128]{1,0:T(8,128)(2,1)S(1)}, bf16[1040,128]{1,0:T(8,128)(2,1)S(1)}, u32[]{:S(2)}, u32[]{:S(2)}) %collective-permute-start.5) | collective-permute-done | bytes 266272 | tf_op jit(solution)/shard_map/ppermute | solution.py:402
  33.3 0.8 %shard_map.121 = (bf16[512,128]{1,0:T(8,128)(2,1)S(1)}, f32[512,128]{1,0:T(8,128)S(1)}, f32[512,128]{1,0:T(8,128)S(1)}, f32[256,128]{1,0:T(8,128)}) custom-call(bf16[1040,128]{1,0:T(8,128)(2,1)S(1)} %collective-permute-done.5.swap, f32[512,128]{1,0:T(8,128)S(1)} %get-tuple-element.46.four, f32[512,128]{1,0:T(8,128)S(1)} %get-tuple-element.47.two, ...), custom_call_target="tpu_custom_call" | custom-call | tf_op jit(solution)/shard_map/pallas_call | solution.py:441
  34.1 1.3 %collective-permute-start.6 = (bf16[512,128]{1,0:T(8,128)(2,1)S(1)}, bf16[512,128]{1,0:T(8,128)(2,1)S(1)}, u32[]{:S(2)}, u32[]{:S(2)}) collective-permute-start(bf16[512,128]{1,0:T(8,128)(2,1)S(1)} %get-tuple-element.52), channel_id=1, source_target_pairs={{16,0},{24,8},{32,16},{40,24},{48,32},{56,40},{64,48},{72,56},{80,... | collective-permute-start | bytes 393224 | tf_op jit(solution)/shard_map/ppermute | solution.py:37
  35.4 16.6 %all-to-all-start = ((f32[128,2,128]{2,1,0:T(2,128)}), f32[128,2,128]{2,1,0:T(2,128)S(1)}, u32[]{:S(2)}, u32[]{:S(2)}) async-start(f32[128,2,128]{2,1,0:T(2,128)} %bitcast.4), calls=%async_computation | async-start | bytes 262144 | tf_op jit(solution)/shard_map/all_to_all | solution.py:480
  52.0 0.0 collective-permute-done.6.hop
  52.0 1.3 %collective-permute-start.7 = (bf16[512,128]{1,0:T(8,128)(2,1)S(1)}, bf16[512,128]{1,0:T(8,128)(2,1)S(1)}, u32[]{:S(2)}, u32[]{:S(2)}) collective-permute-start(bf16[512,128]{1,0:T(8,128)(2,1)S(1)} %shard_map.122), channel_id=1, source_target_pairs={{16,0},{24,8},{32,16},{40,24},{48,32},{56,40},{64,48},{72,56},{80,... | collective-permute-start | bytes 393224 | tf_op jit(solution)/shard_map/ppermute | solution.py:37
  53.3 10.1 %all-to-all-done = f32[128,2,128]{2,1,0:T(2,128)S(1)} async-done(((f32[128,2,128]{2,1,0:T(2,128)}), f32[128,2,128]{2,1,0:T(2,128)S(1)}, u32[]{:S(2)}, u32[]{:S(2)}) %all-to-all-start) | async-done | bytes 131104 | tf_op jit(solution)/shard_map/all_to_all | solution.py:480
  63.4 0.0 collective-permute-done.7.hop
  63.4 0.7 %shard_map.123 = (bf16[256,128]{1,0:T(8,128)(2,1)}, bf16[256,128]{1,0:T(8,128)(2,1)}, f32[1,128]{1,0:T(1,128)}, f32[1,128]{1,0:T(1,128)}) custom-call(f32[512,128]{1,0:T(8,128)S(1)} %get-tuple-element.50.own, bf16[512,128]{1,0:T(8,128)(2,1)S(1)} %collective-permute-done.7.hop, f32[256,128]{1,0:T(8,128)S(1)} %bitcast.9), custom_call_target="tpu_custom_call" | custom-call | tf_op jit(solution)/shard_map/pallas_call | solution.py:441
  (4 shorter events, 0.0 us)
Async XLA Ops:
  2.2 12.9 %collective-permute-start.1 = (bf16[528,128]{1,0:T(8,128)(2,1)}, bf16[528,128]{1,0:T(8,128)(2,1)S(1)}, u32[]{:S(2)}, u32[]{:S(2)}) collective-permute-start(bf16[528,128]{1,0:T(8,128)(2,1)} %shard_map.118.b0), channel_id=1, source_target_pairs={{0,16},{8,24},{16,32},{24,40},{32,48},{40,56},{48,64},{56,72},{64,... | collective-permute-start | bytes 405512 | tf_op jit(solution)/shard_map/ppermute | solution.py:37
  6.1 10.3 %collective-permute-start = (bf16[528,128]{1,0:T(8,128)(2,1)}, bf16[528,128]{1,0:T(8,128)(2,1)S(1)}, u32[]{:S(2)}, u32[]{:S(2)}) collective-permute-start(bf16[528,128]{1,0:T(8,128)(2,1)} %shard_map.118.b0), channel_id=1, source_target_pairs={{0,32},{8,40},{16,48},{24,56},{32,64},{40,72},{48,80},{56,88},{64,... | collective-permute-start | bytes 405512 | tf_op jit(solution)/shard_map/ppermute | solution.py:37
  10.5 8.0 %collective-permute-start.2 = (bf16[528,128]{1,0:T(8,128)(2,1)}, bf16[528,128]{1,0:T(8,128)(2,1)S(1)}, u32[]{:S(2)}, u32[]{:S(2)}) collective-permute-start(bf16[528,128]{1,0:T(8,128)(2,1)} %shard_map.118.b0), channel_id=1, source_target_pairs={{0,8},{16,24},{32,40},{48,56},{64,72},{80,88},{96,104},{112,120},{... | collective-permute-start | bytes 405512 | tf_op jit(solution)/shard_map/ppermute | solution.py:402
  11.8 0.7 %copy-start.3 = (f32[128]{0:T(128)S(1)}, f32[128]{0:T(128)}, u32[]{:S(2)}) copy-start(f32[128]{0:T(128)} %param.11) | copy-start | bytes 1540
  11.8 0.7 %copy-start.4 = (f32[128]{0:T(128)S(1)}, f32[128]{0:T(128)}, u32[]{:S(2)}) copy-start(f32[128]{0:T(128)} %param.12) | copy-start | bytes 1540
  12.5 1.0 %copy-start.1 = (bf16[256,1024]{1,0:T(8,128)(2,1)S(1)}, bf16[256,1024]{1,0:T(8,128)(2,1)}, u32[]{:S(2)}) copy-start(bf16[256,1024]{1,0:T(8,128)(2,1)} %q_ref.1) | copy-start | bytes 1572868
  13.5 1.0 %copy-start.2 = (bf16[256,1024]{1,0:T(8,128)(2,1)S(1)}, bf16[256,1024]{1,0:T(8,128)(2,1)}, u32[]{:S(2)}) copy-start(bf16[256,1024]{1,0:T(8,128)(2,1)} %d_ref.1) | copy-start | bytes 1572868
  14.5 4.8 %copy-start = (bf16[528,128]{1,0:T(8,128)(2,1)S(1)}, bf16[528,128]{1,0:T(8,128)(2,1)}, u32[]{:S(2)}) copy-start(bf16[528,128]{1,0:T(8,128)(2,1)} %shard_map.118.b0) | copy-start | bytes 405508
  15.1 4.2 %collective-permute-start.3 = (bf16[528,128]{1,0:T(8,128)(2,1)S(1)}, bf16[528,128]{1,0:T(8,128)(2,1)S(1)}, u32[]{:S(2)}, u32[]{:S(2)}) collective-permute-start(bf16[528,128]{1,0:T(8,128)(2,1)S(1)} %collective-permute-done.1.b2), channel_id=1, source_target_pairs={{0,8},{8,0},{16,24},{24,16},{32,40},{40,32},{48,56},{56,48},{64,72... | collective-permute-start | bytes 405512 | tf_op jit(solution)/shard_map/ppermute | solution.py:402
  16.4 2.9 %collective-permute-start.4 = (bf16[528,128]{1,0:T(8,128)(2,1)S(1)}, bf16[528,128]{1,0:T(8,128)(2,1)S(1)}, u32[]{:S(2)}, u32[]{:S(2)}) collective-permute-start(bf16[528,128]{1,0:T(8,128)(2,1)S(1)} %collective-permute-done.b4), channel_id=1, source_target_pairs={{8,0},{24,16},{40,32},{56,48},{72,64},{88,80},{104,96},{120,112},{... | collective-permute-start | bytes 405512 | tf_op jit(solution)/shard_map/ppermute | solution.py:402
  31.7 1.6 %collective-permute-start.5 = (bf16[1040,128]{1,0:T(8,128)(2,1)S(1)}, bf16[1040,128]{1,0:T(8,128)(2,1)S(1)}, u32[]{:S(2)}, u32[]{:S(2)}) collective-permute-start(bf16[1040,128]{1,0:T(8,128)(2,1)S(1)} %get-tuple-element.45), channel_id=1, source_target_pairs={{0,8},{8,0},{16,24},{24,16},{32,40},{40,32},{48,56},{56,48},{64,72... | collective-permute-start | bytes 798728 | tf_op jit(solution)/shard_map/ppermute | solution.py:402
  34.1 17.9 %collective-permute-start.6 = (bf16[512,128]{1,0:T(8,128)(2,1)S(1)}, bf16[512,128]{1,0:T(8,128)(2,1)S(1)}, u32[]{:S(2)}, u32[]{:S(2)}) collective-permute-start(bf16[512,128]{1,0:T(8,128)(2,1)S(1)} %get-tuple-element.52), channel_id=1, source_target_pairs={{16,0},{24,8},{32,16},{40,24},{48,32},{56,40},{64,48},{72,56},{80,... | collective-permute-start | bytes 393224 | tf_op jit(solution)/shard_map/ppermute | solution.py:37
  35.4 28.0 %all-to-all-start = ((f32[128,2,128]{2,1,0:T(2,128)}), f32[128,2,128]{2,1,0:T(2,128)S(1)}, u32[]{:S(2)}, u32[]{:S(2)}) async-start(f32[128,2,128]{2,1,0:T(2,128)} %bitcast.4), calls=%async_computation | async-start | bytes 262144 | tf_op jit(solution)/shard_map/all_to_all | solution.py:480
  52.0 11.4 %collective-permute-start.7 = (bf16[512,128]{1,0:T(8,128)(2,1)S(1)}, bf16[512,128]{1,0:T(8,128)(2,1)S(1)}, u32[]{:S(2)}, u32[]{:S(2)}) collective-permute-start(bf16[512,128]{1,0:T(8,128)(2,1)S(1)} %shard_map.122), channel_id=1, source_target_pairs={{16,0},{24,8},{32,16},{40,24},{48,32},{56,40},{64,48},{72,56},{80,... | collective-permute-start | bytes 393224 | tf_op jit(solution)/shard_map/ppermute | solution.py:37

commit v11 on v10

--- a/solution.py
+++ b/solution.py
@@ -16,6 +16,7 @@
 SUB = 128
 SPAN = 1152
 CHUNKS = SPAN // SUB
+FINE = 64
 KEY_BLOCKS = (
     [(0, SUB, 0, 256)]
     + [(start, start + 256, 0, 512) for start in range(SUB, SPAN, 256)]
@@ -188,7 +189,7 @@
             pltpu.make_async_copy(gq_ref.at[:, columns], gq_hbm.at[:, columns], gq_sem.at[pair]),
         )
 
-    shifts, inverses, centers = {}, {}, {}
+    shifts, inverses, centers, queries_t = {}, {}, {}, {}
 
     def scores(pair, sub):
         q = qext_t[pair, :, columns_of[sub]]
@@ -202,20 +203,24 @@
             yield
         shifts[pair, sub] = jnp.max(top, axis=0, keepdims=True) * EXP2
 
-    def weights(pair, sub):
+    def exponents(pair, sub):
         slot = pair % 2
         shift = shifts[pair, sub]
         total = jnp.zeros((8, 256), jnp.float32)
-        for c in range(CHUNKS):
-            e = jnp.exp2(s_ref[slot, sub, c * SUB : (c + 1) * SUB, :] * EXP2 - shift)
-            s_ref[slot, sub, c * SUB : (c + 1) * SUB, :] = e
-            total = total + jnp.sum(e.reshape(SUB // 8, 8, 256), axis=0)
-            yield
-        inverse = 1.0 / jnp.sum(total, axis=0, keepdims=True)
-        for c in range(CHUNKS):
-            keys = slice((sub + c) * SUB, (sub + c + 1) * SUB)
-            w = s_ref[slot, sub, c * SUB : (c + 1) * SUB, :] * inverse
-            w_ref[slot, keys, columns_of[sub]] = w.astype(jnp.bfloat16)
+        for at in range(0, SPAN, FINE):
+            rows = slice(at, at + FINE)
+            e = jnp.exp2(s_ref[slot, sub, rows, :] * EXP2 - shift)
+            s_ref[slot, sub, rows, :] = e
+            total = total + jnp.sum(e.reshape(FINE // 8, 8, 256), axis=0)
+            yield
+        inverses[pair, sub] = 1.0 / jnp.sum(total, axis=0, keepdims=True)
+
+    def weights(pair, sub):
+        inverse = inverses[pair, sub]
+        for at in range(0, SPAN, FINE):
+            w = s_ref[pair % 2, sub, at : at + FINE, :] * inverse
+            keys = slice(sub * SUB + at, sub * SUB + at + FINE)
+            w_ref[pair % 2, keys, columns_of[sub]] = w.astype(jnp.bfloat16)
             yield
 
     def attend(pair, sub):
@@ -240,9 +245,13 @@
             ds_ref[slot, keys, columns_of[sub]] = (w * (dw - center)).astype(jnp.bfloat16)
             yield
 
+    def query_sums(pair, sub):
+        dq_t = dot(khat_t[:, spans[sub]], ds_ref[pair % 2, spans[sub], columns_of[sub]])
+        queries_t[pair, sub] = dq_t * SCALING
+        yield
+
     def query_terms(pair, sub):
-        dq_t = dot(khat_t[:, spans[sub]], ds_ref[pair % 2, spans[sub], columns_of[sub]]) * SCALING
-        yield
+        dq_t = queries_t[pair, sub]
         tokens = slice(sub * SUB, (sub + 1) * SUB)
         window_rows = slice(REACH * TOK + sub * SUB, REACH * TOK + (sub + 1) * SUB)
         c_q = cosine[window_rows, :]
@@ -269,42 +278,41 @@
             dv[keys, :] += dot(w_ref[pair % 2, keys, lanes], dcat[rows, :])
             yield
 
-    def in_turn(*streams):
-        for stream in streams:
-            yield from stream
-
-    def weave(first, second):
-        first, second = iter(first), iter(second)
-        done = object()
-        while True:
-            ends = [next(first, done) is done, next(second, done) is done]
-            if all(ends):
+    def first_of(stream, count):
+        for _ in range(count):
+            if next(stream, stop) is stop:
                 return
-
+            yield
+
+    def weave(*streams):
+        streams = [iter(stream) for stream in streams]
+        while streams:
+            streams = [stream for stream in streams if next(stream, stop) is not stop]
+
+    stop = object()
     chains = [(pair, sub) for pair in range(HEADS // 2) for sub in range(2)]
-    weave(scores(*chains[0]), ())
+    keys_before = iter(())
+    weave(scores(*chains[0]))
     for i, (pair, sub) in enumerate(chains):
-        ahead, behind = [], []
-        if i + 1 < len(chains):
-            ahead.append(scores(*chains[i + 1]))
-        if i > 0:
-            behind.append(query_terms(*chains[i - 1]))
         if sub == 0 and pair > 0:
-            behind.append(key_terms(pair - 1))
-        weave(weights(pair, sub), in_turn(*ahead, *behind[:1]))
-        weave(attend(pair, sub), ())
-        weave(score_terms(pair, sub), in_turn(*behind[1:]))
+            keys_before = key_terms(pair - 1)
+        ahead = [scores(*chains[i + 1])] if i + 1 < len(chains) else []
+        weave(exponents(pair, sub), *ahead)
+        behind = [query_sums(*chains[i - 1])] if i > 0 else []
+        weave(weights(pair, sub), *behind, first_of(keys_before, 3))
+        behind = [query_terms(*chains[i - 1])] if i > 0 else []
+        weave(attend(pair, sub), *behind)
+        weave(score_terms(pair, sub), first_of(keys_before, 3))
         if sub == 0 and pair > 0:
             for copy in copies(pair - 1):
                 copy.start()
     last = HEADS // 2 - 1
-    weave(query_terms(last, 1), key_terms(last))
-    for copy in copies(last):
-        copy.start()
-
-    kg = jnp.zeros((8, HEAD), jnp.float32)
+    weave(query_sums(last, 1))
+
     outs = ((four_ref, 0), (swap_ref, 2 * TOK), (two_ref, 0), (swap_ref, 0), (own_ref, 0))
-    for j in range(parts):
+    k_sums = [jnp.zeros((8, HEAD), jnp.float32)]
+
+    def key_ends(j):
         rows = slice(j * SUB, (j + 1) * SUB)
         here = slice((j % 2) * SUB, (j % 2 + 1) * SUB)
         x = blocks[j // 2][here, :].astype(jnp.float32)
@@ -312,13 +320,29 @@
         xh = x * r
         d = dk[rows, :] * SCALING
         dn = d * cosine[rows, :] - half_turned(d) * sine[rows, :]
-        kg = kg + jnp.sum((dn * xh).reshape(SUB // 8, 8, HEAD), axis=0)
+        k_sums[0] = k_sums[0] + jnp.sum((dn * xh).reshape(SUB // 8, 8, HEAD), axis=0)
         dxh = dn * k_gain
         gk = r * (dxh - xh * jnp.mean(dxh * xh, axis=1, keepdims=True))
         out, at = outs[j // 2]
         at = at + (j % 2) * SUB
         out[at : at + SUB, :] = gk.astype(out.dtype)
         out[at + TOK : at + TOK + SUB, :] = dv[rows, :].astype(out.dtype)
+
+    def all_key_ends():
+        yield
+        yield
+        yield
+        key_ends(0)
+        yield
+        for j in range(1, parts - 1):
+            key_ends(j)
+            yield
+
+    weave(key_terms(last), all_key_ends(), query_terms(last, 1))
+    key_ends(parts - 1)
+    for copy in copies(last):
+        copy.start()
+    kg = k_sums[0]
     gains = jnp.concatenate(
         [jnp.sum(qg_acc[...], axis=0, keepdims=True), jnp.sum(kg, axis=0, keepdims=True)]
     )
@@ -378,22 +402,30 @@
     )(*blocks, *prepared, frequency)
 
 
-def pack_kernel(keys, values, ids, out):
-    out[0:TOK, :] = keys[...]
-    out[TOK : 2 * TOK, :] = values[...]
+def pack_kernel(keys, values, ids, out, marks, sems):
+    parts = ((keys, 0, TOK), (values, TOK, TOK), (marks, 2 * TOK, ID_ROWS))
+    moves = [
+        pltpu.make_async_copy(part, out.at[pl.ds(at, size)], sems.at[i])
+        for i, (part, at, size) in enumerate(parts)
+    ]
+    moves[0].start()
+    moves[1].start()
     marked = (ids[...] + 1).astype(jnp.float32)
-    out[2 * TOK :, :] = jnp.concatenate(
-        [marked, jnp.zeros((ID_ROWS - 2, HEAD), jnp.float32)]
-    ).astype(jnp.bfloat16)
+    rest = jnp.zeros((ID_ROWS - 2, HEAD), jnp.float32)
+    marks[...] = jnp.concatenate([marked, rest]).astype(jnp.bfloat16)
+    moves[2].start()
+    for move in moves:
+        move.wait()
 
 
 def pack(keys, values, ids):
-    vmem = pl.BlockSpec(memory_space=pltpu.VMEM)
+    anywhere = pl.BlockSpec(memory_space=pl.ANY)
     return pl.pallas_call(
         pack_kernel,
         out_shape=jax.ShapeDtypeStruct((MSG, HEAD), jnp.bfloat16),
-        in_specs=[vmem] * 3,
-        out_specs=vmem,
+        in_specs=[anywhere, anywhere, pl.BlockSpec(memory_space=pltpu.VMEM)],
+        out_specs=anywhere,
+        scratch_shapes=[pltpu.VMEM((ID_ROWS, HEAD), jnp.bfloat16), pltpu.SemaphoreType.DMA((3,))],
     )(keys, values, ids)
 
 

time: 64.5 us -> 68.5 us (1.062)
  Pallas kernels: 15.9 us -> 19.9 us
    pallas_call x1, Pallas kernels: 1.54 us -> 5.78 us  [pack(): pl.pallas_call(pack_kernel, out_shape=jax.ShapeDtypeStruct((MSG, HEAD), j...]
where the time goes in v11:
time: 68.5 us; the launch traced here: 68.1 us
  starting transfers between devices  32.5 us (47%)
  Pallas kernels  19.9 us (29%)
  waiting for transfers between devices  12.1 us (18%)
  local copies, waits for them, and re-layouts  2.74 us (4%)
  between operations  0.76 us (1%)
    all_to_all x1, starting transfers between devices, body(): lax.all_to_all(gains.reshape(chips, 2, HEAD), axes, 0, 0, axis_index_grou...  16.6 us
    pallas_call x1, Pallas kernels, attention(): pl.pallas_call(kernel, out_shape=[shape((TOK, HEADS * HEAD), bf16), shape...  12.2 us
    ppermute x4, starting transfers between devices, passed_along(): return lax.ppermute(block, axis, route)  10.9 us
    all_to_all x1, waiting for transfers between devices, body(): lax.all_to_all(gains.reshape(chips, 2, HEAD), axes, 0, 0, axis_index_grou...  10.1 us
    pallas_call x1, Pallas kernels, pack(): pl.pallas_call(pack_kernel, out_shape=jax.ShapeDtypeStruct((MSG, HEAD), j...  5.78 us
    ppermute x4, starting transfers between devices, swapped(): return lax.ppermute(block, 'context', route)  5 us
    unnamed x10, local copies, waits for them, and re-layouts  2.74 us
    ppermute x4, waiting for transfers between devices, swapped(): return lax.ppermute(block, 'context', route)  2.06 us
  transfers between devices with their start and end apart: 9, of which 3 were waited for; matrix products, arithmetic and copies ran while one was open for 0% of the time, Pallas kernels for 1%

profile of v11, /device:TPU:1, one launch (start us, length us, event | category | flops | bytes accessed | tf_op | source)
XLA Modules:
  0.0 68.1 jit_solution(10801347152191573058)
XLA Ops:
  0.6 5.8 %shard_map.118.b0 = bf16[528,128]{1,0:T(8,128)(2,1)} custom-call(bf16[256,128]{1,0:T(8,128)(2,1)} %keys.1, bf16[256,128]{1,0:T(8,128)(2,1)} %values.1, s32[2,128]{1,0:T(2,128)} %bitcast.12), custom_call_target="tpu_custom_call" | custom-call | tf_op jit(solution)/shard_map/pallas_call | solution.py:423
  6.4 4.0 %collective-permute-start.1 = (bf16[528,128]{1,0:T(8,128)(2,1)}, bf16[528,128]{1,0:T(8,128)(2,1)S(1)}, u32[]{:S(2)}, u32[]{:S(2)}) collective-permute-start(bf16[528,128]{1,0:T(8,128)(2,1)} %shard_map.118.b0), channel_id=1, source_target_pairs={{0,16},{8,24},{16,32},{24,40},{32,48},{40,56},{48,64},{56,72},{64,... | collective-permute-start | bytes 405512 | tf_op jit(solution)/shard_map/ppermute | solution.py:38
  10.4 4.4 %collective-permute-start = (bf16[528,128]{1,0:T(8,128)(2,1)}, bf16[528,128]{1,0:T(8,128)(2,1)S(1)}, u32[]{:S(2)}, u32[]{:S(2)}) collective-permute-start(bf16[528,128]{1,0:T(8,128)(2,1)} %shard_map.118.b0), channel_id=1, source_target_pairs={{0,32},{8,40},{16,48},{24,56},{32,64},{40,72},{48,80},{56,88},{64,... | collective-permute-start | bytes 405512 | tf_op jit(solution)/shard_map/ppermute | solution.py:38
  14.7 1.3 %collective-permute-start.2 = (bf16[528,128]{1,0:T(8,128)(2,1)}, bf16[528,128]{1,0:T(8,128)(2,1)S(1)}, u32[]{:S(2)}, u32[]{:S(2)}) collective-permute-start(bf16[528,128]{1,0:T(8,128)(2,1)} %shard_map.118.b0), channel_id=1, source_target_pairs={{0,8},{16,24},{32,40},{48,56},{64,72},{80,88},{96,104},{112,120},{... | collective-permute-start | bytes 405512 | tf_op jit(solution)/shard_map/ppermute | solution.py:434
  16.0 0.0 copy-start.3
  16.1 0.0 copy-start.4
  16.1 0.6 copy-done.3
  16.7 0.0 copy-done.4
  16.7 0.0 copy-start.1
  16.7 1.0 %copy-done.1 = bf16[256,1024]{1,0:T(8,128)(2,1)S(1)} copy-done((bf16[256,1024]{1,0:T(8,128)(2,1)S(1)}, bf16[256,1024]{1,0:T(8,128)(2,1)}, u32[]{:S(2)}) %copy-start.1) | copy-done | bytes 524312
  17.8 1.0 %copy-done.2 = bf16[256,1024]{1,0:T(8,128)(2,1)S(1)} copy-done((bf16[256,1024]{1,0:T(8,128)(2,1)S(1)}, bf16[256,1024]{1,0:T(8,128)(2,1)}, u32[]{:S(2)}) %copy-start.2) | copy-done | bytes 524312
  18.8 0.5 shard_map.119
  19.3 0.0 collective-permute-done.1.b2
  19.3 1.3 %collective-permute-start.3 = (bf16[528,128]{1,0:T(8,128)(2,1)S(1)}, bf16[528,128]{1,0:T(8,128)(2,1)S(1)}, u32[]{:S(2)}, u32[]{:S(2)}) collective-permute-start(bf16[528,128]{1,0:T(8,128)(2,1)S(1)} %collective-permute-done.1.b2), channel_id=1, source_target_pairs={{0,8},{8,0},{16,24},{24,16},{32,40},{40,32},{48,56},{56,48},{64,72... | collective-permute-start | bytes 405512 | tf_op jit(solution)/shard_map/ppermute | solution.py:434
  20.7 0.0 collective-permute-done.b4
  20.7 1.9 %collective-permute-start.4 = (bf16[528,128]{1,0:T(8,128)(2,1)S(1)}, bf16[528,128]{1,0:T(8,128)(2,1)S(1)}, u32[]{:S(2)}, u32[]{:S(2)}) collective-permute-start(bf16[528,128]{1,0:T(8,128)(2,1)S(1)} %collective-permute-done.b4), channel_id=1, source_target_pairs={{8,0},{24,16},{40,32},{56,48},{72,64},{88,80},{104,96},{120,112},{... | collective-permute-start | bytes 405512 | tf_op jit(solution)/shard_map/ppermute | solution.py:434
  22.6 0.1 maximum_bitcast_fusion.f_ref
  22.7 0.0 collective-permute-done.2.first_swap
  22.7 0.9 %collective-permute-done.4.last_swap = bf16[528,128]{1,0:T(8,128)(2,1)S(1)} collective-permute-done((bf16[528,128]{1,0:T(8,128)(2,1)S(1)}, bf16[528,128]{1,0:T(8,128)(2,1)S(1)}, u32[]{:S(2)}, u32[]{:S(2)}) %collective-permute-start.4) | collective-permute-done | bytes 135200 | tf_op jit(solution)/shard_map/ppermute | solution.py:434
  23.6 0.0 collective-permute-done.3.middle_swap
  23.6 0.0 copy-done
  23.6 12.2 %shard_map.120 = (bf16[256,1024]{1,0:T(8,128)(2,1)}, bf16[256,1024]{1,0:T(8,128)(2,1)}, f32[512,128]{1,0:T(8,128)S(1)}, f32[512,128]{1,0:T(8,128)S(1)}, f32[512,...) custom-call(bf16[528,128]{1,0:T(8,128)(2,1)S(1)} %collective-permute-done.b4, ...), custom_call_target="tpu_custom_call" | custom-call | tf_op jit(solution)/shard_map/pallas_call | solution.py:366
  35.8 0.4 collective-permute-start.5
  36.2 1.2 %collective-permute-done.5.swap = bf16[1040,128]{1,0:T(8,128)(2,1)S(1)} collective-permute-done((bf16[1040,128]{1,0:T(8,128)(2,1)S(1)}, bf16[1040,128]{1,0:T(8,128)(2,1)S(1)}, u32[]{:S(2)}, u32[]{:S(2)}) %collective-permute-start.5) | collective-permute-done | bytes 266272 | tf_op jit(solution)/shard_map/ppermute | solution.py:434
  37.4 0.8 %shard_map.121 = (bf16[512,128]{1,0:T(8,128)(2,1)S(1)}, f32[512,128]{1,0:T(8,128)S(1)}, f32[512,128]{1,0:T(8,128)S(1)}, f32[256,128]{1,0:T(8,128)}) custom-call(bf16[1040,128]{1,0:T(8,128)(2,1)S(1)} %collective-permute-done.5.swap, f32[512,128]{1,0:T(8,128)S(1)} %get-tuple-element.46.four, f32[512,128]{1,0:T(8,128)S(1)} %get-tuple-element.47.two, ...), custom_call_target="tpu_custom_call" | custom-call | tf_op jit(solution)/shard_map/pallas_call | solution.py:473
  38.2 1.3 %collective-permute-start.6 = (bf16[512,128]{1,0:T(8,128)(2,1)S(1)}, bf16[512,128]{1,0:T(8,128)(2,1)S(1)}, u32[]{:S(2)}, u32[]{:S(2)}) collective-permute-start(bf16[512,128]{1,0:T(8,128)(2,1)S(1)} %get-tuple-element.52), channel_id=1, source_target_pairs={{16,0},{24,8},{32,16},{40,24},{48,32},{56,40},{64,48},{72,56},{80,... | collective-permute-start | bytes 393224 | tf_op jit(solution)/shard_map/ppermute | solution.py:38
  39.5 16.6 %all-to-all-start = ((f32[128,2,128]{2,1,0:T(2,128)}), f32[128,2,128]{2,1,0:T(2,128)S(1)}, u32[]{:S(2)}, u32[]{:S(2)}) async-start(f32[128,2,128]{2,1,0:T(2,128)} %bitcast.4), calls=%async_computation | async-start | bytes 262144 | tf_op jit(solution)/shard_map/all_to_all | solution.py:512
  56.0 0.0 collective-permute-done.6.hop
  56.1 1.3 %collective-permute-start.7 = (bf16[512,128]{1,0:T(8,128)(2,1)S(1)}, bf16[512,128]{1,0:T(8,128)(2,1)S(1)}, u32[]{:S(2)}, u32[]{:S(2)}) collective-permute-start(bf16[512,128]{1,0:T(8,128)(2,1)S(1)} %shard_map.122), channel_id=1, source_target_pairs={{16,0},{24,8},{32,16},{40,24},{48,32},{56,40},{64,48},{72,56},{80,... | collective-permute-start | bytes 393224 | tf_op jit(solution)/shard_map/ppermute | solution.py:38
  57.4 10.1 %all-to-all-done = f32[128,2,128]{2,1,0:T(2,128)S(1)} async-done(((f32[128,2,128]{2,1,0:T(2,128)}), f32[128,2,128]{2,1,0:T(2,128)S(1)}, u32[]{:S(2)}, u32[]{:S(2)}) %all-to-all-start) | async-done | bytes 131104 | tf_op jit(solution)/shard_map/all_to_all | solution.py:512
  67.4 0.0 collective-permute-done.7.hop
  67.4 0.7 shard_map.123
  (4 shorter events, 0.0 us)
Async XLA Ops:
  6.4 12.9 %collective-permute-start.1 = (bf16[528,128]{1,0:T(8,128)(2,1)}, bf16[528,128]{1,0:T(8,128)(2,1)S(1)}, u32[]{:S(2)}, u32[]{:S(2)}) collective-permute-start(bf16[528,128]{1,0:T(8,128)(2,1)} %shard_map.118.b0), channel_id=1, source_target_pairs={{0,16},{8,24},{16,32},{24,40},{32,48},{40,56},{48,64},{56,72},{64,... | collective-permute-start | bytes 405512 | tf_op jit(solution)/shard_map/ppermute | solution.py:38
  10.4 10.3 %collective-permute-start = (bf16[528,128]{1,0:T(8,128)(2,1)}, bf16[528,128]{1,0:T(8,128)(2,1)S(1)}, u32[]{:S(2)}, u32[]{:S(2)}) collective-permute-start(bf16[528,128]{1,0:T(8,128)(2,1)} %shard_map.118.b0), channel_id=1, source_target_pairs={{0,32},{8,40},{16,48},{24,56},{32,64},{40,72},{48,80},{56,88},{64,... | collective-permute-start | bytes 405512 | tf_op jit(solution)/shard_map/ppermute | solution.py:38
  14.7 8.0 %collective-permute-start.2 = (bf16[528,128]{1,0:T(8,128)(2,1)}, bf16[528,128]{1,0:T(8,128)(2,1)S(1)}, u32[]{:S(2)}, u32[]{:S(2)}) collective-permute-start(bf16[528,128]{1,0:T(8,128)(2,1)} %shard_map.118.b0), channel_id=1, source_target_pairs={{0,8},{16,24},{32,40},{48,56},{64,72},{80,88},{96,104},{112,120},{... | collective-permute-start | bytes 405512 | tf_op jit(solution)/shard_map/ppermute | solution.py:434
  16.0 0.7 copy-start.3
  16.1 0.7 copy-start.4
  16.7 1.0 %copy-start.1 = (bf16[256,1024]{1,0:T(8,128)(2,1)S(1)}, bf16[256,1024]{1,0:T(8,128)(2,1)}, u32[]{:S(2)}) copy-start(bf16[256,1024]{1,0:T(8,128)(2,1)} %q_ref.1) | copy-start | bytes 1572868
  17.8 1.0 %copy-start.2 = (bf16[256,1024]{1,0:T(8,128)(2,1)S(1)}, bf16[256,1024]{1,0:T(8,128)(2,1)}, u32[]{:S(2)}) copy-start(bf16[256,1024]{1,0:T(8,128)(2,1)} %d_ref.1) | copy-start | bytes 1572868
  18.8 4.8 %copy-start = (bf16[528,128]{1,0:T(8,128)(2,1)S(1)}, bf16[528,128]{1,0:T(8,128)(2,1)}, u32[]{:S(2)}) copy-start(bf16[528,128]{1,0:T(8,128)(2,1)} %shard_map.118.b0) | copy-start | bytes 405508
  19.3 4.2 %collective-permute-start.3 = (bf16[528,128]{1,0:T(8,128)(2,1)S(1)}, bf16[528,128]{1,0:T(8,128)(2,1)S(1)}, u32[]{:S(2)}, u32[]{:S(2)}) collective-permute-start(bf16[528,128]{1,0:T(8,128)(2,1)S(1)} %collective-permute-done.1.b2), channel_id=1, source_target_pairs={{0,8},{8,0},{16,24},{24,16},{32,40},{40,32},{48,56},{56,48},{64,72... | collective-permute-start | bytes 405512 | tf_op jit(solution)/shard_map/ppermute | solution.py:434
  20.7 2.9 %collective-permute-start.4 = (bf16[528,128]{1,0:T(8,128)(2,1)S(1)}, bf16[528,128]{1,0:T(8,128)(2,1)S(1)}, u32[]{:S(2)}, u32[]{:S(2)}) collective-permute-start(bf16[528,128]{1,0:T(8,128)(2,1)S(1)} %collective-permute-done.b4), channel_id=1, source_target_pairs={{8,0},{24,16},{40,32},{56,48},{72,64},{88,80},{104,96},{120,112},{... | collective-permute-start | bytes 405512 | tf_op jit(solution)/shard_map/ppermute | solution.py:434
  35.8 1.6 %collective-permute-start.5 = (bf16[1040,128]{1,0:T(8,128)(2,1)S(1)}, bf16[1040,128]{1,0:T(8,128)(2,1)S(1)}, u32[]{:S(2)}, u32[]{:S(2)}) collective-permute-start(bf16[1040,128]{1,0:T(8,128)(2,1)S(1)} %get-tuple-element.45), channel_id=1, source_target_pairs={{0,8},{8,0},{16,24},{24,16},{32,40},{40,32},{48,56},{56,48},{64,72... | collective-permute-start | bytes 798728 | tf_op jit(solution)/shard_map/ppermute | solution.py:434
  38.2 17.9 %collective-permute-start.6 = (bf16[512,128]{1,0:T(8,128)(2,1)S(1)}, bf16[512,128]{1,0:T(8,128)(2,1)S(1)}, u32[]{:S(2)}, u32[]{:S(2)}) collective-permute-start(bf16[512,128]{1,0:T(8,128)(2,1)S(1)} %get-tuple-element.52), channel_id=1, source_target_pairs={{16,0},{24,8},{32,16},{40,24},{48,32},{56,40},{64,48},{72,56},{80,... | collective-permute-start | bytes 393224 | tf_op jit(solution)/shard_map/ppermute | solution.py:38
  39.5 28.0 %all-to-all-start = ((f32[128,2,128]{2,1,0:T(2,128)}), f32[128,2,128]{2,1,0:T(2,128)S(1)}, u32[]{:S(2)}, u32[]{:S(2)}) async-start(f32[128,2,128]{2,1,0:T(2,128)} %bitcast.4), calls=%async_computation | async-start | bytes 262144 | tf_op jit(solution)/shard_map/all_to_all | solution.py:512
  56.1 11.4 %collective-permute-start.7 = (bf16[512,128]{1,0:T(8,128)(2,1)S(1)}, bf16[512,128]{1,0:T(8,128)(2,1)S(1)}, u32[]{:S(2)}, u32[]{:S(2)}) collective-permute-start(bf16[512,128]{1,0:T(8,128)(2,1)S(1)} %shard_map.122), channel_id=1, source_target_pairs={{16,0},{24,8},{32,16},{40,24},{48,32},{56,40},{64,48},{72,56},{80,... | collective-permute-start | bytes 393224 | tf_op jit(solution)/shard_map/ppermute | solution.py:38

commit v12 on v11

--- a/solution.py
+++ b/solution.py
@@ -346,13 +346,7 @@
     gains = jnp.concatenate(
         [jnp.sum(qg_acc[...], axis=0, keepdims=True), jnp.sum(kg, axis=0, keepdims=True)]
     )
-    gain_ref[...] = gains
-    high = gains.astype(jnp.bfloat16).astype(jnp.float32)
-    middle = (gains - high).astype(jnp.bfloat16).astype(jnp.float32)
-    low = gains - high - middle
-    swap_ref[4 * TOK :, :] = jnp.concatenate(
-        [high, middle, low, jnp.zeros((ID_ROWS - 6, HEAD), jnp.float32)]
-    ).astype(jnp.bfloat16)
+    gain_ref[...] = jnp.concatenate([gains, jnp.zeros((6, HEAD), jnp.float32)])
     for pair in range(HEADS // 2):
         for copy in copies(pair):
             copy.wait()
@@ -371,8 +365,8 @@
             shape((2 * TOK, HEAD), f32),
             shape((2 * TOK, HEAD), f32),
             shape((2 * TOK, HEAD), f32),
-            shape((4 * TOK + ID_ROWS, HEAD), bf16),
-            shape((2, HEAD), f32),
+            shape((4 * TOK, HEAD), bf16),
+            shape((8, HEAD), f32),
         ],
         in_specs=[vmem] * 12,
         out_specs=[hbm] * 2 + [vmem] * 5,
@@ -402,30 +396,22 @@
     )(*blocks, *prepared, frequency)
 
 
-def pack_kernel(keys, values, ids, out, marks, sems):
-    parts = ((keys, 0, TOK), (values, TOK, TOK), (marks, 2 * TOK, ID_ROWS))
-    moves = [
-        pltpu.make_async_copy(part, out.at[pl.ds(at, size)], sems.at[i])
-        for i, (part, at, size) in enumerate(parts)
-    ]
-    moves[0].start()
-    moves[1].start()
+def pack_kernel(keys, values, ids, out):
+    out[0:TOK, :] = keys[...]
+    out[TOK : 2 * TOK, :] = values[...]
     marked = (ids[...] + 1).astype(jnp.float32)
-    rest = jnp.zeros((ID_ROWS - 2, HEAD), jnp.float32)
-    marks[...] = jnp.concatenate([marked, rest]).astype(jnp.bfloat16)
-    moves[2].start()
-    for move in moves:
-        move.wait()
+    out[2 * TOK :, :] = jnp.concatenate(
+        [marked, jnp.zeros((ID_ROWS - 2, HEAD), jnp.float32)]
+    ).astype(jnp.bfloat16)
 
 
 def pack(keys, values, ids):
-    anywhere = pl.BlockSpec(memory_space=pl.ANY)
+    vmem = pl.BlockSpec(memory_space=pltpu.VMEM)
     return pl.pallas_call(
         pack_kernel,
         out_shape=jax.ShapeDtypeStruct((MSG, HEAD), jnp.bfloat16),
-        in_specs=[anywhere, anywhere, pl.BlockSpec(memory_space=pltpu.VMEM)],
-        out_specs=anywhere,
-        scratch_shapes=[pltpu.VMEM((ID_ROWS, HEAD), jnp.bfloat16), pltpu.SemaphoreType.DMA((3,))],
+        in_specs=[vmem] * 3,
+        out_specs=vmem,
     )(keys, values, ids)
 
 
@@ -434,7 +420,7 @@
     return lax.ppermute(block, "context", route)
 
 
-def chip_kernel(swap, four, two, own, gains, four_out, two_out, own_out, gains_out):
+def chip_kernel(swap, four, two, own, four_out, two_out, own_out):
     even = lax.rem(lax.axis_index("context"), 2) == 0
     one, three = slice(0, 2 * TOK), slice(2 * TOK, 4 * TOK)
 
@@ -450,10 +436,6 @@
         two_out[...] = two[...] + swap[one, :].astype(jnp.float32)
         own_out[...] = own[...]
 
-    split = swap[4 * TOK :, :].astype(jnp.float32)
-    total = gains[...] + ((split[0:2] + split[2:4]) + split[4:6])
-    gains_out[...] = jnp.concatenate([total] * (gains_out.shape[0] // 2))
-
 
 def hop_kernel(two, hop, two_out):
     two_out[...] = (two[...] + hop[...].astype(jnp.float32)).astype(jnp.bfloat16)
@@ -464,8 +446,8 @@
     keys[...] = total[:TOK]
     values[...] = total[TOK:]
     gains = jnp.sum(terms[...].reshape(-1, 8, HEAD), axis=0)
-    q_gain[...] = (gains[0:1] + gains[2:3]) + (gains[4:5] + gains[6:7])
-    k_gain[...] = (gains[1:2] + gains[3:4]) + (gains[5:6] + gains[7:8])
+    q_gain[...] = gains[0:1]
+    k_gain[...] = gains[1:2]
 
 
 def small_call(kernel, out_shape, *operands):
@@ -495,22 +477,14 @@
     frequency = jnp.concatenate([frequency, frequency]).reshape(1, HEAD)
     attended, query_gradient, four, two, own, swap, gains = attention(blocks, prepared, frequency)
 
-    axes = ("context", "tensor")
-    chips = lax.axis_size(axes) // 2
+    gains = lax.all_gather(gains, ("context", "tensor"), tiled=True)
     block = (2 * TOK, HEAD)
-    four, two, own, gains = small_call(
+    four, two, own = small_call(
         chip_kernel,
-        [(block, bf16), (block, f32), (block, f32), ((2 * chips, HEAD), f32)],
-        *(swapped(swap), four, two, own, gains),
+        [(block, bf16), (block, f32), (block, f32)],
+        *(swapped(swap), four, two, own),
     )
     hop = passed_along(four, "context", -2)
-    width = lax.axis_size("tensor")
-    cores = [
-        [(2 * n + core) * width + z for n in range(chips // width) for z in range(width)]
-        for core in range(2)
-    ]
-    gains = lax.all_to_all(gains.reshape(chips, 2, HEAD), axes, 0, 0, axis_index_groups=cores)
-    gains = gains.reshape(2 * chips, HEAD)
     (two,) = small_call(hop_kernel, [(block, bf16)], two, hop)
     hop = passed_along(two, "context", -2)
     half_block = (TOK, HEAD)

time: 68.5 us -> 153 us (2.23)
  waiting for transfers between devices: 12.1 us -> 102 us
  starting transfers between devices: 32.5 us -> 15.9 us
  between operations: 0.76 us -> 14.1 us
  Pallas kernels: 19.9 us -> 16.2 us
    all_gather x0 -> x1, waiting for transfers between devices: none -> 90.4 us  [body(): gains = lax.all_gather(gains, ('context', 'tensor'), tiled=True)]
    all_to_all x1 -> x0, starting transfers between devices: 16.6 us -> none  [body(): lax.all_to_all(gains.reshape(chips, 2, HEAD), axes, 0, 0, axis_index_grou...]
    all_to_all x1 -> x0, waiting for transfers between devices: 10.1 us -> none  [body(): lax.all_to_all(gains.reshape(chips, 2, HEAD), axes, 0, 0, axis_index_grou...]
    ppermute x4, waiting for transfers between devices: 0.01 us -> 9.72 us  [passed_along(): return lax.ppermute(block, axis, route)]
    pallas_call x1, Pallas kernels: 5.78 us -> 1.54 us  [pack(): pl.pallas_call(pack_kernel, out_shape=jax.ShapeDtypeStruct((MSG, HEAD), j...]
    unnamed x10 -> x12, local copies, waits for them, and re-layouts: 2.74 us -> 3.97 us
  transfers between devices with their start and end apart: 9 -> 9, of which waited for: 3 -> 5; matrix products, arithmetic and copies ran while one was open for 0% -> 0% of each run, Pallas kernels for 1% -> 0%
where the time goes in v12:
time: 153 us; the launch traced here: 152 us
  waiting for transfers between devices  102 us (67%)
  Pallas kernels  16.2 us (11%)
  starting transfers between devices  15.9 us (10%)
  between operations  14.1 us (9%)
  local copies, waits for them, and re-layouts  3.97 us (3%)
    all_gather x1, waiting for transfers between devices, body(): gains = lax.all_gather(gains, ('context', 'tensor'), tiled=True)  90.4 us
    pallas_call x1, Pallas kernels, attention(): pl.pallas_call(kernel, out_shape=[shape((TOK, HEADS * HEAD), bf16), shape...  13.2 us
    ppermute x4, starting transfers between devices, passed_along(): return lax.ppermute(block, axis, route)  10.9 us
    ppermute x4, waiting for transfers between devices, passed_along(): return lax.ppermute(block, axis, route)  9.72 us
    ppermute x4, starting transfers between devices, swapped(): return lax.ppermute(block, 'context', route)  5.01 us
    unnamed x12, local copies, waits for them, and re-layouts  3.97 us
  transfers between devices with their start and end apart: 9, of which 5 were waited for; matrix products, arithmetic and copies ran while one was open for 0% of the time, Pallas kernels for 0%

profile of v12, /device:TPU:1, one launch (start us, length us, event | category | flops | bytes accessed | tf_op | source)
XLA Modules:
  0.0 152.4 jit_solution(9134922134076733356)
XLA Ops:
  7.2 0.0 all-gather.2.cloned.1.call-start
  7.2 1.5 %shard_map.118.b0 = bf16[528,128]{1,0:T(8,128)(2,1)} custom-call(bf16[256,128]{1,0:T(8,128)(2,1)} %keys.1, bf16[256,128]{1,0:T(8,128)(2,1)} %values.1, s32[2,128]{1,0:T(2,128)} %bitcast.9), custom_call_target="tpu_custom_call" | custom-call | tf_op jit(solution)/shard_map/pallas_call | solution.py:410
  8.8 3.9 %collective-permute-start.1 = (bf16[528,128]{1,0:T(8,128)(2,1)}, bf16[528,128]{1,0:T(8,128)(2,1)S(1)}, u32[]{:S(2)}, u32[]{:S(2)}) collective-permute-start(bf16[528,128]{1,0:T(8,128)(2,1)} %shard_map.118.b0), channel_id=1, source_target_pairs={{0,16},{8,24},{16,32},{24,40},{32,48},{40,56},{48,64},{56,72},{64,... | collective-permute-start | bytes 405512 | tf_op jit(solution)/shard_map/ppermute | solution.py:38
  12.7 4.4 %collective-permute-start = (bf16[528,128]{1,0:T(8,128)(2,1)}, bf16[528,128]{1,0:T(8,128)(2,1)S(1)}, u32[]{:S(2)}, u32[]{:S(2)}) collective-permute-start(bf16[528,128]{1,0:T(8,128)(2,1)} %shard_map.118.b0), channel_id=1, source_target_pairs={{0,32},{8,40},{16,48},{24,56},{32,64},{40,72},{48,80},{56,88},{64,... | collective-permute-start | bytes 405512 | tf_op jit(solution)/shard_map/ppermute | solution.py:38
  17.1 1.3 collective-permute-start.2
  18.4 0.0 copy-start.4
  18.4 0.0 copy-start.5
  18.4 0.6 copy-done.4
  19.0 0.0 copy-done.5
  19.0 1.0 copy-done.2
  20.1 1.0 copy-done.3
  21.1 0.5 shard_map.119
  21.7 0.0 collective-permute-done.1.b2
  21.7 1.3 collective-permute-start.3
  23.0 0.0 collective-permute-done.b4
  23.0 1.9 %collective-permute-start.4 = (bf16[528,128]{1,0:T(8,128)(2,1)S(1)}, bf16[528,128]{1,0:T(8,128)(2,1)S(1)}, u32[]{:S(2)}, u32[]{:S(2)}) collective-permute-start(bf16[528,128]{1,0:T(8,128)(2,1)S(1)} %collective-permute-done.b4), channel_id=1, source_target_pairs={{8,0},{24,16},{40,32},{56,48},{72,64},{88,80},{104,96},{120,112},{... | collective-permute-start | bytes 405512 | tf_op jit(solution)/shard_map/ppermute | solution.py:420
  24.9 0.1 maximum_bitcast_fusion.f_ref
  25.0 0.0 collective-permute-done.2.first_swap
  25.0 0.9 collective-permute-done.4.last_swap
  25.9 0.0 collective-permute-done.3.middle_swap
  25.9 13.2 %shard_map.120 = (bf16[256,1024]{1,0:T(8,128)(2,1)}, bf16[256,1024]{1,0:T(8,128)(2,1)}, f32[512,128]{1,0:T(8,128)S(1)}, f32[512,128]{1,0:T(8,128)S(1)}, f32[512,...) custom-call(bf16[528,128]{1,0:T(8,128)(2,1)S(1)} %collective-permute-done.b4, ...), custom_call_target="tpu_custom_call" | custom-call | tf_op jit(solution)/shard_map/pallas_call | solution.py:360
  39.1 0.0 all-gather.2.cloned.1.call-update
  39.2 0.5 collective-permute-start.5
  39.6 1.2 collective-permute-done.5.swap
  40.8 0.1 shard_map.121
  40.8 1.3 collective-permute-start.6
  42.1 5.3 %collective-permute-done.6.hop = bf16[512,128]{1,0:T(8,128)(2,1)S(1)} collective-permute-done((bf16[512,128]{1,0:T(8,128)(2,1)S(1)}, bf16[512,128]{1,0:T(8,128)(2,1)S(1)}, u32[]{:S(2)}, u32[]{:S(2)}) %collective-permute-start.6) | collective-permute-done | bytes 131104 | tf_op jit(solution)/shard_map/ppermute | solution.py:38
  47.5 1.3 collective-permute-start.7
  48.8 4.4 %collective-permute-done.7.hop = bf16[512,128]{1,0:T(8,128)(2,1)S(1)} collective-permute-done((bf16[512,128]{1,0:T(8,128)(2,1)S(1)}, bf16[512,128]{1,0:T(8,128)(2,1)S(1)}, u32[]{:S(2)}, u32[]{:S(2)}) %collective-permute-start.7) | collective-permute-done | bytes 131104 | tf_op jit(solution)/shard_map/ppermute | solution.py:38
  53.2 90.4 %all-gather.2.cloned.1.call-done.terms = f32[2048,128]{1,0:T(8,128)} async-done(((f32[8,128]{1,0:T(8,128)}), f32[2048,128]{1,0:T(8,128)}) %all-gather.2.cloned.1.call-update) | async-done | bytes 1048592 | tf_op jit(solution)/shard_map/all_gather | solution.py:480
  143.6 1.2 copy-done
  144.8 0.8 shard_map.123
  (7 shorter events, 0.0 us)
Async XLA Ops:
  7.2 136.4 %all-gather.2.cloned.1.call-start = ((), (), s32[]{:S(2)}) async-start(), calls=%async_computation | async-start | bytes 1052672 | tf_op jit(solution)/shard_map/all_gather | solution.py:480
  8.8 12.9 %collective-permute-start.1 = (bf16[528,128]{1,0:T(8,128)(2,1)}, bf16[528,128]{1,0:T(8,128)(2,1)S(1)}, u32[]{:S(2)}, u32[]{:S(2)}) collective-permute-start(bf16[528,128]{1,0:T(8,128)(2,1)} %shard_map.118.b0), channel_id=1, source_target_pairs={{0,16},{8,24},{16,32},{24,40},{32,48},{40,56},{48,64},{56,72},{64,... | collective-permute-start | bytes 405512 | tf_op jit(solution)/shard_map/ppermute | solution.py:38
  12.7 10.3 %collective-permute-start = (bf16[528,128]{1,0:T(8,128)(2,1)}, bf16[528,128]{1,0:T(8,128)(2,1)S(1)}, u32[]{:S(2)}, u32[]{:S(2)}) collective-permute-start(bf16[528,128]{1,0:T(8,128)(2,1)} %shard_map.118.b0), channel_id=1, source_target_pairs={{0,32},{8,40},{16,48},{24,56},{32,64},{40,72},{48,80},{56,88},{64,... | collective-permute-start | bytes 405512 | tf_op jit(solution)/shard_map/ppermute | solution.py:38
  17.1 8.0 %collective-permute-start.2 = (bf16[528,128]{1,0:T(8,128)(2,1)}, bf16[528,128]{1,0:T(8,128)(2,1)S(1)}, u32[]{:S(2)}, u32[]{:S(2)}) collective-permute-start(bf16[528,128]{1,0:T(8,128)(2,1)} %shard_map.118.b0), channel_id=1, source_target_pairs={{0,8},{16,24},{32,40},{48,56},{64,72},{80,88},{96,104},{112,120},{... | collective-permute-start | bytes 405512 | tf_op jit(solution)/shard_map/ppermute | solution.py:420
  18.4 0.7 copy-start.4
  18.4 0.7 copy-start.5
  19.0 1.0 copy-start.2
  20.1 1.0 copy-start.3
  21.1 4.8 %copy-start.1 = (bf16[528,128]{1,0:T(8,128)(2,1)S(1)}, bf16[528,128]{1,0:T(8,128)(2,1)}, u32[]{:S(2)}) copy-start(bf16[528,128]{1,0:T(8,128)(2,1)} %shard_map.118.b0) | copy-start | bytes 405508
  21.7 4.2 %collective-permute-start.3 = (bf16[528,128]{1,0:T(8,128)(2,1)S(1)}, bf16[528,128]{1,0:T(8,128)(2,1)S(1)}, u32[]{:S(2)}, u32[]{:S(2)}) collective-permute-start(bf16[528,128]{1,0:T(8,128)(2,1)S(1)} %collective-permute-done.1.b2), channel_id=1, source_target_pairs={{0,8},{8,0},{16,24},{24,16},{32,40},{40,32},{48,56},{56,48},{64,72... | collective-permute-start | bytes 405512 | tf_op jit(solution)/shard_map/ppermute | solution.py:420
  23.0 2.9 %collective-permute-start.4 = (bf16[528,128]{1,0:T(8,128)(2,1)S(1)}, bf16[528,128]{1,0:T(8,128)(2,1)S(1)}, u32[]{:S(2)}, u32[]{:S(2)}) collective-permute-start(bf16[528,128]{1,0:T(8,128)(2,1)S(1)} %collective-permute-done.b4), channel_id=1, source_target_pairs={{8,0},{24,16},{40,32},{56,48},{72,64},{88,80},{104,96},{120,112},{... | collective-permute-start | bytes 405512 | tf_op jit(solution)/shard_map/ppermute | solution.py:420
  39.2 1.6 %collective-permute-start.5 = (bf16[1024,128]{1,0:T(8,128)(2,1)S(1)}, bf16[1024,128]{1,0:T(8,128)(2,1)S(1)}, u32[]{:S(2)}, u32[]{:S(2)}) collective-permute-start(bf16[1024,128]{1,0:T(8,128)(2,1)S(1)} %get-tuple-element.44), channel_id=1, source_target_pairs={{0,8},{8,0},{16,24},{24,16},{32,40},{40,32},{48,56},{56,48},{64,72... | collective-permute-start | bytes 786440 | tf_op jit(solution)/shard_map/ppermute | solution.py:420
  40.8 6.6 %collective-permute-start.6 = (bf16[512,128]{1,0:T(8,128)(2,1)S(1)}, bf16[512,128]{1,0:T(8,128)(2,1)S(1)}, u32[]{:S(2)}, u32[]{:S(2)}) collective-permute-start(bf16[512,128]{1,0:T(8,128)(2,1)S(1)} %get-tuple-element.50), channel_id=1, source_target_pairs={{16,0},{24,8},{32,16},{40,24},{48,32},{56,40},{64,48},{72,56},{80,... | collective-permute-start | bytes 393224 | tf_op jit(solution)/shard_map/ppermute | solution.py:38
  47.5 5.7 %collective-permute-start.7 = (bf16[512,128]{1,0:T(8,128)(2,1)S(1)}, bf16[512,128]{1,0:T(8,128)(2,1)S(1)}, u32[]{:S(2)}, u32[]{:S(2)}) collective-permute-start(bf16[512,128]{1,0:T(8,128)(2,1)S(1)} %shard_map.122), channel_id=1, source_target_pairs={{16,0},{24,8},{32,16},{40,24},{48,32},{56,40},{64,48},{72,56},{80,... | collective-permute-start | bytes 393224 | tf_op jit(solution)/shard_map/ppermute | solution.py:38
  143.6 1.2 copy-start
Sparse Core Ops, SparseCore 0:
  39.3 104.2 all-gather.1

commit v13 on v11

--- a/solution.py
+++ b/solution.py
@@ -138,7 +138,7 @@
         below = below + jnp.where(column < lane_f, 1.0, 0.0)
     first = jnp.sum(below, axis=0, keepdims=True)
 
-    for j in range(parts):
+    def key_part(j):
         rows = slice(j * SUB, (j + 1) * SUB)
         here = slice((j % 2) * SUB, (j % 2 + 1) * SUB)
         block = blocks[j // 2]
@@ -160,19 +160,19 @@
         vwin[rows, :] = values
         v_t[:, rows] = values.astype(jnp.float32).T.astype(jnp.bfloat16)
 
-    for sub in range(2):
-        window_rows = slice(REACH * TOK + sub * SUB, REACH * TOK + (sub + 1) * SUB)
-        c_q = cosine[window_rows, :]
-        s_q = sine[window_rows, :]
-        other = jnp.where(row_f == id_rows[2 * REACH + sub], 0.0, -1e30).astype(jnp.bfloat16)
-        for h in range(HEADS):
-            at = (h // 2) * 512 + sub * 256 + (h % 2) * SUB
-            lanes = slice(at % 512, at % 512 + SUB)
-            normed = xh_ref[at : at + SUB, :] * q_gain
-            hat = normed * c_q + half_turned(normed) * s_q
-            qhat[at : at + SUB, :] = hat.astype(jnp.bfloat16)
-            qext_t[h // 2, 0:HEAD, lanes] = hat.T.astype(jnp.bfloat16)
-            qext_t[h // 2, HEAD:, lanes] = other
+    def query_part(pair):
+        for sub in range(2):
+            window_rows = slice(REACH * TOK + sub * SUB, REACH * TOK + (sub + 1) * SUB)
+            other = jnp.where(row_f == id_rows[2 * REACH + sub], 0.0, -1e30).astype(jnp.bfloat16)
+            for g in range(2):
+                at = pair * 512 + sub * 256 + g * SUB
+                lanes = slice(at % 512, at % 512 + SUB)
+                normed = xh_ref[at : at + SUB, :] * q_gain
+                hat = normed * cosine[window_rows, :] + half_turned(normed) * sine[window_rows, :]
+                qhat[at : at + SUB, :] = hat.astype(jnp.bfloat16)
+                qext_t[pair, 0:HEAD, lanes] = hat.T.astype(jnp.bfloat16)
+                qext_t[pair, HEAD:, lanes] = other
+                yield
 
     dk[...] = jnp.zeros_like(dk)
     dv[...] = jnp.zeros_like(dv)
@@ -292,7 +292,16 @@
     stop = object()
     chains = [(pair, sub) for pair in range(HEADS // 2) for sub in range(2)]
     keys_before = iter(())
-    weave(scores(*chains[0]))
+
+    def first_keys():
+        for j in range(parts - 2):
+            key_part(j)
+            yield
+
+    key_part(parts - 2)
+    key_part(parts - 1)
+    weave(query_part(0))
+    weave(first_keys(), scores(*chains[0]))
     for i, (pair, sub) in enumerate(chains):
         if sub == 0 and pair > 0:
             keys_before = key_terms(pair - 1)
@@ -301,6 +310,8 @@
         behind = [query_sums(*chains[i - 1])] if i > 0 else []
         weave(weights(pair, sub), *behind, first_of(keys_before, 3))
         behind = [query_terms(*chains[i - 1])] if i > 0 else []
+        if sub == 0 and pair + 1 < HEADS // 2:
+            behind.append(query_part(pair + 1))
         weave(attend(pair, sub), *behind)
         weave(score_terms(pair, sub), first_of(keys_before, 3))
         if sub == 0 and pair > 0:
@@ -402,30 +413,22 @@
     )(*blocks, *prepared, frequency)
 
 
-def pack_kernel(keys, values, ids, out, marks, sems):
-    parts = ((keys, 0, TOK), (values, TOK, TOK), (marks, 2 * TOK, ID_ROWS))
-    moves = [
-        pltpu.make_async_copy(part, out.at[pl.ds(at, size)], sems.at[i])
-        for i, (part, at, size) in enumerate(parts)
-    ]
-    moves[0].start()
-    moves[1].start()
+def pack_kernel(keys, values, ids, out):
+    out[0:TOK, :] = keys[...]
+    out[TOK : 2 * TOK, :] = values[...]
     marked = (ids[...] + 1).astype(jnp.float32)
-    rest = jnp.zeros((ID_ROWS - 2, HEAD), jnp.float32)
-    marks[...] = jnp.concatenate([marked, rest]).astype(jnp.bfloat16)
-    moves[2].start()
-    for move in moves:
-        move.wait()
+    out[2 * TOK :, :] = jnp.concatenate(
+        [marked, jnp.zeros((ID_ROWS - 2, HEAD), jnp.float32)]
+    ).astype(jnp.bfloat16)
 
 
 def pack(keys, values, ids):
-    anywhere = pl.BlockSpec(memory_space=pl.ANY)
+    vmem = pl.BlockSpec(memory_space=pltpu.VMEM)
     return pl.pallas_call(
         pack_kernel,
         out_shape=jax.ShapeDtypeStruct((MSG, HEAD), jnp.bfloat16),
-        in_specs=[anywhere, anywhere, pl.BlockSpec(memory_space=pltpu.VMEM)],
-        out_specs=anywhere,
-        scratch_shapes=[pltpu.VMEM((ID_ROWS, HEAD), jnp.bfloat16), pltpu.SemaphoreType.DMA((3,))],
+        in_specs=[vmem] * 3,
+        out_specs=vmem,
     )(keys, values, ids)
 
 

time: 68.5 us -> 64.4 us (0.940)
  Pallas kernels: 19.9 us -> 15.8 us
    pallas_call x1, Pallas kernels: 5.78 us -> 1.54 us  [pack(): pl.pallas_call(pack_kernel, out_shape=jax.ShapeDtypeStruct((MSG, HEAD), j...]
where the time goes in v13:
time: 64.4 us; the launch traced here: 64 us
  starting transfers between devices  32.4 us (50%)
  Pallas kernels  15.8 us (25%)
  waiting for transfers between devices  12.1 us (19%)
  local copies, waits for them, and re-layouts  2.74 us (4%)
  between operations  0.75 us (1%)
    all_to_all x1, starting transfers between devices, body(): lax.all_to_all(gains.reshape(chips, 2, HEAD), axes, 0, 0, axis_index_grou...  16.6 us
    pallas_call x1, Pallas kernels, attention(): pl.pallas_call(kernel, out_shape=[shape((TOK, HEADS * HEAD), bf16), shape...  12.3 us
    ppermute x4, starting transfers between devices, passed_along(): return lax.ppermute(block, axis, route)  10.9 us
    all_to_all x1, waiting for transfers between devices, body(): lax.all_to_all(gains.reshape(chips, 2, HEAD), axes, 0, 0, axis_index_grou...  10.1 us
    ppermute x4, starting transfers between devices, swapped(): return lax.ppermute(block, 'context', route)  5 us
    unnamed x10, local copies, waits for them, and re-layouts  2.74 us
    ppermute x4, waiting for transfers between devices, swapped(): return lax.ppermute(block, 'context', route)  2.06 us
    pallas_call x1, Pallas kernels, pack(): pl.pallas_call(pack_kernel, out_shape=jax.ShapeDtypeStruct((MSG, HEAD), j...  1.54 us
  transfers between devices with their start and end apart: 9, of which 3 were waited for; matrix products, arithmetic and copies ran while one was open for 0% of the time, Pallas kernels for 1%

profile of v13, /device:TPU:1, one launch (start us, length us, event | category | flops | bytes accessed | tf_op | source)
XLA Modules:
  0.0 64.0 jit_solution(2479021524440594190)
XLA Ops:
  0.6 1.5 %shard_map.118.b0 = bf16[528,128]{1,0:T(8,128)(2,1)} custom-call(bf16[256,128]{1,0:T(8,128)(2,1)} %keys.1, bf16[256,128]{1,0:T(8,128)(2,1)} %values.1, s32[2,128]{1,0:T(2,128)} %bitcast.12), custom_call_target="tpu_custom_call" | custom-call | tf_op jit(solution)/shard_map/pallas_call | solution.py:427
  2.2 3.9 %collective-permute-start.1 = (bf16[528,128]{1,0:T(8,128)(2,1)}, bf16[528,128]{1,0:T(8,128)(2,1)S(1)}, u32[]{:S(2)}, u32[]{:S(2)}) collective-permute-start(bf16[528,128]{1,0:T(8,128)(2,1)} %shard_map.118.b0), channel_id=1, source_target_pairs={{0,16},{8,24},{16,32},{24,40},{32,48},{40,56},{48,64},{56,72},{64,... | collective-permute-start | bytes 405512 | tf_op jit(solution)/shard_map/ppermute | solution.py:38
  6.1 4.4 %collective-permute-start = (bf16[528,128]{1,0:T(8,128)(2,1)}, bf16[528,128]{1,0:T(8,128)(2,1)S(1)}, u32[]{:S(2)}, u32[]{:S(2)}) collective-permute-start(bf16[528,128]{1,0:T(8,128)(2,1)} %shard_map.118.b0), channel_id=1, source_target_pairs={{0,32},{8,40},{16,48},{24,56},{32,64},{40,72},{48,80},{56,88},{64,... | collective-permute-start | bytes 405512 | tf_op jit(solution)/shard_map/ppermute | solution.py:38
  10.5 1.3 %collective-permute-start.2 = (bf16[528,128]{1,0:T(8,128)(2,1)}, bf16[528,128]{1,0:T(8,128)(2,1)S(1)}, u32[]{:S(2)}, u32[]{:S(2)}) collective-permute-start(bf16[528,128]{1,0:T(8,128)(2,1)} %shard_map.118.b0), channel_id=1, source_target_pairs={{0,8},{16,24},{32,40},{48,56},{64,72},{80,88},{96,104},{112,120},{... | collective-permute-start | bytes 405512 | tf_op jit(solution)/shard_map/ppermute | solution.py:437
  11.8 0.0 copy-start.3
  11.8 0.0 copy-start.4
  11.8 0.6 copy-done.3
  12.4 0.0 copy-done.4
  12.5 0.0 copy-start.1
  12.5 1.0 %copy-done.1 = bf16[256,1024]{1,0:T(8,128)(2,1)S(1)} copy-done((bf16[256,1024]{1,0:T(8,128)(2,1)S(1)}, bf16[256,1024]{1,0:T(8,128)(2,1)}, u32[]{:S(2)}) %copy-start.1) | copy-done | bytes 524312
  13.5 1.0 %copy-done.2 = bf16[256,1024]{1,0:T(8,128)(2,1)S(1)} copy-done((bf16[256,1024]{1,0:T(8,128)(2,1)S(1)}, bf16[256,1024]{1,0:T(8,128)(2,1)}, u32[]{:S(2)}) %copy-start.2) | copy-done | bytes 524312
  14.6 0.5 shard_map.119
  15.1 0.0 collective-permute-done.1.b2
  15.1 1.3 %collective-permute-start.3 = (bf16[528,128]{1,0:T(8,128)(2,1)S(1)}, bf16[528,128]{1,0:T(8,128)(2,1)S(1)}, u32[]{:S(2)}, u32[]{:S(2)}) collective-permute-start(bf16[528,128]{1,0:T(8,128)(2,1)S(1)} %collective-permute-done.1.b2), channel_id=1, source_target_pairs={{0,8},{8,0},{16,24},{24,16},{32,40},{40,32},{48,56},{56,48},{64,72... | collective-permute-start | bytes 405512 | tf_op jit(solution)/shard_map/ppermute | solution.py:437
  16.4 0.0 collective-permute-done.b4
  16.4 1.9 %collective-permute-start.4 = (bf16[528,128]{1,0:T(8,128)(2,1)S(1)}, bf16[528,128]{1,0:T(8,128)(2,1)S(1)}, u32[]{:S(2)}, u32[]{:S(2)}) collective-permute-start(bf16[528,128]{1,0:T(8,128)(2,1)S(1)} %collective-permute-done.b4), channel_id=1, source_target_pairs={{8,0},{24,16},{40,32},{56,48},{72,64},{88,80},{104,96},{120,112},{... | collective-permute-start | bytes 405512 | tf_op jit(solution)/shard_map/ppermute | solution.py:437
  18.4 0.1 maximum_bitcast_fusion.f_ref
  18.4 0.0 collective-permute-done.2.first_swap
  18.4 0.9 %collective-permute-done.4.last_swap = bf16[528,128]{1,0:T(8,128)(2,1)S(1)} collective-permute-done((bf16[528,128]{1,0:T(8,128)(2,1)S(1)}, bf16[528,128]{1,0:T(8,128)(2,1)S(1)}, u32[]{:S(2)}, u32[]{:S(2)}) %collective-permute-start.4) | collective-permute-done | bytes 135200 | tf_op jit(solution)/shard_map/ppermute | solution.py:437
  19.3 0.0 collective-permute-done.3.middle_swap
  19.3 0.0 copy-done
  19.3 12.3 %shard_map.120 = (bf16[256,1024]{1,0:T(8,128)(2,1)}, bf16[256,1024]{1,0:T(8,128)(2,1)}, f32[512,128]{1,0:T(8,128)S(1)}, f32[512,128]{1,0:T(8,128)S(1)}, f32[512,...) custom-call(bf16[528,128]{1,0:T(8,128)(2,1)S(1)} %collective-permute-done.b4, ...), custom_call_target="tpu_custom_call" | custom-call | tf_op jit(solution)/shard_map/pallas_call | solution.py:377
  31.6 0.4 collective-permute-start.5
  32.1 1.2 %collective-permute-done.5.swap = bf16[1040,128]{1,0:T(8,128)(2,1)S(1)} collective-permute-done((bf16[1040,128]{1,0:T(8,128)(2,1)S(1)}, bf16[1040,128]{1,0:T(8,128)(2,1)S(1)}, u32[]{:S(2)}, u32[]{:S(2)}) %collective-permute-start.5) | collective-permute-done | bytes 266272 | tf_op jit(solution)/shard_map/ppermute | solution.py:437
  33.3 0.8 %shard_map.121 = (bf16[512,128]{1,0:T(8,128)(2,1)S(1)}, f32[512,128]{1,0:T(8,128)S(1)}, f32[512,128]{1,0:T(8,128)S(1)}, f32[256,128]{1,0:T(8,128)}) custom-call(bf16[1040,128]{1,0:T(8,128)(2,1)S(1)} %collective-permute-done.5.swap, f32[512,128]{1,0:T(8,128)S(1)} %get-tuple-element.46.four, f32[512,128]{1,0:T(8,128)S(1)} %get-tuple-element.47.two, ...), custom_call_target="tpu_custom_call" | custom-call | tf_op jit(solution)/shard_map/pallas_call | solution.py:476
  34.0 1.3 %collective-permute-start.6 = (bf16[512,128]{1,0:T(8,128)(2,1)S(1)}, bf16[512,128]{1,0:T(8,128)(2,1)S(1)}, u32[]{:S(2)}, u32[]{:S(2)}) collective-permute-start(bf16[512,128]{1,0:T(8,128)(2,1)S(1)} %get-tuple-element.52), channel_id=1, source_target_pairs={{16,0},{24,8},{32,16},{40,24},{48,32},{56,40},{64,48},{72,56},{80,... | collective-permute-start | bytes 393224 | tf_op jit(solution)/shard_map/ppermute | solution.py:38
  35.3 16.6 %all-to-all-start = ((f32[128,2,128]{2,1,0:T(2,128)}), f32[128,2,128]{2,1,0:T(2,128)S(1)}, u32[]{:S(2)}, u32[]{:S(2)}) async-start(f32[128,2,128]{2,1,0:T(2,128)} %bitcast.4), calls=%async_computation | async-start | bytes 262144 | tf_op jit(solution)/shard_map/all_to_all | solution.py:515
  51.9 0.0 collective-permute-done.6.hop
  51.9 1.3 %collective-permute-start.7 = (bf16[512,128]{1,0:T(8,128)(2,1)S(1)}, bf16[512,128]{1,0:T(8,128)(2,1)S(1)}, u32[]{:S(2)}, u32[]{:S(2)}) collective-permute-start(bf16[512,128]{1,0:T(8,128)(2,1)S(1)} %shard_map.122), channel_id=1, source_target_pairs={{16,0},{24,8},{32,16},{40,24},{48,32},{56,40},{64,48},{72,56},{80,... | collective-permute-start | bytes 393224 | tf_op jit(solution)/shard_map/ppermute | solution.py:38
  53.2 10.1 %all-to-all-done = f32[128,2,128]{2,1,0:T(2,128)S(1)} async-done(((f32[128,2,128]{2,1,0:T(2,128)}), f32[128,2,128]{2,1,0:T(2,128)S(1)}, u32[]{:S(2)}, u32[]{:S(2)}) %all-to-all-start) | async-done | bytes 131104 | tf_op jit(solution)/shard_map/all_to_all | solution.py:515
  63.3 0.0 collective-permute-done.7.hop
  63.3 0.7 %shard_map.123 = (bf16[256,128]{1,0:T(8,128)(2,1)}, bf16[256,128]{1,0:T(8,128)(2,1)}, f32[1,128]{1,0:T(1,128)}, f32[1,128]{1,0:T(1,128)}) custom-call(f32[512,128]{1,0:T(8,128)S(1)} %get-tuple-element.50.own, bf16[512,128]{1,0:T(8,128)(2,1)S(1)} %collective-permute-done.7.hop, f32[256,128]{1,0:T(8,128)S(1)} %bitcast.9), custom_call_target="tpu_custom_call" | custom-call | tf_op jit(solution)/shard_map/pallas_call | solution.py:476
  (4 shorter events, 0.0 us)
Async XLA Ops:
  2.2 12.9 %collective-permute-start.1 = (bf16[528,128]{1,0:T(8,128)(2,1)}, bf16[528,128]{1,0:T(8,128)(2,1)S(1)}, u32[]{:S(2)}, u32[]{:S(2)}) collective-permute-start(bf16[528,128]{1,0:T(8,128)(2,1)} %shard_map.118.b0), channel_id=1, source_target_pairs={{0,16},{8,24},{16,32},{24,40},{32,48},{40,56},{48,64},{56,72},{64,... | collective-permute-start | bytes 405512 | tf_op jit(solution)/shard_map/ppermute | solution.py:38
  6.1 10.3 %collective-permute-start = (bf16[528,128]{1,0:T(8,128)(2,1)}, bf16[528,128]{1,0:T(8,128)(2,1)S(1)}, u32[]{:S(2)}, u32[]{:S(2)}) collective-permute-start(bf16[528,128]{1,0:T(8,128)(2,1)} %shard_map.118.b0), channel_id=1, source_target_pairs={{0,32},{8,40},{16,48},{24,56},{32,64},{40,72},{48,80},{56,88},{64,... | collective-permute-start | bytes 405512 | tf_op jit(solution)/shard_map/ppermute | solution.py:38
  10.5 8.0 %collective-permute-start.2 = (bf16[528,128]{1,0:T(8,128)(2,1)}, bf16[528,128]{1,0:T(8,128)(2,1)S(1)}, u32[]{:S(2)}, u32[]{:S(2)}) collective-permute-start(bf16[528,128]{1,0:T(8,128)(2,1)} %shard_map.118.b0), channel_id=1, source_target_pairs={{0,8},{16,24},{32,40},{48,56},{64,72},{80,88},{96,104},{112,120},{... | collective-permute-start | bytes 405512 | tf_op jit(solution)/shard_map/ppermute | solution.py:437
  11.8 0.7 %copy-start.3 = (f32[128]{0:T(128)S(1)}, f32[128]{0:T(128)}, u32[]{:S(2)}) copy-start(f32[128]{0:T(128)} %param.11) | copy-start | bytes 1540
  11.8 0.7 %copy-start.4 = (f32[128]{0:T(128)S(1)}, f32[128]{0:T(128)}, u32[]{:S(2)}) copy-start(f32[128]{0:T(128)} %param.12) | copy-start | bytes 1540
  12.5 1.0 %copy-start.1 = (bf16[256,1024]{1,0:T(8,128)(2,1)S(1)}, bf16[256,1024]{1,0:T(8,128)(2,1)}, u32[]{:S(2)}) copy-start(bf16[256,1024]{1,0:T(8,128)(2,1)} %q_ref.1) | copy-start | bytes 1572868
  13.5 1.0 %copy-start.2 = (bf16[256,1024]{1,0:T(8,128)(2,1)S(1)}, bf16[256,1024]{1,0:T(8,128)(2,1)}, u32[]{:S(2)}) copy-start(bf16[256,1024]{1,0:T(8,128)(2,1)} %d_ref.1) | copy-start | bytes 1572868
  14.5 4.8 %copy-start = (bf16[528,128]{1,0:T(8,128)(2,1)S(1)}, bf16[528,128]{1,0:T(8,128)(2,1)}, u32[]{:S(2)}) copy-start(bf16[528,128]{1,0:T(8,128)(2,1)} %shard_map.118.b0) | copy-start | bytes 405508
  15.1 4.2 %collective-permute-start.3 = (bf16[528,128]{1,0:T(8,128)(2,1)S(1)}, bf16[528,128]{1,0:T(8,128)(2,1)S(1)}, u32[]{:S(2)}, u32[]{:S(2)}) collective-permute-start(bf16[528,128]{1,0:T(8,128)(2,1)S(1)} %collective-permute-done.1.b2), channel_id=1, source_target_pairs={{0,8},{8,0},{16,24},{24,16},{32,40},{40,32},{48,56},{56,48},{64,72... | collective-permute-start | bytes 405512 | tf_op jit(solution)/shard_map/ppermute | solution.py:437
  16.4 2.9 %collective-permute-start.4 = (bf16[528,128]{1,0:T(8,128)(2,1)S(1)}, bf16[528,128]{1,0:T(8,128)(2,1)S(1)}, u32[]{:S(2)}, u32[]{:S(2)}) collective-permute-start(bf16[528,128]{1,0:T(8,128)(2,1)S(1)} %collective-permute-done.b4), channel_id=1, source_target_pairs={{8,0},{24,16},{40,32},{56,48},{72,64},{88,80},{104,96},{120,112},{... | collective-permute-start | bytes 405512 | tf_op jit(solution)/shard_map/ppermute | solution.py:437
  31.6 1.6 %collective-permute-start.5 = (bf16[1040,128]{1,0:T(8,128)(2,1)S(1)}, bf16[1040,128]{1,0:T(8,128)(2,1)S(1)}, u32[]{:S(2)}, u32[]{:S(2)}) collective-permute-start(bf16[1040,128]{1,0:T(8,128)(2,1)S(1)} %get-tuple-element.45), channel_id=1, source_target_pairs={{0,8},{8,0},{16,24},{24,16},{32,40},{40,32},{48,56},{56,48},{64,72... | collective-permute-start | bytes 798728 | tf_op jit(solution)/shard_map/ppermute | solution.py:437
  34.0 17.9 %collective-permute-start.6 = (bf16[512,128]{1,0:T(8,128)(2,1)S(1)}, bf16[512,128]{1,0:T(8,128)(2,1)S(1)}, u32[]{:S(2)}, u32[]{:S(2)}) collective-permute-start(bf16[512,128]{1,0:T(8,128)(2,1)S(1)} %get-tuple-element.52), channel_id=1, source_target_pairs={{16,0},{24,8},{32,16},{40,24},{48,32},{56,40},{64,48},{72,56},{80,... | collective-permute-start | bytes 393224 | tf_op jit(solution)/shard_map/ppermute | solution.py:38
  35.3 28.0 %all-to-all-start = ((f32[128,2,128]{2,1,0:T(2,128)}), f32[128,2,128]{2,1,0:T(2,128)S(1)}, u32[]{:S(2)}, u32[]{:S(2)}) async-start(f32[128,2,128]{2,1,0:T(2,128)} %bitcast.4), calls=%async_computation | async-start | bytes 262144 | tf_op jit(solution)/shard_map/all_to_all | solution.py:515
  51.9 11.4 %collective-permute-start.7 = (bf16[512,128]{1,0:T(8,128)(2,1)S(1)}, bf16[512,128]{1,0:T(8,128)(2,1)S(1)}, u32[]{:S(2)}, u32[]{:S(2)}) collective-permute-start(bf16[512,128]{1,0:T(8,128)(2,1)S(1)} %shard_map.122), channel_id=1, source_target_pairs={{16,0},{24,8},{32,16},{40,24},{48,32},{56,40},{64,48},{72,56},{80,... | collective-permute-start | bytes 393224 | tf_op jit(solution)/shard_map/ppermute | solution.py:38

commit v14 on v13

--- a/solution.py
+++ b/solution.py
@@ -15,11 +15,11 @@
 WINDOW = (REACH + 1) * TOK
 SUB = 128
 SPAN = 1152
-CHUNKS = SPAN // SUB
+WIDE = 192
 FINE = 64
 KEY_BLOCKS = (
     [(0, SUB, 0, 256)]
-    + [(start, start + 256, 0, 512) for start in range(SUB, SPAN, 256)]
+    + [(start, start + 512, 0, 512) for start in range(SUB, SPAN, 512)]
     + [(SPAN, WINDOW, 256, 512)]
 )
 ID_ROWS = 16
@@ -194,12 +194,12 @@
     def scores(pair, sub):
         q = qext_t[pair, :, columns_of[sub]]
         top = jnp.full((8, 256), -1e30, jnp.float32)
-        for start in range(0, SPAN, SUB):
-            s = dot(kext[sub * SUB + start : sub * SUB + start + SUB, :], q)
-            if start + SUB == SPAN:
-                s = s + later
-            s_ref[pair % 2, sub, start : start + SUB, :] = s
-            top = jnp.maximum(top, jnp.max(s.reshape(SUB // 8, 8, 256), axis=0))
+        for start in range(0, SPAN, WIDE):
+            s = dot(kext[sub * SUB + start : sub * SUB + start + WIDE, :], q)
+            if start + WIDE == SPAN:
+                s = jnp.concatenate([s[: WIDE - SUB], s[WIDE - SUB :] + later])
+            s_ref[pair % 2, sub, start : start + WIDE, :] = s
+            top = jnp.maximum(top, jnp.max(s.reshape(WIDE // 8, 8, 256), axis=0))
             yield
         shifts[pair, sub] = jnp.max(top, axis=0, keepdims=True) * EXP2
 
@@ -238,8 +238,8 @@
         slot = pair % 2
         d_t = dcat_t[pair, :, columns_of[sub]]
         center = centers[pair, sub]
-        for c in range(CHUNKS):
-            keys = slice((sub + c) * SUB, (sub + c + 1) * SUB)
+        for start in range(0, SPAN, WIDE):
+            keys = slice(sub * SUB + start, sub * SUB + start + WIDE)
             dw = dot(vwin[keys, :], d_t)
             w = w_ref[slot, keys, columns_of[sub]].astype(jnp.float32)
             ds_ref[slot, keys, columns_of[sub]] = (w * (dw - center)).astype(jnp.bfloat16)
@@ -294,8 +294,9 @@
     keys_before = iter(())
 
     def first_keys():
-        for j in range(parts - 2):
+        for j in range(0, parts - 2, 2):
             key_part(j)
+            key_part(j + 1)
             yield
 
     key_part(parts - 2)
@@ -308,12 +309,12 @@
         ahead = [scores(*chains[i + 1])] if i + 1 < len(chains) else []
         weave(exponents(pair, sub), *ahead)
         behind = [query_sums(*chains[i - 1])] if i > 0 else []
-        weave(weights(pair, sub), *behind, first_of(keys_before, 3))
+        weave(weights(pair, sub), *behind, first_of(keys_before, 2))
         behind = [query_terms(*chains[i - 1])] if i > 0 else []
         if sub == 0 and pair + 1 < HEADS // 2:
             behind.append(query_part(pair + 1))
         weave(attend(pair, sub), *behind)
-        weave(score_terms(pair, sub), first_of(keys_before, 3))
+        weave(score_terms(pair, sub), first_of(keys_before, 2))
         if sub == 0 and pair > 0:
             for copy in copies(pair - 1):
                 copy.start()
@@ -342,15 +343,16 @@
     def all_key_ends():
         yield
         yield
-        yield
         key_ends(0)
         yield
-        for j in range(1, parts - 1):
+        yield
+        for j in range(1, 5):
             key_ends(j)
             yield
 
     weave(key_terms(last), all_key_ends(), query_terms(last, 1))
-    key_ends(parts - 1)
+    for j in range(5, parts):
+        key_ends(j)
     for copy in copies(last):
         copy.start()
     kg = k_sums[0]

time: 64.4 us -> 64.4 us (level)
  no operation moved by 1% of the time
where the time goes in v14:
time: 64.4 us; the launch traced here: 64 us
  starting transfers between devices  32.4 us (50%)
  Pallas kernels  15.8 us (25%)
  waiting for transfers between devices  12.1 us (19%)
  local copies, waits for them, and re-layouts  2.74 us (4%)
  between operations  0.75 us (1%)
    all_to_all x1, starting transfers between devices, body(): lax.all_to_all(gains.reshape(chips, 2, HEAD), axes, 0, 0, axis_index_grou...  16.6 us
    pallas_call x1, Pallas kernels, attention(): pl.pallas_call(kernel, out_shape=[shape((TOK, HEADS * HEAD), bf16), shape...  12.3 us
    ppermute x4, starting transfers between devices, passed_along(): return lax.ppermute(block, axis, route)  10.9 us
    all_to_all x1, waiting for transfers between devices, body(): lax.all_to_all(gains.reshape(chips, 2, HEAD), axes, 0, 0, axis_index_grou...  10.1 us
    ppermute x4, starting transfers between devices, swapped(): return lax.ppermute(block, 'context', route)  5 us
    unnamed x10, local copies, waits for them, and re-layouts  2.74 us
    ppermute x4, waiting for transfers between devices, swapped(): return lax.ppermute(block, 'context', route)  2.06 us
    pallas_call x1, Pallas kernels, pack(): pl.pallas_call(pack_kernel, out_shape=jax.ShapeDtypeStruct((MSG, HEAD), j...  1.54 us
  transfers between devices with their start and end apart: 9, of which 3 were waited for; matrix products, arithmetic and copies ran while one was open for 0% of the time, Pallas kernels for 1%

profile of v14, /device:TPU:1, one launch (start us, length us, event | category | flops | bytes accessed | tf_op | source)
XLA Modules:
  0.0 64.0 jit_solution(16309854261048145513)
XLA Ops:
  0.6 1.5 %shard_map.118.b0 = bf16[528,128]{1,0:T(8,128)(2,1)} custom-call(bf16[256,128]{1,0:T(8,128)(2,1)} %keys.1, bf16[256,128]{1,0:T(8,128)(2,1)} %values.1, s32[2,128]{1,0:T(2,128)} %bitcast.12), custom_call_target="tpu_custom_call" | custom-call | tf_op jit(solution)/shard_map/pallas_call | solution.py:429
  2.2 3.9 %collective-permute-start.1 = (bf16[528,128]{1,0:T(8,128)(2,1)}, bf16[528,128]{1,0:T(8,128)(2,1)S(1)}, u32[]{:S(2)}, u32[]{:S(2)}) collective-permute-start(bf16[528,128]{1,0:T(8,128)(2,1)} %shard_map.118.b0), channel_id=1, source_target_pairs={{0,16},{8,24},{16,32},{24,40},{32,48},{40,56},{48,64},{56,72},{64,... | collective-permute-start | bytes 405512 | tf_op jit(solution)/shard_map/ppermute | solution.py:38
  6.1 4.4 %collective-permute-start = (bf16[528,128]{1,0:T(8,128)(2,1)}, bf16[528,128]{1,0:T(8,128)(2,1)S(1)}, u32[]{:S(2)}, u32[]{:S(2)}) collective-permute-start(bf16[528,128]{1,0:T(8,128)(2,1)} %shard_map.118.b0), channel_id=1, source_target_pairs={{0,32},{8,40},{16,48},{24,56},{32,64},{40,72},{48,80},{56,88},{64,... | collective-permute-start | bytes 405512 | tf_op jit(solution)/shard_map/ppermute | solution.py:38
  10.5 1.3 %collective-permute-start.2 = (bf16[528,128]{1,0:T(8,128)(2,1)}, bf16[528,128]{1,0:T(8,128)(2,1)S(1)}, u32[]{:S(2)}, u32[]{:S(2)}) collective-permute-start(bf16[528,128]{1,0:T(8,128)(2,1)} %shard_map.118.b0), channel_id=1, source_target_pairs={{0,8},{16,24},{32,40},{48,56},{64,72},{80,88},{96,104},{112,120},{... | collective-permute-start | bytes 405512 | tf_op jit(solution)/shard_map/ppermute | solution.py:439
  11.8 0.0 copy-start.3
  11.8 0.0 copy-start.4
  11.8 0.6 copy-done.3
  12.4 0.0 copy-done.4
  12.5 0.0 copy-start.1
  12.5 1.0 %copy-done.1 = bf16[256,1024]{1,0:T(8,128)(2,1)S(1)} copy-done((bf16[256,1024]{1,0:T(8,128)(2,1)S(1)}, bf16[256,1024]{1,0:T(8,128)(2,1)}, u32[]{:S(2)}) %copy-start.1) | copy-done | bytes 524312
  13.5 1.0 %copy-done.2 = bf16[256,1024]{1,0:T(8,128)(2,1)S(1)} copy-done((bf16[256,1024]{1,0:T(8,128)(2,1)S(1)}, bf16[256,1024]{1,0:T(8,128)(2,1)}, u32[]{:S(2)}) %copy-start.2) | copy-done | bytes 524312
  14.6 0.5 shard_map.119
  15.1 0.0 collective-permute-done.1.b2
  15.1 1.3 %collective-permute-start.3 = (bf16[528,128]{1,0:T(8,128)(2,1)S(1)}, bf16[528,128]{1,0:T(8,128)(2,1)S(1)}, u32[]{:S(2)}, u32[]{:S(2)}) collective-permute-start(bf16[528,128]{1,0:T(8,128)(2,1)S(1)} %collective-permute-done.1.b2), channel_id=1, source_target_pairs={{0,8},{8,0},{16,24},{24,16},{32,40},{40,32},{48,56},{56,48},{64,72... | collective-permute-start | bytes 405512 | tf_op jit(solution)/shard_map/ppermute | solution.py:439
  16.4 0.0 collective-permute-done.b4
  16.4 1.9 %collective-permute-start.4 = (bf16[528,128]{1,0:T(8,128)(2,1)S(1)}, bf16[528,128]{1,0:T(8,128)(2,1)S(1)}, u32[]{:S(2)}, u32[]{:S(2)}) collective-permute-start(bf16[528,128]{1,0:T(8,128)(2,1)S(1)} %collective-permute-done.b4), channel_id=1, source_target_pairs={{8,0},{24,16},{40,32},{56,48},{72,64},{88,80},{104,96},{120,112},{... | collective-permute-start | bytes 405512 | tf_op jit(solution)/shard_map/ppermute | solution.py:439
  18.4 0.1 maximum_bitcast_fusion.f_ref
  18.4 0.0 collective-permute-done.2.first_swap
  18.4 0.9 %collective-permute-done.4.last_swap = bf16[528,128]{1,0:T(8,128)(2,1)S(1)} collective-permute-done((bf16[528,128]{1,0:T(8,128)(2,1)S(1)}, bf16[528,128]{1,0:T(8,128)(2,1)S(1)}, u32[]{:S(2)}, u32[]{:S(2)}) %collective-permute-start.4) | collective-permute-done | bytes 135200 | tf_op jit(solution)/shard_map/ppermute | solution.py:439
  19.3 0.0 collective-permute-done.3.middle_swap
  19.3 0.0 copy-done
  19.3 12.3 %shard_map.120 = (bf16[256,1024]{1,0:T(8,128)(2,1)}, bf16[256,1024]{1,0:T(8,128)(2,1)}, f32[512,128]{1,0:T(8,128)S(1)}, f32[512,128]{1,0:T(8,128)S(1)}, f32[512,...) custom-call(bf16[528,128]{1,0:T(8,128)(2,1)S(1)} %collective-permute-done.b4, ...), custom_call_target="tpu_custom_call" | custom-call | tf_op jit(solution)/shard_map/pallas_call | solution.py:379
  31.6 0.4 collective-permute-start.5
  32.1 1.2 %collective-permute-done.5.swap = bf16[1040,128]{1,0:T(8,128)(2,1)S(1)} collective-permute-done((bf16[1040,128]{1,0:T(8,128)(2,1)S(1)}, bf16[1040,128]{1,0:T(8,128)(2,1)S(1)}, u32[]{:S(2)}, u32[]{:S(2)}) %collective-permute-start.5) | collective-permute-done | bytes 266272 | tf_op jit(solution)/shard_map/ppermute | solution.py:439
  33.3 0.8 %shard_map.121 = (bf16[512,128]{1,0:T(8,128)(2,1)S(1)}, f32[512,128]{1,0:T(8,128)S(1)}, f32[512,128]{1,0:T(8,128)S(1)}, f32[256,128]{1,0:T(8,128)}) custom-call(bf16[1040,128]{1,0:T(8,128)(2,1)S(1)} %collective-permute-done.5.swap, f32[512,128]{1,0:T(8,128)S(1)} %get-tuple-element.46.four, f32[512,128]{1,0:T(8,128)S(1)} %get-tuple-element.47.two, ...), custom_call_target="tpu_custom_call" | custom-call | tf_op jit(solution)/shard_map/pallas_call | solution.py:478
  34.0 1.3 %collective-permute-start.6 = (bf16[512,128]{1,0:T(8,128)(2,1)S(1)}, bf16[512,128]{1,0:T(8,128)(2,1)S(1)}, u32[]{:S(2)}, u32[]{:S(2)}) collective-permute-start(bf16[512,128]{1,0:T(8,128)(2,1)S(1)} %get-tuple-element.52), channel_id=1, source_target_pairs={{16,0},{24,8},{32,16},{40,24},{48,32},{56,40},{64,48},{72,56},{80,... | collective-permute-start | bytes 393224 | tf_op jit(solution)/shard_map/ppermute | solution.py:38
  35.3 16.6 %all-to-all-start = ((f32[128,2,128]{2,1,0:T(2,128)}), f32[128,2,128]{2,1,0:T(2,128)S(1)}, u32[]{:S(2)}, u32[]{:S(2)}) async-start(f32[128,2,128]{2,1,0:T(2,128)} %bitcast.4), calls=%async_computation | async-start | bytes 262144 | tf_op jit(solution)/shard_map/all_to_all | solution.py:517
  51.9 0.0 collective-permute-done.6.hop
  51.9 1.3 %collective-permute-start.7 = (bf16[512,128]{1,0:T(8,128)(2,1)S(1)}, bf16[512,128]{1,0:T(8,128)(2,1)S(1)}, u32[]{:S(2)}, u32[]{:S(2)}) collective-permute-start(bf16[512,128]{1,0:T(8,128)(2,1)S(1)} %shard_map.122), channel_id=1, source_target_pairs={{16,0},{24,8},{32,16},{40,24},{48,32},{56,40},{64,48},{72,56},{80,... | collective-permute-start | bytes 393224 | tf_op jit(solution)/shard_map/ppermute | solution.py:38
  53.2 10.1 %all-to-all-done = f32[128,2,128]{2,1,0:T(2,128)S(1)} async-done(((f32[128,2,128]{2,1,0:T(2,128)}), f32[128,2,128]{2,1,0:T(2,128)S(1)}, u32[]{:S(2)}, u32[]{:S(2)}) %all-to-all-start) | async-done | bytes 131104 | tf_op jit(solution)/shard_map/all_to_all | solution.py:517
  63.3 0.0 collective-permute-done.7.hop
  63.3 0.7 %shard_map.123 = (bf16[256,128]{1,0:T(8,128)(2,1)}, bf16[256,128]{1,0:T(8,128)(2,1)}, f32[1,128]{1,0:T(1,128)}, f32[1,128]{1,0:T(1,128)}) custom-call(f32[512,128]{1,0:T(8,128)S(1)} %get-tuple-element.50.own, bf16[512,128]{1,0:T(8,128)(2,1)S(1)} %collective-permute-done.7.hop, f32[256,128]{1,0:T(8,128)S(1)} %bitcast.9), custom_call_target="tpu_custom_call" | custom-call | tf_op jit(solution)/shard_map/pallas_call | solution.py:478
  (4 shorter events, 0.0 us)
Async XLA Ops:
  2.2 12.9 %collective-permute-start.1 = (bf16[528,128]{1,0:T(8,128)(2,1)}, bf16[528,128]{1,0:T(8,128)(2,1)S(1)}, u32[]{:S(2)}, u32[]{:S(2)}) collective-permute-start(bf16[528,128]{1,0:T(8,128)(2,1)} %shard_map.118.b0), channel_id=1, source_target_pairs={{0,16},{8,24},{16,32},{24,40},{32,48},{40,56},{48,64},{56,72},{64,... | collective-permute-start | bytes 405512 | tf_op jit(solution)/shard_map/ppermute | solution.py:38
  6.1 10.3 %collective-permute-start = (bf16[528,128]{1,0:T(8,128)(2,1)}, bf16[528,128]{1,0:T(8,128)(2,1)S(1)}, u32[]{:S(2)}, u32[]{:S(2)}) collective-permute-start(bf16[528,128]{1,0:T(8,128)(2,1)} %shard_map.118.b0), channel_id=1, source_target_pairs={{0,32},{8,40},{16,48},{24,56},{32,64},{40,72},{48,80},{56,88},{64,... | collective-permute-start | bytes 405512 | tf_op jit(solution)/shard_map/ppermute | solution.py:38
  10.5 8.0 %collective-permute-start.2 = (bf16[528,128]{1,0:T(8,128)(2,1)}, bf16[528,128]{1,0:T(8,128)(2,1)S(1)}, u32[]{:S(2)}, u32[]{:S(2)}) collective-permute-start(bf16[528,128]{1,0:T(8,128)(2,1)} %shard_map.118.b0), channel_id=1, source_target_pairs={{0,8},{16,24},{32,40},{48,56},{64,72},{80,88},{96,104},{112,120},{... | collective-permute-start | bytes 405512 | tf_op jit(solution)/shard_map/ppermute | solution.py:439
  11.8 0.7 %copy-start.3 = (f32[128]{0:T(128)S(1)}, f32[128]{0:T(128)}, u32[]{:S(2)}) copy-start(f32[128]{0:T(128)} %param.11) | copy-start | bytes 1540
  11.8 0.7 %copy-start.4 = (f32[128]{0:T(128)S(1)}, f32[128]{0:T(128)}, u32[]{:S(2)}) copy-start(f32[128]{0:T(128)} %param.12) | copy-start | bytes 1540
  12.5 1.0 %copy-start.1 = (bf16[256,1024]{1,0:T(8,128)(2,1)S(1)}, bf16[256,1024]{1,0:T(8,128)(2,1)}, u32[]{:S(2)}) copy-start(bf16[256,1024]{1,0:T(8,128)(2,1)} %q_ref.1) | copy-start | bytes 1572868
  13.5 1.0 %copy-start.2 = (bf16[256,1024]{1,0:T(8,128)(2,1)S(1)}, bf16[256,1024]{1,0:T(8,128)(2,1)}, u32[]{:S(2)}) copy-start(bf16[256,1024]{1,0:T(8,128)(2,1)} %d_ref.1) | copy-start | bytes 1572868
  14.5 4.8 %copy-start = (bf16[528,128]{1,0:T(8,128)(2,1)S(1)}, bf16[528,128]{1,0:T(8,128)(2,1)}, u32[]{:S(2)}) copy-start(bf16[528,128]{1,0:T(8,128)(2,1)} %shard_map.118.b0) | copy-start | bytes 405508
  15.1 4.2 %collective-permute-start.3 = (bf16[528,128]{1,0:T(8,128)(2,1)S(1)}, bf16[528,128]{1,0:T(8,128)(2,1)S(1)}, u32[]{:S(2)}, u32[]{:S(2)}) collective-permute-start(bf16[528,128]{1,0:T(8,128)(2,1)S(1)} %collective-permute-done.1.b2), channel_id=1, source_target_pairs={{0,8},{8,0},{16,24},{24,16},{32,40},{40,32},{48,56},{56,48},{64,72... | collective-permute-start | bytes 405512 | tf_op jit(solution)/shard_map/ppermute | solution.py:439
  16.4 2.9 %collective-permute-start.4 = (bf16[528,128]{1,0:T(8,128)(2,1)S(1)}, bf16[528,128]{1,0:T(8,128)(2,1)S(1)}, u32[]{:S(2)}, u32[]{:S(2)}) collective-permute-start(bf16[528,128]{1,0:T(8,128)(2,1)S(1)} %collective-permute-done.b4), channel_id=1, source_target_pairs={{8,0},{24,16},{40,32},{56,48},{72,64},{88,80},{104,96},{120,112},{... | collective-permute-start | bytes 405512 | tf_op jit(solution)/shard_map/ppermute | solution.py:439
  31.6 1.6 %collective-permute-start.5 = (bf16[1040,128]{1,0:T(8,128)(2,1)S(1)}, bf16[1040,128]{1,0:T(8,128)(2,1)S(1)}, u32[]{:S(2)}, u32[]{:S(2)}) collective-permute-start(bf16[1040,128]{1,0:T(8,128)(2,1)S(1)} %get-tuple-element.45), channel_id=1, source_target_pairs={{0,8},{8,0},{16,24},{24,16},{32,40},{40,32},{48,56},{56,48},{64,72... | collective-permute-start | bytes 798728 | tf_op jit(solution)/shard_map/ppermute | solution.py:439
  34.0 17.9 %collective-permute-start.6 = (bf16[512,128]{1,0:T(8,128)(2,1)S(1)}, bf16[512,128]{1,0:T(8,128)(2,1)S(1)}, u32[]{:S(2)}, u32[]{:S(2)}) collective-permute-start(bf16[512,128]{1,0:T(8,128)(2,1)S(1)} %get-tuple-element.52), channel_id=1, source_target_pairs={{16,0},{24,8},{32,16},{40,24},{48,32},{56,40},{64,48},{72,56},{80,... | collective-permute-start | bytes 393224 | tf_op jit(solution)/shard_map/ppermute | solution.py:38
  35.3 28.0 %all-to-all-start = ((f32[128,2,128]{2,1,0:T(2,128)}), f32[128,2,128]{2,1,0:T(2,128)S(1)}, u32[]{:S(2)}, u32[]{:S(2)}) async-start(f32[128,2,128]{2,1,0:T(2,128)} %bitcast.4), calls=%async_computation | async-start | bytes 262144 | tf_op jit(solution)/shard_map/all_to_all | solution.py:517
  51.9 11.4 %collective-permute-start.7 = (bf16[512,128]{1,0:T(8,128)(2,1)S(1)}, bf16[512,128]{1,0:T(8,128)(2,1)S(1)}, u32[]{:S(2)}, u32[]{:S(2)}) collective-permute-start(bf16[512,128]{1,0:T(8,128)(2,1)S(1)} %shard_map.122), channel_id=1, source_target_pairs={{16,0},{24,8},{32,16},{40,24},{48,32},{56,40},{64,48},{72,56},{80,... | collective-permute-start | bytes 393224 | tf_op jit(solution)/shard_map/ppermute | solution.py:38

commit v15 on v13

--- a/solution.py
+++ b/solution.py
@@ -102,7 +102,7 @@
     b4, b2, b0, first_swap, middle_swap, last_swap, xh_ref, scale_ref, dcat, dcat_t, gains_ref, f_ref,
     att_hbm, gq_hbm, four_ref, two_ref, own_ref, swap_ref, gain_ref,
     att_ref, gq_ref, cosine, sine, kext, vwin, khat_t, v_t, qhat, qext_t,
-    s_ref, w_ref, ds_ref, dk, dv, qg_acc, b3, b1, att_sem, gq_sem,
+    s_ref, w_ref, ds_ref, dk, dv, qg_acc, b3, b1, bounds, att_sem, gq_sem,
 ):
     even = lax.rem(lax.axis_index("context"), 2) == 0
 
@@ -137,6 +137,8 @@
         kext[j * SUB : (j + 1) * SUB, HEAD:] = jnp.where(column == lane_f, 1.0, 0.0).astype(jnp.bfloat16)
         below = below + jnp.where(column < lane_f, 1.0, 0.0)
     first = jnp.sum(below, axis=0, keepdims=True)
+
+    k_norm = [jnp.zeros((SUB, 1), jnp.float32)]
 
     def key_part(j):
         rows = slice(j * SUB, (j + 1) * SUB)
@@ -154,6 +156,7 @@
         x = block[here, :].astype(jnp.float32)
         normed = x * lax.rsqrt(jnp.mean(x * x, axis=1, keepdims=True) + EPSILON) * k_gain
         hat = normed * c + half_turned(normed) * s
+        k_norm[0] = jnp.maximum(k_norm[0], jnp.sum(hat * hat, axis=1, keepdims=True))
         kext[rows, 0:HEAD] = hat.astype(jnp.bfloat16)
         khat_t[:, rows] = hat.T.astype(jnp.bfloat16)
         values = block[TOK + (j % 2) * SUB : TOK + (j % 2 + 1) * SUB, :]
@@ -170,7 +173,9 @@
                 normed = xh_ref[at : at + SUB, :] * q_gain
                 hat = normed * cosine[window_rows, :] + half_turned(normed) * sine[window_rows, :]
                 qhat[at : at + SUB, :] = hat.astype(jnp.bfloat16)
-                qext_t[pair, 0:HEAD, lanes] = hat.T.astype(jnp.bfloat16)
+                hat_t = hat.T
+                bounds[pair, 0:1, lanes] = jnp.sum(hat_t * hat_t, axis=0, keepdims=True)
+                qext_t[pair, 0:HEAD, lanes] = hat_t.astype(jnp.bfloat16)
                 qext_t[pair, HEAD:, lanes] = other
                 yield
 
@@ -212,6 +217,20 @@
             e = jnp.exp2(s_ref[slot, sub, rows, :] * EXP2 - shift)
             s_ref[slot, sub, rows, :] = e
             total = total + jnp.sum(e.reshape(FINE // 8, 8, 256), axis=0)
+            yield
+        inverses[pair, sub] = 1.0 / jnp.sum(total, axis=0, keepdims=True)
+
+    def bounded_exponents(pair, sub):
+        q = qext_t[pair, :, columns_of[sub]]
+        shift = bounds[pair, 0:1, columns_of[sub]]
+        total = jnp.zeros((8, 256), jnp.float32)
+        for start in range(0, SPAN, SUB):
+            s = dot(kext[sub * SUB + start : sub * SUB + start + SUB, :], q)
+            if start + SUB == SPAN:
+                s = s + later
+            e = jnp.exp2(s * EXP2 - shift)
+            s_ref[pair % 2, sub, start : start + SUB, :] = e
+            total = total + jnp.sum(e.reshape(SUB // 8, 8, 256), axis=0)
             yield
         inverses[pair, sub] = 1.0 / jnp.sum(total, axis=0, keepdims=True)
 
@@ -291,79 +310,92 @@
 
     stop = object()
     chains = [(pair, sub) for pair in range(HEADS // 2) for sub in range(2)]
-    keys_before = iter(())
-
-    def first_keys():
-        for j in range(parts - 2):
-            key_part(j)
-            yield
-
-    key_part(parts - 2)
-    key_part(parts - 1)
-    weave(query_part(0))
-    weave(first_keys(), scores(*chains[0]))
-    for i, (pair, sub) in enumerate(chains):
-        if sub == 0 and pair > 0:
-            keys_before = key_terms(pair - 1)
-        ahead = [scores(*chains[i + 1])] if i + 1 < len(chains) else []
-        weave(exponents(pair, sub), *ahead)
-        behind = [query_sums(*chains[i - 1])] if i > 0 else []
-        weave(weights(pair, sub), *behind, first_of(keys_before, 3))
-        behind = [query_terms(*chains[i - 1])] if i > 0 else []
-        if sub == 0 and pair + 1 < HEADS // 2:
-            behind.append(query_part(pair + 1))
-        weave(attend(pair, sub), *behind)
-        weave(score_terms(pair, sub), first_of(keys_before, 3))
-        if sub == 0 and pair > 0:
-            for copy in copies(pair - 1):
-                copy.start()
-    last = HEADS // 2 - 1
-    weave(query_sums(last, 1))
-
-    outs = ((four_ref, 0), (swap_ref, 2 * TOK), (two_ref, 0), (swap_ref, 0), (own_ref, 0))
-    k_sums = [jnp.zeros((8, HEAD), jnp.float32)]
-
-    def key_ends(j):
-        rows = slice(j * SUB, (j + 1) * SUB)
-        here = slice((j % 2) * SUB, (j % 2 + 1) * SUB)
-        x = blocks[j // 2][here, :].astype(jnp.float32)
-        r = lax.rsqrt(jnp.mean(x * x, axis=1, keepdims=True) + EPSILON)
-        xh = x * r
-        d = dk[rows, :] * SCALING
-        dn = d * cosine[rows, :] - half_turned(d) * sine[rows, :]
-        k_sums[0] = k_sums[0] + jnp.sum((dn * xh).reshape(SUB // 8, 8, HEAD), axis=0)
-        dxh = dn * k_gain
-        gk = r * (dxh - xh * jnp.mean(dxh * xh, axis=1, keepdims=True))
-        out, at = outs[j // 2]
-        at = at + (j % 2) * SUB
-        out[at : at + SUB, :] = gk.astype(out.dtype)
-        out[at + TOK : at + TOK + SUB, :] = dv[rows, :].astype(out.dtype)
-
-    def all_key_ends():
-        yield
-        yield
-        yield
-        key_ends(0)
-        yield
-        for j in range(1, parts - 1):
-            key_ends(j)
-            yield
-
-    weave(key_terms(last), all_key_ends(), query_terms(last, 1))
-    key_ends(parts - 1)
-    for copy in copies(last):
-        copy.start()
-    kg = k_sums[0]
-    gains = jnp.concatenate(
-        [jnp.sum(qg_acc[...], axis=0, keepdims=True), jnp.sum(kg, axis=0, keepdims=True)]
+    for j in range(parts):
+        key_part(j)
+    for pair in range(HEADS // 2):
+        weave(query_part(pair))
+
+    longest = jnp.sqrt(jnp.max(k_norm[0], axis=0, keepdims=True)) * (1.02 * EXP2)
+    for pair in range(HEADS // 2):
+        bounds[pair, 0:1, :] = jnp.sqrt(bounds[pair, 0:1, :]) * longest
+    top = jnp.maximum(
+        jnp.maximum(bounds[0, 0:1, :], bounds[1, 0:1, :]), jnp.maximum(bounds[2, 0:1, :], bounds[3, 0:1, :])
     )
-    gain_ref[...] = gains
-    high = gains.astype(jnp.bfloat16).astype(jnp.float32)
-    middle = (gains - high).astype(jnp.bfloat16).astype(jnp.float32)
-    low = gains - high - middle
-    swap_ref[4 * TOK :, :] = jnp.concatenate(
-        [high, middle, low, jnp.zeros((ID_ROWS - 6, HEAD), jnp.float32)]
-    ).astype(jnp.bfloat16)
+    small = jnp.max(top) <= 60.0
+
+    def finish():
+        last = HEADS // 2 - 1
+        weave(query_sums(last, 1))
+
+        outs = ((four_ref, 0), (swap_ref, 2 * TOK), (two_ref, 0), (swap_ref, 0), (own_ref, 0))
+        k_sums = [jnp.zeros((8, HEAD), jnp.float32)]
+
+        def key_ends(j):
+            rows = slice(j * SUB, (j + 1) * SUB)
+            here = slice((j % 2) * SUB, (j % 2 + 1) * SUB)
+            x = blocks[j // 2][here, :].astype(jnp.float32)
+            r = lax.rsqrt(jnp.mean(x * x, axis=1, keepdims=True) + EPSILON)
+            xh = x * r
+            d = dk[rows, :] * SCALING
+            dn = d * cosine[rows, :] - half_turned(d) * sine[rows, :]
+            k_sums[0] = k_sums[0] + jnp.sum((dn * xh).reshape(SUB // 8, 8, HEAD), axis=0)
+            dxh = dn * k_gain
+            gk = r * (dxh - xh * jnp.mean(dxh * xh, axis=1, keepdims=True))
+            out, at = outs[j // 2]
+            at = at + (j % 2) * SUB
+            out[at : at + SUB, :] = gk.astype(out.dtype)
+            out[at + TOK : at + TOK + SUB, :] = dv[rows, :].astype(out.dtype)
+
+        def all_key_ends():
+            yield
+            yield
+            yield
+            key_ends(0)
+            yield
+            for j in range(1, parts - 1):
+                key_ends(j)
+                yield
+
+        weave(key_terms(last), all_key_ends(), query_terms(last, 1))
+        key_ends(parts - 1)
+        for copy in copies(last):
+            copy.start()
+        kg = k_sums[0]
+        gains = jnp.concatenate(
+            [jnp.sum(qg_acc[...], axis=0, keepdims=True), jnp.sum(kg, axis=0, keepdims=True)]
+        )
+        gain_ref[...] = gains
+        high = gains.astype(jnp.bfloat16).astype(jnp.float32)
+        middle = (gains - high).astype(jnp.bfloat16).astype(jnp.float32)
+        low = gains - high - middle
+        swap_ref[4 * TOK :, :] = jnp.concatenate(
+            [high, middle, low, jnp.zeros((ID_ROWS - 6, HEAD), jnp.float32)]
+        ).astype(jnp.bfloat16)
+
+    def run(bounded):
+        keys_before = iter(())
+        first_step = bounded_exponents if bounded else scores
+        weave(first_step(*chains[0]))
+        for i, (pair, sub) in enumerate(chains):
+            if sub == 0 and pair > 0:
+                keys_before = key_terms(pair - 1)
+            ahead = [first_step(*chains[i + 1])] if i + 1 < len(chains) else []
+            behind = [query_sums(*chains[i - 1])] if i > 0 else []
+            if bounded:
+                weave(weights(pair, sub), *ahead, *behind, first_of(keys_before, 3))
+            else:
+                weave(exponents(pair, sub), *ahead)
+                weave(weights(pair, sub), *behind, first_of(keys_before, 3))
+            behind = [query_terms(*chains[i - 1])] if i > 0 else []
+            weave(attend(pair, sub), *behind)
+            weave(score_terms(pair, sub), first_of(keys_before, 3))
+            if sub == 0 and pair > 0:
+                for copy in copies(pair - 1):
+                    copy.start()
+        finish()
+
+    pl.when(small)(lambda: run(True))
+    pl.when(jnp.logical_not(small))(lambda: run(False))
     for pair in range(HEADS // 2):
         for copy in copies(pair):
             copy.wait()
@@ -406,6 +438,7 @@
             pltpu.VMEM((8, HEAD), f32),
             pltpu.VMEM((MSG, HEAD), bf16),
             pltpu.VMEM((MSG, HEAD), bf16),
+            pltpu.VMEM((HEADS // 2, 8, 512), f32),
             pltpu.SemaphoreType.DMA((HEADS // 2,)),
             pltpu.SemaphoreType.DMA((HEADS // 2,)),
         ],

time: 64.4 us -> 67 us (1.040)
  Pallas kernels: 15.8 us -> 18.4 us
    pallas_call x1, Pallas kernels: 12.3 us -> 14.9 us  [attention(): pl.pallas_call(kernel, out_shape=[shape((TOK, HEADS * HEAD), bf16), shape...]
where the time goes in v15:
time: 67 us; the launch traced here: 66.6 us
  starting transfers between devices  32.5 us (49%)
  Pallas kernels  18.4 us (27%)
  waiting for transfers between devices  12.1 us (18%)
  local copies, waits for them, and re-layouts  2.74 us (4%)
  between operations  0.75 us (1%)
    all_to_all x1, starting transfers between devices, body(): lax.all_to_all(gains.reshape(chips, 2, HEAD), axes, 0, 0, axis_index_grou...  16.6 us
    pallas_call x1, Pallas kernels, attention(): pl.pallas_call(kernel, out_shape=[shape((TOK, HEADS * HEAD), bf16), shape...  14.9 us
    ppermute x4, starting transfers between devices, passed_along(): return lax.ppermute(block, axis, route)  10.9 us
    all_to_all x1, waiting for transfers between devices, body(): lax.all_to_all(gains.reshape(chips, 2, HEAD), axes, 0, 0, axis_index_grou...  10.1 us
    ppermute x4, starting transfers between devices, swapped(): return lax.ppermute(block, 'context', route)  5.01 us
    unnamed x10, local copies, waits for them, and re-layouts  2.74 us
    ppermute x4, waiting for transfers between devices, swapped(): return lax.ppermute(block, 'context', route)  2.05 us
    pallas_call x1, Pallas kernels, pack(): pl.pallas_call(pack_kernel, out_shape=jax.ShapeDtypeStruct((MSG, HEAD), j...  1.54 us
  transfers between devices with their start and end apart: 9, of which 3 were waited for; matrix products, arithmetic and copies ran while one was open for 0% of the time, Pallas kernels for 1%

profile of v15, /device:TPU:1, one launch (start us, length us, event | category | flops | bytes accessed | tf_op | source)
XLA Modules:
  0.0 66.6 jit_solution(12978967841408218876)
XLA Ops:
  0.6 1.5 %shard_map.118.b0 = bf16[528,128]{1,0:T(8,128)(2,1)} custom-call(bf16[256,128]{1,0:T(8,128)(2,1)} %keys.1, bf16[256,128]{1,0:T(8,128)(2,1)} %values.1, s32[2,128]{1,0:T(2,128)} %bitcast.12), custom_call_target="tpu_custom_call" | custom-call | tf_op jit(solution)/shard_map/pallas_call | solution.py:460
  2.2 3.9 %collective-permute-start.1 = (bf16[528,128]{1,0:T(8,128)(2,1)}, bf16[528,128]{1,0:T(8,128)(2,1)S(1)}, u32[]{:S(2)}, u32[]{:S(2)}) collective-permute-start(bf16[528,128]{1,0:T(8,128)(2,1)} %shard_map.118.b0), channel_id=1, source_target_pairs={{0,16},{8,24},{16,32},{24,40},{32,48},{40,56},{48,64},{56,72},{64,... | collective-permute-start | bytes 405512 | tf_op jit(solution)/shard_map/ppermute | solution.py:38
  6.1 4.4 %collective-permute-start = (bf16[528,128]{1,0:T(8,128)(2,1)}, bf16[528,128]{1,0:T(8,128)(2,1)S(1)}, u32[]{:S(2)}, u32[]{:S(2)}) collective-permute-start(bf16[528,128]{1,0:T(8,128)(2,1)} %shard_map.118.b0), channel_id=1, source_target_pairs={{0,32},{8,40},{16,48},{24,56},{32,64},{40,72},{48,80},{56,88},{64,... | collective-permute-start | bytes 405512 | tf_op jit(solution)/shard_map/ppermute | solution.py:38
  10.5 1.3 %collective-permute-start.2 = (bf16[528,128]{1,0:T(8,128)(2,1)}, bf16[528,128]{1,0:T(8,128)(2,1)S(1)}, u32[]{:S(2)}, u32[]{:S(2)}) collective-permute-start(bf16[528,128]{1,0:T(8,128)(2,1)} %shard_map.118.b0), channel_id=1, source_target_pairs={{0,8},{16,24},{32,40},{48,56},{64,72},{80,88},{96,104},{112,120},{... | collective-permute-start | bytes 405512 | tf_op jit(solution)/shard_map/ppermute | solution.py:470
  11.8 0.0 copy-start.3
  11.8 0.0 copy-start.4
  11.8 0.6 copy-done.3
  12.4 0.0 copy-done.4
  12.5 0.0 copy-start.1
  12.5 1.0 %copy-done.1 = bf16[256,1024]{1,0:T(8,128)(2,1)S(1)} copy-done((bf16[256,1024]{1,0:T(8,128)(2,1)S(1)}, bf16[256,1024]{1,0:T(8,128)(2,1)}, u32[]{:S(2)}) %copy-start.1) | copy-done | bytes 524312
  13.5 1.0 %copy-done.2 = bf16[256,1024]{1,0:T(8,128)(2,1)S(1)} copy-done((bf16[256,1024]{1,0:T(8,128)(2,1)S(1)}, bf16[256,1024]{1,0:T(8,128)(2,1)}, u32[]{:S(2)}) %copy-start.2) | copy-done | bytes 524312
  14.6 0.5 shard_map.119
  15.1 0.0 collective-permute-done.1.b2
  15.1 1.3 %collective-permute-start.3 = (bf16[528,128]{1,0:T(8,128)(2,1)S(1)}, bf16[528,128]{1,0:T(8,128)(2,1)S(1)}, u32[]{:S(2)}, u32[]{:S(2)}) collective-permute-start(bf16[528,128]{1,0:T(8,128)(2,1)S(1)} %collective-permute-done.1.b2), channel_id=1, source_target_pairs={{0,8},{8,0},{16,24},{24,16},{32,40},{40,32},{48,56},{56,48},{64,72... | collective-permute-start | bytes 405512 | tf_op jit(solution)/shard_map/ppermute | solution.py:470
  16.4 0.0 collective-permute-done.b4
  16.4 1.9 %collective-permute-start.4 = (bf16[528,128]{1,0:T(8,128)(2,1)S(1)}, bf16[528,128]{1,0:T(8,128)(2,1)S(1)}, u32[]{:S(2)}, u32[]{:S(2)}) collective-permute-start(bf16[528,128]{1,0:T(8,128)(2,1)S(1)} %collective-permute-done.b4), channel_id=1, source_target_pairs={{8,0},{24,16},{40,32},{56,48},{72,64},{88,80},{104,96},{120,112},{... | collective-permute-start | bytes 405512 | tf_op jit(solution)/shard_map/ppermute | solution.py:470
  18.4 0.1 maximum_bitcast_fusion.f_ref
  18.4 0.0 collective-permute-done.2.first_swap
  18.4 0.9 %collective-permute-done.4.last_swap = bf16[528,128]{1,0:T(8,128)(2,1)S(1)} collective-permute-done((bf16[528,128]{1,0:T(8,128)(2,1)S(1)}, bf16[528,128]{1,0:T(8,128)(2,1)S(1)}, u32[]{:S(2)}, u32[]{:S(2)}) %collective-permute-start.4) | collective-permute-done | bytes 135200 | tf_op jit(solution)/shard_map/ppermute | solution.py:470
  19.3 0.0 collective-permute-done.3.middle_swap
  19.3 0.0 copy-done
  19.3 14.9 %shard_map.120 = (bf16[256,1024]{1,0:T(8,128)(2,1)}, bf16[256,1024]{1,0:T(8,128)(2,1)}, f32[512,128]{1,0:T(8,128)S(1)}, f32[512,128]{1,0:T(8,128)S(1)}, f32[512,...) custom-call(bf16[528,128]{1,0:T(8,128)(2,1)S(1)} %collective-permute-done.b4, ...), custom_call_target="tpu_custom_call" | custom-call | tf_op jit(solution)/shard_map/pallas_call | solution.py:409
  34.2 0.5 collective-permute-start.5
  34.7 1.2 %collective-permute-done.5.swap = bf16[1040,128]{1,0:T(8,128)(2,1)S(1)} collective-permute-done((bf16[1040,128]{1,0:T(8,128)(2,1)S(1)}, bf16[1040,128]{1,0:T(8,128)(2,1)S(1)}, u32[]{:S(2)}, u32[]{:S(2)}) %collective-permute-start.5) | collective-permute-done | bytes 266272 | tf_op jit(solution)/shard_map/ppermute | solution.py:470
  35.9 0.8 %shard_map.121 = (bf16[512,128]{1,0:T(8,128)(2,1)S(1)}, f32[512,128]{1,0:T(8,128)S(1)}, f32[512,128]{1,0:T(8,128)S(1)}, f32[256,128]{1,0:T(8,128)}) custom-call(bf16[1040,128]{1,0:T(8,128)(2,1)S(1)} %collective-permute-done.5.swap, f32[512,128]{1,0:T(8,128)S(1)} %get-tuple-element.46.four, f32[512,128]{1,0:T(8,128)S(1)} %get-tuple-element.47.two, ...), custom_call_target="tpu_custom_call" | custom-call | tf_op jit(solution)/shard_map/pallas_call | solution.py:509
  36.6 1.3 %collective-permute-start.6 = (bf16[512,128]{1,0:T(8,128)(2,1)S(1)}, bf16[512,128]{1,0:T(8,128)(2,1)S(1)}, u32[]{:S(2)}, u32[]{:S(2)}) collective-permute-start(bf16[512,128]{1,0:T(8,128)(2,1)S(1)} %get-tuple-element.52), channel_id=1, source_target_pairs={{16,0},{24,8},{32,16},{40,24},{48,32},{56,40},{64,48},{72,56},{80,... | collective-permute-start | bytes 393224 | tf_op jit(solution)/shard_map/ppermute | solution.py:38
  37.9 16.6 %all-to-all-start = ((f32[128,2,128]{2,1,0:T(2,128)}), f32[128,2,128]{2,1,0:T(2,128)S(1)}, u32[]{:S(2)}, u32[]{:S(2)}) async-start(f32[128,2,128]{2,1,0:T(2,128)} %bitcast.4), calls=%async_computation | async-start | bytes 262144 | tf_op jit(solution)/shard_map/all_to_all | solution.py:548
  54.5 0.0 collective-permute-done.6.hop
  54.6 1.3 %collective-permute-start.7 = (bf16[512,128]{1,0:T(8,128)(2,1)S(1)}, bf16[512,128]{1,0:T(8,128)(2,1)S(1)}, u32[]{:S(2)}, u32[]{:S(2)}) collective-permute-start(bf16[512,128]{1,0:T(8,128)(2,1)S(1)} %shard_map.122), channel_id=1, source_target_pairs={{16,0},{24,8},{32,16},{40,24},{48,32},{56,40},{64,48},{72,56},{80,... | collective-permute-start | bytes 393224 | tf_op jit(solution)/shard_map/ppermute | solution.py:38
  55.9 10.1 %all-to-all-done = f32[128,2,128]{2,1,0:T(2,128)S(1)} async-done(((f32[128,2,128]{2,1,0:T(2,128)}), f32[128,2,128]{2,1,0:T(2,128)S(1)}, u32[]{:S(2)}, u32[]{:S(2)}) %all-to-all-start) | async-done | bytes 131104 | tf_op jit(solution)/shard_map/all_to_all | solution.py:548
  65.9 0.0 collective-permute-done.7.hop
  65.9 0.7 %shard_map.123 = (bf16[256,128]{1,0:T(8,128)(2,1)}, bf16[256,128]{1,0:T(8,128)(2,1)}, f32[1,128]{1,0:T(1,128)}, f32[1,128]{1,0:T(1,128)}) custom-call(f32[512,128]{1,0:T(8,128)S(1)} %get-tuple-element.50.own, bf16[512,128]{1,0:T(8,128)(2,1)S(1)} %collective-permute-done.7.hop, f32[256,128]{1,0:T(8,128)S(1)} %bitcast.9), custom_call_target="tpu_custom_call" | custom-call | tf_op jit(solution)/shard_map/pallas_call | solution.py:509
  (4 shorter events, 0.0 us)
Async XLA Ops:
  2.2 12.9 %collective-permute-start.1 = (bf16[528,128]{1,0:T(8,128)(2,1)}, bf16[528,128]{1,0:T(8,128)(2,1)S(1)}, u32[]{:S(2)}, u32[]{:S(2)}) collective-permute-start(bf16[528,128]{1,0:T(8,128)(2,1)} %shard_map.118.b0), channel_id=1, source_target_pairs={{0,16},{8,24},{16,32},{24,40},{32,48},{40,56},{48,64},{56,72},{64,... | collective-permute-start | bytes 405512 | tf_op jit(solution)/shard_map/ppermute | solution.py:38
  6.1 10.3 %collective-permute-start = (bf16[528,128]{1,0:T(8,128)(2,1)}, bf16[528,128]{1,0:T(8,128)(2,1)S(1)}, u32[]{:S(2)}, u32[]{:S(2)}) collective-permute-start(bf16[528,128]{1,0:T(8,128)(2,1)} %shard_map.118.b0), channel_id=1, source_target_pairs={{0,32},{8,40},{16,48},{24,56},{32,64},{40,72},{48,80},{56,88},{64,... | collective-permute-start | bytes 405512 | tf_op jit(solution)/shard_map/ppermute | solution.py:38
  10.5 8.0 %collective-permute-start.2 = (bf16[528,128]{1,0:T(8,128)(2,1)}, bf16[528,128]{1,0:T(8,128)(2,1)S(1)}, u32[]{:S(2)}, u32[]{:S(2)}) collective-permute-start(bf16[528,128]{1,0:T(8,128)(2,1)} %shard_map.118.b0), channel_id=1, source_target_pairs={{0,8},{16,24},{32,40},{48,56},{64,72},{80,88},{96,104},{112,120},{... | collective-permute-start | bytes 405512 | tf_op jit(solution)/shard_map/ppermute | solution.py:470
  11.8 0.7 copy-start.3
  11.8 0.7 copy-start.4
  12.5 1.0 %copy-start.1 = (bf16[256,1024]{1,0:T(8,128)(2,1)S(1)}, bf16[256,1024]{1,0:T(8,128)(2,1)}, u32[]{:S(2)}) copy-start(bf16[256,1024]{1,0:T(8,128)(2,1)} %q_ref.1) | copy-start | bytes 1572868
  13.5 1.0 %copy-start.2 = (bf16[256,1024]{1,0:T(8,128)(2,1)S(1)}, bf16[256,1024]{1,0:T(8,128)(2,1)}, u32[]{:S(2)}) copy-start(bf16[256,1024]{1,0:T(8,128)(2,1)} %d_ref.1) | copy-start | bytes 1572868
  14.5 4.8 %copy-start = (bf16[528,128]{1,0:T(8,128)(2,1)S(1)}, bf16[528,128]{1,0:T(8,128)(2,1)}, u32[]{:S(2)}) copy-start(bf16[528,128]{1,0:T(8,128)(2,1)} %shard_map.118.b0) | copy-start | bytes 405508
  15.1 4.2 %collective-permute-start.3 = (bf16[528,128]{1,0:T(8,128)(2,1)S(1)}, bf16[528,128]{1,0:T(8,128)(2,1)S(1)}, u32[]{:S(2)}, u32[]{:S(2)}) collective-permute-start(bf16[528,128]{1,0:T(8,128)(2,1)S(1)} %collective-permute-done.1.b2), channel_id=1, source_target_pairs={{0,8},{8,0},{16,24},{24,16},{32,40},{40,32},{48,56},{56,48},{64,72... | collective-permute-start | bytes 405512 | tf_op jit(solution)/shard_map/ppermute | solution.py:470
  16.4 2.9 %collective-permute-start.4 = (bf16[528,128]{1,0:T(8,128)(2,1)S(1)}, bf16[528,128]{1,0:T(8,128)(2,1)S(1)}, u32[]{:S(2)}, u32[]{:S(2)}) collective-permute-start(bf16[528,128]{1,0:T(8,128)(2,1)S(1)} %collective-permute-done.b4), channel_id=1, source_target_pairs={{8,0},{24,16},{40,32},{56,48},{72,64},{88,80},{104,96},{120,112},{... | collective-permute-start | bytes 405512 | tf_op jit(solution)/shard_map/ppermute | solution.py:470
  34.2 1.6 %collective-permute-start.5 = (bf16[1040,128]{1,0:T(8,128)(2,1)S(1)}, bf16[1040,128]{1,0:T(8,128)(2,1)S(1)}, u32[]{:S(2)}, u32[]{:S(2)}) collective-permute-start(bf16[1040,128]{1,0:T(8,128)(2,1)S(1)} %get-tuple-element.45), channel_id=1, source_target_pairs={{0,8},{8,0},{16,24},{24,16},{32,40},{40,32},{48,56},{56,48},{64,72... | collective-permute-start | bytes 798728 | tf_op jit(solution)/shard_map/ppermute | solution.py:470
  36.6 17.9 %collective-permute-start.6 = (bf16[512,128]{1,0:T(8,128)(2,1)S(1)}, bf16[512,128]{1,0:T(8,128)(2,1)S(1)}, u32[]{:S(2)}, u32[]{:S(2)}) collective-permute-start(bf16[512,128]{1,0:T(8,128)(2,1)S(1)} %get-tuple-element.52), channel_id=1, source_target_pairs={{16,0},{24,8},{32,16},{40,24},{48,32},{56,40},{64,48},{72,56},{80,... | collective-permute-start | bytes 393224 | tf_op jit(solution)/shard_map/ppermute | solution.py:38
  37.9 28.0 %all-to-all-start = ((f32[128,2,128]{2,1,0:T(2,128)}), f32[128,2,128]{2,1,0:T(2,128)S(1)}, u32[]{:S(2)}, u32[]{:S(2)}) async-start(f32[128,2,128]{2,1,0:T(2,128)} %bitcast.4), calls=%async_computation | async-start | bytes 262144 | tf_op jit(solution)/shard_map/all_to_all | solution.py:548
  54.6 11.4 %collective-permute-start.7 = (bf16[512,128]{1,0:T(8,128)(2,1)S(1)}, bf16[512,128]{1,0:T(8,128)(2,1)S(1)}, u32[]{:S(2)}, u32[]{:S(2)}) collective-permute-start(bf16[512,128]{1,0:T(8,128)(2,1)S(1)} %shard_map.122), channel_id=1, source_target_pairs={{16,0},{24,8},{32,16},{40,24},{48,32},{56,40},{64,48},{72,56},{80,... | collective-permute-start | bytes 393224 | tf_op jit(solution)/shard_map/ppermute | solution.py:38

commit v16 on v13

--- a/solution.py
+++ b/solution.py
@@ -102,7 +102,7 @@
     b4, b2, b0, first_swap, middle_swap, last_swap, xh_ref, scale_ref, dcat, dcat_t, gains_ref, f_ref,
     att_hbm, gq_hbm, four_ref, two_ref, own_ref, swap_ref, gain_ref,
     att_ref, gq_ref, cosine, sine, kext, vwin, khat_t, v_t, qhat, qext_t,
-    s_ref, w_ref, ds_ref, dk, dv, qg_acc, b3, b1, att_sem, gq_sem,
+    s_ref, w_ref, ds_ref, dk, dv, qg_acc, b3, b1, bias, att_sem, gq_sem,
 ):
     even = lax.rem(lax.axis_index("context"), 2) == 0
 
@@ -120,7 +120,6 @@
     lane = lax.broadcasted_iota(jnp.int32, (SUB, HEAD), 1)
     row = lax.broadcasted_iota(jnp.int32, (SUB, HEAD), 0)
     lane_f = lane.astype(jnp.float32)
-    row_f = row.astype(jnp.float32)
     left = lane < HEAD // 2
     parts = WINDOW // SUB
     q_gain = gains_ref[0:1, :]
@@ -136,6 +135,12 @@
         column = jnp.broadcast_to(id_rows[j], (SUB, HEAD)).T
         kext[j * SUB : (j + 1) * SUB, HEAD:] = jnp.where(column == lane_f, 1.0, 0.0).astype(jnp.bfloat16)
         below = below + jnp.where(column < lane_f, 1.0, 0.0)
+        for sub in range(2):
+            if sub <= j < sub + SPAN // SUB:
+                kept = column == id_rows[2 * REACH + sub]
+                if j == sub + SPAN // SUB - 1:
+                    kept = kept & (row <= lane)
+                bias[sub, (j - sub) * SUB : (j - sub + 1) * SUB, :] = jnp.where(kept, 0.0, -1e30)
     first = jnp.sum(below, axis=0, keepdims=True)
 
     def key_part(j):
@@ -163,7 +168,6 @@
     def query_part(pair):
         for sub in range(2):
             window_rows = slice(REACH * TOK + sub * SUB, REACH * TOK + (sub + 1) * SUB)
-            other = jnp.where(row_f == id_rows[2 * REACH + sub], 0.0, -1e30).astype(jnp.bfloat16)
             for g in range(2):
                 at = pair * 512 + sub * 256 + g * SUB
                 lanes = slice(at % 512, at % 512 + SUB)
@@ -171,14 +175,11 @@
                 hat = normed * cosine[window_rows, :] + half_turned(normed) * sine[window_rows, :]
                 qhat[at : at + SUB, :] = hat.astype(jnp.bfloat16)
                 qext_t[pair, 0:HEAD, lanes] = hat.T.astype(jnp.bfloat16)
-                qext_t[pair, HEAD:, lanes] = other
                 yield
 
     dk[...] = jnp.zeros_like(dk)
     dv[...] = jnp.zeros_like(dv)
     qg_acc[...] = jnp.zeros_like(qg_acc)
-    later = jnp.where(row <= lane, 0.0, -1e30)
-    later = jnp.concatenate([later, later], axis=1)
     spans = (slice(0, SPAN), slice(SUB, WINDOW))
     columns_of = (slice(0, 256), slice(256, 512))
 
@@ -192,12 +193,12 @@
     shifts, inverses, centers, queries_t = {}, {}, {}, {}
 
     def scores(pair, sub):
-        q = qext_t[pair, :, columns_of[sub]]
+        q = qext_t[pair, 0:HEAD, columns_of[sub]]
         top = jnp.full((8, 256), -1e30, jnp.float32)
         for start in range(0, SPAN, SUB):
-            s = dot(kext[sub * SUB + start : sub * SUB + start + SUB, :], q)
-            if start + SUB == SPAN:
-                s = s + later
+            s = dot(kext[sub * SUB + start : sub * SUB + start + SUB, 0:HEAD], q)
+            kept = bias[sub, start : start + SUB, :]
+            s = s + jnp.concatenate([kept, kept], axis=1)
             s_ref[pair % 2, sub, start : start + SUB, :] = s
             top = jnp.maximum(top, jnp.max(s.reshape(SUB // 8, 8, 256), axis=0))
             yield
@@ -397,7 +398,7 @@
             pltpu.VMEM((HEAD, WINDOW), bf16),
             pltpu.VMEM((HEAD, WINDOW), bf16),
             pltpu.VMEM((HEADS * TOK, HEAD), bf16),
-            pltpu.VMEM((HEADS // 2, 2 * HEAD, 512), bf16),
+            pltpu.VMEM((HEADS // 2, HEAD, 512), bf16),
             pltpu.VMEM((2, 2, SPAN, 256), f32),
             pltpu.VMEM((2, WINDOW, 512), bf16),
             pltpu.VMEM((2, WINDOW, 512), bf16),
@@ -406,6 +407,7 @@
             pltpu.VMEM((8, HEAD), f32),
             pltpu.VMEM((MSG, HEAD), bf16),
             pltpu.VMEM((MSG, HEAD), bf16),
+            pltpu.VMEM((2, SPAN, SUB), f32),
             pltpu.SemaphoreType.DMA((HEADS // 2,)),
             pltpu.SemaphoreType.DMA((HEADS // 2,)),
         ],

time: 64.4 us -> 65.3 us (1.014)
  Pallas kernels: 15.8 us -> 16.7 us
    pallas_call x1, Pallas kernels: 12.3 us -> 13.2 us  [attention(): pl.pallas_call(kernel, out_shape=[shape((TOK, HEADS * HEAD), bf16), shape...]
where the time goes in v16:
time: 65.3 us; the launch traced here: 64.8 us
  starting transfers between devices  32.5 us (50%)
  Pallas kernels  16.7 us (26%)
  waiting for transfers between devices  12.1 us (19%)
  local copies, waits for them, and re-layouts  2.74 us (4%)
  between operations  0.75 us (1%)
    all_to_all x1, starting transfers between devices, body(): lax.all_to_all(gains.reshape(chips, 2, HEAD), axes, 0, 0, axis_index_grou...  16.6 us
    pallas_call x1, Pallas kernels, attention(): pl.pallas_call(kernel, out_shape=[shape((TOK, HEADS * HEAD), bf16), shape...  13.2 us
    ppermute x4, starting transfers between devices, passed_along(): return lax.ppermute(block, axis, route)  10.9 us
    all_to_all x1, waiting for transfers between devices, body(): lax.all_to_all(gains.reshape(chips, 2, HEAD), axes, 0, 0, axis_index_grou...  10.1 us
    ppermute x4, starting transfers between devices, swapped(): return lax.ppermute(block, 'context', route)  5 us
    unnamed x10, local copies, waits for them, and re-layouts  2.74 us
    ppermute x4, waiting for transfers between devices, swapped(): return lax.ppermute(block, 'context', route)  2.06 us
    pallas_call x1, Pallas kernels, pack(): pl.pallas_call(pack_kernel, out_shape=jax.ShapeDtypeStruct((MSG, HEAD), j...  1.54 us
  transfers between devices with their start and end apart: 9, of which 3 were waited for; matrix products, arithmetic and copies ran while one was open for 0% of the time, Pallas kernels for 1%

profile of v16, /device:TPU:1, one launch (start us, length us, event | category | flops | bytes accessed | tf_op | source)
XLA Modules:
  0.0 64.8 jit_solution(8102066988844847213)
XLA Ops:
  0.6 1.5 %shard_map.118.b0 = bf16[528,128]{1,0:T(8,128)(2,1)} custom-call(bf16[256,128]{1,0:T(8,128)(2,1)} %keys.1, bf16[256,128]{1,0:T(8,128)(2,1)} %values.1, s32[2,128]{1,0:T(2,128)} %bitcast.12), custom_call_target="tpu_custom_call" | custom-call | tf_op jit(solution)/shard_map/pallas_call | solution.py:429
  2.2 3.9 %collective-permute-start.1 = (bf16[528,128]{1,0:T(8,128)(2,1)}, bf16[528,128]{1,0:T(8,128)(2,1)S(1)}, u32[]{:S(2)}, u32[]{:S(2)}) collective-permute-start(bf16[528,128]{1,0:T(8,128)(2,1)} %shard_map.118.b0), channel_id=1, source_target_pairs={{0,16},{8,24},{16,32},{24,40},{32,48},{40,56},{48,64},{56,72},{64,... | collective-permute-start | bytes 405512 | tf_op jit(solution)/shard_map/ppermute | solution.py:38
  6.1 4.4 %collective-permute-start = (bf16[528,128]{1,0:T(8,128)(2,1)}, bf16[528,128]{1,0:T(8,128)(2,1)S(1)}, u32[]{:S(2)}, u32[]{:S(2)}) collective-permute-start(bf16[528,128]{1,0:T(8,128)(2,1)} %shard_map.118.b0), channel_id=1, source_target_pairs={{0,32},{8,40},{16,48},{24,56},{32,64},{40,72},{48,80},{56,88},{64,... | collective-permute-start | bytes 405512 | tf_op jit(solution)/shard_map/ppermute | solution.py:38
  10.5 1.3 %collective-permute-start.2 = (bf16[528,128]{1,0:T(8,128)(2,1)}, bf16[528,128]{1,0:T(8,128)(2,1)S(1)}, u32[]{:S(2)}, u32[]{:S(2)}) collective-permute-start(bf16[528,128]{1,0:T(8,128)(2,1)} %shard_map.118.b0), channel_id=1, source_target_pairs={{0,8},{16,24},{32,40},{48,56},{64,72},{80,88},{96,104},{112,120},{... | collective-permute-start | bytes 405512 | tf_op jit(solution)/shard_map/ppermute | solution.py:439
  11.8 0.0 copy-start.3
  11.8 0.0 copy-start.4
  11.8 0.6 copy-done.3
  12.4 0.0 copy-done.4
  12.5 0.0 copy-start.1
  12.5 1.0 %copy-done.1 = bf16[256,1024]{1,0:T(8,128)(2,1)S(1)} copy-done((bf16[256,1024]{1,0:T(8,128)(2,1)S(1)}, bf16[256,1024]{1,0:T(8,128)(2,1)}, u32[]{:S(2)}) %copy-start.1) | copy-done | bytes 524312
  13.5 1.0 %copy-done.2 = bf16[256,1024]{1,0:T(8,128)(2,1)S(1)} copy-done((bf16[256,1024]{1,0:T(8,128)(2,1)S(1)}, bf16[256,1024]{1,0:T(8,128)(2,1)}, u32[]{:S(2)}) %copy-start.2) | copy-done | bytes 524312
  14.6 0.5 shard_map.119
  15.1 0.0 collective-permute-done.1.b2
  15.1 1.3 %collective-permute-start.3 = (bf16[528,128]{1,0:T(8,128)(2,1)S(1)}, bf16[528,128]{1,0:T(8,128)(2,1)S(1)}, u32[]{:S(2)}, u32[]{:S(2)}) collective-permute-start(bf16[528,128]{1,0:T(8,128)(2,1)S(1)} %collective-permute-done.1.b2), channel_id=1, source_target_pairs={{0,8},{8,0},{16,24},{24,16},{32,40},{40,32},{48,56},{56,48},{64,72... | collective-permute-start | bytes 405512 | tf_op jit(solution)/shard_map/ppermute | solution.py:439
  16.4 0.0 collective-permute-done.b4
  16.4 1.9 %collective-permute-start.4 = (bf16[528,128]{1,0:T(8,128)(2,1)S(1)}, bf16[528,128]{1,0:T(8,128)(2,1)S(1)}, u32[]{:S(2)}, u32[]{:S(2)}) collective-permute-start(bf16[528,128]{1,0:T(8,128)(2,1)S(1)} %collective-permute-done.b4), channel_id=1, source_target_pairs={{8,0},{24,16},{40,32},{56,48},{72,64},{88,80},{104,96},{120,112},{... | collective-permute-start | bytes 405512 | tf_op jit(solution)/shard_map/ppermute | solution.py:439
  18.4 0.1 maximum_bitcast_fusion.f_ref
  18.4 0.0 collective-permute-done.2.first_swap
  18.4 0.9 %collective-permute-done.4.last_swap = bf16[528,128]{1,0:T(8,128)(2,1)S(1)} collective-permute-done((bf16[528,128]{1,0:T(8,128)(2,1)S(1)}, bf16[528,128]{1,0:T(8,128)(2,1)S(1)}, u32[]{:S(2)}, u32[]{:S(2)}) %collective-permute-start.4) | collective-permute-done | bytes 135200 | tf_op jit(solution)/shard_map/ppermute | solution.py:439
  19.3 0.0 collective-permute-done.3.middle_swap
  19.3 0.0 copy-done
  19.3 13.2 %shard_map.120 = (bf16[256,1024]{1,0:T(8,128)(2,1)}, bf16[256,1024]{1,0:T(8,128)(2,1)}, f32[512,128]{1,0:T(8,128)S(1)}, f32[512,128]{1,0:T(8,128)S(1)}, f32[512,...) custom-call(bf16[528,128]{1,0:T(8,128)(2,1)S(1)} %collective-permute-done.b4, ...), custom_call_target="tpu_custom_call" | custom-call | tf_op jit(solution)/shard_map/pallas_call | solution.py:378
  32.5 0.4 collective-permute-start.5
  32.9 1.2 %collective-permute-done.5.swap = bf16[1040,128]{1,0:T(8,128)(2,1)S(1)} collective-permute-done((bf16[1040,128]{1,0:T(8,128)(2,1)S(1)}, bf16[1040,128]{1,0:T(8,128)(2,1)S(1)}, u32[]{:S(2)}, u32[]{:S(2)}) %collective-permute-start.5) | collective-permute-done | bytes 266272 | tf_op jit(solution)/shard_map/ppermute | solution.py:439
  34.1 0.8 %shard_map.121 = (bf16[512,128]{1,0:T(8,128)(2,1)S(1)}, f32[512,128]{1,0:T(8,128)S(1)}, f32[512,128]{1,0:T(8,128)S(1)}, f32[256,128]{1,0:T(8,128)}) custom-call(bf16[1040,128]{1,0:T(8,128)(2,1)S(1)} %collective-permute-done.5.swap, f32[512,128]{1,0:T(8,128)S(1)} %get-tuple-element.46.four, f32[512,128]{1,0:T(8,128)S(1)} %get-tuple-element.47.two, ...), custom_call_target="tpu_custom_call" | custom-call | tf_op jit(solution)/shard_map/pallas_call | solution.py:478
  34.9 1.3 %collective-permute-start.6 = (bf16[512,128]{1,0:T(8,128)(2,1)S(1)}, bf16[512,128]{1,0:T(8,128)(2,1)S(1)}, u32[]{:S(2)}, u32[]{:S(2)}) collective-permute-start(bf16[512,128]{1,0:T(8,128)(2,1)S(1)} %get-tuple-element.52), channel_id=1, source_target_pairs={{16,0},{24,8},{32,16},{40,24},{48,32},{56,40},{64,48},{72,56},{80,... | collective-permute-start | bytes 393224 | tf_op jit(solution)/shard_map/ppermute | solution.py:38
  36.2 16.6 %all-to-all-start = ((f32[128,2,128]{2,1,0:T(2,128)}), f32[128,2,128]{2,1,0:T(2,128)S(1)}, u32[]{:S(2)}, u32[]{:S(2)}) async-start(f32[128,2,128]{2,1,0:T(2,128)} %bitcast.4), calls=%async_computation | async-start | bytes 262144 | tf_op jit(solution)/shard_map/all_to_all | solution.py:517
  52.7 0.0 collective-permute-done.6.hop
  52.8 1.3 %collective-permute-start.7 = (bf16[512,128]{1,0:T(8,128)(2,1)S(1)}, bf16[512,128]{1,0:T(8,128)(2,1)S(1)}, u32[]{:S(2)}, u32[]{:S(2)}) collective-permute-start(bf16[512,128]{1,0:T(8,128)(2,1)S(1)} %shard_map.122), channel_id=1, source_target_pairs={{16,0},{24,8},{32,16},{40,24},{48,32},{56,40},{64,48},{72,56},{80,... | collective-permute-start | bytes 393224 | tf_op jit(solution)/shard_map/ppermute | solution.py:38
  54.1 10.1 %all-to-all-done = f32[128,2,128]{2,1,0:T(2,128)S(1)} async-done(((f32[128,2,128]{2,1,0:T(2,128)}), f32[128,2,128]{2,1,0:T(2,128)S(1)}, u32[]{:S(2)}, u32[]{:S(2)}) %all-to-all-start) | async-done | bytes 131104 | tf_op jit(solution)/shard_map/all_to_all | solution.py:517
  64.1 0.0 collective-permute-done.7.hop
  64.1 0.7 %shard_map.123 = (bf16[256,128]{1,0:T(8,128)(2,1)}, bf16[256,128]{1,0:T(8,128)(2,1)}, f32[1,128]{1,0:T(1,128)}, f32[1,128]{1,0:T(1,128)}) custom-call(f32[512,128]{1,0:T(8,128)S(1)} %get-tuple-element.50.own, bf16[512,128]{1,0:T(8,128)(2,1)S(1)} %collective-permute-done.7.hop, f32[256,128]{1,0:T(8,128)S(1)} %bitcast.9), custom_call_target="tpu_custom_call" | custom-call | tf_op jit(solution)/shard_map/pallas_call | solution.py:478
  (4 shorter events, 0.0 us)
Async XLA Ops:
  2.2 12.9 %collective-permute-start.1 = (bf16[528,128]{1,0:T(8,128)(2,1)}, bf16[528,128]{1,0:T(8,128)(2,1)S(1)}, u32[]{:S(2)}, u32[]{:S(2)}) collective-permute-start(bf16[528,128]{1,0:T(8,128)(2,1)} %shard_map.118.b0), channel_id=1, source_target_pairs={{0,16},{8,24},{16,32},{24,40},{32,48},{40,56},{48,64},{56,72},{64,... | collective-permute-start | bytes 405512 | tf_op jit(solution)/shard_map/ppermute | solution.py:38
  6.1 10.3 %collective-permute-start = (bf16[528,128]{1,0:T(8,128)(2,1)}, bf16[528,128]{1,0:T(8,128)(2,1)S(1)}, u32[]{:S(2)}, u32[]{:S(2)}) collective-permute-start(bf16[528,128]{1,0:T(8,128)(2,1)} %shard_map.118.b0), channel_id=1, source_target_pairs={{0,32},{8,40},{16,48},{24,56},{32,64},{40,72},{48,80},{56,88},{64,... | collective-permute-start | bytes 405512 | tf_op jit(solution)/shard_map/ppermute | solution.py:38
  10.5 8.0 %collective-permute-start.2 = (bf16[528,128]{1,0:T(8,128)(2,1)}, bf16[528,128]{1,0:T(8,128)(2,1)S(1)}, u32[]{:S(2)}, u32[]{:S(2)}) collective-permute-start(bf16[528,128]{1,0:T(8,128)(2,1)} %shard_map.118.b0), channel_id=1, source_target_pairs={{0,8},{16,24},{32,40},{48,56},{64,72},{80,88},{96,104},{112,120},{... | collective-permute-start | bytes 405512 | tf_op jit(solution)/shard_map/ppermute | solution.py:439
  11.8 0.7 %copy-start.3 = (f32[128]{0:T(128)S(1)}, f32[128]{0:T(128)}, u32[]{:S(2)}) copy-start(f32[128]{0:T(128)} %param.11) | copy-start | bytes 1540
  11.8 0.7 %copy-start.4 = (f32[128]{0:T(128)S(1)}, f32[128]{0:T(128)}, u32[]{:S(2)}) copy-start(f32[128]{0:T(128)} %param.12) | copy-start | bytes 1540
  12.5 1.0 %copy-start.1 = (bf16[256,1024]{1,0:T(8,128)(2,1)S(1)}, bf16[256,1024]{1,0:T(8,128)(2,1)}, u32[]{:S(2)}) copy-start(bf16[256,1024]{1,0:T(8,128)(2,1)} %q_ref.1) | copy-start | bytes 1572868
  13.5 1.0 %copy-start.2 = (bf16[256,1024]{1,0:T(8,128)(2,1)S(1)}, bf16[256,1024]{1,0:T(8,128)(2,1)}, u32[]{:S(2)}) copy-start(bf16[256,1024]{1,0:T(8,128)(2,1)} %d_ref.1) | copy-start | bytes 1572868
  14.5 4.8 %copy-start = (bf16[528,128]{1,0:T(8,128)(2,1)S(1)}, bf16[528,128]{1,0:T(8,128)(2,1)}, u32[]{:S(2)}) copy-start(bf16[528,128]{1,0:T(8,128)(2,1)} %shard_map.118.b0) | copy-start | bytes 405508
  15.1 4.2 %collective-permute-start.3 = (bf16[528,128]{1,0:T(8,128)(2,1)S(1)}, bf16[528,128]{1,0:T(8,128)(2,1)S(1)}, u32[]{:S(2)}, u32[]{:S(2)}) collective-permute-start(bf16[528,128]{1,0:T(8,128)(2,1)S(1)} %collective-permute-done.1.b2), channel_id=1, source_target_pairs={{0,8},{8,0},{16,24},{24,16},{32,40},{40,32},{48,56},{56,48},{64,72... | collective-permute-start | bytes 405512 | tf_op jit(solution)/shard_map/ppermute | solution.py:439
  16.4 2.9 %collective-permute-start.4 = (bf16[528,128]{1,0:T(8,128)(2,1)S(1)}, bf16[528,128]{1,0:T(8,128)(2,1)S(1)}, u32[]{:S(2)}, u32[]{:S(2)}) collective-permute-start(bf16[528,128]{1,0:T(8,128)(2,1)S(1)} %collective-permute-done.b4), channel_id=1, source_target_pairs={{8,0},{24,16},{40,32},{56,48},{72,64},{88,80},{104,96},{120,112},{... | collective-permute-start | bytes 405512 | tf_op jit(solution)/shard_map/ppermute | solution.py:439
  32.5 1.6 %collective-permute-start.5 = (bf16[1040,128]{1,0:T(8,128)(2,1)S(1)}, bf16[1040,128]{1,0:T(8,128)(2,1)S(1)}, u32[]{:S(2)}, u32[]{:S(2)}) collective-permute-start(bf16[1040,128]{1,0:T(8,128)(2,1)S(1)} %get-tuple-element.45), channel_id=1, source_target_pairs={{0,8},{8,0},{16,24},{24,16},{32,40},{40,32},{48,56},{56,48},{64,72... | collective-permute-start | bytes 798728 | tf_op jit(solution)/shard_map/ppermute | solution.py:439
  34.9 17.9 %collective-permute-start.6 = (bf16[512,128]{1,0:T(8,128)(2,1)S(1)}, bf16[512,128]{1,0:T(8,128)(2,1)S(1)}, u32[]{:S(2)}, u32[]{:S(2)}) collective-permute-start(bf16[512,128]{1,0:T(8,128)(2,1)S(1)} %get-tuple-element.52), channel_id=1, source_target_pairs={{16,0},{24,8},{32,16},{40,24},{48,32},{56,40},{64,48},{72,56},{80,... | collective-permute-start | bytes 393224 | tf_op jit(solution)/shard_map/ppermute | solution.py:38
  36.2 28.0 %all-to-all-start = ((f32[128,2,128]{2,1,0:T(2,128)}), f32[128,2,128]{2,1,0:T(2,128)S(1)}, u32[]{:S(2)}, u32[]{:S(2)}) async-start(f32[128,2,128]{2,1,0:T(2,128)} %bitcast.4), calls=%async_computation | async-start | bytes 262144 | tf_op jit(solution)/shard_map/all_to_all | solution.py:517
  52.8 11.4 %collective-permute-start.7 = (bf16[512,128]{1,0:T(8,128)(2,1)S(1)}, bf16[512,128]{1,0:T(8,128)(2,1)S(1)}, u32[]{:S(2)}, u32[]{:S(2)}) collective-permute-start(bf16[512,128]{1,0:T(8,128)(2,1)S(1)} %shard_map.122), channel_id=1, source_target_pairs={{16,0},{24,8},{32,16},{40,24},{48,32},{56,40},{64,48},{72,56},{80,... | collective-permute-start | bytes 393224 | tf_op jit(solution)/shard_map/ppermute | solution.py:38

commit v17 on v13

--- a/solution.py
+++ b/solution.py
@@ -100,7 +100,7 @@
 
 def kernel(
     b4, b2, b0, first_swap, middle_swap, last_swap, xh_ref, scale_ref, dcat, dcat_t, gains_ref, f_ref,
-    att_hbm, gq_hbm, four_ref, two_ref, own_ref, swap_ref, gain_ref,
+    att_hbm, gq_hbm, four_ref, two_ref, own_ref, swap_ref, near_ref, gain_ref,
     att_ref, gq_ref, cosine, sine, kext, vwin, khat_t, v_t, qhat, qext_t,
     s_ref, w_ref, ds_ref, dk, dv, qg_acc, b3, b1, att_sem, gq_sem,
 ):
@@ -320,7 +320,7 @@
     last = HEADS // 2 - 1
     weave(query_sums(last, 1))
 
-    outs = ((four_ref, 0), (swap_ref, 2 * TOK), (two_ref, 0), (swap_ref, 0), (own_ref, 0))
+    outs = ((four_ref, 0), (swap_ref, 0), (two_ref, 0), (near_ref, 0), (own_ref, 0))
     k_sums = [jnp.zeros((8, HEAD), jnp.float32)]
 
     def key_ends(j):
@@ -361,7 +361,7 @@
     high = gains.astype(jnp.bfloat16).astype(jnp.float32)
     middle = (gains - high).astype(jnp.bfloat16).astype(jnp.float32)
     low = gains - high - middle
-    swap_ref[4 * TOK :, :] = jnp.concatenate(
+    swap_ref[2 * TOK :, :] = jnp.concatenate(
         [high, middle, low, jnp.zeros((ID_ROWS - 6, HEAD), jnp.float32)]
     ).astype(jnp.bfloat16)
     for pair in range(HEADS // 2):
@@ -382,11 +382,12 @@
             shape((2 * TOK, HEAD), f32),
             shape((2 * TOK, HEAD), f32),
             shape((2 * TOK, HEAD), f32),
-            shape((4 * TOK + ID_ROWS, HEAD), bf16),
+            shape((2 * TOK + ID_ROWS, HEAD), bf16),
+            shape((2 * TOK, HEAD), bf16),
             shape((2, HEAD), f32),
         ],
         in_specs=[vmem] * 12,
-        out_specs=[hbm] * 2 + [vmem] * 5,
+        out_specs=[hbm] * 2 + [vmem] * 6,
         scratch_shapes=[
             pltpu.VMEM((TOK, HEADS * HEAD), bf16),
             pltpu.VMEM((TOK, HEADS * HEAD), bf16),
@@ -437,33 +438,26 @@
     return lax.ppermute(block, "context", route)
 
 
-def chip_kernel(swap, four, two, own, gains, four_out, two_out, own_out, gains_out):
-    even = lax.rem(lax.axis_index("context"), 2) == 0
-    one, three = slice(0, 2 * TOK), slice(2 * TOK, 4 * TOK)
-
-    @pl.when(even)
-    def _():
-        four_out[...] = four[...].astype(jnp.bfloat16)
-        two_out[...] = two[...] + swap[three, :].astype(jnp.float32)
-        own_out[...] = own[...] + swap[one, :].astype(jnp.float32)
-
-    @pl.when(jnp.logical_not(even))
-    def _():
-        four_out[...] = (four[...] + swap[three, :].astype(jnp.float32)).astype(jnp.bfloat16)
-        two_out[...] = two[...] + swap[one, :].astype(jnp.float32)
-        own_out[...] = own[...]
-
-    split = swap[4 * TOK :, :].astype(jnp.float32)
+def on_even():
+    return lax.rem(lax.axis_index("context"), 2) == 0
+
+
+def chip_kernel(swap, four, gains, four_out, gains_out):
+    far = jnp.where(on_even(), 0.0, swap[0 : 2 * TOK, :].astype(jnp.float32))
+    four_out[...] = (four[...] + far).astype(jnp.bfloat16)
+    split = swap[2 * TOK :, :].astype(jnp.float32)
     total = gains[...] + ((split[0:2] + split[2:4]) + split[4:6])
     gains_out[...] = jnp.concatenate([total] * (gains_out.shape[0] // 2))
 
 
-def hop_kernel(two, hop, two_out):
-    two_out[...] = (two[...] + hop[...].astype(jnp.float32)).astype(jnp.bfloat16)
-
-
-def last_kernel(own, hop, terms, keys, values, q_gain, k_gain):
-    total = (own[...] + hop[...].astype(jnp.float32)).astype(jnp.bfloat16)
+def hop_kernel(two, hop, swap, near, two_out):
+    other = jnp.where(on_even(), swap[0 : 2 * TOK, :].astype(jnp.float32), near[...].astype(jnp.float32))
+    two_out[...] = ((two[...] + other) + hop[...].astype(jnp.float32)).astype(jnp.bfloat16)
+
+
+def last_kernel(own, hop, near, terms, keys, values, q_gain, k_gain):
+    other = jnp.where(on_even(), near[...].astype(jnp.float32), 0.0)
+    total = ((own[...] + other) + hop[...].astype(jnp.float32)).astype(jnp.bfloat16)
     keys[...] = total[:TOK]
     values[...] = total[TOK:]
     gains = jnp.sum(terms[...].reshape(-1, 8, HEAD), axis=0)
@@ -496,16 +490,16 @@
     half = jnp.arange(HEAD // 2, dtype=jnp.float32)
     frequency = THETA ** (-(half * 2.0 / HEAD))
     frequency = jnp.concatenate([frequency, frequency]).reshape(1, HEAD)
-    attended, query_gradient, four, two, own, swap, gains = attention(blocks, prepared, frequency)
+    attended, query_gradient, four, two, own, swap, near, gains = attention(blocks, prepared, frequency)
 
     axes = ("context", "tensor")
     chips = lax.axis_size(axes) // 2
     block = (2 * TOK, HEAD)
-    four, two, own, gains = small_call(
-        chip_kernel,
-        [(block, bf16), (block, f32), (block, f32), ((2 * chips, HEAD), f32)],
-        *(swapped(swap), four, two, own, gains),
+    swap = swapped(swap)
+    four, gains = small_call(
+        chip_kernel, [(block, bf16), ((2 * chips, HEAD), f32)], swap, four, gains
     )
+    near = swapped(near)
     hop = passed_along(four, "context", -2)
     width = lax.axis_size("tensor")
     cores = [
@@ -514,13 +508,13 @@
     ]
     gains = lax.all_to_all(gains.reshape(chips, 2, HEAD), axes, 0, 0, axis_index_groups=cores)
     gains = gains.reshape(2 * chips, HEAD)
-    (two,) = small_call(hop_kernel, [(block, bf16)], two, hop)
+    (two,) = small_call(hop_kernel, [(block, bf16)], two, hop, swap, near)
     hop = passed_along(two, "context", -2)
     half_block = (TOK, HEAD)
     key_gradient, value_gradient, q_total, k_total = small_call(
         last_kernel,
         [(half_block, bf16), (half_block, bf16), ((1, HEAD), f32), ((1, HEAD), f32)],
-        *(own, hop, gains),
+        *(own, hop, near, gains),
     )
     return (
         attended,

time: 64.4 us -> 64.6 us (level)
    ppermute x4 -> x5, waiting for transfers between devices: 2.06 us -> 1.72 us  [swapped(): return lax.ppermute(block, 'context', route)]
    ppermute x4 -> x5, starting transfers between devices: 5 us -> 5.33 us  [swapped(): return lax.ppermute(block, 'context', route)]
  transfers between devices with their start and end apart: 9 -> 10, of which waited for: 3 -> 3; matrix products, arithmetic and copies ran while one was open for 0% -> 0% of each run, Pallas kernels for 1% -> 2%
where the time goes in v17:
time: 64.6 us; the launch traced here: 64.2 us
  starting transfers between devices  32.8 us (51%)
  Pallas kernels  16.1 us (25%)
  waiting for transfers between devices  11.7 us (18%)
  local copies, waits for them, and re-layouts  2.74 us (4%)
  between operations  0.76 us (1%)
    all_to_all x1, starting transfers between devices, body(): lax.all_to_all(gains.reshape(chips, 2, HEAD), axes, 0, 0, axis_index_grou...  16.6 us
    pallas_call x1, Pallas kernels, attention(): pl.pallas_call(kernel, out_shape=[shape((TOK, HEADS * HEAD), bf16), shape...  12.6 us
    ppermute x4, starting transfers between devices, passed_along(): return lax.ppermute(block, axis, route)  10.9 us
    all_to_all x1, waiting for transfers between devices, body(): lax.all_to_all(gains.reshape(chips, 2, HEAD), axes, 0, 0, axis_index_grou...  10 us
    ppermute x5, starting transfers between devices, swapped(): return lax.ppermute(block, 'context', route)  5.33 us
    unnamed x10, local copies, waits for them, and re-layouts  2.74 us
    ppermute x5, waiting for transfers between devices, swapped(): return lax.ppermute(block, 'context', route)  1.72 us
    pallas_call x1, Pallas kernels, pack(): pl.pallas_call(pack_kernel, out_shape=jax.ShapeDtypeStruct((MSG, HEAD), j...  1.54 us
  transfers between devices with their start and end apart: 10, of which 3 were waited for; matrix products, arithmetic and copies ran while one was open for 0% of the time, Pallas kernels for 2%

profile of v17, /device:TPU:1, one launch (start us, length us, event | category | flops | bytes accessed | tf_op | source)
XLA Modules:
  0.0 64.2 jit_solution(13915035092291010666)
XLA Ops:
  0.6 1.5 %shard_map.118.b0 = bf16[528,128]{1,0:T(8,128)(2,1)} custom-call(bf16[256,128]{1,0:T(8,128)(2,1)} %keys.1, bf16[256,128]{1,0:T(8,128)(2,1)} %values.1, s32[2,128]{1,0:T(2,128)} %bitcast.12), custom_call_target="tpu_custom_call" | custom-call | tf_op jit(solution)/shard_map/pallas_call | solution.py:428
  2.2 3.9 %collective-permute-start.1 = (bf16[528,128]{1,0:T(8,128)(2,1)}, bf16[528,128]{1,0:T(8,128)(2,1)S(1)}, u32[]{:S(2)}, u32[]{:S(2)}) collective-permute-start(bf16[528,128]{1,0:T(8,128)(2,1)} %shard_map.118.b0), channel_id=1, source_target_pairs={{0,16},{8,24},{16,32},{24,40},{32,48},{40,56},{48,64},{56,72},{64,... | collective-permute-start | bytes 405512 | tf_op jit(solution)/shard_map/ppermute | solution.py:38
  6.1 4.4 %collective-permute-start = (bf16[528,128]{1,0:T(8,128)(2,1)}, bf16[528,128]{1,0:T(8,128)(2,1)S(1)}, u32[]{:S(2)}, u32[]{:S(2)}) collective-permute-start(bf16[528,128]{1,0:T(8,128)(2,1)} %shard_map.118.b0), channel_id=1, source_target_pairs={{0,32},{8,40},{16,48},{24,56},{32,64},{40,72},{48,80},{56,88},{64,... | collective-permute-start | bytes 405512 | tf_op jit(solution)/shard_map/ppermute | solution.py:38
  10.5 1.3 %collective-permute-start.2 = (bf16[528,128]{1,0:T(8,128)(2,1)}, bf16[528,128]{1,0:T(8,128)(2,1)S(1)}, u32[]{:S(2)}, u32[]{:S(2)}) collective-permute-start(bf16[528,128]{1,0:T(8,128)(2,1)} %shard_map.118.b0), channel_id=1, source_target_pairs={{0,8},{16,24},{32,40},{48,56},{64,72},{80,88},{96,104},{112,120},{... | collective-permute-start | bytes 405512 | tf_op jit(solution)/shard_map/ppermute | solution.py:438
  11.8 0.0 copy-start.3
  11.8 0.0 copy-start.4
  11.8 0.6 copy-done.3
  12.4 0.0 copy-done.4
  12.5 1.0 %copy-done.1 = bf16[256,1024]{1,0:T(8,128)(2,1)S(1)} copy-done((bf16[256,1024]{1,0:T(8,128)(2,1)S(1)}, bf16[256,1024]{1,0:T(8,128)(2,1)}, u32[]{:S(2)}) %copy-start.1) | copy-done | bytes 524312
  13.5 1.0 %copy-done.2 = bf16[256,1024]{1,0:T(8,128)(2,1)S(1)} copy-done((bf16[256,1024]{1,0:T(8,128)(2,1)S(1)}, bf16[256,1024]{1,0:T(8,128)(2,1)}, u32[]{:S(2)}) %copy-start.2) | copy-done | bytes 524312
  14.6 0.5 shard_map.119
  15.1 0.0 collective-permute-done.1.b2
  15.1 1.3 %collective-permute-start.3 = (bf16[528,128]{1,0:T(8,128)(2,1)S(1)}, bf16[528,128]{1,0:T(8,128)(2,1)S(1)}, u32[]{:S(2)}, u32[]{:S(2)}) collective-permute-start(bf16[528,128]{1,0:T(8,128)(2,1)S(1)} %collective-permute-done.1.b2), channel_id=1, source_target_pairs={{0,8},{8,0},{16,24},{24,16},{32,40},{40,32},{48,56},{56,48},{64,72... | collective-permute-start | bytes 405512 | tf_op jit(solution)/shard_map/ppermute | solution.py:438
  16.4 0.0 collective-permute-done.b4
  16.4 1.9 %collective-permute-start.4 = (bf16[528,128]{1,0:T(8,128)(2,1)S(1)}, bf16[528,128]{1,0:T(8,128)(2,1)S(1)}, u32[]{:S(2)}, u32[]{:S(2)}) collective-permute-start(bf16[528,128]{1,0:T(8,128)(2,1)S(1)} %collective-permute-done.b4), channel_id=1, source_target_pairs={{8,0},{24,16},{40,32},{56,48},{72,64},{88,80},{104,96},{120,112},{... | collective-permute-start | bytes 405512 | tf_op jit(solution)/shard_map/ppermute | solution.py:438
  18.4 0.1 maximum_bitcast_fusion.f_ref
  18.4 0.0 collective-permute-done.2.first_swap
  18.4 0.9 %collective-permute-done.4.last_swap = bf16[528,128]{1,0:T(8,128)(2,1)S(1)} collective-permute-done((bf16[528,128]{1,0:T(8,128)(2,1)S(1)}, bf16[528,128]{1,0:T(8,128)(2,1)S(1)}, u32[]{:S(2)}, u32[]{:S(2)}) %collective-permute-start.4) | collective-permute-done | bytes 135200 | tf_op jit(solution)/shard_map/ppermute | solution.py:438
  19.3 0.0 collective-permute-done.3.middle_swap
  19.3 12.6 %shard_map.120 = (bf16[256,1024]{1,0:T(8,128)(2,1)}, bf16[256,1024]{1,0:T(8,128)(2,1)}, f32[512,128]{1,0:T(8,128)S(1)}, f32[512,128]{1,0:T(8,128)S(1)}, f32[512,...) custom-call(bf16[528,128]{1,0:T(8,128)(2,1)S(1)} %collective-permute-done.b4, ...), custom_call_target="tpu_custom_call" | custom-call | tf_op jit(solution)/shard_map/pallas_call | solution.py:377
  31.9 0.6 collective-permute-start.5
  32.5 0.1 collective-permute-start.7
  32.7 0.8 %collective-permute-done.5.swap = bf16[528,128]{1,0:T(8,128)(2,1)S(1)} collective-permute-done((bf16[528,128]{1,0:T(8,128)(2,1)S(1)}, bf16[528,128]{1,0:T(8,128)(2,1)S(1)}, u32[]{:S(2)}, u32[]{:S(2)}) %collective-permute-start.5) | collective-permute-done | bytes 135200 | tf_op jit(solution)/shard_map/ppermute | solution.py:438
  33.5 0.7 %shard_map.121 = (bf16[512,128]{1,0:T(8,128)(2,1)S(1)}, f32[256,128]{1,0:T(8,128)}) custom-call(bf16[528,128]{1,0:T(8,128)(2,1)S(1)} %collective-permute-done.5.swap, f32[512,128]{1,0:T(8,128)S(1)} %get-tuple-element.47.four, f32[2,128]{1,0:T(2,128)S(1)} %get-tuple-element.48.gains), custom_call_target="tpu_custom_call" | custom-call | tf_op jit(solution)/shard_map/pallas_call | solution.py:470
  34.2 1.3 %collective-permute-start.6 = (bf16[512,128]{1,0:T(8,128)(2,1)S(1)}, bf16[512,128]{1,0:T(8,128)(2,1)S(1)}, u32[]{:S(2)}, u32[]{:S(2)}) collective-permute-start(bf16[512,128]{1,0:T(8,128)(2,1)S(1)} %get-tuple-element.49), channel_id=1, source_target_pairs={{16,0},{24,8},{32,16},{40,24},{48,32},{56,40},{64,48},{72,56},{80,... | collective-permute-start | bytes 393224 | tf_op jit(solution)/shard_map/ppermute | solution.py:38
  35.5 16.6 %all-to-all-start = ((f32[128,2,128]{2,1,0:T(2,128)}), f32[128,2,128]{2,1,0:T(2,128)S(1)}, u32[]{:S(2)}, u32[]{:S(2)}) async-start(f32[128,2,128]{2,1,0:T(2,128)} %bitcast.4), calls=%async_computation | async-start | bytes 262144 | tf_op jit(solution)/shard_map/all_to_all | solution.py:509
  52.1 0.0 collective-permute-done.7.near
  52.1 0.0 collective-permute-done.6.hop
  52.1 0.1 shard_map.122
  52.2 1.3 %collective-permute-start.8 = (bf16[512,128]{1,0:T(8,128)(2,1)S(1)}, bf16[512,128]{1,0:T(8,128)(2,1)S(1)}, u32[]{:S(2)}, u32[]{:S(2)}) collective-permute-start(bf16[512,128]{1,0:T(8,128)(2,1)S(1)} %shard_map.122), channel_id=1, source_target_pairs={{16,0},{24,8},{32,16},{40,24},{48,32},{56,40},{64,48},{72,56},{80,... | collective-permute-start | bytes 393224 | tf_op jit(solution)/shard_map/ppermute | solution.py:38
  53.5 10.0 %all-to-all-done = f32[128,2,128]{2,1,0:T(2,128)S(1)} async-done(((f32[128,2,128]{2,1,0:T(2,128)}), f32[128,2,128]{2,1,0:T(2,128)S(1)}, u32[]{:S(2)}, u32[]{:S(2)}) %all-to-all-start) | async-done | bytes 131104 | tf_op jit(solution)/shard_map/all_to_all | solution.py:509
  63.5 0.7 %shard_map.123 = (bf16[256,128]{1,0:T(8,128)(2,1)}, bf16[256,128]{1,0:T(8,128)(2,1)}, f32[1,128]{1,0:T(1,128)}, f32[1,128]{1,0:T(1,128)}) custom-call(f32[512,128]{1,0:T(8,128)S(1)} %get-tuple-element.44.own, bf16[512,128]{1,0:T(8,128)(2,1)S(1)} %collective-permute-done.8.hop, bf16[512,128]{1,0:T(8,128)(2,1)S(1)} %collective-permute-done.7.near, ...), custom_call_target="tpu_custom_call" | custom-call | tf_op jit(solution)/shard_map/pallas_call | solution.py:470
  (6 shorter events, 0.0 us)
Async XLA Ops:
  2.2 12.9 %collective-permute-start.1 = (bf16[528,128]{1,0:T(8,128)(2,1)}, bf16[528,128]{1,0:T(8,128)(2,1)S(1)}, u32[]{:S(2)}, u32[]{:S(2)}) collective-permute-start(bf16[528,128]{1,0:T(8,128)(2,1)} %shard_map.118.b0), channel_id=1, source_target_pairs={{0,16},{8,24},{16,32},{24,40},{32,48},{40,56},{48,64},{56,72},{64,... | collective-permute-start | bytes 405512 | tf_op jit(solution)/shard_map/ppermute | solution.py:38
  6.1 10.3 %collective-permute-start = (bf16[528,128]{1,0:T(8,128)(2,1)}, bf16[528,128]{1,0:T(8,128)(2,1)S(1)}, u32[]{:S(2)}, u32[]{:S(2)}) collective-permute-start(bf16[528,128]{1,0:T(8,128)(2,1)} %shard_map.118.b0), channel_id=1, source_target_pairs={{0,32},{8,40},{16,48},{24,56},{32,64},{40,72},{48,80},{56,88},{64,... | collective-permute-start | bytes 405512 | tf_op jit(solution)/shard_map/ppermute | solution.py:38
  10.5 8.0 %collective-permute-start.2 = (bf16[528,128]{1,0:T(8,128)(2,1)}, bf16[528,128]{1,0:T(8,128)(2,1)S(1)}, u32[]{:S(2)}, u32[]{:S(2)}) collective-permute-start(bf16[528,128]{1,0:T(8,128)(2,1)} %shard_map.118.b0), channel_id=1, source_target_pairs={{0,8},{16,24},{32,40},{48,56},{64,72},{80,88},{96,104},{112,120},{... | collective-permute-start | bytes 405512 | tf_op jit(solution)/shard_map/ppermute | solution.py:438
  11.8 0.7 %copy-start.3 = (f32[128]{0:T(128)S(1)}, f32[128]{0:T(128)}, u32[]{:S(2)}) copy-start(f32[128]{0:T(128)} %param.11) | copy-start | bytes 1540
  11.8 0.7 %copy-start.4 = (f32[128]{0:T(128)S(1)}, f32[128]{0:T(128)}, u32[]{:S(2)}) copy-start(f32[128]{0:T(128)} %param.12) | copy-start | bytes 1540
  12.5 1.0 %copy-start.1 = (bf16[256,1024]{1,0:T(8,128)(2,1)S(1)}, bf16[256,1024]{1,0:T(8,128)(2,1)}, u32[]{:S(2)}) copy-start(bf16[256,1024]{1,0:T(8,128)(2,1)} %q_ref.1) | copy-start | bytes 1572868
  13.5 1.0 %copy-start.2 = (bf16[256,1024]{1,0:T(8,128)(2,1)S(1)}, bf16[256,1024]{1,0:T(8,128)(2,1)}, u32[]{:S(2)}) copy-start(bf16[256,1024]{1,0:T(8,128)(2,1)} %d_ref.1) | copy-start | bytes 1572868
  14.5 4.8 %copy-start = (bf16[528,128]{1,0:T(8,128)(2,1)S(1)}, bf16[528,128]{1,0:T(8,128)(2,1)}, u32[]{:S(2)}) copy-start(bf16[528,128]{1,0:T(8,128)(2,1)} %shard_map.118.b0) | copy-start | bytes 405508
  15.1 4.2 %collective-permute-start.3 = (bf16[528,128]{1,0:T(8,128)(2,1)S(1)}, bf16[528,128]{1,0:T(8,128)(2,1)S(1)}, u32[]{:S(2)}, u32[]{:S(2)}) collective-permute-start(bf16[528,128]{1,0:T(8,128)(2,1)S(1)} %collective-permute-done.1.b2), channel_id=1, source_target_pairs={{0,8},{8,0},{16,24},{24,16},{32,40},{40,32},{48,56},{56,48},{64,72... | collective-permute-start | bytes 405512 | tf_op jit(solution)/shard_map/ppermute | solution.py:438
  16.4 2.9 %collective-permute-start.4 = (bf16[528,128]{1,0:T(8,128)(2,1)S(1)}, bf16[528,128]{1,0:T(8,128)(2,1)S(1)}, u32[]{:S(2)}, u32[]{:S(2)}) collective-permute-start(bf16[528,128]{1,0:T(8,128)(2,1)S(1)} %collective-permute-done.b4), channel_id=1, source_target_pairs={{8,0},{24,16},{40,32},{56,48},{72,64},{88,80},{104,96},{120,112},{... | collective-permute-start | bytes 405512 | tf_op jit(solution)/shard_map/ppermute | solution.py:438
  31.9 1.6 %collective-permute-start.5 = (bf16[528,128]{1,0:T(8,128)(2,1)S(1)}, bf16[528,128]{1,0:T(8,128)(2,1)S(1)}, u32[]{:S(2)}, u32[]{:S(2)}) collective-permute-start(bf16[528,128]{1,0:T(8,128)(2,1)S(1)} %get-tuple-element.46), channel_id=1, source_target_pairs={{0,8},{8,0},{16,24},{24,16},{32,40},{40,32},{48,56},{56,48},{64,72... | collective-permute-start | bytes 405512 | tf_op jit(solution)/shard_map/ppermute | solution.py:438
  32.5 19.5 %collective-permute-start.7 = (bf16[512,128]{1,0:T(8,128)(2,1)S(1)}, bf16[512,128]{1,0:T(8,128)(2,1)S(1)}, u32[]{:S(2)}, u32[]{:S(2)}) collective-permute-start(bf16[512,128]{1,0:T(8,128)(2,1)S(1)} %get-tuple-element.50), channel_id=1, source_target_pairs={{0,8},{8,0},{16,24},{24,16},{32,40},{40,32},{48,56},{56,48},{64,72... | collective-permute-start | bytes 393224 | tf_op jit(solution)/shard_map/ppermute | solution.py:438
  34.2 17.9 %collective-permute-start.6 = (bf16[512,128]{1,0:T(8,128)(2,1)S(1)}, bf16[512,128]{1,0:T(8,128)(2,1)S(1)}, u32[]{:S(2)}, u32[]{:S(2)}) collective-permute-start(bf16[512,128]{1,0:T(8,128)(2,1)S(1)} %get-tuple-element.49), channel_id=1, source_target_pairs={{16,0},{24,8},{32,16},{40,24},{48,32},{56,40},{64,48},{72,56},{80,... | collective-permute-start | bytes 393224 | tf_op jit(solution)/shard_map/ppermute | solution.py:38
  35.5 28.0 %all-to-all-start = ((f32[128,2,128]{2,1,0:T(2,128)}), f32[128,2,128]{2,1,0:T(2,128)S(1)}, u32[]{:S(2)}, u32[]{:S(2)}) async-start(f32[128,2,128]{2,1,0:T(2,128)} %bitcast.4), calls=%async_computation | async-start | bytes 262144 | tf_op jit(solution)/shard_map/all_to_all | solution.py:509
  52.2 11.3 %collective-permute-start.8 = (bf16[512,128]{1,0:T(8,128)(2,1)S(1)}, bf16[512,128]{1,0:T(8,128)(2,1)S(1)}, u32[]{:S(2)}, u32[]{:S(2)}) collective-permute-start(bf16[512,128]{1,0:T(8,128)(2,1)S(1)} %shard_map.122), channel_id=1, source_target_pairs={{16,0},{24,8},{32,16},{40,24},{48,32},{56,40},{64,48},{72,56},{80,... | collective-permute-start | bytes 393224 | tf_op jit(solution)/shard_map/ppermute | solution.py:38
